TPU v7x, 32 devices: a whole 2x2x4 slice. The times are simulated.
32 devices in a mesh: dp: 4 (over z), tensor: 4 (over y, x), seq: 2 (over core).
Axes of the slice: x: 2, y: 2, z: 4, core: 2. Of those that a mesh axis runs over, the one named last changes fastest.
Arguments:
- token_ids: int32 [4, 1024], P('dp', 'seq'), may hold values from 0 to 50303
- labels: int32 [4, 1024], P('dp', 'seq'), may hold values from 0 to 50303
- real_counts: int32 [8], P(('dp', 'seq')), may hold values from 1 to 512, as said below
- owners: int32 [179], replicated, may hold values from 0 to 3, as said below
- master: float32 [268, 384, 768], P('dp', ('tensor', 'seq')), may hold values from -0.4330127 to 0.4330127
- first_moment: float32 [268, 384, 768], P('dp', ('tensor', 'seq')), may hold values from -9.536743e-07 to 9.536743e-07
- second_moment: float32 [268, 384, 768], P('dp', ('tensor', 'seq')), may hold values from 4.9252455e-14 to 3.9780828e-13
- gains: float32 [5, 768], replicated, may hold values from 0.25 to 1.75
- gains_first: float32 [5, 768], replicated, may hold values from -9.536743e-06 to 9.536743e-06
- gains_second: float32 [5, 768], replicated, may hold values from 4.9252455e-12 to 3.9780828e-11
- mix: float32 [5], replicated, may hold values from -0.5 to 1.3
- mix_first: float32 [5], replicated, may hold values from -9.1552734e-05 to 9.1552734e-05
- mix_second: float32 [5], replicated, may hold values from 4.925245e-10 to 3.9780828e-09
Outputs:
- new_master: float32 [268, 384, 768], P('dp', ('tensor', 'seq'))
- new_first: float32 [268, 384, 768], P('dp', ('tensor', 'seq'))
- new_second: float32 [268, 384, 768], P('dp', ('tensor', 'seq'))
- new_gains: float32 [5, 768], replicated
- new_gains_first: float32 [5, 768], replicated
- new_gains_second: float32 [5, 768], replicated
- new_mix: float32 [5], replicated
- new_mix_first: float32 [5], replicated
- new_mix_second: float32 [5], replicated
- loss_sum: float32 [], replicated
- token_count: float32 [], replicated
- clip_norm: float32 [], replicated
Inputs may be any that keep to these rules, and one draw needn't show every extreme that they name: `owners`: each owner holds at most 67 row blocks and some owner holds exactly 67. `real_counts`: some device has all 512 tokens real.
All inputs are finite; a program needn't handle non-finite values.
Results may differ from a plain program's by a relative error of at most 0.023.
Values may be sent and summed in bfloat16 or wider, within the bound.
A program may use at most 384 MiB of HBM per device.

v0:
```python
from functools import partial

import jax
import jax.numpy as jnp
from jax import lax
from jax.sharding import PartitionSpec as P

D = 768
HEADS = 12
HEAD_DIM = 64
FF = 3072
VOCAB = 50304
LAYERS = 2
STEP_COUNT = 10
MIX_WEIGHTS = 5


EPS_NORM = 1e-05
CLIP_NORM = 0.01
BETA_ONE = 0.9
BETA_TWO = 0.95
ADAM_EPS = 1e-08
RATE_MATRIX = 0.04
RATE_SMALL = 0.4
DECAY_MATRIX = 0.1


def from_behind(block, axis, distance):
    devices = range(lax.axis_size(axis))
    route = [(i - distance, i) for i in devices if i - distance in devices]
    return lax.ppermute(block, axis, route)


def contract_last(left, right):
    return lax.dot_general(
        left, right, (((1,), (1,)), ((), ())), preferred_element_type=jnp.float32
    )


def contract_first(left, right):
    return lax.dot_general(
        left, right, (((0,), (0,)), ((), ())), preferred_element_type=jnp.float32
    )


def normalize(stream):
    center = stream - jnp.mean(stream, -1, keepdims=True)
    inverse = lax.rsqrt(jnp.mean(center * center, -1, keepdims=True) + EPS_NORM)
    return (center * inverse, inverse)


def norm_back(grad_normed, gain, scaled, inverse):
    grad_scaled = grad_normed * gain
    grad_stream = inverse * (
        grad_scaled
        - jnp.mean(grad_scaled, -1, keepdims=True)
        - scaled * jnp.mean(grad_scaled * scaled, -1, keepdims=True)
    )
    return (grad_stream, jnp.sum(grad_normed * scaled, axis=0))


def rotary(positions):
    steps_half = jnp.arange(HEAD_DIM // 2).astype(jnp.float32)
    freqs = 10000.0 ** (-2.0 * steps_half / HEAD_DIM)
    angles = positions.astype(jnp.float32)[:, None] * freqs[None, :]
    return (jnp.cos(angles)[:, None, :], jnp.sin(angles)[:, None, :])


def rotate(tensor, cosine, sine):
    first, second = jnp.split(tensor, 2, axis=-1)
    return jnp.concatenate(
        [first * cosine - second * sine, second * cosine + first * sine], axis=-1
    )


def slot_table(owners):
    ranks = jnp.arange(owners.shape[0])
    same = (owners[None, :] == owners[:, None]) & (ranks[None, :] < ranks[:, None])
    return jnp.sum(jnp.where(same, 1, 0), axis=1).astype(jnp.int32)


def branch_sum(term):
    return lax.psum(term, "tensor")


def input_sum(term):
    return lax.psum(term, "tensor")


def attention_scores(queries, keys_all, allowed):
    raw = jnp.einsum(
        "bqhd,bkhd->bhqk", queries, keys_all, preferred_element_type=jnp.float32
    ) * HEAD_DIM ** (-0.5)
    return jnp.where(allowed[None, None], raw, -1e30)


def layer_forward(stream, weights, gain_one, gain_two, geometry):
    qkv_w, out_w, up_w, down_w = weights
    cosine, sine, allowed, seq_count, half_len, local_heads = geometry
    width = local_heads * HEAD_DIM
    shape_four = (seq_count, half_len, local_heads, HEAD_DIM)
    scaled_one, inverse_one = normalize(stream)
    normed = (scaled_one * gain_one).astype(jnp.bfloat16)
    joined = contract_last(normed, qkv_w)
    queries = (
        rotate(joined[:, :width].reshape(-1, local_heads, HEAD_DIM), cosine, sine)
        .astype(jnp.bfloat16)
        .reshape(shape_four)
    )
    own_keys = (
        rotate(joined[:, width : 2 * width].reshape(-1, local_heads, HEAD_DIM), cosine, sine)
        .astype(jnp.bfloat16)
        .reshape(shape_four)
    )
    own_values = joined[:, 2 * width :].astype(jnp.bfloat16).reshape(shape_four)
    far_keys, far_values = from_behind((own_keys, own_values), "seq", 1)
    keys_all = jnp.concatenate([far_keys, own_keys], axis=1)
    values_all = jnp.concatenate([far_values, own_values], axis=1)
    scores = attention_scores(queries, keys_all, allowed)
    peak = jnp.max(scores, -1, keepdims=True)
    log_total = peak + jnp.log(jnp.sum(jnp.exp(scores - peak), -1, keepdims=True))
    probs = jnp.exp(scores - log_total).astype(jnp.bfloat16)
    attended = jnp.einsum("bhqk,bkhd->bqhd", probs, values_all, preferred_element_type=jnp.float32)
    attended = attended.astype(jnp.bfloat16).reshape(-1, width)
    inner = stream + branch_sum(jnp.dot(attended, out_w, preferred_element_type=jnp.float32))
    scaled_two, inverse_two = normalize(inner)
    normed_two = (scaled_two * gain_two).astype(jnp.bfloat16)
    hidden = contract_last(normed_two, up_w)
    activated = jax.nn.gelu(hidden, approximate=True).astype(jnp.bfloat16)
    outcome = inner + branch_sum(jnp.dot(activated, down_w, preferred_element_type=jnp.float32))
    kept = (
        scaled_one,
        inverse_one,
        normed,
        queries,
        keys_all,
        values_all,
        log_total,
        attended,
        scaled_two,
        inverse_two,
        normed_two,
        hidden,
        activated,
    )
    return (outcome, kept)


def layer_backward(grad_out, kept, weights, gain_one, gain_two, geometry):
    qkv_w, out_w, up_w, down_w = weights
    cosine, sine, allowed, seq_count, half_len, local_heads = geometry
    width = local_heads * HEAD_DIM
    (
        scaled_one,
        inverse_one,
        normed,
        queries,
        keys_all,
        values_all,
        log_total,
        attended,
        scaled_two,
        inverse_two,
        normed_two,
        hidden,
        activated,
    ) = kept
    grad_branch = grad_out.astype(jnp.bfloat16)
    grad_down = contract_first(activated, grad_branch)
    grad_act = contract_last(grad_branch, down_w)
    _, gelu_pull = jax.vjp(partial(jax.nn.gelu, approximate=True), hidden)
    grad_hidden = gelu_pull(grad_act)[0].astype(jnp.bfloat16)
    grad_up = contract_first(grad_hidden, normed_two)
    grad_normed_two = input_sum(jnp.dot(grad_hidden, up_w, preferred_element_type=jnp.float32))
    grad_inner, grad_gain_two = norm_back(grad_normed_two, gain_two, scaled_two, inverse_two)
    grad_inner = grad_out + grad_inner
    grad_attn = grad_inner.astype(jnp.bfloat16)
    grad_out_w = contract_first(attended, grad_attn)
    grad_attended = contract_last(grad_attn, out_w).astype(jnp.bfloat16)
    grad_attended = grad_attended.reshape(seq_count, half_len, local_heads, HEAD_DIM)
    probs = jnp.exp(attention_scores(queries, keys_all, allowed) - log_total)
    grad_probs = jnp.einsum(
        "bqhd,bkhd->bhqk", grad_attended, values_all, preferred_element_type=jnp.float32
    )
    grad_scores = (probs * (grad_probs - jnp.sum(probs * grad_probs, -1, keepdims=True))).astype(
        jnp.bfloat16
    )
    scale = HEAD_DIM ** (-0.5)
    grad_queries = (
        jnp.einsum("bhqk,bkhd->bqhd", grad_scores, keys_all, preferred_element_type=jnp.float32)
        * scale
    )
    grad_keys = (
        jnp.einsum("bhqk,bqhd->bkhd", grad_scores, queries, preferred_element_type=jnp.float32)
        * scale
    )
    grad_values = jnp.einsum(
        "bhqk,bqhd->bkhd",
        probs.astype(jnp.bfloat16),
        grad_attended,
        preferred_element_type=jnp.float32,
    )
    back_keys, back_values = (
        from_behind(grad_keys[:, :half_len].astype(jnp.bfloat16), "seq", -1).astype(jnp.float32),
        from_behind(grad_values[:, :half_len].astype(jnp.bfloat16), "seq", -1).astype(jnp.float32),
    )
    grad_keys = grad_keys[:, half_len:] + back_keys
    grad_values = grad_values[:, half_len:] + back_values
    grad_joined = jnp.concatenate(
        [
            rotate(grad_queries.reshape(-1, local_heads, HEAD_DIM), cosine, -sine).reshape(
                -1, width
            ),
            rotate(grad_keys.reshape(-1, local_heads, HEAD_DIM), cosine, -sine).reshape(-1, width),
            grad_values.reshape(-1, width),
        ],
        axis=1,
    ).astype(jnp.bfloat16)
    grad_qkv = contract_first(grad_joined, normed)
    grad_normed = input_sum(jnp.dot(grad_joined, qkv_w, preferred_element_type=jnp.float32))
    grad_stream, grad_gain_one = norm_back(grad_normed, gain_one, scaled_one, inverse_one)
    layer_grads = jnp.concatenate([grad_qkv, grad_out_w, grad_up, grad_down], axis=0)
    return (grad_inner + grad_stream, layer_grads, grad_gain_one, grad_gain_two)


def adam_update(weight, first, second, grad, rate, decay):
    first = BETA_ONE * first + (1.0 - BETA_ONE) * grad
    second = BETA_TWO * second + (1.0 - BETA_TWO) * grad * grad
    first_hat = first / (1.0 - BETA_ONE**STEP_COUNT)
    second_hat = second / (1.0 - BETA_TWO**STEP_COUNT)
    weight = weight - rate * (first_hat / (jnp.sqrt(second_hat) + ADAM_EPS) + decay * weight)
    return (weight, first, second)


def body(
    token_ids,
    labels,
    real_counts,
    owners,
    master,
    first_moment,
    second_moment,
    gains,
    gains_first,
    gains_second,
    mix,
    mix_first,
    mix_second,
):
    tensors = lax.axis_size("tensor")
    groups = lax.axis_size("dp")
    tensor_part = lax.axis_index("tensor")
    seq_part = lax.axis_index("seq")
    slabs = owners.shape[0]
    slots = master.shape[0]
    half_rows = master.shape[1]
    seq_count, half_len = token_ids.shape
    row_count = seq_count * half_len
    head_rows = 3 * D // tensors
    out_rows = D // tensors
    unit_rows = FF // tensors
    layer_rows = head_rows + out_rows + 2 * unit_rows
    vocab_rows = VOCAB // tensors
    local_heads = HEADS // tensors
    slot_rank = slot_table(owners)
    gather_rows = (
        (owners[:, None] * 2 + jnp.arange(2, dtype=jnp.int32)[None, :]) * slots + slot_rank[:, None]
    ).reshape(-1)
    gathered = lax.all_gather(master.astype(jnp.bfloat16), ("dp", "seq"), axis=0, tiled=True)
    table = jnp.take(gathered, gather_rows, axis=0).reshape(slabs * 2 * half_rows, D)
    weights_all = []
    for level in range(LAYERS):
        start = level * layer_rows
        weights_all.append(
            (
                table[start : start + head_rows],
                table[start + head_rows : start + head_rows + out_rows],
                table[start + head_rows + out_rows : start + head_rows + out_rows + unit_rows],
                table[start + head_rows + out_rows + unit_rows : start + layer_rows],
            )
        )
    embedding = table[LAYERS * layer_rows :]
    positions = seq_part * half_len + jnp.arange(row_count) % half_len
    cosine, sine = rotary(positions)
    query_pos = seq_part * half_len + jnp.arange(half_len)
    key_pos = jnp.concatenate([(seq_part - 1) * half_len + jnp.arange(half_len), query_pos])
    allowed = (key_pos[None, :] <= query_pos[:, None]) & (key_pos[None, :] >= 0)
    geometry = (cosine, sine, allowed, seq_count, half_len, local_heads)
    local_ids = token_ids.reshape(-1) - tensor_part * vocab_rows
    inside = (local_ids >= 0) & (local_ids < vocab_rows)
    clipped_ids = jnp.clip(local_ids, 0, vocab_rows - 1)
    looked = jnp.take(embedding, clipped_ids, axis=0).astype(jnp.float32)
    states = [branch_sum(jnp.where(inside[:, None], looked, 0.0))]
    stream = states[0]
    kept_all = []
    for level in range(LAYERS):
        outcome, kept = layer_forward(
            stream, weights_all[level], gains[2 * level], gains[2 * level + 1], geometry
        )
        kept_all.append(kept)
        states.append(outcome)
        base = (level + 1) * (level + 2) // 2 - 1
        stream = mix[base] * states[0]
        for source in range(1, level + 2):
            stream = stream + mix[base + source] * states[source]
    final_scaled, final_inverse = normalize(stream)
    final = (final_scaled * gains[2 * LAYERS]).astype(jnp.bfloat16)
    logits = contract_last(final, embedding)
    local_labels = labels.reshape(-1) - tensor_part * vocab_rows
    hits = jnp.arange(vocab_rows)[None, :] == local_labels[:, None]
    target = jnp.sum(jnp.where(hits, logits, 0.0), axis=1)
    peak = jnp.max(logits, axis=1)
    top = lax.pmax(peak, "tensor")
    spread, target = lax.psum((jnp.sum(jnp.exp(logits - top[:, None]), axis=1), target), "tensor")
    log_total = top + jnp.log(spread)
    keep = jnp.where(jnp.arange(row_count) < real_counts[0], 1.0, 0.0).astype(jnp.float32)
    loss_local = jnp.sum((log_total - target) * keep)
    grad_logits = (
        (jnp.exp(logits - log_total[:, None]) - jnp.where(hits, 1.0, 0.0)) * keep[:, None]
    ).astype(jnp.bfloat16)
    grad_table = contract_first(grad_logits, final)
    grad_final = input_sum(jnp.dot(grad_logits, embedding, preferred_element_type=jnp.float32))
    grad_top, grad_gain_final = norm_back(
        grad_final, gains[2 * LAYERS], final_scaled, final_inverse
    )
    grad_ys = [None] * (LAYERS + 1)
    grad_ys[LAYERS] = grad_top
    grad_mix = [jnp.zeros((), jnp.float32)] * MIX_WEIGHTS
    layer_grads = [None] * LAYERS
    gain_grads = [None] * (2 * LAYERS + 1)
    gain_grads[2 * LAYERS] = grad_gain_final
    for level in reversed(range(LAYERS)):
        block = level + 1
        grad_state = jnp.zeros_like(grad_top)
        for later in range(block, LAYERS + 1):
            base = later * (later + 1) // 2 - 1
            grad_mix[base + block] = jnp.sum(grad_ys[later] * states[block])
            grad_state = grad_state + mix[base + block] * grad_ys[later]
        grad_ys[level], layer_grads[level], gain_grads[2 * level], gain_grads[2 * level + 1] = (
            layer_backward(
                grad_state,
                kept_all[level],
                weights_all[level],
                gains[2 * level],
                gains[2 * level + 1],
                geometry,
            )
        )
    grad_start = grad_ys[0]
    for later in range(1, LAYERS + 1):
        base = later * (later + 1) // 2 - 1
        grad_mix[base] = jnp.sum(grad_ys[later] * states[0])
        grad_start = grad_start + mix[base] * grad_ys[later]
    grad_table = grad_table.at[clipped_ids].add(jnp.where(inside[:, None], grad_start, 0.0))
    grads = jnp.concatenate(layer_grads + [grad_table], axis=0)
    placed = (
        jnp.zeros((groups * 2 * slots, half_rows, D), jnp.float32)
        .at[gather_rows]
        .set(grads.reshape(slabs * 2, half_rows, D))
    )
    owned = lax.psum_scatter(
        placed.astype(jnp.bfloat16), ("dp", "seq"), scatter_dimension=0, tiled=True
    ).astype(jnp.float32)
    gain_grad = jnp.stack(gain_grads, axis=0)
    mix_grad = jnp.stack(grad_mix, axis=0)
    squares, gain_total, mix_total, loss_sum, token_count = lax.psum(
        (
            jnp.sum(owned * owned),
            gain_grad / tensors,
            mix_grad / tensors,
            loss_local / tensors,
            real_counts[0].astype(jnp.float32) / tensors,
        ),
        ("dp", "tensor", "seq"),
    )
    clip_norm = (
        jnp.sqrt(squares + jnp.sum(gain_total * gain_total) + jnp.sum(mix_total * mix_total))
        / token_count
    )
    factor = jnp.minimum(1.0, CLIP_NORM / clip_norm) / token_count
    new_master, new_first, new_second = adam_update(
        master, first_moment, second_moment, owned * factor, RATE_MATRIX, DECAY_MATRIX
    )
    new_gains, new_gains_first, new_gains_second = adam_update(
        gains, gains_first, gains_second, gain_total * factor, RATE_SMALL, 0.0
    )
    new_mix, new_mix_first, new_mix_second = adam_update(
        mix, mix_first, mix_second, mix_total * factor, RATE_SMALL, 0.0
    )
    return (
        new_master,
        new_first,
        new_second,
        new_gains,
        new_gains_first,
        new_gains_second,
        new_mix,
        new_mix_first,
        new_mix_second,
        loss_sum,
        token_count,
        clip_norm,
    )


def solution(mesh):
    return jax.shard_map(
        body,
        mesh=mesh,
        in_specs=(
            P("dp", "seq"),
            P("dp", "seq"),
            P(("dp", "seq")),
            P(),
            P("dp", ("tensor", "seq"), None),
            P("dp", ("tensor", "seq"), None),
            P("dp", ("tensor", "seq"), None),
            P(),
            P(),
            P(),
            P(),
            P(),
            P(),
        ),
        out_specs=(
            P("dp", ("tensor", "seq"), None),
            P("dp", ("tensor", "seq"), None),
            P("dp", ("tensor", "seq"), None),
            P(),
            P(),
            P(),
            P(),
            P(),
            P(),
            P(),
            P(),
            P(),
        ),
        check_vma=False,
    )
```

profile of v0, /device:TPU:0, one launch (start us, length us, event | category | flops | bytes accessed | tf_op | source)
XLA Modules:
  0.0 1922.6 jit_solution(10662195518384408846)
XLA Ops:
  7.2 6.6 convert_element_type.157
  15.9 339.9 %all-gather.2.cloned.1.call-done = bf16[536,48,768]{2,1,0:T(8,128)(2,1)} async-done(((bf16[67,48,768]{2,1,0:T(8,128)(2,1)}), bf16[536,48,768]{2,1,0:T(8,128)(2,1)}) %all-gather.2.cloned.1.call-update) | async-done | bytes 39518224 | tf_op jit(solution)/shard_map/all_gather | solution.py:269
  355.8 19.0 gather_fusion
  374.7 18.3 broadcast_select_fusion
  393.0 17.1 slice.188
  410.1 11.4 gather_fusion.1
  424.5 2.7 fusion.101
  427.2 55.5 %all-reduce.14.cloned.1.call-done = f32[512,768]{1,0:T(8,128)} async-done(((f32[512,768]{1,0:T(8,128)}), f32[512,768]{1,0:T(8,128)}) %all-reduce.14.cloned.1.call-update) | async-done | bytes 1572880 | tf_op jit(solution)/shard_map/psum | solution.py:83
  498.7 4.2 fusion.99
  503.0 56.8 %all-reduce.16.cloned.1.call-done = f32[512,768]{1,0:T(8,128)} async-done(((f32[512,768]{1,0:T(8,128)}), f32[512,768]{1,0:T(8,128)}) %all-reduce.16.cloned.1.call-update) | async-done | bytes 1572880 | tf_op jit(solution)/shard_map/psum | solution.py:83
  567.3 59.8 %all-reduce.18.cloned.1.call-done = f32[512,768]{1,0:T(8,128)} async-done(((f32[512,768]{1,0:T(8,128)}), f32[512,768]{1,0:T(8,128)}) %all-reduce.18.cloned.1.call-update) | async-done | bytes 1572880 | tf_op jit(solution)/shard_map/psum | solution.py:83
  627.1 4.6 fusion.97
  646.9 61.0 %all-reduce.20.cloned.1.call-done = f32[512,768]{1,0:T(8,128)} async-done(((f32[512,768]{1,0:T(8,128)}), f32[512,768]{1,0:T(8,128)}) %all-reduce.20.cloned.1.call-update) | async-done | bytes 1572880 | tf_op jit(solution)/shard_map/psum | solution.py:83
  718.7 58.0 %all-reduce.22.cloned.1.call-done = f32[512,768]{1,0:T(8,128)} async-done(((f32[512,768]{1,0:T(8,128)}), f32[512,768]{1,0:T(8,128)}) %all-reduce.22.cloned.1.call-update) | async-done | bytes 1572880 | tf_op jit(solution)/shard_map/psum | solution.py:83
  776.7 5.4 fusion.95
  783.6 19.6 %fusion.105 = (f32[512]{0:T(512)S(1)}, f32[512,12576]{0,1:T(8,128)}) fusion(bf16[12576,768]{1,0:T(8,128)(2,1)} %bitcast.161, f32[512,768]{1,0:T(8,128)} %copy-done.19, f32[768]{0:T(1024)S(1)} %get-tuple-element.37, f32[512]{0:T(512)S(1)} %add_rsqrt_fusion, f32[512]{0:T(512)S(1)} %broadcast_multiply_fusion.11), kind=kOutput, calls=%fused_computation.295 | convolution fusion | flops 9898180608 | bytes 46654464 | tf_op jit(solution)/shard_map/dot_general | solution.py:35
  803.2 8.9 pmax.7
  812.2 11.8 select_reduce_fusion
  824.0 9.0 all-reduce.2
  834.2 22.1 %fusion.90 = f32[512,768]{1,0:T(8,128)} fusion(bf16[12576,768]{1,0:T(8,128)(2,1)} %bitcast.162, f32[512,12576]{0,1:T(8,128)} %get-tuple-element.123, f32[512]{0:T(512)S(1)} %copy-done.135, s32[512]{0:T(512)S(1)} %bitcast.210, f32[512]{0:T(512)S(1)} %get-tuple-element.59), kind=kOutput, calls=%fused_computation.284 | convolution fusion | flops 9928802304 | bytes 46651392 | tf_op jit(solution)/shard_map/dot_general | solution.py:322
  856.4 61.1 %all-reduce.24.cloned.1.call-done = f32[512,768]{1,0:T(8,128)} async-done(((f32[512,768]{1,0:T(8,128)}), f32[512,768]{1,0:T(8,128)}) %all-reduce.24.cloned.1.call-update) | async-done | bytes 1572880 | tf_op jit(solution)/shard_map/psum | solution.py:87
  917.4 2.8 multiply_reduce_fusion.7
  927.3 61.0 %all-reduce.26.cloned.1.call-done = f32[512,768]{1,0:T(8,128)} async-done(((f32[512,768]{1,0:T(8,128)}), f32[512,768]{1,0:T(8,128)}) %all-reduce.26.cloned.1.call-update) | async-done | bytes 1572880 | tf_op jit(solution)/shard_map/psum | solution.py:87
  988.3 3.3 multiply_reduce_fusion.8
  991.6 3.2 multiply_add_fusion.4
  1011.7 61.0 %all-reduce.28.cloned.1.call-done = f32[512,768]{1,0:T(8,128)} async-done(((f32[512,768]{1,0:T(8,128)}), f32[512,768]{1,0:T(8,128)}) %all-reduce.28.cloned.1.call-update) | async-done | bytes 1572880 | tf_op jit(solution)/shard_map/psum | solution.py:87
  1072.7 3.3 multiply_reduce_fusion.9
  1076.1 4.7 fusion.33
  1085.9 28.2 %fusion.86 = f32[12576,768]{1,0:T(8,128)} fusion(f32[512,768]{1,0:T(8,128)} %copy-done.19, f32[768]{0:T(1024)S(1)} %get-tuple-element.37, f32[512]{0:T(512)S(1)} %copy-done.119, f32[512]{0:T(512)S(1)} %copy-done.113, f32[512,12576]{0,1:T(8,128)} %get-tuple-element.123, f32[512]{0:T(512)S(1)} %copy-done.136, s32[512]{0:T(512)S(1)} %bitcast.211, ...), kind=kOutput, calls=%fused_computation.280 | convolution fusion | flops 9930375168 | bytes 65975296 | tf_op jit(solution)/shard_map/dot_general | solution.py:41
  1114.1 32.2 %all-reduce.30.cloned.1.call-done = f32[512,768]{1,0:T(8,128)} async-done(((f32[512,768]{1,0:T(8,128)}), f32[512,768]{1,0:T(8,128)}) %all-reduce.30.cloned.1.call-update) | async-done | bytes 1572880 | tf_op jit(solution)/shard_map/psum | solution.py:87
  1146.3 3.3 multiply_reduce_fusion.10
  1149.6 3.9 multiply_add_fusion.1
  1154.0 5.3 convolution_bitcast_fusion
  1160.7 2.5 multiply_reduce_fusion
  1173.4 3.2 convolution_dynamic-update-slice_fusion.5
  1189.7 3.2 convolution_dynamic-update-slice_fusion
  1192.9 40.9 %all-reduce.32.cloned.1.call-done = f32[512,768]{1,0:T(8,128)} async-done(((f32[512,768]{1,0:T(8,128)}), f32[512,768]{1,0:T(8,128)}) %all-reduce.32.cloned.1.call-update) | async-done | bytes 1572880 | tf_op jit(solution)/shard_map/psum | solution.py:87
  1233.8 4.4 multiply_reduce_fusion.2
  1240.6 30.4 %scatter_custom_fusion = f32[12576,768]{1,0:T(8,128)} fusion(f32[12576,768]{1,0:T(8,128)} %fusion.86, s32[512]{0:T(512)} %bitcast.213, f32[512,768]{1,0:T(8,128)} %multiply_add_fusion, f32[512,768]{1,0:T(8,128)S(1)} %subtract_multiply_fusion, f32[]{:T(128)} %bitcast.12, f32[]{:T(128)} %constant.60.clone.1, pred[512]{0:T(512)(128)(4,1)S(1)} %copy-done.134), kind=kCustom, calls=%fused_computation.66 | custom fusion | flops 1572864 | bytes 41780736 | tf_op jit(solution)/shard_map/scatter-add | solution.py:354
  1271.1 27.4 %constant_dynamic-update-slice_fusion = f32[17184,768]{1,0:T(8,128)} fusion(f32[17184,768]{1,0:T(8,128)} %convolution_dynamic-update-slice_fusion, f32[12576,768]{1,0:T(8,128)} %scatter_custom_fusion), kind=kLoop, calls=%fused_computation.198 | loop fusion | bytes 77266944 | tf_op jit(solution)/shard_map/concatenate | solution.py:355
  1298.4 25.0 %broadcast_in_dim.88 = f32[536,48,768]{2,1,0:T(8,128)} broadcast(f32[]{:T(128)} %constant.60.clone.1), dimensions={} | broadcast | bytes 79036416 | tf_op jit(solution)/shard_map/broadcast_in_dim | solution.py:357
  1323.5 95.8 %scatter_fusion = f32[536,48,768]{2,1,0:T(8,128)} fusion(f32[536,48,768]{2,1,0:T(8,128)} %broadcast_in_dim.88, s32[358]{0:T(512)S(1)} %copy-done.121, f32[358,48,768]{2,1,0:T(8,128)} %bitcast.159), kind=kCustom, calls=%fused_computation.3 | custom fusion | bytes 158369184 | tf_op jit(solution)/shard_map/scatter | solution.py:359
  1419.3 37.9 %convert_element_type.191 = bf16[536,48,768]{2,1,0:T(8,128)(2,1)} convert(f32[536,48,768]{2,1,0:T(8,128)} %scatter_fusion) | non-fusion elementwise | flops 19759104 | bytes 118554624 | tf_op jit(solution)/shard_map/convert_element_type | solution.py:362
  1458.0 3.3 stack.47
  1461.4 377.8 %reduce-scatter.4.cloned.1.call-done = bf16[67,48,768]{2,1,0:T(8,128)(2,1)} async-done(((bf16[536,48,768]{2,1,0:T(8,128)(2,1)}), bf16[67,48,768]{2,1,0:T(8,128)(2,1)}) %reduce-scatter.4.cloned.1.call-update) | async-done | bytes 4939792
  1839.2 5.5 fusion.2
  1844.7 38.4 %all-reduce.1 = (f32[]{:T(128)}, f32[]{:T(128)}, f32[5,768]{1,0:T(8,128)S(1)}, f32[5]{0:T(128)S(1)}, f32[]{:T(128)}) all-reduce(f32[]{:T(128)S(6)} %div.151, f32[]{:T(128)} %fusion.2, f32[5,768]{1,0:T(8,128)S(1)} %broadcast_multiply_fusion, ...), channel_id=1, replica_groups=mesh['dp'=4,'tensor'=4,'seq'=2] {'dp','tensor','seq'}, use_global_device_ids=true, to_apply=%region_44.45 | all-reduce | flops 3848 | bytes 30784 | tf_op jit(solution)/shard_map/psum | solution.py:366
  1889.6 24.8 %multiply_subtract_fusion = (f32[67,48,768]{2,1,0:T(8,128)}, f32[67,48,768]{2,1,0:T(8,128)}, f32[67,48,768]{2,1,0:T(8,128)}) fusion(f32[67,48,768]{2,1,0:T(8,128)} %param.17, f32[]{:T(128)S(6)} %div.156, bf16[67,48,768]{2,1,0:T(8,128)(2,1)} %reduce-scatter.4.cloned.1.call-done, f32[67,48,768]{2,1,0:T(8,128)} %param.18, f32[67,48,768]{2,1,0:T(8,128)} %param.19), kind=kLoop, calls=%fused_computation.16 | loop fusion | flops 41988096 | bytes 64217092 | tf_op jit(solution)/shard_map/sub | solution.py:231
  (470 shorter events, 114.2 us)
Async XLA Ops:
  7.2 348.6 %all-gather.2.cloned.1.call-start = ((), (), s32[]{:S(2)}) async-start(), calls=%async_computation.1 | async-start | bytes 44457984 | tf_op jit(solution)/shard_map/all_gather | solution.py:269
  13.9 468.9 %all-reduce.14.cloned.1.call-start = ((), (), s32[]{:S(2)}) async-start(), calls=%async_computation.2 | async-start | bytes 3145728 | tf_op jit(solution)/shard_map/psum | solution.py:83
  15.2 359.6 %copy-start.131 = (s32[512,1]{0,1:T(1,128)}, s32[512,1]{0,1:T(1,128)S(1)}, u32[]{:S(2)}) copy-start(s32[512,1]{0,1:T(1,128)S(1)} %get-tuple-element.72) | copy-start | bytes 6148
  15.8 405.7 %copy-start.133 = (pred[512]{0:T(512)(128)(4,1)}, pred[512]{0:T(512)(128)(4,1)S(1)}, u32[]{:S(2)}) copy-start(pred[512]{0:T(512)(128)(4,1)S(1)} %and_reduce_fusion) | copy-start | bytes 1540
  423.0 136.8 %all-reduce.16.cloned.1.call-start = ((), (), s32[]{:S(2)}) async-start(), calls=%async_computation.3 | async-start | bytes 3145728 | tf_op jit(solution)/shard_map/psum | solution.py:83
  423.2 61.8 %copy-start.93 = (f32[768]{0:T(1024)}, f32[768]{0:T(1024)S(1)}, u32[]{:S(2)}) copy-start(f32[768]{0:T(1024)S(1)} %get-tuple-element.41) | copy-start | bytes 9220
  424.1 61.7 %copy-start.67 = (f32[512,32]{0,1:T(8,128)}, f32[512,32]{0,1:T(8,128)S(1)}, u32[]{:S(2)}) copy-start(f32[512,32]{0,1:T(8,128)S(1)} %get-tuple-element.111) | copy-start | bytes 196612
  424.5 69.9 %copy-start.12 = (pred[512,1024]{1,0:T(8,128)(4,1)}, pred[512,1024]{1,0:T(8,128)(4,1)S(1)}, u32[]{:S(2)}) copy-start(pred[512,1024]{1,0:T(8,128)(4,1)S(1)} %compare_and_fusion) | copy-start | bytes 1572868
  427.2 57.7 %copy-start.29 = (bf16[12,48,768]{2,1,0:T(8,128)(2,1)}, bf16[12,48,768]{2,1,0:T(8,128)(2,1)S(1)}, u32[]{:S(2)}) copy-start(bf16[12,48,768]{2,1,0:T(8,128)(2,1)S(1)} %get-tuple-element.81) | copy-start | bytes 2654212
  486.1 5.1 collective-permute-start
  489.7 4.8 collective-permute-start.1
  498.7 128.4 %all-reduce.18.cloned.1.call-start = ((), (), s32[]{:S(2)}) async-start(), calls=%async_computation.4 | async-start | bytes 3145728 | tf_op jit(solution)/shard_map/psum | solution.py:83
  503.0 58.8 %copy-start.35 = (bf16[16,48,768]{2,1,0:T(8,128)(2,1)}, bf16[16,48,768]{2,1,0:T(8,128)(2,1)S(1)}, u32[]{:S(2)}) copy-start(bf16[16,48,768]{2,1,0:T(8,128)(2,1)S(1)} %get-tuple-element.77) | copy-start | bytes 3538948
  561.4 588.2 %copy-start.99 = (f32[512]{0:T(512)}, f32[512]{0:T(512)S(1)}, u32[]{:S(2)}) copy-start(f32[512]{0:T(512)S(1)} %broadcast_multiply_fusion.14) | copy-start | bytes 6148
  566.0 141.8 %all-reduce.20.cloned.1.call-start = ((), (), s32[]{:S(2)}) async-start(), calls=%async_computation.5 | async-start | bytes 3145728 | tf_op jit(solution)/shard_map/psum | solution.py:83
  631.7 76.2 %copy-start.1 = (f32[512,768]{1,0:T(8,128)}, f32[512,768]{1,0:T(8,128)S(1)}, u32[]{:S(2)}) copy-start(f32[512,768]{1,0:T(8,128)S(1)} %get-tuple-element.68) | copy-start | bytes 4718596
  631.7 444.3 %copy-start.97 = (f32[512]{0:T(512)}, f32[512]{0:T(512)S(1)}, u32[]{:S(2)}) copy-start(f32[512]{0:T(512)S(1)} %broadcast_multiply_fusion.13) | copy-start | bytes 6148
  632.0 444.0 %copy-start.105 = (f32[512]{0:T(512)}, f32[512]{0:T(512)S(1)}, u32[]{:S(2)}) copy-start(f32[512]{0:T(512)S(1)} %add_rsqrt_fusion.2) | copy-start | bytes 6148
  635.3 3.4 collective-permute-start.3
  637.1 4.8 collective-permute-start.2
  646.8 129.9 %all-reduce.22.cloned.1.call-start = ((), (), s32[]{:S(2)}) async-start(), calls=%async_computation.6 | async-start | bytes 3145728 | tf_op jit(solution)/shard_map/psum | solution.py:83
  709.6 282.0 %copy-start.101 = (f32[512]{0:T(512)}, f32[512]{0:T(512)S(1)}, u32[]{:S(2)}) copy-start(f32[512]{0:T(512)S(1)} %broadcast_multiply_fusion.12) | copy-start | bytes 6148
  715.7 61.1 %copy-start.10 = (f32[512,768]{1,0:T(8,128)S(1)}, f32[512,768]{1,0:T(8,128)}, u32[]{:S(2)}) copy-start(f32[512,768]{1,0:T(8,128)} %copy-done.9) | copy-start | bytes 4718596
  715.7 201.7 %all-reduce.24.cloned.1.call-start = ((), (), s32[]{:S(2)}) async-start(), calls=%async_computation.7 | async-start | bytes 3145728 | tf_op jit(solution)/shard_map/psum | solution.py:87
  782.1 21.1 %copy-start.112 = (f32[512]{0:T(512)}, f32[512]{0:T(512)S(1)}, u32[]{:S(2)}) copy-start(f32[512]{0:T(512)S(1)} %broadcast_multiply_fusion.11) | copy-start | bytes 6148
  783.6 19.7 %copy-start.118 = (f32[512]{0:T(512)}, f32[512]{0:T(512)S(1)}, u32[]{:S(2)}) copy-start(f32[512]{0:T(512)S(1)} %add_rsqrt_fusion) | copy-start | bytes 6148
  783.6 28.6 %copy-start.129 = (s32[1,512]{1,0:T(1,128)S(1)}, s32[1,512]{1,0:T(1,128)}, u32[]{:S(2)}) copy-start(s32[1,512]{1,0:T(1,128)} %broadcast_subtract_fusion) | copy-start | bytes 6148
  812.2 22.0 %copy-start.135 = (f32[512]{0:T(512)S(1)}, f32[512]{0:T(512)}, u32[]{:S(2)}) copy-start(f32[512]{0:T(512)} %fusion.61) | copy-start | bytes 6148
  856.3 61.1 %copy-start.20 = (f32[512,768]{1,0:T(8,128)S(1)}, f32[512,768]{1,0:T(8,128)}, u32[]{:S(2)}) copy-start(f32[512,768]{1,0:T(8,128)} %copy-done.19) | copy-start | bytes 4718596
  856.3 131.9 %all-reduce.26.cloned.1.call-start = ((), (), s32[]{:S(2)}) async-start(), calls=%async_computation.8 | async-start | bytes 3145728 | tf_op jit(solution)/shard_map/psum | solution.py:87
  927.2 145.5 %all-reduce.28.cloned.1.call-start = ((), (), s32[]{:S(2)}) async-start(), calls=%async_computation.9 | async-start | bytes 3145728 | tf_op jit(solution)/shard_map/psum | solution.py:87
  998.2 10.4 collective-permute-start.5
  1004.8 3.5 collective-permute-start.4
  1011.7 134.6 %all-reduce.30.cloned.1.call-start = ((), (), s32[]{:S(2)}) async-start(), calls=%async_computation.10 | async-start | bytes 3145728 | tf_op jit(solution)/shard_map/psum | solution.py:87
  1085.3 61.0 %copy-start.108 = (f32[512]{0:T(512)S(1)}, f32[512]{0:T(512)}, u32[]{:S(2)}) copy-start(f32[512]{0:T(512)} %copy-done.107) | copy-start | bytes 6148
  1085.3 148.5 %all-reduce.32.cloned.1.call-start = ((), (), s32[]{:S(2)}) async-start(), calls=%async_computation.11 | async-start | bytes 3145728 | tf_op jit(solution)/shard_map/psum | solution.py:87
  1159.4 10.2 collective-permute-start.7
  1165.9 3.5 collective-permute-start.6
  1172.7 666.5 %reduce-scatter.4.cloned.1.call-start = ((), (), s32[]{:S(2)}) async-start(), calls=%async_computation.12 | async-start | bytes 44457984
  1189.7 44.0 %copy-start.104 = (f32[512]{0:T(512)S(1)}, f32[512]{0:T(512)}, u32[]{:S(2)}) copy-start(f32[512]{0:T(512)} %copy-done.103) | copy-start | bytes 6148
  1189.7 44.0 %copy-start.115 = (f32[512]{0:T(512)S(1)}, f32[512]{0:T(512)}, u32[]{:S(2)}) copy-start(f32[512]{0:T(512)} %copy-done.114) | copy-start | bytes 6148
  1298.4 25.0 %copy-start.121 = (s32[358]{0:T(512)S(1)}, s32[358]{0:T(512)}, u32[]{:S(2)}) copy-start(s32[358]{0:T(512)} %copy-done.120) | copy-start | bytes 4300
  1461.3 427.0 %copy-start.123 = (f32[5]{0:T(128)S(1)}, f32[5]{0:T(128)}, u32[]{:S(2)}) copy-start(f32[5]{0:T(128)} %param.23) | copy-start | bytes 64
  1461.4 427.0 %copy-start.138 = (f32[5]{0:T(128)S(1)}, f32[5]{0:T(128)}, u32[]{:S(2)}) copy-start(f32[5]{0:T(128)} %param.24) | copy-start | bytes 64
  1461.4 427.0 %copy-start.139 = (f32[5]{0:T(128)S(1)}, f32[5]{0:T(128)}, u32[]{:S(2)}) copy-start(f32[5]{0:T(128)} %param.25) | copy-start | bytes 64
  1461.4 427.6 %copy-start.96 = (f32[5,768]{1,0:T(8,128)S(1)}, f32[5,768]{1,0:T(8,128)}, u32[]{:S(2)}) copy-start(f32[5,768]{1,0:T(8,128)} %param.20) | copy-start | bytes 46084
  1461.4 427.6 %copy-start.116 = (f32[5,768]{1,0:T(8,128)S(1)}, f32[5,768]{1,0:T(8,128)}, u32[]{:S(2)}) copy-start(f32[5,768]{1,0:T(8,128)} %param.21) | copy-start | bytes 46084
  1461.4 427.6 %copy-start.117 = (f32[5,768]{1,0:T(8,128)S(1)}, f32[5,768]{1,0:T(8,128)}, u32[]{:S(2)}) copy-start(f32[5,768]{1,0:T(8,128)} %param.22) | copy-start | bytes 46084
  (122 other events, 327.0 us)
Sparse Core Ops, SparseCore 0:
  14.0 341.7 all-gather.1
  423.1 59.6 all-reduce.13
  498.8 60.8 all-reduce.15
  566.2 60.8 all-reduce.17
  646.9 60.8 all-reduce.19
  715.8 60.8 all-reduce.21
  856.4 60.9 all-reduce.23
  927.3 60.8 all-reduce.25
  1011.8 60.8 all-reduce.27
  1085.4 60.8 all-reduce.29
  1172.8 60.8 all-reduce.31
  1457.4 381.7 reduce-scatter.3
where the time goes:
time: 1930 us; the launch traced here: 1920 us
  waiting for transfers between devices  1270 us (66%)
  local copies, waits for them, and re-layouts  229 us (12%)
  other arithmetic  200 us (10%)
  matrix products  133 us (7%)
  blocking collectives  56.3 us (3%)
  between operations  23 us (1%)
    unnamed x13, waiting for transfers between devices  378 us
    all_gather x1, waiting for transfers between devices, body(): lax.all_gather(master.astype(jnp.bfloat16), ('dp', 'seq'), axis=0, tiled=...  340 us
    psum x5, waiting for transfers between devices, branch_sum(): return lax.psum(term, 'tensor')  291 us
    psum x5, waiting for transfers between devices, input_sum(): return lax.psum(term, 'tensor')  256 us
    scatter x1, local copies, waits for them, and re-layouts, body(): placed = jnp.zeros((groups * 2 * slots, half_rows, D), jnp.float32).at[ga...  95.8 us
    dot_general x9, matrix products, contract_first(): lax.dot_general(left, right, (((0,), (0,)), ((), ())), preferred_element_...  46 us
  transfers between devices with their start and end apart: 20, of which 14 were waited for; matrix products, arithmetic and copies ran while one was open for 4% of the time, Pallas kernels for 0%

commit v1 on v0

v1 whole, which is shorter than its diff:
```python
from functools import partial

import jax
import jax.numpy as jnp
from jax import lax
from jax.experimental import pallas as pl
from jax.experimental.pallas import tpu as pltpu
from jax.sharding import PartitionSpec as P

D = 768
HEADS = 12
HEAD_DIM = 64
FF = 3072
VOCAB = 50304
LAYERS = 2
STEP_COUNT = 10
MIX_WEIGHTS = 5


EPS_NORM = 1e-05
CLIP_NORM = 0.01
BETA_ONE = 0.9
BETA_TWO = 0.95
ADAM_EPS = 1e-08
RATE_MATRIX = 0.04
RATE_SMALL = 0.4
DECAY_MATRIX = 0.1


def from_behind(block, axis, distance):
    devices = range(lax.axis_size(axis))
    route = [(i - distance, i) for i in devices if i - distance in devices]
    return lax.ppermute(block, axis, route)


def contract_last(left, right):
    return lax.dot_general(
        left, right, (((1,), (1,)), ((), ())), preferred_element_type=jnp.float32
    )


def contract_first(left, right):
    return lax.dot_general(
        left, right, (((0,), (0,)), ((), ())), preferred_element_type=jnp.float32
    )


def normalize(stream):
    center = stream - jnp.mean(stream, -1, keepdims=True)
    inverse = lax.rsqrt(jnp.mean(center * center, -1, keepdims=True) + EPS_NORM)
    return (center * inverse, inverse)


def norm_back(grad_normed, gain, scaled, inverse):
    grad_scaled = grad_normed * gain
    grad_stream = inverse * (
        grad_scaled
        - jnp.mean(grad_scaled, -1, keepdims=True)
        - scaled * jnp.mean(grad_scaled * scaled, -1, keepdims=True)
    )
    return (grad_stream, jnp.sum(grad_normed * scaled, axis=0))


def rotary(positions):
    steps_half = jnp.arange(HEAD_DIM // 2).astype(jnp.float32)
    freqs = 10000.0 ** (-2.0 * steps_half / HEAD_DIM)
    angles = positions.astype(jnp.float32)[:, None] * freqs[None, :]
    return (jnp.cos(angles)[:, None, :], jnp.sin(angles)[:, None, :])


def rotate(tensor, cosine, sine):
    first, second = jnp.split(tensor, 2, axis=-1)
    return jnp.concatenate(
        [first * cosine - second * sine, second * cosine + first * sine], axis=-1
    )


def slot_table(owners):
    ranks = jnp.arange(owners.shape[0])
    same = (owners[None, :] == owners[:, None]) & (ranks[None, :] < ranks[:, None])
    return jnp.sum(jnp.where(same, 1, 0), axis=1).astype(jnp.int32)


def attention_scores(queries, keys_all, allowed):
    raw = jnp.einsum(
        "bqhd,bkhd->bhqk", queries, keys_all, preferred_element_type=jnp.float32
    ) * HEAD_DIM ** (-0.5)
    return jnp.where(allowed[None, None], raw, -1e30)


def adam_update(weight, first, second, grad, rate, decay):
    first = BETA_ONE * first + (1.0 - BETA_ONE) * grad
    second = BETA_TWO * second + (1.0 - BETA_TWO) * grad * grad
    first_hat = first / (1.0 - BETA_ONE**STEP_COUNT)
    second_hat = second / (1.0 - BETA_TWO**STEP_COUNT)
    weight = weight - rate * (first_hat / (jnp.sqrt(second_hat) + ADAM_EPS) + decay * weight)
    return (weight, first, second)


MESH = pl.DeviceIdType.MESH
ROW_STEP = 256
TILE_GROUPS = 4
LANES = 128


def meet(peers):
    gate = pltpu.get_barrier_semaphore()
    for peer in peers:
        pl.semaphore_signal(gate, inc=1, device_id=peer, device_id_type=MESH)
    pl.semaphore_wait(gate, len(peers))


def others(axis):
    count, me = lax.axis_size(axis), lax.axis_index(axis)
    return [lax.rem(me + step, count) for step in range(1, count)]


def behind(axis, step):
    count, me = lax.axis_size(axis), lax.axis_index(axis)
    return lax.rem(me + count - step, count)


def send(source, target, send_sem, recv_sem, device):
    copy = pltpu.make_async_remote_copy(
        src_ref=source,
        dst_ref=target,
        send_sem=send_sem,
        recv_sem=recv_sem,
        device_id=device,
        device_id_type=MESH,
    )
    copy.start()
    return copy


def layer_norm_parts(stream):
    center = stream - jnp.mean(stream, -1, keepdims=True)
    inverse = lax.rsqrt(jnp.mean(center * center, -1, keepdims=True) + EPS_NORM)
    return center * inverse, inverse


def norm_pull(grad_normed, gain, stream):
    scaled, inverse = layer_norm_parts(stream)
    grad_scaled = grad_normed * gain
    grad_stream = inverse * (
        grad_scaled
        - jnp.mean(grad_scaled, -1, keepdims=True)
        - scaled * jnp.mean(grad_scaled * scaled, -1, keepdims=True)
    )
    return grad_stream, jnp.sum(grad_normed * scaled, axis=0, keepdims=True)


def tensor_step(name, function, partial, extras, scalars, outs, gather, collective_id):
    parts = lax.axis_size("tensor")
    share = extras[0].shape[0]
    reduce = partial is not None

    def kernel(*refs):
        refs = list(refs)
        partial_ref = refs.pop(0) if reduce else None
        extra_refs = [refs.pop(0) for _ in extras]
        scalar_refs = [refs.pop(0) for _ in scalars]
        out_refs = [refs.pop(0) for _ in outs]
        full = refs.pop(0) if gather else None
        outgoing = refs.pop(0) if reduce else None
        arrived = refs.pop(0) if reduce else None
        send_sems, recv_sems = refs
        me = lax.axis_index("tensor")
        peers = others("tensor")
        meet([{"tensor": peer} for peer in peers])
        total = None
        if reduce:
            copies = []
            for step, peer in enumerate(peers):
                rows = pl.ds(pl.multiple_of(peer * share, share), share)
                outgoing[step] = partial_ref[rows, :].astype(jnp.bfloat16)
                copies.append(
                    send(
                        outgoing.at[step],
                        arrived.at[step],
                        send_sems.at[0, step],
                        recv_sems.at[0, step],
                        {"tensor": peer},
                    )
                )
            total = partial_ref[pl.ds(pl.multiple_of(me * share, share), share), :]
            for step, copy in enumerate(copies):
                copy.wait()
                total = total + arrived[step].astype(jnp.float32)
        results = function(total, *[ref[...] for ref in extra_refs], *scalar_refs)
        for ref, value in zip(out_refs, results):
            ref[...] = value.astype(ref.dtype)
        if gather:
            full[me] = results[len(outs)].astype(jnp.bfloat16)
            copies = [
                send(
                    full.at[me],
                    full.at[me],
                    send_sems.at[1, step],
                    recv_sems.at[1, step],
                    {"tensor": peer},
                )
                for step, peer in enumerate(peers)
            ]
            for copy in copies:
                copy.wait()

    vmem = pl.BlockSpec(memory_space=pltpu.VMEM)
    smem = pl.BlockSpec(memory_space=pltpu.SMEM)
    shapes = [jax.ShapeDtypeStruct(shape, dtype) for shape, dtype in outs]
    if gather:
        shapes.append(jax.ShapeDtypeStruct((parts, share, D), jnp.bfloat16))
    buffers = [pltpu.VMEM((parts - 1, share, D), jnp.bfloat16)] * (2 if reduce else 0)
    operands = ([partial] if reduce else []) + list(extras) + list(scalars)
    return pl.pallas_call(
        kernel,
        name=name,
        out_shape=shapes,
        in_specs=[vmem] * (len(operands) - len(scalars)) + [smem] * len(scalars),
        out_specs=[vmem] * len(shapes),
        scratch_shapes=buffers + [pltpu.SemaphoreType.DMA((2, parts - 1))] * 2,
        compiler_params=pltpu.CompilerParams(
            collective_id=collective_id, has_side_effects=True, vmem_limit_bytes=40 << 20
        ),
    )(*operands)


def reduce_all(terms, collective_id):
    _, tensors, groups, count, _ = terms.shape

    def kernel(
        terms_ref, out_ref, near, own, mid, mid_in, far, far_in,
        own_sems, near_send, near_recv, mid_send, mid_recv, far_send, far_recv,
    ):
        group, part, side = lax.axis_index("dp"), lax.axis_index("tensor"), lax.axis_index("seq")
        twin = 1 - side
        parts = others("tensor")
        order = others("dp") + [group]
        meet(
            [{"seq": twin}]
            + [{"tensor": peer} for peer in parts]
            + [{"dp": peer} for peer in order[:-1]]
        )
        waits, near_copies, own_copies = [], [], []
        for place, target in enumerate(order):
            near_copies.append(
                send(
                    terms_ref.at[twin, :, target],
                    near.at[place],
                    near_send.at[place],
                    near_recv.at[place],
                    {"seq": twin},
                )
            )
            copy = pltpu.make_async_copy(
                terms_ref.at[side, :, target], own.at[place], own_sems.at[place]
            )
            copy.start()
            own_copies.append(copy)
        mid_copies = []
        for place in range(groups):
            near_copies[place].wait_recv()
            own_copies[place].wait()
            for slot in range(tensors):
                mid[place, slot] = (
                    own[place, slot].astype(jnp.float32) + near[place, slot].astype(jnp.float32)
                ).astype(jnp.bfloat16)
            mid_copies.append(
                [
                    send(
                        mid.at[place, peer],
                        mid_in.at[place, step],
                        mid_send.at[place, step],
                        mid_recv.at[place, step],
                        {"tensor": peer},
                    )
                    for step, peer in enumerate(parts)
                ]
            )
        far_copies = []
        for place, target in enumerate(order):
            total = mid[place, part].astype(jnp.float32)
            for step in range(tensors - 1):
                mid_copies[place][step].wait_recv()
                total = total + mid_in[place, step].astype(jnp.float32)
            if place < groups - 1:
                far[place] = total.astype(jnp.bfloat16)
                far_copies.append(
                    send(
                        far.at[place],
                        far_in.at[place],
                        far_send.at[place],
                        far_recv.at[place],
                        {"dp": target},
                    )
                )
        for place, copy in enumerate(far_copies):
            copy.wait_recv()
            total = total + far_in[place].astype(jnp.float32)
        out_ref[...] = total
        for copy in near_copies + far_copies + [c for row in mid_copies for c in row]:
            copy.wait_send()

    block = (count, D)
    dma = pltpu.SemaphoreType.DMA
    return pl.pallas_call(
        kernel,
        name="reduce_all",
        out_shape=jax.ShapeDtypeStruct(block, jnp.float32),
        in_specs=[pl.BlockSpec(memory_space=pl.ANY)],
        out_specs=pl.BlockSpec(memory_space=pltpu.VMEM),
        scratch_shapes=[pltpu.VMEM((groups, tensors) + block, jnp.bfloat16)] * 3
        + [
            pltpu.VMEM((groups, tensors - 1) + block, jnp.bfloat16),
            pltpu.VMEM((groups,) + block, jnp.bfloat16),
            pltpu.VMEM((groups,) + block, jnp.bfloat16),
            dma((groups,)),
            dma((groups,)),
            dma((groups,)),
            dma((groups, tensors - 1)),
            dma((groups, tensors - 1)),
            dma((groups,)),
            dma((groups,)),
        ],
        compiler_params=pltpu.CompilerParams(
            collective_id=collective_id, has_side_effects=True, vmem_limit_bytes=56 << 20
        ),
    )(terms)


def gather_all(block, collective_id):
    tensors, groups = lax.axis_size("tensor"), lax.axis_size("dp")

    def kernel(block_ref, out, own_sem, far_send, far_recv, mid_send, mid_recv, near_send, near_recv):
        group, part, side = lax.axis_index("dp"), lax.axis_index("tensor"), lax.axis_index("seq")
        twin = 1 - side
        parts = others("tensor")
        meet(
            [{"seq": twin}]
            + [{"tensor": peer} for peer in parts]
            + [{"dp": peer} for peer in others("dp")]
        )
        far_copies = [
            send(
                block_ref,
                out.at[side, part, group],
                far_send.at[step],
                far_recv.at[step],
                {"dp": peer},
            )
            for step, peer in enumerate(others("dp"))
        ]
        own = pltpu.make_async_copy(block_ref, out.at[side, part, group], own_sem)
        own.start()
        own.wait()
        mid_copies, near_copies = [], []
        for place in range(groups):
            source = behind("dp", place)
            if place:
                far_copies[place - 1].wait_recv()
            held = out.at[side, part, source]
            mid_copies.append(
                [
                    send(held, held, mid_send.at[place, step], mid_recv.at[place, step], {"tensor": peer})
                    for step, peer in enumerate(parts)
                ]
            )
            near_copies.append(
                send(held, held, near_send.at[place, 0], near_recv.at[place, 0], {"seq": twin})
            )
        for place in range(groups):
            source = behind("dp", place)
            for step in range(tensors - 1):
                mid_copies[place][step].wait_recv()
                held = out.at[side, behind("tensor", step + 1), source]
                near_copies.append(
                    send(
                        held,
                        held,
                        near_send.at[place, step + 1],
                        near_recv.at[place, step + 1],
                        {"seq": twin},
                    )
                )
        for copy in near_copies:
            copy.wait_recv()
        for copy in near_copies + far_copies + [c for row in mid_copies for c in row]:
            copy.wait_send()

    dma = pltpu.SemaphoreType.DMA
    return pl.pallas_call(
        kernel,
        name="gather_all",
        out_shape=jax.ShapeDtypeStruct((2, tensors, groups) + block.shape, block.dtype),
        in_specs=[pl.BlockSpec(memory_space=pl.ANY)],
        out_specs=pl.BlockSpec(memory_space=pl.ANY),
        scratch_shapes=[
            dma,
            dma((groups - 1,)),
            dma((groups - 1,)),
            dma((groups, tensors - 1)),
            dma((groups, tensors - 1)),
            dma((groups, tensors)),
            dma((groups, tensors)),
        ],
        compiler_params=pltpu.CompilerParams(collective_id=collective_id, has_side_effects=True),
    )(block)


def reduce_rows(terms, collective_id):
    count, groups = terms.shape[3], terms.shape[2]
    pieces = max(1, groups // 4)
    part = count // pieces
    sums = [
        reduce_all(terms[:, :, :, i * part : (i + 1) * part] if pieces > 1 else terms, collective_id)
        for i in range(pieces)
    ]
    return jnp.concatenate(sums, axis=0) if pieces > 1 else sums[0]


def join_stats(stats, collective_id):
    _, tensors, groups, _, _ = stats.shape

    def join(left, right):
        top = jnp.maximum(left[..., 0:1, :], right[..., 0:1, :])
        total = left[..., 1:2, :] * jnp.exp(left[..., 0:1, :] - top) + right[..., 1:2, :] * jnp.exp(
            right[..., 0:1, :] - top
        )
        return jnp.concatenate(
            [top, total, left[..., 2:3, :] + right[..., 2:3, :], left[..., 3:, :]], axis=-2
        )

    def kernel(
        stats_ref, home, full, near, mid, mid_in, far, far_in,
        near_send, near_recv, mid_send, mid_recv, far_send, far_recv,
    ):
        group, part, side = lax.axis_index("dp"), lax.axis_index("tensor"), lax.axis_index("seq")
        twin = 1 - side
        parts, groups_else = others("tensor"), others("dp")
        meet(
            [{"seq": twin}]
            + [{"tensor": peer} for peer in parts]
            + [{"dp": peer} for peer in groups_else]
        )
        copy = send(stats_ref.at[twin], near, near_send.at[0], near_recv.at[0], {"seq": twin})
        copy.wait()
        for slot in range(tensors):
            for spot in range(groups):
                mid[slot, spot] = join(stats_ref[side, slot, spot], near[slot, spot])
        copies = [
            send(mid.at[peer], mid_in.at[step], mid_send.at[0, step], mid_recv.at[0, step], {"tensor": peer})
            for step, peer in enumerate(parts)
        ]
        for copy in copies:
            copy.wait()
        for spot in range(groups):
            total = mid[part, spot]
            for step in range(tensors - 1):
                total = join(total, mid_in[step, spot])
            far[spot] = total
        copies = [
            send(far.at[peer], far_in.at[step], far_send.at[0, step], far_recv.at[0, step], {"dp": peer})
            for step, peer in enumerate(groups_else)
        ]
        total = far[group]
        for step, copy in enumerate(copies):
            copy.wait()
            total = join(total, far_in[step])
        log_total = total[0:1] + jnp.log(total[1:2])
        home[...] = jnp.concatenate([log_total, total[2:3], total[2:]], axis=0)
        full[side, part, group] = jnp.broadcast_to(log_total, (8, LANES))
        held = full.at[side, part, group]
        copies = [
            send(held, held, far_send.at[1, step], far_recv.at[1, step], {"dp": peer})
            for step, peer in enumerate(groups_else)
        ]
        for copy in copies:
            copy.wait()
        held = full.at[side, part]
        copies = [
            send(held, held, mid_send.at[1, step], mid_recv.at[1, step], {"tensor": peer})
            for step, peer in enumerate(parts)
        ]
        for copy in copies:
            copy.wait()
        held = full.at[side]
        send(held, held, near_send.at[1], near_recv.at[1], {"seq": twin}).wait()

    tile = (8, LANES)
    dma = pltpu.SemaphoreType.DMA
    vmem = pl.BlockSpec(memory_space=pltpu.VMEM)
    return pl.pallas_call(
        kernel,
        name="join_stats",
        out_shape=[
            jax.ShapeDtypeStruct(tile, jnp.float32),
            jax.ShapeDtypeStruct(stats.shape, jnp.float32),
        ],
        in_specs=[vmem],
        out_specs=[vmem, vmem],
        scratch_shapes=[
            pltpu.VMEM((tensors, groups) + tile, jnp.float32),
            pltpu.VMEM((tensors, groups) + tile, jnp.float32),
            pltpu.VMEM((tensors - 1, groups) + tile, jnp.float32),
            pltpu.VMEM((groups,) + tile, jnp.float32),
            pltpu.VMEM((groups - 1,) + tile, jnp.float32),
            dma((2,)),
            dma((2,)),
            dma((2, tensors - 1)),
            dma((2, tensors - 1)),
            dma((2, groups - 1)),
            dma((2, groups - 1)),
        ],
        compiler_params=pltpu.CompilerParams(collective_id=collective_id, has_side_effects=True),
    )(stats)


def sum_small(block, collective_id):
    tensors, groups = lax.axis_size("tensor"), lax.axis_size("dp")

    def kernel(block_ref, out, near, mid, far, near_send, near_recv, mid_send, mid_recv, far_send, far_recv):
        group, part, side = lax.axis_index("dp"), lax.axis_index("tensor"), lax.axis_index("seq")
        parts, groups_else = others("tensor"), others("dp")
        meet(
            [{"seq": 1 - side}]
            + [{"tensor": peer} for peer in parts]
            + [{"dp": peer} for peer in groups_else]
        )
        stages = [
            ("seq", near, side, [1 - side], near_send, near_recv),
            ("tensor", mid, part, parts, mid_send, mid_recv),
            ("dp", far, group, groups_else, far_send, far_recv),
        ]
        total = block_ref[...]
        for axis, slots, me, peers, send_sems, recv_sems in stages:
            slots[me] = total
            copies = [
                send(slots.at[me], slots.at[me], send_sems.at[step], recv_sems.at[step], {axis: peer})
                for step, peer in enumerate(peers)
            ]
            for copy in copies:
                copy.wait()
            total = slots[0]
            for index in range(1, slots.shape[0]):
                total = total + slots[index]
        out[...] = total

    dma = pltpu.SemaphoreType.DMA
    vmem = pl.BlockSpec(memory_space=pltpu.VMEM)
    return pl.pallas_call(
        kernel,
        name="sum_small",
        out_shape=jax.ShapeDtypeStruct(block.shape, jnp.float32),
        in_specs=[vmem],
        out_specs=vmem,
        scratch_shapes=[
            pltpu.VMEM((2,) + block.shape, jnp.float32),
            pltpu.VMEM((tensors,) + block.shape, jnp.float32),
            pltpu.VMEM((groups,) + block.shape, jnp.float32),
            dma((1,)),
            dma((1,)),
            dma((tensors - 1,)),
            dma((tensors - 1,)),
            dma((groups - 1,)),
            dma((groups - 1,)),
        ],
        compiler_params=pltpu.CompilerParams(collective_id=collective_id, has_side_effects=True),
    )(block)


def row_of(groups_ref):
    return jnp.concatenate([groups_ref[0, g : g + 1, :] for g in range(TILE_GROUPS)], axis=1)


def stat_row(stat_ref, row):
    return jnp.concatenate([stat_ref[g, row : row + 1, :] for g in range(TILE_GROUPS)], axis=1)


def chunk_of(step):
    return pl.ds(pl.multiple_of(step * ROW_STEP, ROW_STEP), ROW_STEP)


def whole(shape):
    return pl.BlockSpec(shape, lambda step, span: (0,) * len(shape), pipeline_mode=pl.Buffered(1))


TILE = TILE_GROUPS * LANES
TOKENS_SPEC = pl.BlockSpec((1, TILE_GROUPS, LANES), lambda step, span: (step, 0, 0))
STATS_SPEC = pl.BlockSpec((TILE_GROUPS, 8, LANES), lambda step, span: (step, 0, 0))
ROWS_SPEC = pl.BlockSpec((TILE, D), lambda step, span: (step, 0))


def local_call(name, kernel, steps, span, operands, in_specs, out_shape, out_specs, scratch):
    return pl.pallas_call(
        kernel,
        name=name,
        grid_spec=pltpu.PrefetchScalarGridSpec(
            num_scalar_prefetch=1,
            grid=(steps,),
            in_specs=in_specs,
            out_specs=out_specs,
            scratch_shapes=scratch,
        ),
        out_shape=out_shape,
        compiler_params=pltpu.CompilerParams(vmem_limit_bytes=56 << 20),
    )(span, *operands)


def look_up(span, row_ids, tokens, table_t):
    rows = table_t.shape[1]
    steps = tokens.shape[0]

    def kernel(span_ref, ids_ref, tokens_ref, table_ref, out_ref, acc):
        acc[...] = jnp.zeros_like(acc)
        wanted = row_of(tokens_ref)

        def one(step, carry):
            chunk = chunk_of(step)
            hits = jnp.where(ids_ref[chunk, :] == wanted, 1.0, 0.0).astype(jnp.bfloat16)
            acc[...] += jnp.dot(table_ref[:, chunk], hits, preferred_element_type=jnp.float32)
            return carry

        lax.fori_loop(span_ref[0], span_ref[1], one, 0)
        out_ref[...] = acc[...].T.astype(jnp.bfloat16)

    return local_call(
        "look_up",
        kernel,
        steps,
        span,
        (row_ids, tokens, table_t),
        [whole((rows, 1)), TOKENS_SPEC, whole((D, rows))],
        jax.ShapeDtypeStruct((steps * TILE, D), jnp.bfloat16),
        ROWS_SPEC,
        [pltpu.VMEM((D, TILE), jnp.float32)],
    )


def head_forward(span, row_ids, labels, table, final):
    rows = table.shape[0]
    steps = labels.shape[0]

    def kernel(span_ref, ids_ref, labels_ref, table_ref, final_ref, powers_ref, stats_ref, scores):
        wanted = row_of(labels_ref)
        hidden = final_ref[...]

        def first(step, carry):
            top, target = carry
            chunk = chunk_of(step)
            ids = ids_ref[chunk, :]
            raw = contract_last(table_ref[chunk, :], hidden)
            raw = jnp.where(ids >= 0, raw, -1e30)
            scores[chunk, :] = raw
            top = jnp.maximum(top, jnp.max(raw, axis=0, keepdims=True))
            target = target + jnp.sum(jnp.where(ids == wanted, raw, 0.0), axis=0, keepdims=True)
            return (top, target)

        blank = jnp.zeros((1, TILE), jnp.float32)
        top, target = lax.fori_loop(span_ref[0], span_ref[1], first, (blank - 1e30, blank))

        def second(step, total):
            chunk = chunk_of(step)
            powers = jnp.exp(scores[chunk, :] - top)
            powers_ref[chunk, :] = powers.astype(jnp.bfloat16)
            return total + jnp.sum(powers, axis=0, keepdims=True)

        total = lax.fori_loop(span_ref[0], span_ref[1], second, blank)
        rest = jnp.zeros((5, LANES), jnp.float32)
        for g in range(TILE_GROUPS):
            lanes = slice(g * LANES, (g + 1) * LANES)
            stats_ref[g] = jnp.concatenate(
                [top[:, lanes], total[:, lanes], target[:, lanes], rest], axis=0
            )

    return local_call(
        "head_forward",
        kernel,
        steps,
        span,
        (row_ids, labels, table, final),
        [whole((rows, 1)), TOKENS_SPEC, whole((rows, D)), ROWS_SPEC],
        [
            jax.ShapeDtypeStruct((rows, steps * TILE), jnp.bfloat16),
            jax.ShapeDtypeStruct((steps * TILE_GROUPS, 8, LANES), jnp.float32),
        ],
        [pl.BlockSpec((rows, TILE), lambda step, span: (0, step)), STATS_SPEC],
        [pltpu.VMEM((rows, TILE), jnp.float32)],
    )


def head_backward(span, row_ids, labels, keep, stats, log_totals, table_t, final, powers):
    rows = table_t.shape[1]
    steps = labels.shape[0]

    def kernel(
        span_ref, ids_ref, labels_ref, keep_ref, stats_ref, logs_ref, table_ref, final_ref,
        powers_ref, grad_final_ref, grad_table_ref, acc,
    ):
        @pl.when(pl.program_id(0) == 0)
        def _():
            grad_table_ref[...] = jnp.zeros_like(grad_table_ref)

        acc[...] = jnp.zeros_like(acc)
        wanted, kept = row_of(labels_ref), row_of(keep_ref)
        scale = jnp.exp(stat_row(stats_ref, 0) - stat_row(logs_ref, 0)) * kept
        hidden = final_ref[...]

        def one(step, carry):
            chunk = chunk_of(step)
            grads = powers_ref[chunk, :].astype(jnp.float32) * scale
            grads = grads - jnp.where(ids_ref[chunk, :] == wanted, kept, 0.0)
            grads = grads.astype(jnp.bfloat16)
            grad_table_ref[chunk, :] += jnp.dot(grads, hidden, preferred_element_type=jnp.float32)
            acc[...] += jnp.dot(table_ref[:, chunk], grads, preferred_element_type=jnp.float32)
            return carry

        lax.fori_loop(span_ref[0], span_ref[1], one, 0)
        grad_final_ref[...] = acc[...].T.astype(jnp.bfloat16)

    return local_call(
        "head_backward",
        kernel,
        steps,
        span,
        (row_ids, labels, keep, stats, log_totals, table_t, final, powers),
        [
            whole((rows, 1)),
            TOKENS_SPEC,
            TOKENS_SPEC,
            STATS_SPEC,
            STATS_SPEC,
            whole((D, rows)),
            ROWS_SPEC,
            pl.BlockSpec((rows, TILE), lambda step, span: (0, step)),
        ],
        [
            jax.ShapeDtypeStruct((steps * TILE, D), jnp.bfloat16),
            jax.ShapeDtypeStruct((rows, D), jnp.float32),
        ],
        [ROWS_SPEC, whole((rows, D))],
        [pltpu.VMEM((D, TILE), jnp.float32)],
    )


def look_back(span, row_ids, tokens, grad_start, grad_table):
    rows = grad_table.shape[0]
    steps = tokens.shape[0]

    def kernel(span_ref, ids_ref, tokens_ref, grad_ref, table_ref, out_ref):
        @pl.when(pl.program_id(0) == 0)
        def _():
            out_ref[...] = table_ref[...]

        wanted = row_of(tokens_ref)
        grads = grad_ref[...]

        def one(step, carry):
            chunk = chunk_of(step)
            hits = jnp.where(ids_ref[chunk, :] == wanted, 1.0, 0.0).astype(jnp.bfloat16)
            out_ref[chunk, :] += jnp.dot(hits, grads, preferred_element_type=jnp.float32)
            return carry

        lax.fori_loop(span_ref[0], span_ref[1], one, 0)

    return local_call(
        "look_back",
        kernel,
        steps,
        span,
        (row_ids, tokens, grad_start, grad_table),
        [whole((rows, 1)), TOKENS_SPEC, ROWS_SPEC, whole((rows, D))],
        jax.ShapeDtypeStruct((rows, D), jnp.float32),
        whole((rows, D)),
        [],
    )


def attend(joined, geometry):
    cosine, sine, allowed, seq_count, half_len, local_heads = geometry
    width = local_heads * HEAD_DIM
    shape_four = (seq_count, half_len, local_heads, HEAD_DIM)
    queries = (
        rotate(joined[:, :width].reshape(-1, local_heads, HEAD_DIM), cosine, sine)
        .astype(jnp.bfloat16)
        .reshape(shape_four)
    )
    own_keys = (
        rotate(joined[:, width : 2 * width].reshape(-1, local_heads, HEAD_DIM), cosine, sine)
        .astype(jnp.bfloat16)
        .reshape(shape_four)
    )
    own_values = joined[:, 2 * width :].astype(jnp.bfloat16).reshape(shape_four)
    far_keys, far_values = from_behind((own_keys, own_values), "seq", 1)
    keys_all = jnp.concatenate([far_keys, own_keys], axis=1)
    values_all = jnp.concatenate([far_values, own_values], axis=1)
    scores = attention_scores(queries, keys_all, allowed)
    peak = jnp.max(scores, -1, keepdims=True)
    log_total = peak + jnp.log(jnp.sum(jnp.exp(scores - peak), -1, keepdims=True))
    probs = jnp.exp(scores - log_total).astype(jnp.bfloat16)
    attended = jnp.einsum("bhqk,bkhd->bqhd", probs, values_all, preferred_element_type=jnp.float32)
    attended = attended.astype(jnp.bfloat16).reshape(-1, width)
    return attended, (queries, keys_all, values_all, log_total)


def attend_back(grad_attended, kept, geometry):
    queries, keys_all, values_all, log_total = kept
    cosine, sine, allowed, seq_count, half_len, local_heads = geometry
    width = local_heads * HEAD_DIM
    grad_attended = grad_attended.reshape(seq_count, half_len, local_heads, HEAD_DIM)
    probs = jnp.exp(attention_scores(queries, keys_all, allowed) - log_total)
    grad_probs = jnp.einsum(
        "bqhd,bkhd->bhqk", grad_attended, values_all, preferred_element_type=jnp.float32
    )
    grad_scores = (probs * (grad_probs - jnp.sum(probs * grad_probs, -1, keepdims=True))).astype(
        jnp.bfloat16
    )
    scale = HEAD_DIM ** (-0.5)
    grad_queries = (
        jnp.einsum("bhqk,bkhd->bqhd", grad_scores, keys_all, preferred_element_type=jnp.float32)
        * scale
    )
    grad_keys = (
        jnp.einsum("bhqk,bqhd->bkhd", grad_scores, queries, preferred_element_type=jnp.float32)
        * scale
    )
    grad_values = jnp.einsum(
        "bhqk,bqhd->bkhd",
        probs.astype(jnp.bfloat16),
        grad_attended,
        preferred_element_type=jnp.float32,
    )
    back_keys, back_values = (
        from_behind(grad_keys[:, :half_len].astype(jnp.bfloat16), "seq", -1).astype(jnp.float32),
        from_behind(grad_values[:, :half_len].astype(jnp.bfloat16), "seq", -1).astype(jnp.float32),
    )
    grad_keys = grad_keys[:, half_len:] + back_keys
    grad_values = grad_values[:, half_len:] + back_values
    return jnp.concatenate(
        [
            rotate(grad_queries.reshape(-1, local_heads, HEAD_DIM), cosine, -sine).reshape(
                -1, width
            ),
            rotate(grad_keys.reshape(-1, local_heads, HEAD_DIM), cosine, -sine).reshape(-1, width),
            grad_values.reshape(-1, width),
        ],
        axis=1,
    ).astype(jnp.bfloat16)


def body(
    token_ids,
    labels,
    real_counts,
    owners,
    master,
    first_moment,
    second_moment,
    gains,
    gains_first,
    gains_second,
    mix,
    mix_first,
    mix_second,
):
    tensors = lax.axis_size("tensor")
    groups = lax.axis_size("dp")
    group = lax.axis_index("dp")
    tensor_part = lax.axis_index("tensor")
    seq_part = lax.axis_index("seq")
    slots, half_rows, _ = master.shape
    seq_count, half_len = token_ids.shape
    row_count = seq_count * half_len
    share = row_count // tensors
    head_rows = 3 * D // tensors
    out_rows = D // tensors
    unit_rows = FF // tensors
    layer_rows = head_rows + out_rows + 2 * unit_rows
    layer_blocks = layer_rows // (2 * half_rows)
    blocks = LAYERS * layer_blocks
    vocab_rows = VOCAB // tensors
    local_heads = HEADS // tensors

    slot_rank = slot_table(owners)
    block_ids = jnp.arange(owners.shape[0], dtype=jnp.int32)
    mine = owners == group
    match = (jnp.arange(slots)[:, None] == slot_rank[None, :]) & mine[None, :]
    slot_block = jnp.sum(jnp.where(match, block_ids[None, :] + 1, 0), axis=1) - 1
    row_ids = (
        tensor_part * vocab_rows
        + (slot_block[:, None] - blocks) * (2 * half_rows)
        + seq_part * half_rows
        + jnp.arange(half_rows, dtype=jnp.int32)[None, :]
    )
    row_ids = jnp.where(slot_block[:, None] >= blocks, row_ids, -1).reshape(-1, 1)
    rows = slots * half_rows
    padded = -(-rows // ROW_STEP) * ROW_STEP
    row_ids = jnp.pad(row_ids, ((0, padded - rows), (0, 0)), constant_values=-1)
    held = jnp.sum(jnp.where(mine, 1, 0)) * half_rows
    first_held = jnp.sum(jnp.where(mine & (block_ids < blocks), 1, 0)) * half_rows
    span = jnp.stack([first_held // ROW_STEP, (held + ROW_STEP - 1) // ROW_STEP]).astype(jnp.int32)

    packed = jnp.concatenate([token_ids.reshape(-1), labels.reshape(-1), real_counts])
    packed = lax.all_gather(packed, ("dp", "seq")).reshape(groups, 2, -1)

    def by_home(tokens):
        tokens = tokens.reshape(groups, 2, tensors, share).transpose(1, 2, 0, 3)
        return tokens.reshape(-1, TILE_GROUPS, LANES)

    ids_all = by_home(packed[:, :, :row_count])
    labels_all = by_home(packed[:, :, row_count : 2 * row_count])
    counts_all = packed[:, :, 2 * row_count]
    token_count = jnp.sum(counts_all).astype(jnp.float32)
    keep_all = by_home(
        jnp.where(jnp.arange(row_count)[None, None, :] < counts_all[:, :, None], 1.0, 0.0)
    )
    order = (2, tensors, groups, share)

    master_low = master.astype(jnp.bfloat16)
    table = jnp.pad(master_low.reshape(rows, D), ((0, padded - rows), (0, 0)))
    table_t = table.T

    weights_all = []
    for level in range(LAYERS):
        chosen = slice(level * layer_blocks, (level + 1) * layer_blocks)
        own = jnp.where(
            mine[chosen][:, None, None], jnp.take(master_low, slot_rank[chosen], axis=0), 0.0
        ).astype(jnp.bfloat16)
        own = lax.psum(own, "dp")
        own = lax.all_gather(own, "seq", axis=1).reshape(layer_rows, D)
        cut_one, cut_two = head_rows + out_rows, head_rows + out_rows + unit_rows
        weights_all.append(
            (own[:head_rows], own[head_rows:cut_one], own[cut_one:cut_two], own[cut_two:])
        )

    positions = seq_part * half_len + jnp.arange(row_count) % half_len
    cosine, sine = rotary(positions)
    query_pos = seq_part * half_len + jnp.arange(half_len)
    key_pos = jnp.concatenate([(seq_part - 1) * half_len + jnp.arange(half_len), query_pos])
    allowed = (key_pos[None, :] <= query_pos[:, None]) & (key_pos[None, :] >= 0)
    geometry = (cosine, sine, allowed, seq_count, half_len, local_heads)

    looked = look_up(span, row_ids, ids_all, table_t).reshape(order + (D,))
    start = reduce_rows(looked, 0)
    gain = [gains[i : i + 1] for i in range(2 * LAYERS + 1)]
    piece = ((share, D), jnp.float32)

    def normed_of(total, stream, gain_row):
        return (layer_norm_parts(stream)[0] * gain_row,)

    def inner_of(total, stream, gain_row):
        inner = stream + total
        return (inner, layer_norm_parts(inner)[0] * gain_row)

    def outcome_of(base, total, inner, gain_row, *rest):
        states, scalars = rest[:-1], rest[-1]
        outcome = inner + total
        stream = scalars[base + len(states)] * outcome
        for source, state in enumerate(states):
            stream = stream + scalars[base + source] * state
        return (outcome, stream, layer_norm_parts(stream)[0] * gain_row)

    (normed,) = tensor_step("normed", normed_of, None, (start, gain[0]), (), [], True, 1)
    states, streams, inners, kept_all = [start], [start], [], []
    for level in range(LAYERS):
        qkv_w, out_w, up_w, down_w = weights_all[level]
        normed = normed.reshape(row_count, D)
        attended, kept = attend(contract_last(normed, qkv_w), geometry)
        inner, normed_two = tensor_step(
            "inner",
            inner_of,
            jnp.dot(attended, out_w, preferred_element_type=jnp.float32),
            (streams[level], gain[2 * level + 1]),
            (),
            [piece],
            True,
            2,
        )
        normed_two = normed_two.reshape(row_count, D)
        hidden = contract_last(normed_two, up_w)
        activated = jax.nn.gelu(hidden, approximate=True).astype(jnp.bfloat16)
        last = level == LAYERS - 1
        results = tensor_step(
            f"outcome_{level}",
            partial(outcome_of, (level + 1) * (level + 2) // 2 - 1),
            jnp.dot(activated, down_w, preferred_element_type=jnp.float32),
            [inner, gain[2 * level + 2]] + states,
            (mix,),
            [piece, piece] + ([((share, D), jnp.bfloat16)] if last else []),
            not last,
            3 + level,
        )
        inners.append(inner)
        kept_all.append((normed, kept, attended, normed_two, hidden, activated))
        states.append(results[0])
        streams.append(results[1])
        normed = results[2]

    final_all = gather_all(normed, 3 + LAYERS).reshape(-1, D)
    powers, stats = head_forward(span, row_ids, labels_all, table, final_all)
    home, log_totals = join_stats(
        stats.reshape((2, tensors, groups, 8, LANES)), 4 + LAYERS
    )
    keep = jnp.where(
        tensor_part * share + jnp.arange(share) < real_counts[0], 1.0, 0.0
    ).astype(jnp.float32)
    loss_local = jnp.sum((home[0] - home[1]) * keep)
    grad_final, grad_table = head_backward(
        span,
        row_ids,
        labels_all,
        keep_all,
        stats,
        log_totals.reshape(-1, 8, LANES),
        table_t,
        final_all,
        powers,
    )
    grad_final = reduce_rows(grad_final.reshape(order + (D,)), 0)

    row = ((1, D), jnp.float32)

    def top_of(total, grad, stream, gain_row, scalars):
        grad_top, grad_gain = norm_pull(grad, gain_row, stream)
        grad_state = scalars[MIX_WEIGHTS - 1] * grad_top
        return (grad_top, grad_state, grad_gain, grad_state)

    def inner_back(total, grad_out, inner, gain_row):
        grad, grad_gain = norm_pull(total, gain_row, inner)
        grad = grad_out + grad
        return (grad, grad_gain, grad)

    def stream_back(block, total, grad_inner, stream, gain_row, *rest):
        grad_ys, scalars = rest[:-1], rest[-1]
        grad, grad_gain = norm_pull(total, gain_row, stream)
        grad = grad_inner + grad
        state = grad if block == 0 else scalars[block * (block + 1) // 2 - 1 + block] * grad
        for offset, grad_y in enumerate(grad_ys):
            later = block + 1 + offset
            state = state + scalars[later * (later + 1) // 2 - 1 + block] * grad_y
        return (grad, state, grad_gain, state)

    grad_ys = [None] * (LAYERS + 1)
    gain_grads = [None] * (2 * LAYERS + 1)
    layer_grads = [None] * LAYERS
    grad_ys[LAYERS], grad_state, gain_grads[2 * LAYERS], grad_branch = tensor_step(
        "top_back",
        top_of,
        None,
        (grad_final, streams[LAYERS], gain[2 * LAYERS]),
        (mix,),
        [piece, piece, row],
        True,
        5 + LAYERS,
    )
    for level in reversed(range(LAYERS)):
        qkv_w, out_w, up_w, down_w = weights_all[level]
        normed, kept, attended, normed_two, hidden, activated = kept_all[level]
        grad_branch = grad_branch.reshape(row_count, D)
        grad_act = contract_last(grad_branch, down_w)
        _, gelu_pull = jax.vjp(partial(jax.nn.gelu, approximate=True), hidden)
        grad_hidden = gelu_pull(grad_act)[0].astype(jnp.bfloat16)
        grad_inner, gain_grads[2 * level + 1], grad_attn = tensor_step(
            "inner_back",
            inner_back,
            jnp.dot(grad_hidden, up_w, preferred_element_type=jnp.float32),
            (grad_state, inners[level], gain[2 * level + 1]),
            (),
            [piece, row],
            True,
            6 + LAYERS,
        )
        grad_attn = grad_attn.reshape(row_count, D)
        grad_attended = contract_last(grad_attn, out_w).astype(jnp.bfloat16)
        grad_joined = attend_back(grad_attended, kept, geometry)
        results = tensor_step(
            f"stream_back_{level}",
            partial(stream_back, level),
            jnp.dot(grad_joined, qkv_w, preferred_element_type=jnp.float32),
            [grad_inner, streams[level], gain[2 * level]] + grad_ys[level + 1 :],
            (mix,),
            [piece, piece, row] + ([] if level else [((share, D), jnp.bfloat16)]),
            level > 0,
            7 + LAYERS + level,
        )
        grad_ys[level], grad_state, gain_grads[2 * level] = results[:3]
        branch_before, grad_branch = grad_branch, results[3]
        grads = jnp.concatenate(
            [
                contract_first(grad_joined, normed),
                contract_first(attended, grad_attn),
                contract_first(grad_hidden, normed_two),
                contract_first(activated, branch_before),
            ],
            axis=0,
        ).astype(jnp.bfloat16)
        grads = lax.psum_scatter(
            grads.reshape(layer_blocks, 2, half_rows, D), "seq", scatter_dimension=1, tiled=False
        )
        layer_grads[level] = lax.psum(grads, "dp")

    grad_mix = [None] * MIX_WEIGHTS
    for later in range(1, LAYERS + 1):
        for block in range(later + 1):
            grad_mix[later * (later + 1) // 2 - 1 + block] = jnp.sum(grad_ys[later] * states[block])

    grad_start_all = gather_all(grad_branch, 3 + LAYERS).reshape(-1, D)
    grad_table = look_back(span, row_ids, ids_all, grad_start_all, grad_table)
    layer_grad = jnp.concatenate(layer_grads, axis=0)
    placed = jnp.take(layer_grad, jnp.clip(slot_block, 0, blocks - 1), axis=0).astype(jnp.float32)
    owned = jnp.where(
        ((slot_block >= 0) & (slot_block < blocks))[:, None, None],
        placed,
        grad_table[:rows].reshape(slots, half_rows, D),
    )
    small = jnp.concatenate([jnp.stack(grad_mix), loss_local[None], jnp.sum(owned * owned)[None]])
    small = jnp.concatenate(
        [
            jnp.concatenate(gain_grads, axis=0),
            jnp.pad(small, (0, D - small.shape[0]))[None],
            jnp.zeros((7 - 2 * LAYERS - 1, D), jnp.float32),
        ],
        axis=0,
    )
    small = sum_small(small, 7 + 2 * LAYERS)
    gain_total = small[: 2 * LAYERS + 1]
    mix_total = small[2 * LAYERS + 1, :MIX_WEIGHTS]
    loss_sum = small[2 * LAYERS + 1, MIX_WEIGHTS]
    squares = small[2 * LAYERS + 1, MIX_WEIGHTS + 1]
    clip_norm = (
        jnp.sqrt(squares + jnp.sum(gain_total * gain_total) + jnp.sum(mix_total * mix_total))
        / token_count
    )
    factor = jnp.minimum(1.0, CLIP_NORM / clip_norm) / token_count
    new_master, new_first, new_second = adam_update(
        master, first_moment, second_moment, owned * factor, RATE_MATRIX, DECAY_MATRIX
    )
    new_gains, new_gains_first, new_gains_second = adam_update(
        gains, gains_first, gains_second, gain_total * factor, RATE_SMALL, 0.0
    )
    new_mix, new_mix_first, new_mix_second = adam_update(
        mix, mix_first, mix_second, mix_total * factor, RATE_SMALL, 0.0
    )
    return (
        new_master,
        new_first,
        new_second,
        new_gains,
        new_gains_first,
        new_gains_second,
        new_mix,
        new_mix_first,
        new_mix_second,
        loss_sum,
        token_count,
        clip_norm,
    )


def solution(mesh):
    return jax.shard_map(
        body,
        mesh=mesh,
        in_specs=(
            P("dp", "seq"),
            P("dp", "seq"),
            P(("dp", "seq")),
            P(),
            P("dp", ("tensor", "seq"), None),
            P("dp", ("tensor", "seq"), None),
            P("dp", ("tensor", "seq"), None),
            P(),
            P(),
            P(),
            P(),
            P(),
            P(),
        ),
        out_specs=(
            P("dp", ("tensor", "seq"), None),
            P("dp", ("tensor", "seq"), None),
            P("dp", ("tensor", "seq"), None),
            P(),
            P(),
            P(),
            P(),
            P(),
            P(),
            P(),
            P(),
            P(),
        ),
        check_vma=False,
    )
```

time: 1930 us -> 1040 us (0.54)
  waiting for transfers between devices: 1270 us -> 199 us
  Pallas kernels: 0 us -> 577 us
  local copies, waits for them, and re-layouts: 229 us -> 71.6 us
  other arithmetic: 200 us -> 73.4 us
  matrix products: 133 us -> 39.1 us
  blocking collectives: 56.3 us -> 26.8 us
    pallas_call x0 -> x20, Pallas kernels: none -> 577 us  [the longest x10 182 us: tensor_step(): pl.pallas_call(kernel, name=name, out_shape=shapes, in_specs=[vmem] * (le...]
    unnamed x13 -> x6, waiting for transfers between devices: 378 us -> 0.1 us
    psum x10 -> x2, waiting for transfers between devices: 547 us -> 187 us  [the longest x1 137 us: body(): own = lax.psum(own, 'dp')]
    all_gather x1 -> x2, waiting for transfers between devices: 340 us -> 0.02 us  [body(): own = lax.all_gather(own, 'seq', axis=1).reshape(layer_rows, D)]
    scatter x1 -> x0, local copies, waits for them, and re-layouts: 95.8 us -> none  [body(): placed = jnp.zeros((groups * 2 * slots, half_rows, D), jnp.float32).at[ga...]
    reduce_sum x20 -> x6, other arithmetic: 55 us -> 7.23 us  [the longest x2 3.52 us: attend(): jnp.sum(jnp.exp(scores - peak), -1, keepdims=True)]
    psum x2 -> x0, blocking collectives: 47.4 us -> none  [the longest x1 38.4 us: body(): lax.psum((jnp.sum(owned * owned), gain_grad / tensors, mix_grad / tensors...]
    convert_element_type x5 -> x3, other arithmetic: 52.8 us -> 10.3 us  [the longest x1 6.61 us: body(): master_low = master.astype(jnp.bfloat16)]
  transfers between devices with their start and end apart: 20 -> 14, of which waited for: 14 -> 3; matrix products, arithmetic and copies ran while one was open for 4% -> 7% of each run, Pallas kernels for 0% -> 23%
where the time goes in v1:
time: 1040 us; the launch traced here: 1030 us
  Pallas kernels  577 us (55%)
  waiting for transfers between devices  199 us (19%)
  other arithmetic  73.4 us (7%)
  local copies, waits for them, and re-layouts  71.6 us (7%)
  matrix products  39.1 us (4%)
  blocking collectives  26.8 us (3%)
  between operations  24.4 us (2%)
  starting transfers between devices  13.9 us (1%)
    pallas_call x10, Pallas kernels, tensor_step(): pl.pallas_call(kernel, name=name, out_shape=shapes, in_specs=[vmem] * (le...  182 us
    pallas_call x4, Pallas kernels, local_call(): pl.pallas_call(kernel, name=name, grid_spec=pltpu.PrefetchScalarGridSpec(...  138 us
    psum x1, waiting for transfers between devices, body(): own = lax.psum(own, 'dp')  137 us
    pallas_call x2, Pallas kernels, reduce_all(): pl.pallas_call(kernel, name='reduce_all', out_shape=jax.ShapeDtypeStruct(...  112 us
    pallas_call x2, Pallas kernels, gather_all(): pl.pallas_call(kernel, name='gather_all', out_shape=jax.ShapeDtypeStruct(...  96.6 us
    psum x1, waiting for transfers between devices, body(): layer_grads[level] = lax.psum(grads, 'dp')  50 us
    pallas_call x1, Pallas kernels, join_stats(): pl.pallas_call(kernel, name='join_stats', out_shape=[jax.ShapeDtypeStruct...  36 us
    sub x3, other arithmetic, adam_update(): weight - rate * (first_hat / (jnp.sqrt(second_hat) + ADAM_EPS) + decay *...  27.6 us
  transfers between devices with their start and end apart: 14, of which 3 were waited for; matrix products, arithmetic and copies ran while one was open for 7% of the time, Pallas kernels for 23%

profile of v1, /device:TPU:0, one launch (start us, length us, event | category | flops | bytes accessed | tf_op | source)
XLA Modules:
  0.0 1025.3 jit_solution(10160833470793307225)
XLA Ops:
  9.5 6.6 convert_element_type.141
  17.2 3.1 gather_fusion.1
  20.3 3.1 gather_fusion.2
  23.4 3.0 fusion.5
  26.4 137.0 %all-reduce.11.cloned.1.call-done = (bf16[24,1,48,768]{3,2,0,1:T(8,128)(2,1)}, bf16[24,1,48,768]{3,2,0,1:T(8,128)(2,1)}) async-done(((bf16[24,1,48,768]{3,2,0,1:T(8,128)(2,1)}, bf16[24,1,48,768]{3,2,0,1:T(8,128)(2,1)}), (bf16[24,1,48,768]{3,2,0,1:T(8,128)(2,1)}, bf16[24,1,48,768]{3,2,0,1:T(8,128)(2,1)})) %all-reduce.11.cloned.1.call-update) | async-done | bytes 3538960 | tf_op jit(solution)/shard_map/psum | solution.py:928
  169.9 26.8 %all-reduce.3 = s32[8200]{0:T(1024)S(1)} all-reduce(s32[8200]{0:T(1024)S(1)} %add_dynamic-update-slice_fusion), channel_id=2, replica_groups=mesh['dp'=4,'tensor'=4,'seq'=2] {'dp','seq'}, use_global_device_ids=true, to_apply=%add.3 | all-reduce | flops 8200 | bytes 65600
  197.5 7.5 copy.70
  205.0 7.8 copy.96
  213.5 5.1 pad_bitcast_fusion.table_ref
  218.5 29.7 %look_up.1 = bf16[4096,768]{1,0:T(8,128)(2,1)} custom-call(s32[2]{0:T(128)} %pad_add_fusion.1.span_ref, s32[3328,1]{1,0:T(8,128)} %pad.12.ids_ref, s32[8,4,128]{2,1,0:T(4,128)} %bitcast.294, bf16[768,3328]{1,0:T(8,128)(2,1)} %pad_bitcast_fusion.table_ref), custom_call_target="tpu_custom_call" | custom-call | tf_op jit(solution)/shard_map/look_up/pallas_call | solution.py:594
  248.2 49.9 %reduce_all.2.refs_0_.refs_1_.refs_3_.refs_2_ = f32[128,768]{1,0:T(8,128)} custom-call(bf16[2,4,4,128,768]{4,3,2,1,0:T(8,128)(2,1)} %bitcast.241), custom_call_target="tpu_custom_call" | custom-call | tf_op jit(solution)/shard_map/reduce_all/pallas_call | solution.py:306
  300.5 12.0 %normed.1 = bf16[4,128,768]{2,1,0:T(8,128)(2,1)S(1)} custom-call(f32[128,768]{1,0:T(8,128)S(1)} %copy-done, f32[1,768]{1,0:T(1,128)S(1)} %get-tuple-element.146.refs_1_.refs_3_), custom_call_target="tpu_custom_call" | custom-call | tf_op jit(solution)/shard_map/normed/pallas_call | solution.py:215
  312.5 5.0 pad.13.clone.table_ref
  322.2 2.0 collective-permute-start
  336.8 19.6 %inner.2 = (f32[128,768]{1,0:T(8,128)S(1)}, bf16[4,128,768]{2,1,0:T(8,128)(2,1)S(1)}) custom-call(f32[512,768]{1,0:T(8,128)S(1)} %fusion.89.refs_0_, f32[128,768]{1,0:T(8,128)S(1)} %copy-done.1, f32[1,768]{1,0:T(1,128)S(1)} %get-tuple-element.145.refs_2_.refs_3_), custom_call_target="tpu_custom_call" | custom-call | tf_op jit(solution)/shard_map/inner/pallas_call | solution.py:215
  359.2 21.7 %outcome_0.1 = (f32[128,768]{1,0:T(8,128)S(1)}, f32[128,768]{1,0:T(8,128)S(1)}, bf16[4,128,768]{2,1,0:T(8,128)(2,1)S(1)}) custom-call(f32[512,768]{1,0:T(8,128)S(1)} %fusion.72.refs_0_, f32[128,768]{1,0:T(8,128)S(1)} %get-tuple-element.46.refs_1_.refs_2_, f32[1,768]{1,0:T(1,128)S(1)} %get-tuple-element.144.refs_2_.refs_3_, f32[128,768]{1,0:T(8,128)S(1)} %copy-done.1, ...), custom_call_target="tpu_custom_call" | custom-call | tf_op jit(solution)/shard_map/outcome_0/pallas_call | solution.py:215
  381.9 2.1 collective-permute-start.2
  392.4 21.2 %inner.3 = (f32[128,768]{1,0:T(8,128)S(1)}, bf16[4,128,768]{2,1,0:T(8,128)(2,1)S(1)}) custom-call(f32[512,768]{1,0:T(8,128)S(1)} %fusion.92.refs_0_, f32[128,768]{1,0:T(8,128)S(1)} %get-tuple-element.48.refs_1_.refs_2_, f32[1,768]{1,0:T(1,128)S(1)} %get-tuple-element.143.refs_2_.refs_3_), custom_call_target="tpu_custom_call" | custom-call | tf_op jit(solution)/shard_map/inner/pallas_call | solution.py:215
  415.6 13.2 %outcome_1.1 = (f32[128,768]{1,0:T(8,128)S(1)}, f32[128,768]{1,0:T(8,128)S(1)}, bf16[128,768]{1,0:T(8,128)(2,1)S(1)}) custom-call(f32[512,768]{1,0:T(8,128)S(1)} %fusion.73.refs_0_, f32[128,768]{1,0:T(8,128)S(1)} %get-tuple-element.50.refs_1_.refs_2_, f32[1,768]{1,0:T(1,128)S(1)} %get-tuple-element.142.refs_2_, f32[128,768]{1,0:T(8,128)S(1)} %copy-done.1, ...), custom_call_target="tpu_custom_call" | custom-call | tf_op jit(solution)/shard_map/outcome_1/pallas_call | solution.py:215
  430.4 46.0 %gather_all.2 = bf16[2,4,4,128,768]{4,3,2,1,0:T(8,128)(2,1)} custom-call(bf16[128,768]{1,0:T(8,128)(2,1)} %copy-done.10), custom_call_target="tpu_custom_call" | custom-call | tf_op jit(solution)/shard_map/gather_all/pallas_call | solution.py:391
  476.4 32.3 %head_forward.1 = (bf16[3328,4096]{1,0:T(8,128)(2,1)}, f32[32,8,128]{2,1,0:T(8,128)}) custom-call(s32[2]{0:T(128)} %pad_add_fusion.1.span_ref, s32[3328,1]{1,0:T(8,128)} %pad.12.ids_ref, s32[8,4,128]{2,1,0:T(4,128)} %bitcast.296, bf16[3328,768]{1,0:T(8,128)(2,1)} %pad.13.clone.table_ref, bf16[4096,768]{1,0:T(8,128)(2,1)} %bitcast.232), custom_call_target="tpu_custom_call" | custom-call | tf_op jit(solution)/shard_map/head_forward/pallas_call | solution.py:594
  508.7 36.0 %join_stats.1 = (f32[8,128]{1,0:T(8,128)}, f32[2,4,4,8,128]{4,3,2,1,0:T(8,128)}) custom-call(f32[2,4,4,8,128]{4,3,2,1,0:T(8,128)} %bitcast.281), custom_call_target="tpu_custom_call" | custom-call | tf_op jit(solution)/shard_map/join_stats/pallas_call | solution.py:492
  544.7 44.9 %head_backward.1 = (bf16[4096,768]{1,0:T(8,128)(2,1)}, f32[3328,768]{1,0:T(8,128)}) custom-call(s32[2]{0:T(128)} %pad_add_fusion.1.span_ref, s32[3328,1]{1,0:T(8,128)} %pad.12.ids_ref, s32[8,4,128]{2,1,0:T(4,128)} %bitcast.297, f32[8,4,128]{2,1,0:T(4,128)} %compare_select_fusion.keep_ref, f32[32,8,128]{2,1,0:T(8,128)} %get-tuple-element.53.stats_ref, ...), custom_call_target="tpu_custom_call" | custom-call | tf_op jit(solution)/shard_map/head_backward/pallas_call | solution.py:594
  589.6 61.7 %reduce_all.3.refs_0_ = f32[128,768]{1,0:T(8,128)} custom-call(bf16[2,4,4,128,768]{4,3,2,1,0:T(8,128)(2,1)} %bitcast.244), custom_call_target="tpu_custom_call" | custom-call | tf_op jit(solution)/shard_map/reduce_all/pallas_call | solution.py:306
  652.3 12.7 %top_back.1 = (f32[128,768]{1,0:T(8,128)S(1)}, f32[128,768]{1,0:T(8,128)S(1)}, f32[1,768]{1,0:T(1,128)S(1)}, bf16[4,128,768]{2,1,0:T(8,128)(2,1)S(1)}) custom-call(f32[128,768]{1,0:T(8,128)S(1)} %copy-done.2, f32[128,768]{1,0:T(8,128)S(1)} %copy-done.8, f32[1,768]{1,0:T(1,128)S(1)} %get-tuple-element.142.refs_2_, f32[5]{0:T(128)S(1)} %copy-done.14), custom_call_target="tpu_custom_call" | custom-call | tf_op jit(solution)/shard_map/top_back/pallas_call | solution.py:215
  669.5 20.9 %inner_back.2 = (f32[128,768]{1,0:T(8,128)S(1)}, f32[1,768]{1,0:T(1,128)S(1)}, bf16[4,128,768]{2,1,0:T(8,128)(2,1)S(1)}) custom-call(f32[512,768]{1,0:T(8,128)S(1)} %fusion.94.refs_0_, f32[128,768]{1,0:T(8,128)S(1)} %get-tuple-element.59.refs_1_, f32[128,768]{1,0:T(8,128)S(1)} %get-tuple-element.50.refs_1_.refs_2_, ...), custom_call_target="tpu_custom_call" | custom-call | tf_op jit(solution)/shard_map/inner_back/pallas_call | solution.py:215
  691.0 1.8 convolution_bitcast_fusion.1
  692.8 2.5 multiply_reduce_fusion.2
  695.3 1.8 multiply_convert_fusion.1
  704.8 2.0 copy.85
  706.9 2.1 fusion.32.refs_0_
  709.1 24.9 %stream_back_1.1 = (f32[128,768]{1,0:T(8,128)S(1)}, f32[128,768]{1,0:T(8,128)S(1)}, f32[1,768]{1,0:T(1,128)S(1)}, bf16[4,128,768]{2,1,0:T(8,128)(2,1)S(1)}) custom-call(f32[512,768]{1,0:T(8,128)S(1)} %fusion.32.refs_0_, f32[128,768]{1,0:T(8,128)S(1)} %copy-done.6, f32[128,768]{1,0:T(8,128)S(1)} %get-tuple-element.48.refs_1_.refs_2_, ...), custom_call_target="tpu_custom_call" | custom-call | tf_op jit(solution)/shard_map/stream_back_1/pallas_call | solution.py:215
  736.5 21.5 %inner_back.3 = (f32[128,768]{1,0:T(8,128)S(1)}, f32[1,768]{1,0:T(1,128)S(1)}, bf16[4,128,768]{2,1,0:T(8,128)(2,1)S(1)}) custom-call(f32[512,768]{1,0:T(8,128)S(1)} %fusion.95.refs_0_, f32[128,768]{1,0:T(8,128)S(1)} %get-tuple-element.64.refs_1_, f32[128,768]{1,0:T(8,128)S(1)} %get-tuple-element.46.refs_1_.refs_2_, ...), custom_call_target="tpu_custom_call" | custom-call | tf_op jit(solution)/shard_map/inner_back/pallas_call | solution.py:215
  758.6 2.5 multiply_reduce_fusion.1
  761.0 1.8 multiply_convert_fusion
  773.7 2.0 copy.84
  775.8 12.1 %reduce-scatter.3.cloned.1.call-done = bf16[24,1,48,768]{3,2,0,1:T(8,128)(2,1)} async-done(((bf16[24,2,48,768]{3,2,0,1:T(8,128)(2,1)}), bf16[24,1,48,768]{3,2,0,1:T(8,128)(2,1)}) %reduce-scatter.3.cloned.1.call-update) | async-done | bytes 1769488 | tf_op jit(solution)/shard_map/reduce_scatter | solution.py:1096
  793.0 2.0 fusion.31.refs_0_
  795.0 14.6 %stream_back_0.1 = (f32[128,768]{1,0:T(8,128)}, f32[128,768]{1,0:T(8,128)}, f32[1,768]{1,0:T(1,128)S(1)}, bf16[128,768]{1,0:T(8,128)(2,1)S(1)}) custom-call(f32[512,768]{1,0:T(8,128)S(1)} %fusion.31.refs_0_, f32[128,768]{1,0:T(8,128)S(1)} %get-tuple-element.66.refs_1_, f32[128,768]{1,0:T(8,128)S(1)} %copy-done.1, ...), custom_call_target="tpu_custom_call" | custom-call | tf_op jit(solution)/shard_map/stream_back_0/pallas_call | solution.py:215
  810.3 50.6 %gather_all.3 = bf16[2,4,4,128,768]{4,3,2,1,0:T(8,128)(2,1)} custom-call(bf16[128,768]{1,0:T(8,128)(2,1)} %copy-done.9), custom_call_target="tpu_custom_call" | custom-call | tf_op jit(solution)/shard_map/gather_all/pallas_call | solution.py:391
  860.9 31.1 %look_back.1 = f32[3328,768]{1,0:T(8,128)} custom-call(s32[2]{0:T(128)} %pad_add_fusion.1.span_ref, s32[3328,1]{1,0:T(8,128)} %pad.12.ids_ref, s32[8,4,128]{2,1,0:T(4,128)} %bitcast.295, bf16[4096,768]{1,0:T(8,128)(2,1)} %bitcast.240, f32[3328,768]{1,0:T(8,128)} %get-tuple-element.69.table_ref), custom_call_target="tpu_custom_call" | custom-call | tf_op jit(solution)/shard_map/look_back/pallas_call | solution.py:594
  892.1 50.0 %all-reduce.9.cloned.1.call-done = (bf16[24,48,768]{2,1,0:T(8,128)(2,1)}, bf16[24,48,768]{2,1,0:T(8,128)(2,1)}) async-done(((bf16[24,48,768]{2,1,0:T(8,128)(2,1)}, bf16[24,48,768]{2,1,0:T(8,128)(2,1)}), (bf16[24,48,768]{2,1,0:T(8,128)(2,1)}, bf16[24,48,768]{2,1,0:T(8,128)(2,1)})) %all-reduce.9.cloned.1.call-update) | async-done | bytes 3538960 | tf_op jit(solution)/shard_map/psum | solution.py:1099
  942.1 4.1 pad_maximum_fusion.2
  946.2 7.7 gather_fusion
  954.0 10.8 %fusion.78 = (f32[3216,768]{1,0:T(8,128)}, f32[]{:T(128)}) fusion(f32[3328,768]{1,0:T(8,128)} %look_back.1, bf16[67,48,768]{2,1,0:T(8,128)(2,1)} %gather_fusion, pred[3216]{0:T(1024)(128)(4,1)S(1)} %copy-done.100, pred[3216]{0:T(1024)(128)(4,1)S(1)} %broadcast_in_dim.204), kind=kLoop, calls=%fused_computation.214 | loop fusion | flops 12349439 | bytes 24705316 | tf_op jit(solution)/shard_map/slice | solution.py:1113
  964.7 4.6 concatenate.130
  970.0 12.3 %sum_small.1 = f32[8,768]{1,0:T(8,128)} custom-call(f32[8,768]{1,0:T(8,128)} %concatenate.131.block_ref), custom_call_target="tpu_custom_call" | custom-call | tf_op jit(solution)/shard_map/sum_small/pallas_call | solution.py:550
  991.0 25.0 %multiply_subtract_fusion = (f32[67,48,768]{2,1,0:T(8,128)}, f32[67,48,768]{2,1,0:T(8,128)}, f32[67,48,768]{2,1,0:T(8,128)}) fusion(f32[67,48,768]{2,1,0:T(8,128)} %param.19, f32[]{:T(128)S(6)} %div.78, f32[67,48,768]{2,1,0:T(8,128)} %bitcast.238, bf16[67,48,768]{2,1,0:T(8,128)(2,1)} %gather_fusion, pred[67]{0:T(512)(128)(4,1)S(1)} %copy-done.106, ...), kind=kLoop, calls=%fused_computation.5 | loop fusion | flops 46927872 | bytes 74096776 | tf_op jit(solution)/shard_map/sub | solution.py:96
  (403 shorter events, 82.2 us)
Async XLA Ops:
  7.2 156.2 %all-reduce.11.cloned.1.call-start = ((), (), s32[]{:S(2)}) async-start(), calls=%async_computation.7 | async-start | bytes 7077888 | tf_op jit(solution)/shard_map/psum | solution.py:928
  26.4 293.4 %all-gather.4.cloned.1.call-start = ((), (), s32[]{:S(2)}) async-start(), calls=%async_computation.2 | async-start | bytes 5308416 | tf_op jit(solution)/shard_map/all_gather | solution.py:929
  163.4 165.1 %all-gather.6.cloned.1.call-start = ((), (), s32[]{:S(2)}) async-start(), calls=%async_computation.3 | async-start | bytes 5308416 | tf_op jit(solution)/shard_map/all_gather | solution.py:929
  213.4 562.4 %reduce-scatter.5.cloned.1.call-start = ((), (), s32[]{:S(2)}) async-start(), calls=%async_computation.5 | async-start | bytes 5308416 | tf_op jit(solution)/shard_map/reduce_scatter | solution.py:1096
  248.2 51.3 %copy-start.96 = (f32[5,768]{1,0:T(8,128)S(1)}, f32[5,768]{1,0:T(8,128)}, u32[]{:S(2)}) copy-start(f32[5,768]{1,0:T(8,128)} %param.22) | copy-start | bytes 46084
  299.5 59.6 %copy-start.11 = (f32[1,768]{1,0:T(1,128)}, f32[1,768]{1,0:T(1,128)S(1)}, u32[]{:S(2)}) copy-start(f32[1,768]{1,0:T(1,128)S(1)} %get-tuple-element.144.refs_2_.refs_3_) | copy-start | bytes 9220
  319.3 62.5 %copy-start.40 = (f32[512,32]{0,1:T(8,128)}, f32[512,32]{0,1:T(8,128)S(1)}, u32[]{:S(2)}) copy-start(f32[512,32]{0,1:T(8,128)S(1)} %get-tuple-element.149) | copy-start | bytes 196612
  322.2 7.6 collective-permute-start
  324.3 8.8 collective-permute-start.1
  329.8 51.1 %copy-start.33 = (bf16[6,2,48,768]{3,2,1,0:T(8,128)(2,1)}, bf16[6,2,48,768]{3,2,1,0:T(8,128)(2,1)S(1)}, u32[]{:S(2)}) copy-start(bf16[6,2,48,768]{3,2,1,0:T(8,128)(2,1)S(1)} %copy.91) | copy-start | bytes 2654212
  329.8 62.2 %copy-start.38 = (bf16[2,2,48,768]{3,2,1,0:T(8,128)(2,1)}, bf16[2,2,48,768]{3,2,1,0:T(8,128)(2,1)S(1)}, u32[]{:S(2)}) copy-start(bf16[2,2,48,768]{3,2,1,0:T(8,128)(2,1)S(1)} %copy.92) | copy-start | bytes 884740
  335.7 20.7 %copy-start.59 = (bf16[3,64,512]{2,1,0:T(8,128)(2,1)}, bf16[3,64,512]{2,1,0:T(8,128)(2,1)S(1)}, u32[]{:S(2)}) copy-start(bf16[3,64,512]{2,1,0:T(8,128)(2,1)S(1)} %convolution_convert_fusion.9) | copy-start | bytes 589828
  381.9 4.1 collective-permute-start.2
  384.3 29.3 %copy-start.47 = (bf16[8,2,48,768]{3,2,1,0:T(8,128)(2,1)}, bf16[8,2,48,768]{3,2,1,0:T(8,128)(2,1)S(1)}, u32[]{:S(2)}) copy-start(bf16[8,2,48,768]{3,2,1,0:T(8,128)(2,1)S(1)} %copy.93) | copy-start | bytes 3538948
  384.4 30.1 %copy-start.49 = (bf16[8,2,48,768]{3,2,1,0:T(8,128)(2,1)}, bf16[8,2,48,768]{3,2,1,0:T(8,128)(2,1)S(1)}, u32[]{:S(2)}) copy-start(bf16[8,2,48,768]{3,2,1,0:T(8,128)(2,1)S(1)} %copy.94) | copy-start | bytes 3538948
  384.5 4.9 collective-permute-start.3
  392.0 21.6 %copy-start.61 = (bf16[3,64,512]{2,1,0:T(8,128)(2,1)}, bf16[3,64,512]{2,1,0:T(8,128)(2,1)S(1)}, u32[]{:S(2)}) copy-start(bf16[3,64,512]{2,1,0:T(8,128)(2,1)S(1)} %convolution_convert_fusion.8) | copy-start | bytes 589828
  589.5 61.8 %copy-start.8 = (f32[128,768]{1,0:T(8,128)S(1)}, f32[128,768]{1,0:T(8,128)}, u32[]{:S(2)}) copy-start(f32[128,768]{1,0:T(8,128)} %copy-done.7) | copy-start | bytes 1179652
  589.5 61.8 %copy-start.14 = (f32[5]{0:T(128)S(1)}, f32[5]{0:T(128)}, u32[]{:S(2)}) copy-start(f32[5]{0:T(128)} %refs_6_.1) | copy-start | bytes 64
  589.6 75.5 %copy-start.50 = (bf16[8,2,48,768]{3,2,1,0:T(8,128)(2,1)S(1)}, bf16[8,2,48,768]{3,2,1,0:T(8,128)(2,1)}, u32[]{:S(2)}) copy-start(bf16[8,2,48,768]{3,2,1,0:T(8,128)(2,1)} %copy-done.49) | copy-start | bytes 3538948
  589.6 75.5 %copy-start.115 = (f32[512,768]{1,0:T(8,128)S(1)}, f32[512,768]{1,0:T(8,128)}, u32[]{:S(2)}) copy-start(f32[512,768]{1,0:T(8,128)} %copy-done.114) | copy-start | bytes 4718596
  667.7 23.2 %slice-start.2 = ((s8[6291456]{0:T(1024)(128)(4,1)}), s8[4194304]{0:T(1024)(128)(4,1)S(1)}, s32[]{:S(2)}) async-start(s8[6291456]{0:T(1024)(128)(4,1)} %bitcast.236), calls=%async_computation.10 | async-start | bytes 8388608
  668.6 22.4 %slice-start.3 = ((s8[6291456]{0:T(1024)(128)(4,1)}), s8[2097152]{0:T(1024)(128)(4,1)S(1)}, s32[]{:S(2)}) async-start(s8[6291456]{0:T(1024)(128)(4,1)} %bitcast.236), calls=%async_computation.11 | async-start | bytes 4194304
  669.5 21.0 %copy-start.39 = (bf16[2,2,48,768]{3,2,1,0:T(8,128)(2,1)S(1)}, bf16[2,2,48,768]{3,2,1,0:T(8,128)(2,1)}, u32[]{:S(2)}) copy-start(bf16[2,2,48,768]{3,2,1,0:T(8,128)(2,1)} %copy-done.38) | copy-start | bytes 884740
  669.5 21.4 %copy-start.30 = (pred[512,1024]{1,0:T(8,128)(4,1)S(1)}, pred[512,1024]{1,0:T(8,128)(4,1)}, u32[]{:S(2)}) copy-start(pred[512,1024]{1,0:T(8,128)(4,1)} %copy-done.28) | copy-start | bytes 1572868
  669.5 21.4 %copy-start.95 = (f32[3,512]{1,0:T(4,128)S(1)}, f32[3,512]{1,0:T(4,128)}, u32[]{:S(2)}) copy-start(f32[3,512]{1,0:T(4,128)} %copy-done.94) | copy-start | bytes 18436
  697.9 4.7 collective-permute-start.4
  699.7 3.6 collective-permute-start.5
  706.9 81.0 %reduce-scatter.3.cloned.1.call-start = ((), (), s32[]{:S(2)}) async-start(), calls=%async_computation.4 | async-start | bytes 5308416 | tf_op jit(solution)/shard_map/reduce_scatter | solution.py:1096
  709.1 25.0 %copy-start.46 = (bf16[8,2,48,768]{3,2,1,0:T(8,128)(2,1)S(1)}, bf16[8,2,48,768]{3,2,1,0:T(8,128)(2,1)}, u32[]{:S(2)}) copy-start(bf16[8,2,48,768]{3,2,1,0:T(8,128)(2,1)} %copy.90) | copy-start | bytes 3538948
  709.1 25.0 %copy-start.113 = (f32[512,768]{1,0:T(8,128)S(1)}, f32[512,768]{1,0:T(8,128)}, u32[]{:S(2)}) copy-start(f32[512,768]{1,0:T(8,128)} %copy-done.112) | copy-start | bytes 4718596
  709.1 49.4 %slice-start = ((s8[6291456]{0:T(1024)(128)(4,1)}), s8[4194304]{0:T(1024)(128)(4,1)S(1)}, s32[]{:S(2)}) async-start(s8[6291456]{0:T(1024)(128)(4,1)} %bitcast.234), calls=%async_computation.8 | async-start | bytes 8388608
  734.1 24.4 %slice-start.1 = ((s8[6291456]{0:T(1024)(128)(4,1)}), s8[2097152]{0:T(1024)(128)(4,1)S(1)}, s32[]{:S(2)}) async-start(s8[6291456]{0:T(1024)(128)(4,1)} %bitcast.234), calls=%async_computation.9 | async-start | bytes 4194304
  736.5 21.6 %copy-start.37 = (bf16[2,2,48,768]{3,2,1,0:T(8,128)(2,1)S(1)}, bf16[2,2,48,768]{3,2,1,0:T(8,128)(2,1)}, u32[]{:S(2)}) copy-start(bf16[2,2,48,768]{3,2,1,0:T(8,128)(2,1)} %copy-done.36) | copy-start | bytes 884740
  736.5 22.0 %copy-start.31 = (pred[512,1024]{1,0:T(8,128)(4,1)S(1)}, pred[512,1024]{1,0:T(8,128)(4,1)}, u32[]{:S(2)}) copy-start(pred[512,1024]{1,0:T(8,128)(4,1)} %copy-done.28) | copy-start | bytes 1572868
  736.5 22.0 %copy-start.64 = (bf16[512,192]{0,1:T(8,128)(2,1)S(1)}, bf16[512,192]{0,1:T(8,128)(2,1)}, u32[]{:S(2)}) copy-start(bf16[512,192]{0,1:T(8,128)(2,1)} %copy-done.63) | copy-start | bytes 589828
  736.5 22.0 %copy-start.89 = (bf16[1,512,3,64]{1,3,2,0:T(8,128)(2,1)S(1)}, bf16[1,512,3,64]{1,3,2,0:T(8,128)(2,1)}, u32[]{:S(2)}) copy-start(bf16[1,512,3,64]{1,3,2,0:T(8,128)(2,1)} %copy-done.88) | copy-start | bytes 589828
  736.5 22.0 %copy-start.93 = (f32[3,512]{1,0:T(4,128)S(1)}, f32[3,512]{1,0:T(4,128)}, u32[]{:S(2)}) copy-start(f32[3,512]{1,0:T(4,128)} %copy-done.92) | copy-start | bytes 18436
  763.6 8.2 collective-permute-start.6
  766.9 5.6 collective-permute-start.7
  775.7 166.4 %all-reduce.9.cloned.1.call-start = ((), (), s32[]{:S(2)}) async-start(), calls=%async_computation.6 | async-start | bytes 7077888 | tf_op jit(solution)/shard_map/psum | solution.py:1099
  953.9 34.5 %copy-start.109 = (f32[5]{0:T(128)S(1)}, f32[5]{0:T(128)}, u32[]{:S(2)}) copy-start(f32[5]{0:T(128)} %param.26) | copy-start | bytes 64
  953.9 34.5 %copy-start.110 = (f32[5]{0:T(128)S(1)}, f32[5]{0:T(128)}, u32[]{:S(2)}) copy-start(f32[5]{0:T(128)} %param.27) | copy-start | bytes 64
  953.9 35.7 %copy-start.97 = (f32[5,768]{1,0:T(8,128)S(1)}, f32[5,768]{1,0:T(8,128)}, u32[]{:S(2)}) copy-start(f32[5,768]{1,0:T(8,128)} %param.22) | copy-start | bytes 46084
  953.9 35.7 %copy-start.98 = (f32[5,768]{1,0:T(8,128)S(1)}, f32[5,768]{1,0:T(8,128)}, u32[]{:S(2)}) copy-start(f32[5,768]{1,0:T(8,128)} %param.23) | copy-start | bytes 46084
  953.9 35.7 %copy-start.99 = (f32[5,768]{1,0:T(8,128)S(1)}, f32[5,768]{1,0:T(8,128)}, u32[]{:S(2)}) copy-start(f32[5,768]{1,0:T(8,128)} %param.24) | copy-start | bytes 46084
  954.0 37.1 %copy-start.104 = (pred[67]{0:T(512)(128)(4,1)S(1)}, pred[67]{0:T(512)(128)(4,1)}, u32[]{:S(2)}) copy-start(pred[67]{0:T(512)(128)(4,1)} %get-tuple-element.152) | copy-start | bytes 205
  954.0 37.1 %copy-start.106 = (pred[67]{0:T(512)(128)(4,1)S(1)}, pred[67]{0:T(512)(128)(4,1)}, u32[]{:S(2)}) copy-start(pred[67]{0:T(512)(128)(4,1)} %get-tuple-element.153) | copy-start | bytes 205
  (90 other events, 304.5 us)
Sparse Core Ops, SparseCore 0:
  26.5 136.8 all-reduce.10
  165.0 11.6 all-gather.3
  213.6 11.1 all-gather.5
  707.0 11.6 reduce-scatter.4
  775.8 11.9 reduce-scatter.2
  790.1 151.9 all-reduce.8

commit v2 on v1

--- a/solution.py
+++ b/solution.py
@@ -98,8 +98,8 @@
 
 
 MESH = pl.DeviceIdType.MESH
-ROW_STEP = 256
-TILE_GROUPS = 4
+ROW_STEP = 400
+TILE_GROUPS = 8
 LANES = 128
 
 
@@ -150,24 +150,43 @@
     return grad_stream, jnp.sum(grad_normed * scaled, axis=0, keepdims=True)
 
 
-def tensor_step(name, function, partial, extras, scalars, outs, gather, collective_id):
+def tensor_step(
+    name, function, partial, extras, scalars, outs, gather, collective_id, beside=None, rider=None
+):
     parts = lax.axis_size("tensor")
     share = extras[0].shape[0]
     reduce = partial is not None
+    if beside:
+        count, half_rows = rider.shape[0], rider.shape[-2]
+        half = (count, half_rows, D)
 
     def kernel(*refs):
         refs = list(refs)
         partial_ref = refs.pop(0) if reduce else None
         extra_refs = [refs.pop(0) for _ in extras]
         scalar_refs = [refs.pop(0) for _ in scalars]
+        rider_ref = refs.pop(0) if beside else None
         out_refs = [refs.pop(0) for _ in outs]
         full = refs.pop(0) if gather else None
+        joined = refs.pop(0) if beside else None
         outgoing = refs.pop(0) if reduce else None
         arrived = refs.pop(0) if reduce else None
-        send_sems, recv_sems = refs
+        send_sems, recv_sems = refs[:2]
         me = lax.axis_index("tensor")
         peers = others("tensor")
-        meet([{"tensor": peer} for peer in peers])
+        side = lax.axis_index("seq")
+        twin = [{"seq": 1 - side}] if beside else []
+        meet([{"tensor": peer} for peer in peers] + twin)
+        if beside == "share":
+            _, _, own_sem, twin_send, twin_recv = refs
+            own_copy = pltpu.make_async_copy(rider_ref, joined.at[:, side], own_sem)
+            own_copy.start()
+            twin_copy = send(rider_ref, joined.at[:, side], twin_send, twin_recv, twin[0])
+        if beside == "fold":
+            _, _, own_sem, twin_send, twin_recv, near = refs
+            own_copy = pltpu.make_async_copy(rider_ref.at[:, side], joined, own_sem)
+            own_copy.start()
+            twin_copy = send(rider_ref.at[:, 1 - side], near, twin_send, twin_recv, twin[0])
         total = None
         if reduce:
             copies = []
@@ -202,23 +221,49 @@
                 )
                 for step, peer in enumerate(peers)
             ]
+        if beside:
+            own_copy.wait()
+            twin_copy.wait()
+        if beside == "fold":
+
+            def add_block(block, carry):
+                value = joined[block].astype(jnp.float32) + near[block].astype(jnp.float32)
+                joined[block] = value.astype(jnp.bfloat16)
+                return carry
+
+            lax.fori_loop(0, count, add_block, 0)
+        if gather:
             for copy in copies:
                 copy.wait()
 
     vmem = pl.BlockSpec(memory_space=pltpu.VMEM)
+    anywhere = pl.BlockSpec(memory_space=pl.ANY)
     smem = pl.BlockSpec(memory_space=pltpu.SMEM)
     shapes = [jax.ShapeDtypeStruct(shape, dtype) for shape, dtype in outs]
     if gather:
         shapes.append(jax.ShapeDtypeStruct((parts, share, D), jnp.bfloat16))
     buffers = [pltpu.VMEM((parts - 1, share, D), jnp.bfloat16)] * (2 if reduce else 0)
     operands = ([partial] if reduce else []) + list(extras) + list(scalars)
+    in_specs = [vmem] * (len(operands) - len(scalars)) + [smem] * len(scalars)
+    out_specs = [vmem] * len(shapes)
+    dma = pltpu.SemaphoreType.DMA
+    buffers += [dma((2, parts - 1))] * 2
+    if beside:
+        operands.append(rider)
+        in_specs.append(anywhere)
+        buffers += [dma] * 3
+        folds = beside == "fold"
+        kept = half if folds else (count, 2, half_rows, D)
+        shapes.append(jax.ShapeDtypeStruct(kept, jnp.bfloat16))
+        out_specs.append(vmem if folds else anywhere)
+        buffers += [pltpu.VMEM(half, jnp.bfloat16)] * folds
     return pl.pallas_call(
         kernel,
         name=name,
         out_shape=shapes,
-        in_specs=[vmem] * (len(operands) - len(scalars)) + [smem] * len(scalars),
-        out_specs=[vmem] * len(shapes),
-        scratch_shapes=buffers + [pltpu.SemaphoreType.DMA((2, parts - 1))] * 2,
+        in_specs=in_specs,
+        out_specs=out_specs,
+        scratch_shapes=buffers,
         compiler_params=pltpu.CompilerParams(
             collective_id=collective_id, has_side_effects=True, vmem_limit_bytes=40 << 20
         ),
@@ -515,10 +560,81 @@
     )(stats)
 
 
-def sum_small(block, collective_id):
+def spread_tokens(block, collective_id):
     tensors, groups = lax.axis_size("tensor"), lax.axis_size("dp")
-
-    def kernel(block_ref, out, near, mid, far, near_send, near_recv, mid_send, mid_recv, far_send, far_recv):
+    rows = 2 * tensors * groups
+
+    def kernel(block_ref, ids, targets, kept, count, held, own_sem, send_sems, recv_sems):
+        group, side = lax.axis_index("dp"), lax.axis_index("seq")
+        peers = [
+            {"dp": lax.rem(group + step // 2, groups), "seq": lax.rem(side + step % 2, 2)}
+            for step in range(1, 2 * groups)
+        ]
+        meet(peers)
+        copies = [
+            send(block_ref, held.at[group, side], send_sems.at[step], recv_sems.at[step], peer)
+            for step, peer in enumerate(peers)
+        ]
+        own = pltpu.make_async_copy(block_ref, held.at[group, side], own_sem)
+        own.start()
+        own.wait()
+        for copy in copies:
+            copy.wait()
+        lane = lax.broadcasted_iota(jnp.int32, (1, LANES), 1)
+        total = jnp.zeros((1, LANES), jnp.int32)
+        for half in range(2):
+            for source in range(groups):
+                limit = held[source, half, 2 * tensors : 2 * tensors + 1, :]
+                total = total + limit
+                for part in range(tensors):
+                    row = (half * tensors + part) * groups + source
+                    tile, place = row // TILE_GROUPS, slice(row % TILE_GROUPS, row % TILE_GROUPS + 1)
+                    ids[tile, place, :] = held[source, half, part : part + 1, :]
+                    targets[tile, place, :] = held[source, half, tensors + part : tensors + part + 1, :]
+                    kept[tile, place, :] = jnp.where(lane + part * LANES < limit, 1.0, 0.0)
+        count[...] = total.astype(jnp.float32)
+
+    dma = pltpu.SemaphoreType.DMA
+    vmem = pl.BlockSpec(memory_space=pltpu.VMEM)
+    shape = (rows // TILE_GROUPS, TILE_GROUPS, LANES)
+    return pl.pallas_call(
+        kernel,
+        name="spread_tokens",
+        out_shape=[
+            jax.ShapeDtypeStruct(shape, jnp.int32),
+            jax.ShapeDtypeStruct(shape, jnp.int32),
+            jax.ShapeDtypeStruct(shape, jnp.float32),
+            jax.ShapeDtypeStruct((1, LANES), jnp.float32),
+        ],
+        in_specs=[vmem],
+        out_specs=[vmem] * 4,
+        scratch_shapes=[
+            pltpu.VMEM((groups, 2) + block.shape, jnp.int32),
+            dma,
+            dma((2 * groups - 1,)),
+            dma((2 * groups - 1,)),
+        ],
+        compiler_params=pltpu.CompilerParams(collective_id=collective_id, has_side_effects=True),
+    )(block)
+
+
+def finish(gain_grads, states, grad_ys, home, keep, table_squares, layer_squares, count, smalls, collective_id):
+    tensors, groups = lax.axis_size("tensor"), lax.axis_size("dp")
+    block = (8, D)
+    gain_rows = 2 * LAYERS + 1
+    operands = list(gain_grads) + list(states) + list(grad_ys) + [
+        home, keep, table_squares, layer_squares, count
+    ] + list(smalls)
+
+    def kernel(*refs):
+        refs = list(refs)
+        gain_refs = [refs.pop(0) for _ in gain_grads]
+        state_refs = [refs.pop(0) for _ in states]
+        grad_refs = [refs.pop(0) for _ in grad_ys]
+        home_ref, keep_ref, table_ref, layer_ref, count_ref = [refs.pop(0) for _ in range(5)]
+        small_refs = [refs.pop(0) for _ in smalls]
+        out_refs = [refs.pop(0) for _ in range(8)]
+        near, mid, far, near_send, near_recv, mid_send, mid_recv, far_send, far_recv = refs
         group, part, side = lax.axis_index("dp"), lax.axis_index("tensor"), lax.axis_index("seq")
         parts, groups_else = others("tensor"), others("dp")
         meet(
@@ -526,12 +642,25 @@
             + [{"tensor": peer} for peer in parts]
             + [{"dp": peer} for peer in groups_else]
         )
+        values = []
+        for later in range(1, LAYERS + 1):
+            grad = grad_refs[later - 1][...]
+            for level in range(later + 1):
+                values.append(jnp.sum(grad * state_refs[level][...], keepdims=True))
+        loss = (home_ref[0:1, :] - home_ref[1:2, :]) * keep_ref[...]
+        values.append(jnp.sum(loss, keepdims=True))
+        values.append(jnp.sum(table_ref[...], keepdims=True) + layer_ref[...])
+        lane = lax.broadcasted_iota(jnp.int32, (1, D), 1)
+        row = jnp.zeros((1, D), jnp.float32)
+        for place, value in enumerate(values):
+            row = jnp.where(lane == place, value, row)
+        blank = jnp.zeros((8 - gain_rows - 1, D), jnp.float32)
+        total = jnp.concatenate([ref[...] for ref in gain_refs] + [row, blank], axis=0)
         stages = [
             ("seq", near, side, [1 - side], near_send, near_recv),
             ("tensor", mid, part, parts, mid_send, mid_recv),
             ("dp", far, group, groups_else, far_send, far_recv),
         ]
-        total = block_ref[...]
         for axis, slots, me, peers, send_sems, recv_sems in stages:
             slots[me] = total
             copies = [
@@ -543,20 +672,45 @@
             total = slots[0]
             for index in range(1, slots.shape[0]):
                 total = total + slots[index]
-        out[...] = total
+        gain_total = total[:gain_rows]
+        row = total[gain_rows : gain_rows + 1]
+
+        def pick(place):
+            return jnp.sum(jnp.where(lane == place, row, 0.0), axis=1, keepdims=True)
+
+        mix_squares = jnp.sum(jnp.where(lane < MIX_WEIGHTS, row * row, 0.0), axis=1, keepdims=True)
+        gain_squares = jnp.sum(gain_total * gain_total, keepdims=True)
+        tokens = count_ref[:, 0:1]
+        clip_norm = jnp.sqrt(pick(MIX_WEIGHTS + 1) + gain_squares + mix_squares) / tokens
+        factor = jnp.minimum(1.0, CLIP_NORM / clip_norm) / tokens
+        gain_news = adam_update(
+            *[ref[...] for ref in small_refs[:3]], gain_total * factor, RATE_SMALL, 0.0
+        )
+        mix_news = adam_update(
+            *[ref[...] for ref in small_refs[3:]], row[:, :MIX_WEIGHTS] * factor, RATE_SMALL, 0.0
+        )
+        for ref, value in zip(out_refs[:6], gain_news + mix_news):
+            ref[...] = value
+        ends = jnp.where(lane == 0, pick(MIX_WEIGHTS), jnp.where(lane == 1, clip_norm, factor))
+        out_refs[6][...] = ends[:, :LANES]
+        out_refs[7][...] = jnp.broadcast_to(factor, (8, LANES))
 
     dma = pltpu.SemaphoreType.DMA
     vmem = pl.BlockSpec(memory_space=pltpu.VMEM)
     return pl.pallas_call(
         kernel,
-        name="sum_small",
-        out_shape=jax.ShapeDtypeStruct(block.shape, jnp.float32),
-        in_specs=[vmem],
-        out_specs=vmem,
+        name="finish",
+        out_shape=[jax.ShapeDtypeStruct(value.shape, jnp.float32) for value in smalls]
+        + [
+            jax.ShapeDtypeStruct((1, LANES), jnp.float32),
+            jax.ShapeDtypeStruct((8, LANES), jnp.float32),
+        ],
+        in_specs=[vmem] * len(operands),
+        out_specs=[vmem] * 8,
         scratch_shapes=[
-            pltpu.VMEM((2,) + block.shape, jnp.float32),
-            pltpu.VMEM((tensors,) + block.shape, jnp.float32),
-            pltpu.VMEM((groups,) + block.shape, jnp.float32),
+            pltpu.VMEM((2,) + block, jnp.float32),
+            pltpu.VMEM((tensors,) + block, jnp.float32),
+            pltpu.VMEM((groups,) + block, jnp.float32),
             dma((1,)),
             dma((1,)),
             dma((tensors - 1,)),
@@ -565,7 +719,45 @@
             dma((groups - 1,)),
         ],
         compiler_params=pltpu.CompilerParams(collective_id=collective_id, has_side_effects=True),
-    )(block)
+    )(*operands)
+
+
+def update_slots(plan, factor, master, first, second, layer_grads, grad_table):
+    slots, half_rows, _ = master.shape
+
+    def kernel(plan_ref, factor_ref, master_ref, first_ref, second_ref, *rest):
+        layer_refs, (table_ref, new_master, new_first, new_second) = rest[:LAYERS], rest[LAYERS:]
+        kind = plan_ref[0, pl.program_id(0)]
+        grad = table_ref[...]
+        for level in range(LAYERS):
+            grad = jnp.where(kind == level, layer_refs[level][0].astype(jnp.float32), grad)
+        grad = jnp.where(kind >= 0, grad * factor_ref[0:1, 0:1], 0.0)
+        values = adam_update(
+            master_ref[0], first_ref[0], second_ref[0], grad, RATE_MATRIX, DECAY_MATRIX
+        )
+        for ref, value in zip((new_master, new_first, new_second), values):
+            ref[0] = value
+
+    slot = pl.BlockSpec((1, half_rows, D), lambda step, plan: (step, 0, 0))
+    return pl.pallas_call(
+        kernel,
+        name="update_slots",
+        grid_spec=pltpu.PrefetchScalarGridSpec(
+            num_scalar_prefetch=1,
+            grid=(slots,),
+            in_specs=[pl.BlockSpec((8, LANES), lambda step, plan: (0, 0)), slot, slot, slot]
+            + [
+                pl.BlockSpec(
+                    (1, half_rows, D), lambda step, plan, level=level: (plan[1 + level, step], 0, 0)
+                )
+                for level in range(LAYERS)
+            ]
+            + [pl.BlockSpec((half_rows, D), lambda step, plan: (step, 0))],
+            out_specs=[slot] * 3,
+        ),
+        out_shape=[jax.ShapeDtypeStruct(master.shape, jnp.float32)] * 3,
+        compiler_params=pltpu.CompilerParams(vmem_limit_bytes=32 << 20),
+    )(plan, factor, master, first, second, *layer_grads, grad_table)
 
 
 def row_of(groups_ref):
@@ -576,8 +768,12 @@
     return jnp.concatenate([stat_ref[g, row : row + 1, :] for g in range(TILE_GROUPS)], axis=1)
 
 
-def chunk_of(step):
-    return pl.ds(pl.multiple_of(step * ROW_STEP, ROW_STEP), ROW_STEP)
+def chunk_of(span_ref, step):
+    return pl.ds(pl.multiple_of(span_ref[0] + step * ROW_STEP, 16), ROW_STEP)
+
+
+def chunks_of(span_ref):
+    return (span_ref[1] - span_ref[0] + ROW_STEP - 1) // ROW_STEP
 
 
 def whole(shape):
@@ -602,12 +798,12 @@
             scratch_shapes=scratch,
         ),
         out_shape=out_shape,
-        compiler_params=pltpu.CompilerParams(vmem_limit_bytes=56 << 20),
+        compiler_params=pltpu.CompilerParams(vmem_limit_bytes=60 << 20),
     )(span, *operands)
 
 
-def look_up(span, row_ids, tokens, table_t):
-    rows = table_t.shape[1]
+def look_up(span, row_ids, tokens, table):
+    rows = table.shape[0]
     steps = tokens.shape[0]
 
     def kernel(span_ref, ids_ref, tokens_ref, table_ref, out_ref, acc):
@@ -615,24 +811,24 @@
         wanted = row_of(tokens_ref)
 
         def one(step, carry):
-            chunk = chunk_of(step)
+            chunk = chunk_of(span_ref, step)
             hits = jnp.where(ids_ref[chunk, :] == wanted, 1.0, 0.0).astype(jnp.bfloat16)
-            acc[...] += jnp.dot(table_ref[:, chunk], hits, preferred_element_type=jnp.float32)
+            acc[...] += contract_first(hits, table_ref[chunk, :])
             return carry
 
-        lax.fori_loop(span_ref[0], span_ref[1], one, 0)
-        out_ref[...] = acc[...].T.astype(jnp.bfloat16)
+        lax.fori_loop(0, chunks_of(span_ref), one, 0)
+        out_ref[...] = acc[...].astype(jnp.bfloat16)
 
     return local_call(
         "look_up",
         kernel,
         steps,
         span,
-        (row_ids, tokens, table_t),
-        [whole((rows, 1)), TOKENS_SPEC, whole((D, rows))],
+        (row_ids, tokens, table),
+        [whole((rows, 1)), TOKENS_SPEC, whole((rows, D))],
         jax.ShapeDtypeStruct((steps * TILE, D), jnp.bfloat16),
         ROWS_SPEC,
-        [pltpu.VMEM((D, TILE), jnp.float32)],
+        [pltpu.VMEM((TILE, D), jnp.float32)],
     )
 
 
@@ -646,7 +842,7 @@
 
         def first(step, carry):
             top, target = carry
-            chunk = chunk_of(step)
+            chunk = chunk_of(span_ref, step)
             ids = ids_ref[chunk, :]
             raw = contract_last(table_ref[chunk, :], hidden)
             raw = jnp.where(ids >= 0, raw, -1e30)
@@ -656,15 +852,15 @@
             return (top, target)
 
         blank = jnp.zeros((1, TILE), jnp.float32)
-        top, target = lax.fori_loop(span_ref[0], span_ref[1], first, (blank - 1e30, blank))
+        top, target = lax.fori_loop(0, chunks_of(span_ref), first, (blank - 1e30, blank))
 
         def second(step, total):
-            chunk = chunk_of(step)
+            chunk = chunk_of(span_ref, step)
             powers = jnp.exp(scores[chunk, :] - top)
             powers_ref[chunk, :] = powers.astype(jnp.bfloat16)
             return total + jnp.sum(powers, axis=0, keepdims=True)
 
-        total = lax.fori_loop(span_ref[0], span_ref[1], second, blank)
+        total = lax.fori_loop(0, chunks_of(span_ref), second, blank)
         rest = jnp.zeros((5, LANES), jnp.float32)
         for g in range(TILE_GROUPS):
             lanes = slice(g * LANES, (g + 1) * LANES)
@@ -688,8 +884,8 @@
     )
 
 
-def head_backward(span, row_ids, labels, keep, stats, log_totals, table_t, final, powers):
-    rows = table_t.shape[1]
+def head_backward(span, row_ids, labels, keep, stats, log_totals, table, final, powers):
+    rows = table.shape[0]
     steps = labels.shape[0]
 
     def kernel(
@@ -706,30 +902,30 @@
         hidden = final_ref[...]
 
         def one(step, carry):
-            chunk = chunk_of(step)
+            chunk = chunk_of(span_ref, step)
             grads = powers_ref[chunk, :].astype(jnp.float32) * scale
             grads = grads - jnp.where(ids_ref[chunk, :] == wanted, kept, 0.0)
             grads = grads.astype(jnp.bfloat16)
             grad_table_ref[chunk, :] += jnp.dot(grads, hidden, preferred_element_type=jnp.float32)
-            acc[...] += jnp.dot(table_ref[:, chunk], grads, preferred_element_type=jnp.float32)
+            acc[...] += contract_first(grads, table_ref[chunk, :])
             return carry
 
-        lax.fori_loop(span_ref[0], span_ref[1], one, 0)
-        grad_final_ref[...] = acc[...].T.astype(jnp.bfloat16)
+        lax.fori_loop(0, chunks_of(span_ref), one, 0)
+        grad_final_ref[...] = acc[...].astype(jnp.bfloat16)
 
     return local_call(
         "head_backward",
         kernel,
         steps,
         span,
-        (row_ids, labels, keep, stats, log_totals, table_t, final, powers),
+        (row_ids, labels, keep, stats, log_totals, table, final, powers),
         [
             whole((rows, 1)),
             TOKENS_SPEC,
             TOKENS_SPEC,
             STATS_SPEC,
             STATS_SPEC,
-            whole((D, rows)),
+            whole((rows, D)),
             ROWS_SPEC,
             pl.BlockSpec((rows, TILE), lambda step, span: (0, step)),
         ],
@@ -738,7 +934,7 @@
             jax.ShapeDtypeStruct((rows, D), jnp.float32),
         ],
         [ROWS_SPEC, whole((rows, D))],
-        [pltpu.VMEM((D, TILE), jnp.float32)],
+        [pltpu.VMEM((TILE, D), jnp.float32)],
     )
 
 
@@ -746,7 +942,7 @@
     rows = grad_table.shape[0]
     steps = tokens.shape[0]
 
-    def kernel(span_ref, ids_ref, tokens_ref, grad_ref, table_ref, out_ref):
+    def kernel(span_ref, ids_ref, tokens_ref, grad_ref, table_ref, out_ref, squares_ref):
         @pl.when(pl.program_id(0) == 0)
         def _():
             out_ref[...] = table_ref[...]
@@ -755,12 +951,23 @@
         grads = grad_ref[...]
 
         def one(step, carry):
-            chunk = chunk_of(step)
+            chunk = chunk_of(span_ref, step)
             hits = jnp.where(ids_ref[chunk, :] == wanted, 1.0, 0.0).astype(jnp.bfloat16)
             out_ref[chunk, :] += jnp.dot(hits, grads, preferred_element_type=jnp.float32)
             return carry
 
-        lax.fori_loop(span_ref[0], span_ref[1], one, 0)
+        lax.fori_loop(0, chunks_of(span_ref), one, 0)
+
+        @pl.when(pl.program_id(0) == steps - 1)
+        def _():
+            def square(step, total):
+                values = out_ref[chunk_of(span_ref, step), :]
+                values = (values * values).reshape(ROW_STEP // 8, 8, D).sum(axis=0)
+                return total + values
+
+            squares_ref[...] = lax.fori_loop(
+                0, chunks_of(span_ref), square, jnp.zeros((8, D), jnp.float32)
+            )
 
     return local_call(
         "look_back",
@@ -769,8 +976,11 @@
         span,
         (row_ids, tokens, grad_start, grad_table),
         [whole((rows, 1)), TOKENS_SPEC, ROWS_SPEC, whole((rows, D))],
-        jax.ShapeDtypeStruct((rows, D), jnp.float32),
-        whole((rows, D)),
+        [
+            jax.ShapeDtypeStruct((rows, D), jnp.float32),
+            jax.ShapeDtypeStruct((8, D), jnp.float32),
+        ],
+        [whole((rows, D)), whole((8, D))],
         [],
     )
 
@@ -892,45 +1102,48 @@
         + jnp.arange(half_rows, dtype=jnp.int32)[None, :]
     )
     row_ids = jnp.where(slot_block[:, None] >= blocks, row_ids, -1).reshape(-1, 1)
-    rows = slots * half_rows
-    padded = -(-rows // ROW_STEP) * ROW_STEP
-    row_ids = jnp.pad(row_ids, ((0, padded - rows), (0, 0)), constant_values=-1)
+    spare = -(-ROW_STEP // half_rows)
+    row_ids = jnp.pad(row_ids, ((0, spare * half_rows), (0, 0)), constant_values=-1)
     held = jnp.sum(jnp.where(mine, 1, 0)) * half_rows
     first_held = jnp.sum(jnp.where(mine & (block_ids < blocks), 1, 0)) * half_rows
-    span = jnp.stack([first_held // ROW_STEP, (held + ROW_STEP - 1) // ROW_STEP]).astype(jnp.int32)
-
-    packed = jnp.concatenate([token_ids.reshape(-1), labels.reshape(-1), real_counts])
-    packed = lax.all_gather(packed, ("dp", "seq")).reshape(groups, 2, -1)
-
-    def by_home(tokens):
-        tokens = tokens.reshape(groups, 2, tensors, share).transpose(1, 2, 0, 3)
-        return tokens.reshape(-1, TILE_GROUPS, LANES)
-
-    ids_all = by_home(packed[:, :, :row_count])
-    labels_all = by_home(packed[:, :, row_count : 2 * row_count])
-    counts_all = packed[:, :, 2 * row_count]
-    token_count = jnp.sum(counts_all).astype(jnp.float32)
-    keep_all = by_home(
-        jnp.where(jnp.arange(row_count)[None, None, :] < counts_all[:, :, None], 1.0, 0.0)
-    )
+    span = jnp.stack([first_held, held]).astype(jnp.int32)
+    level_of = jnp.where(slot_block < 0, -1, jnp.minimum(slot_block // layer_blocks, LAYERS))
+    plan = jnp.stack(
+        [level_of]
+        + [
+            jnp.where(level_of == level, slot_block - level * layer_blocks, 0)
+            for level in range(LAYERS)
+        ]
+    ).astype(jnp.int32)
+
+    packed = jnp.concatenate(
+        [
+            token_ids.reshape(tensors, LANES),
+            labels.reshape(tensors, LANES),
+            jnp.broadcast_to(real_counts[:, None], (16 - 2 * tensors, LANES)),
+        ],
+        axis=0,
+    )
+    ids_all, labels_all, keep_all, count = spread_tokens(packed, 15)
     order = (2, tensors, groups, share)
 
-    master_low = master.astype(jnp.bfloat16)
-    table = jnp.pad(master_low.reshape(rows, D), ((0, padded - rows), (0, 0)))
-    table_t = table.T
-
-    weights_all = []
+    table_slots = jnp.pad(master.astype(jnp.bfloat16), ((0, spare), (0, 0), (0, 0)))
+    table = table_slots.reshape(-1, D)
+
+    halves = []
     for level in range(LAYERS):
         chosen = slice(level * layer_blocks, (level + 1) * layer_blocks)
         own = jnp.where(
-            mine[chosen][:, None, None], jnp.take(master_low, slot_rank[chosen], axis=0), 0.0
+            mine[chosen][:, None, None], jnp.take(table_slots, slot_rank[chosen], axis=0), 0.0
         ).astype(jnp.bfloat16)
-        own = lax.psum(own, "dp")
-        own = lax.all_gather(own, "seq", axis=1).reshape(layer_rows, D)
+        if level:
+            own, halves[-1] = lax.optimization_barrier((own, halves[-1]))
+        halves.append(lax.psum(own, "dp"))
+
+    def cut(joined):
+        joined = joined.reshape(layer_rows, D)
         cut_one, cut_two = head_rows + out_rows, head_rows + out_rows + unit_rows
-        weights_all.append(
-            (own[:head_rows], own[head_rows:cut_one], own[cut_one:cut_two], own[cut_two:])
-        )
+        return (joined[:head_rows], joined[head_rows:cut_one], joined[cut_one:cut_two], joined[cut_two:])
 
     positions = seq_part * half_len + jnp.arange(row_count) % half_len
     cosine, sine = rotary(positions)
@@ -939,7 +1152,7 @@
     allowed = (key_pos[None, :] <= query_pos[:, None]) & (key_pos[None, :] >= 0)
     geometry = (cosine, sine, allowed, seq_count, half_len, local_heads)
 
-    looked = look_up(span, row_ids, ids_all, table_t).reshape(order + (D,))
+    looked = look_up(span, row_ids, ids_all, table).reshape(order + (D,))
     start = reduce_rows(looked, 0)
     gain = [gains[i : i + 1] for i in range(2 * LAYERS + 1)]
     piece = ((share, D), jnp.float32)
@@ -959,7 +1172,10 @@
             stream = stream + scalars[base + source] * state
         return (outcome, stream, layer_norm_parts(stream)[0] * gain_row)
 
-    (normed,) = tensor_step("normed", normed_of, None, (start, gain[0]), (), [], True, 1)
+    normed, joined = tensor_step(
+        "normed", normed_of, None, (start, gain[0]), (), [], True, 1, "share", halves[0]
+    )
+    weights_all = [cut(joined)]
     states, streams, inners, kept_all = [start], [start], [], []
     for level in range(LAYERS):
         qkv_w, out_w, up_w, down_w = weights_all[level]
@@ -988,7 +1204,10 @@
             [piece, piece] + ([((share, D), jnp.bfloat16)] if last else []),
             not last,
             3 + level,
+            *((None, None) if last else ("share", halves[level + 1])),
         )
+        if not last:
+            weights_all.append(cut(results[3]))
         inners.append(inner)
         kept_all.append((normed, kept, attended, normed_two, hidden, activated))
         states.append(results[0])
@@ -1000,10 +1219,6 @@
     home, log_totals = join_stats(
         stats.reshape((2, tensors, groups, 8, LANES)), 4 + LAYERS
     )
-    keep = jnp.where(
-        tensor_part * share + jnp.arange(share) < real_counts[0], 1.0, 0.0
-    ).astype(jnp.float32)
-    loss_local = jnp.sum((home[0] - home[1]) * keep)
     grad_final, grad_table = head_backward(
         span,
         row_ids,
@@ -1011,7 +1226,7 @@
         keep_all,
         stats,
         log_totals.reshape(-1, 8, LANES),
-        table_t,
+        table,
         final_all,
         powers,
     )
@@ -1072,6 +1287,15 @@
         grad_attn = grad_attn.reshape(row_count, D)
         grad_attended = contract_last(grad_attn, out_w).astype(jnp.bfloat16)
         grad_joined = attend_back(grad_attended, kept, geometry)
+        grads = jnp.concatenate(
+            [
+                contract_first(grad_joined, normed),
+                contract_first(attended, grad_attn),
+                contract_first(grad_hidden, normed_two),
+                contract_first(activated, grad_branch),
+            ],
+            axis=0,
+        ).astype(jnp.bfloat16)
         results = tensor_step(
             f"stream_back_{level}",
             partial(stream_back, level),
@@ -1081,64 +1305,44 @@
             [piece, piece, row] + ([] if level else [((share, D), jnp.bfloat16)]),
             level > 0,
             7 + LAYERS + level,
+            "fold",
+            grads.reshape(layer_blocks, 2, half_rows, D),
         )
-        grad_ys[level], grad_state, gain_grads[2 * level] = results[:3]
-        branch_before, grad_branch = grad_branch, results[3]
-        grads = jnp.concatenate(
-            [
-                contract_first(grad_joined, normed),
-                contract_first(attended, grad_attn),
-                contract_first(grad_hidden, normed_two),
-                contract_first(activated, branch_before),
-            ],
-            axis=0,
-        ).astype(jnp.bfloat16)
-        grads = lax.psum_scatter(
-            grads.reshape(layer_blocks, 2, half_rows, D), "seq", scatter_dimension=1, tiled=False
-        )
-        layer_grads[level] = lax.psum(grads, "dp")
-
-    grad_mix = [None] * MIX_WEIGHTS
-    for later in range(1, LAYERS + 1):
-        for block in range(later + 1):
-            grad_mix[later * (later + 1) // 2 - 1 + block] = jnp.sum(grad_ys[later] * states[block])
+        grad_ys[level], grad_state, gain_grads[2 * level], grad_branch, folded = results
+        if level < LAYERS - 1:
+            folded, layer_grads[level + 1] = lax.optimization_barrier(
+                (folded, layer_grads[level + 1])
+            )
+        layer_grads[level] = lax.psum(folded, "dp")
 
     grad_start_all = gather_all(grad_branch, 3 + LAYERS).reshape(-1, D)
-    grad_table = look_back(span, row_ids, ids_all, grad_start_all, grad_table)
-    layer_grad = jnp.concatenate(layer_grads, axis=0)
-    placed = jnp.take(layer_grad, jnp.clip(slot_block, 0, blocks - 1), axis=0).astype(jnp.float32)
-    owned = jnp.where(
-        ((slot_block >= 0) & (slot_block < blocks))[:, None, None],
-        placed,
-        grad_table[:rows].reshape(slots, half_rows, D),
-    )
-    small = jnp.concatenate([jnp.stack(grad_mix), loss_local[None], jnp.sum(owned * owned)[None]])
-    small = jnp.concatenate(
-        [
-            jnp.concatenate(gain_grads, axis=0),
-            jnp.pad(small, (0, D - small.shape[0]))[None],
-            jnp.zeros((7 - 2 * LAYERS - 1, D), jnp.float32),
-        ],
-        axis=0,
-    )
-    small = sum_small(small, 7 + 2 * LAYERS)
-    gain_total = small[: 2 * LAYERS + 1]
-    mix_total = small[2 * LAYERS + 1, :MIX_WEIGHTS]
-    loss_sum = small[2 * LAYERS + 1, MIX_WEIGHTS]
-    squares = small[2 * LAYERS + 1, MIX_WEIGHTS + 1]
-    clip_norm = (
-        jnp.sqrt(squares + jnp.sum(gain_total * gain_total) + jnp.sum(mix_total * mix_total))
-        / token_count
-    )
-    factor = jnp.minimum(1.0, CLIP_NORM / clip_norm) / token_count
-    new_master, new_first, new_second = adam_update(
-        master, first_moment, second_moment, owned * factor, RATE_MATRIX, DECAY_MATRIX
-    )
-    new_gains, new_gains_first, new_gains_second = adam_update(
-        gains, gains_first, gains_second, gain_total * factor, RATE_SMALL, 0.0
-    )
-    new_mix, new_mix_first, new_mix_second = adam_update(
-        mix, mix_first, mix_second, mix_total * factor, RATE_SMALL, 0.0
+    grad_table, table_squares = look_back(span, row_ids, ids_all, grad_start_all, grad_table)
+    layer_squares = jnp.zeros((), jnp.float32)
+    for level in range(LAYERS):
+        chosen = slice(level * layer_blocks, (level + 1) * layer_blocks)
+        values = layer_grads[level].astype(jnp.float32)
+        layer_squares += jnp.sum(jnp.where(mine[chosen][:, None, None], values * values, 0.0))
+    keep = jnp.where(
+        tensor_part * share + jnp.arange(share) < real_counts[0], 1.0, 0.0
+    ).astype(jnp.float32)
+    news = finish(
+        gain_grads,
+        states,
+        grad_ys[1:],
+        home,
+        keep[None],
+        table_squares,
+        layer_squares.reshape(1, 1),
+        count,
+        (gains, gains_first, gains_second, mix[None], mix_first[None], mix_second[None]),
+        7 + 2 * LAYERS,
+    )
+    new_gains, new_gains_first, new_gains_second = news[:3]
+    new_mix, new_mix_first, new_mix_second = [value[0] for value in news[3:6]]
+    loss_sum, clip_norm = news[6][0, 0], news[6][0, 1]
+    token_count = count[0, 0]
+    new_master, new_first, new_second = update_slots(
+        plan, news[7], master, first_moment, second_moment, layer_grads, grad_table
     )
     return (
         new_master,

time: 1040 us -> 880 us (0.85)
  waiting for transfers between devices: 199 us -> 107 us
  other arithmetic: 73.4 us -> 28.1 us
  Pallas kernels: 577 us -> 612 us
  local copies, waits for them, and re-layouts: 71.6 us -> 41.2 us
  blocking collectives: 26.8 us -> 0 us
    psum x2 -> x4, waiting for transfers between devices: 187 us -> 107 us  [the longest x2 62.6 us: body(): layer_grads[level] = lax.psum(folded, 'dp')]
    pallas_call x11 -> x13, Pallas kernels: 195 us -> 258 us  [the longest x10 186 us: tensor_step(): pl.pallas_call(kernel, name=name, out_shape=shapes, in_specs=in_specs, ou...]
    sub x3 -> x0, other arithmetic: 27.6 us -> none  [adam_update(): weight - rate * (first_hat / (jnp.sqrt(second_hat) + ADAM_EPS) + decay *...]
    unnamed x1 -> x0, blocking collectives: 26.8 us -> none
    pallas_call x4, Pallas kernels: 138 us -> 121 us  [local_call(): pl.pallas_call(kernel, name=name, grid_spec=pltpu.PrefetchScalarGridSpec(...]
    reduce_scatter x2 -> x0, waiting for transfers between devices: 12.1 us -> none  [body(): lax.psum_scatter(grads.reshape(layer_blocks, 2, half_rows, D), 'seq', sca...]
    slice x2 -> x0, other arithmetic: 11.4 us -> none  [the longest x1 10.8 us: body(): grad_table[:rows].reshape(slots, half_rows, D)]
    unnamed x251 -> x206, local copies, waits for them, and re-layouts: 21.3 us -> 24.6 us
  transfers between devices with their start and end apart: 14 -> 12, of which waited for: 3 -> 4; matrix products, arithmetic and copies ran while one was open for 7% -> 4% of each run, Pallas kernels for 23% -> 23%
where the time goes in v2:
time: 880 us; the launch traced here: 866 us
  Pallas kernels  612 us (70%)
  waiting for transfers between devices  107 us (12%)
  matrix products  43.9 us (5%)
  local copies, waits for them, and re-layouts  41.2 us (5%)
  other arithmetic  28.1 us (3%)
  between operations  20.5 us (2%)
  starting transfers between devices  13.6 us (2%)
    pallas_call x10, Pallas kernels, tensor_step(): pl.pallas_call(kernel, name=name, out_shape=shapes, in_specs=in_specs, ou...  186 us
    pallas_call x4, Pallas kernels, local_call(): pl.pallas_call(kernel, name=name, grid_spec=pltpu.PrefetchScalarGridSpec(...  121 us
    pallas_call x2, Pallas kernels, reduce_all(): pl.pallas_call(kernel, name='reduce_all', out_shape=jax.ShapeDtypeStruct(...  110 us
    pallas_call x2, Pallas kernels, gather_all(): pl.pallas_call(kernel, name='gather_all', out_shape=jax.ShapeDtypeStruct(...  93.7 us
    psum x2, waiting for transfers between devices, body(): layer_grads[level] = lax.psum(folded, 'dp')  62.6 us
    pallas_call x1, Pallas kernels, update_slots(): pl.pallas_call(kernel, name='update_slots', grid_spec=pltpu.PrefetchScala...  47.5 us
    psum x2, waiting for transfers between devices, body(): halves.append(lax.psum(own, 'dp'))  44.1 us
    pallas_call x1, Pallas kernels, join_stats(): pl.pallas_call(kernel, name='join_stats', out_shape=[jax.ShapeDtypeStruct...  29.5 us
  transfers between devices with their start and end apart: 12, of which 4 were waited for; matrix products, arithmetic and copies ran while one was open for 4% of the time, Pallas kernels for 23%

profile of v2, /device:TPU:0, one launch (start us, length us, event | category | flops | bytes accessed | tf_op | source)
XLA Modules:
  0.0 866.2 jit_solution(17352801197516026489)
XLA Ops:
  9.5 4.4 convert_element_type.136
  14.0 2.9 pad.9
  16.9 3.2 gather_fusion.1
  26.9 10.1 %spread_tokens.1 = (s32[4,8,128]{2,1,0:T(8,128)}, s32[4,8,128]{2,1,0:T(8,128)}, f32[4,8,128]{2,1,0:T(8,128)}, f32[1,128]{1,0:T(1,128)}) custom-call(s32[16,128]{1,0:T(8,128)} %add_add_fusion.block_ref), custom_call_target="tpu_custom_call" | custom-call | tf_op jit(solution)/shard_map/spread_tokens/pallas_call | solution.py:600
  37.6 24.9 %look_up.1 = bf16[4096,768]{1,0:T(8,128)(2,1)} custom-call(s32[2]{0:T(128)} %pad_add_fusion.2.span_ref, s32[3648,1]{1,0:T(8,128)} %pad.8.ids_ref, s32[4,8,128]{2,1,0:T(8,128)} %get-tuple-element.71.tokens_ref, bf16[3648,768]{1,0:T(8,128)(2,1)} %bitcast.218), custom_call_target="tpu_custom_call" | custom-call | tf_op jit(solution)/shard_map/look_up/pallas_call | solution.py:790
  62.5 54.6 %reduce_all.2.refs_0_.refs_1_.refs_3_.refs_2_.refs_5_ = f32[128,768]{1,0:T(8,128)} custom-call(bf16[2,4,4,128,768]{4,3,2,1,0:T(8,128)(2,1)} %bitcast.227), custom_call_target="tpu_custom_call" | custom-call | tf_op jit(solution)/shard_map/reduce_all/pallas_call | solution.py:351
  117.2 3.3 gather_fusion
  124.9 12.0 %normed.1 = (bf16[4,128,768]{2,1,0:T(8,128)(2,1)S(1)}, bf16[24,2,48,768]{3,2,1,0:T(8,128)(2,1)S(1)}) custom-call(f32[128,768]{1,0:T(8,128)S(1)} %copy-done.1, f32[1,768]{1,0:T(1,128)S(1)} %get-tuple-element.172.refs_1_.refs_3_, bf16[24,48,768]{2,1,0:T(8,128)(2,1)S(1)} %copy-done.7), custom_call_target="tpu_custom_call" | custom-call | tf_op jit(solution)/shard_map/normed/pallas_call | solution.py:260
  139.4 2.0 collective-permute-start
  141.4 2.0 collective-permute-start.1
  143.7 1.8 fusion.67
  145.5 2.5 fusion
  148.1 1.8 exponential_reduce_fusion.1
  150.8 2.7 convolution_convert_fusion.9
  153.9 19.1 %inner.2 = (f32[128,768]{1,0:T(8,128)S(1)}, bf16[4,128,768]{2,1,0:T(8,128)(2,1)S(1)}) custom-call(f32[512,768]{1,0:T(8,128)S(1)} %fusion.74.refs_0_, f32[128,768]{1,0:T(8,128)S(1)} %copy-done.1, f32[1,768]{1,0:T(1,128)S(1)} %get-tuple-element.171.refs_2_.refs_3_), custom_call_target="tpu_custom_call" | custom-call | tf_op jit(solution)/shard_map/inner/pallas_call | solution.py:260
  176.1 44.1 %all-reduce.9.cloned.1.call-done.refs_5_ = bf16[24,48,768]{2,1,0:T(8,128)(2,1)} async-done(((bf16[24,48,768]{2,1,0:T(8,128)(2,1)}), bf16[24,48,768]{2,1,0:T(8,128)(2,1)}) %all-reduce.9.cloned.1.call-update) | async-done | bytes 1769488 | tf_op jit(solution)/shard_map/psum | solution.py:1141
  222.4 21.6 %outcome_0.1 = (f32[128,768]{1,0:T(8,128)S(1)}, f32[128,768]{1,0:T(8,128)S(1)}, bf16[4,128,768]{2,1,0:T(8,128)(2,1)S(1)}, bf16[24,2,48,768]{3,2,1,0:T(8,128)(2,1)S(1)}) custom-call(f32[512,768]{1,0:T(8,128)S(1)} %fusion.64.refs_0_, f32[128,768]{1,0:T(8,128)S(1)} %get-tuple-element.76.refs_1_.refs_2_, f32[1,768]{1,0:T(1,128)S(1)} %get-tuple-element.170.refs_2_.refs_3_, ...), custom_call_target="tpu_custom_call" | custom-call | tf_op jit(solution)/shard_map/outcome_0/pallas_call | solution.py:260
  246.2 1.9 collective-permute-start.2
  251.4 1.8 exponential_reduce_fusion
  256.6 21.5 %inner.3 = (f32[128,768]{1,0:T(8,128)S(1)}, bf16[4,128,768]{2,1,0:T(8,128)(2,1)S(1)}) custom-call(f32[512,768]{1,0:T(8,128)S(1)} %fusion.77.refs_0_, f32[128,768]{1,0:T(8,128)S(1)} %get-tuple-element.82.refs_1_.refs_2_, f32[1,768]{1,0:T(1,128)S(1)} %get-tuple-element.169.refs_2_.refs_3_), custom_call_target="tpu_custom_call" | custom-call | tf_op jit(solution)/shard_map/inner/pallas_call | solution.py:260
  280.2 13.1 %outcome_1.1 = (f32[128,768]{1,0:T(8,128)S(1)}, f32[128,768]{1,0:T(8,128)S(1)}, bf16[128,768]{1,0:T(8,128)(2,1)S(1)}) custom-call(f32[512,768]{1,0:T(8,128)S(1)} %fusion.65.refs_0_, f32[128,768]{1,0:T(8,128)S(1)} %get-tuple-element.84.refs_1_.refs_2_, f32[1,768]{1,0:T(1,128)S(1)} %copy-done.18, f32[128,768]{1,0:T(8,128)S(1)} %copy-done.1, ...), custom_call_target="tpu_custom_call" | custom-call | tf_op jit(solution)/shard_map/outcome_1/pallas_call | solution.py:260
  293.9 46.8 %gather_all.2 = bf16[2,4,4,128,768]{4,3,2,1,0:T(8,128)(2,1)} custom-call(bf16[128,768]{1,0:T(8,128)(2,1)} %copy-done.17), custom_call_target="tpu_custom_call" | custom-call | tf_op jit(solution)/shard_map/gather_all/pallas_call | solution.py:436
  340.7 27.4 %head_forward.1 = (bf16[3648,4096]{1,0:T(8,128)(2,1)}, f32[32,8,128]{2,1,0:T(8,128)}) custom-call(s32[2]{0:T(128)} %pad_add_fusion.2.span_ref, s32[3648,1]{1,0:T(8,128)} %pad.8.ids_ref, s32[4,8,128]{2,1,0:T(8,128)} %get-tuple-element.80.labels_ref, bf16[3648,768]{1,0:T(8,128)(2,1)} %bitcast.219, bf16[4096,768]{1,0:T(8,128)(2,1)} %bitcast.221), custom_call_target="tpu_custom_call" | custom-call | tf_op jit(solution)/shard_map/head_forward/pallas_call | solution.py:790
  368.1 29.5 %join_stats.1 = (f32[8,128]{1,0:T(8,128)}, f32[2,4,4,8,128]{4,3,2,1,0:T(8,128)}) custom-call(f32[2,4,4,8,128]{4,3,2,1,0:T(8,128)} %bitcast.264), custom_call_target="tpu_custom_call" | custom-call | tf_op jit(solution)/shard_map/join_stats/pallas_call | solution.py:537
  397.6 42.1 %head_backward.1 = (bf16[4096,768]{1,0:T(8,128)(2,1)}, f32[3648,768]{1,0:T(8,128)}) custom-call(s32[2]{0:T(128)} %pad_add_fusion.2.span_ref, s32[3648,1]{1,0:T(8,128)} %pad.8.ids_ref, s32[4,8,128]{2,1,0:T(8,128)} %get-tuple-element.80.labels_ref, f32[4,8,128]{2,1,0:T(8,128)} %get-tuple-element.81.keep_ref, f32[32,8,128]{2,1,0:T(8,128)} %get-tuple-element.87.stats_ref, ...), custom_call_target="tpu_custom_call" | custom-call | tf_op jit(solution)/shard_map/head_backward/pallas_call | solution.py:790
  439.7 55.6 %reduce_all.3.refs_0_ = f32[128,768]{1,0:T(8,128)} custom-call(bf16[2,4,4,128,768]{4,3,2,1,0:T(8,128)(2,1)} %bitcast.229), custom_call_target="tpu_custom_call" | custom-call | tf_op jit(solution)/shard_map/reduce_all/pallas_call | solution.py:351
  496.3 12.9 %top_back.1 = (f32[128,768]{1,0:T(8,128)S(1)}, f32[128,768]{1,0:T(8,128)S(1)}, f32[1,768]{1,0:T(1,128)S(1)}, bf16[4,128,768]{2,1,0:T(8,128)(2,1)S(1)}) custom-call(f32[128,768]{1,0:T(8,128)S(1)} %copy-done.9, f32[128,768]{1,0:T(8,128)S(1)} %get-tuple-element.91.refs_1_, f32[1,768]{1,0:T(1,128)S(1)} %copy-done.18, f32[5]{0:T(128)S(1)} %copy-done.20), custom_call_target="tpu_custom_call" | custom-call | tf_op jit(solution)/shard_map/top_back/pallas_call | solution.py:260
  513.7 20.6 %inner_back.2 = (f32[128,768]{1,0:T(8,128)S(1)}, f32[1,768]{1,0:T(1,128)S(1)}, bf16[4,128,768]{2,1,0:T(8,128)(2,1)S(1)}) custom-call(f32[512,768]{1,0:T(8,128)S(1)} %fusion.79.refs_0_, f32[128,768]{1,0:T(8,128)S(1)} %get-tuple-element.93.refs_1_, f32[128,768]{1,0:T(8,128)S(1)} %get-tuple-element.84.refs_1_.refs_2_, ...), custom_call_target="tpu_custom_call" | custom-call | tf_op jit(solution)/shard_map/inner_back/pallas_call | solution.py:260
  534.7 1.8 convolution_bitcast_fusion.1
  536.5 2.5 multiply_reduce_fusion.1
  539.1 1.9 multiply_convert_fusion.1
  549.1 27.1 %stream_back_1.1 = (f32[128,768]{1,0:T(8,128)S(1)}, f32[128,768]{1,0:T(8,128)S(1)}, f32[1,768]{1,0:T(1,128)S(1)}, bf16[4,128,768]{2,1,0:T(8,128)(2,1)S(1)}, bf16[24,48,768]{2,1,0:T(8,128)(2,1)}) custom-call(f32[512,768]{1,0:T(8,128)S(1)} %fusion.29.refs_0_, f32[128,768]{1,0:T(8,128)S(1)} %get-tuple-element.95.refs_1_, ...), custom_call_target="tpu_custom_call" | custom-call | tf_op jit(solution)/shard_map/stream_back_1/pallas_call | solution.py:260
  578.9 1.9 convolution_convert_fusion.1
  580.8 2.0 convolution_convert_fusion
  582.8 21.5 %inner_back.3 = (f32[128,768]{1,0:T(8,128)S(1)}, f32[1,768]{1,0:T(1,128)S(1)}, bf16[4,128,768]{2,1,0:T(8,128)(2,1)S(1)}) custom-call(f32[512,768]{1,0:T(8,128)S(1)} %fusion.80.refs_0_, f32[128,768]{1,0:T(8,128)S(1)} %get-tuple-element.98.refs_1_, f32[128,768]{1,0:T(8,128)S(1)} %get-tuple-element.76.refs_1_.refs_2_, ...), custom_call_target="tpu_custom_call" | custom-call | tf_op jit(solution)/shard_map/inner_back/pallas_call | solution.py:260
  604.7 1.8 convolution_bitcast_fusion
  606.6 3.7 multiply_reduce_fusion
  610.2 1.9 multiply_convert_fusion
  618.3 3.1 fusion.20
  627.4 17.0 %stream_back_0.1 = (f32[128,768]{1,0:T(8,128)}, f32[128,768]{1,0:T(8,128)}, f32[1,768]{1,0:T(1,128)S(1)}, bf16[128,768]{1,0:T(8,128)(2,1)S(1)}, bf16[24,48,768]{2,1,0:T(8,128)(2,1)}) custom-call(f32[512,768]{1,0:T(8,128)S(1)} %fusion.28.refs_0_, f32[128,768]{1,0:T(8,128)S(1)} %get-tuple-element.100.refs_1_, f32[128,768]{1,0:T(8,128)S(1)} %copy-done.1, ...), custom_call_target="tpu_custom_call" | custom-call | tf_op jit(solution)/shard_map/stream_back_0/pallas_call | solution.py:260
  645.1 49.5 %all-reduce.11.cloned.1.call-done.rest_1_ = bf16[24,48,768]{2,1,0:T(8,128)(2,1)} async-done(((bf16[24,48,768]{2,1,0:T(8,128)(2,1)}), bf16[24,48,768]{2,1,0:T(8,128)(2,1)}) %all-reduce.11.cloned.1.call-update) | async-done | bytes 1769488 | tf_op jit(solution)/shard_map/psum | solution.py:1316
  695.2 46.9 %gather_all.3 = bf16[2,4,4,128,768]{4,3,2,1,0:T(8,128)(2,1)} custom-call(bf16[128,768]{1,0:T(8,128)(2,1)} %copy-done.16), custom_call_target="tpu_custom_call" | custom-call | tf_op jit(solution)/shard_map/gather_all/pallas_call | solution.py:436
  742.1 26.4 %look_back.1 = (f32[3648,768]{1,0:T(8,128)}, f32[8,768]{1,0:T(8,128)}) custom-call(s32[2]{0:T(128)} %pad_add_fusion.2.span_ref, s32[3648,1]{1,0:T(8,128)} %pad.8.ids_ref, s32[4,8,128]{2,1,0:T(8,128)} %get-tuple-element.71.tokens_ref, bf16[4096,768]{1,0:T(8,128)(2,1)} %bitcast.228, f32[3648,768]{1,0:T(8,128)} %get-tuple-element.110.table_ref), custom_call_target="tpu_custom_call" | custom-call | tf_op jit(solution)/shard_map/look_back/pallas_call | solution.py:790
  770.1 13.0 %all-reduce.13.cloned.1.call-done.rest_0_ = bf16[24,48,768]{2,1,0:T(8,128)(2,1)} async-done(((bf16[24,48,768]{2,1,0:T(8,128)(2,1)}), bf16[24,48,768]{2,1,0:T(8,128)(2,1)}) %all-reduce.13.cloned.1.call-update) | async-done | bytes 1769488 | tf_op jit(solution)/shard_map/psum | solution.py:1316
  783.1 3.2 select_reduce_fusion.1
  787.6 13.8 %finish.1 = (f32[5,768]{1,0:T(8,128)}, f32[5,768]{1,0:T(8,128)}, f32[5,768]{1,0:T(8,128)}, f32[1,5]{1,0:T(1,128)}, f32[1,5]{1,0:T(1,128)}, /*index=5*/f32[1,5]{1,0:T(1,128)}, f32[1,128]{1,0:T(1,128)}, f32[8,128]{1,0:T(8,128)}) custom-call(f32[1,768]{1,0:T(1,128)} %copy-done.26, f32[1,768]{1,0:T(1,128)} %copy-done.25, f32[1,768]{1,0:T(1,128)} %copy-done.24, ...), custom_call_target="tpu_custom_call" | custom-call | tf_op jit(solution)/shard_map/finish/pallas_call | solution.py:700
  802.7 3.8 copy-done
  807.3 47.5 %update_slots.1 = (f32[67,48,768]{2,1,0:T(8,128)}, f32[67,48,768]{2,1,0:T(8,128)}, f32[67,48,768]{2,1,0:T(8,128)}) custom-call(s32[3,67]{1,0:T(4,128)S(1)} %pad_add_fusion.1.plan_ref, f32[8,128]{1,0:T(8,128)S(1)} %copy-done.21, f32[67,48,768]{2,1,0:T(8,128)S(1)} %copy-done, f32[67,48,768]{2,1,0:T(8,128)} %first_ref.1, f32[67,48,768]{2,1,0:T(8,128)} %second_ref.1, ...), custom_call_target="tpu_custom_call" | custom-call | tf_op jit(solution)/shard_map/update_slots/pallas_call | solution.py:742
  (319 shorter events, 69.7 us)
Async XLA Ops:
  7.2 116.2 %all-reduce.7.cloned.1.call-start = ((), (), s32[]{:S(2)}) async-start(), calls=%async_computation | async-start | bytes 3538944 | tf_op jit(solution)/shard_map/psum | solution.py:1141
  21.7 198.6 %all-reduce.9.cloned.1.call-start = ((), (), s32[]{:S(2)}) async-start(), calls=%async_computation.1 | async-start | bytes 3538944 | tf_op jit(solution)/shard_map/psum | solution.py:1141
  121.4 17.8 %copy-start.66 = (f32[512,32]{0,1:T(8,128)}, f32[512,32]{0,1:T(8,128)S(1)}, u32[]{:S(2)}) copy-start(f32[512,32]{0,1:T(8,128)S(1)} %get-tuple-element.174) | copy-start | bytes 196612
  139.1 10.7 %copy-start.62 = (bf16[512,192]{0,1:T(8,128)(2,1)}, bf16[512,192]{0,1:T(8,128)(2,1)S(1)}, u32[]{:S(2)}) copy-start(bf16[512,192]{0,1:T(8,128)(2,1)S(1)} %slice.219) | copy-start | bytes 589828
  139.2 14.3 %copy-start.38 = (bf16[2,2,48,768]{3,2,1,0:T(8,128)(2,1)}, bf16[2,2,48,768]{3,2,1,0:T(8,128)(2,1)S(1)}, u32[]{:S(2)}) copy-start(bf16[2,2,48,768]{3,2,1,0:T(8,128)(2,1)S(1)} %slice.144) | copy-start | bytes 884740
  139.3 6.2 copy-start.52
  139.3 6.2 copy-start.70
  139.4 6.1 collective-permute-start
  141.4 8.4 collective-permute-start.1
  143.4 551.2 %all-reduce.11.cloned.1.call-start = ((), (), s32[]{:S(2)}) async-start(), calls=%async_computation.2 | async-start | bytes 3538944 | tf_op jit(solution)/shard_map/psum | solution.py:1316
  145.5 27.6 %copy-start.44 = (bf16[8,2,48,768]{3,2,1,0:T(8,128)(2,1)}, bf16[8,2,48,768]{3,2,1,0:T(8,128)(2,1)S(1)}, u32[]{:S(2)}) copy-start(bf16[8,2,48,768]{3,2,1,0:T(8,128)(2,1)S(1)} %get-tuple-element.139) | copy-start | bytes 3538948
  145.5 28.4 %copy-start.46 = (bf16[8,2,48,768]{3,2,1,0:T(8,128)(2,1)}, bf16[8,2,48,768]{3,2,1,0:T(8,128)(2,1)S(1)}, u32[]{:S(2)}) copy-start(bf16[8,2,48,768]{3,2,1,0:T(8,128)(2,1)S(1)} %get-tuple-element.138) | copy-start | bytes 3538948
  153.4 19.6 %copy-start.58 = (bf16[3,64,512]{2,1,0:T(8,128)(2,1)}, bf16[3,64,512]{2,1,0:T(8,128)(2,1)S(1)}, u32[]{:S(2)}) copy-start(bf16[3,64,512]{2,1,0:T(8,128)(2,1)S(1)} %convolution_convert_fusion.9) | copy-start | bytes 589828
  244.0 36.2 %copy-start.8 = (f32[128,768]{1,0:T(8,128)}, f32[128,768]{1,0:T(8,128)S(1)}, u32[]{:S(2)}) copy-start(f32[128,768]{1,0:T(8,128)S(1)} %get-tuple-element.85.refs_4_.refs_6_) | copy-start | bytes 1179652
  245.3 8.0 copy-start.64
  246.2 3.8 collective-permute-start.2
  248.1 5.1 collective-permute-start.3
  250.0 28.1 %copy-start.48 = (bf16[8,2,48,768]{3,2,1,0:T(8,128)(2,1)}, bf16[8,2,48,768]{3,2,1,0:T(8,128)(2,1)S(1)}, u32[]{:S(2)}) copy-start(bf16[8,2,48,768]{3,2,1,0:T(8,128)(2,1)S(1)} %get-tuple-element.137) | copy-start | bytes 3538948
  250.0 29.0 %copy-start.50 = (bf16[8,2,48,768]{3,2,1,0:T(8,128)(2,1)}, bf16[8,2,48,768]{3,2,1,0:T(8,128)(2,1)S(1)}, u32[]{:S(2)}) copy-start(bf16[8,2,48,768]{3,2,1,0:T(8,128)(2,1)S(1)} %get-tuple-element.136) | copy-start | bytes 3538948
  293.9 46.8 %copy-start.15 = (f32[128,768]{1,0:T(8,128)}, f32[128,768]{1,0:T(8,128)S(1)}, u32[]{:S(2)}) copy-start(f32[128,768]{1,0:T(8,128)S(1)} %get-tuple-element.107.refs_7_) | copy-start | bytes 1179652
  439.6 55.7 %copy-start.20 = (f32[5]{0:T(128)S(1)}, f32[5]{0:T(128)}, u32[]{:S(2)}) copy-start(f32[5]{0:T(128)} %refs_6_.1) | copy-start | bytes 64
  439.7 69.6 %copy-start.51 = (bf16[8,2,48,768]{3,2,1,0:T(8,128)(2,1)S(1)}, bf16[8,2,48,768]{3,2,1,0:T(8,128)(2,1)}, u32[]{:S(2)}) copy-start(bf16[8,2,48,768]{3,2,1,0:T(8,128)(2,1)} %copy-done.50) | copy-start | bytes 3538948
  439.7 69.6 %copy-start.95 = (f32[512,768]{1,0:T(8,128)S(1)}, f32[512,768]{1,0:T(8,128)}, u32[]{:S(2)}) copy-start(f32[512,768]{1,0:T(8,128)} %copy-done.94) | copy-start | bytes 4718596
  509.2 118.1 %copy-start.5 = (f32[128,768]{1,0:T(8,128)}, f32[128,768]{1,0:T(8,128)S(1)}, u32[]{:S(2)}) copy-start(f32[128,768]{1,0:T(8,128)S(1)} %get-tuple-element.96.refs_4_.refs_5_.refs_9_) | copy-start | bytes 1179652
  511.9 22.8 %slice-start.2 = ((s8[6291456]{0:T(1024)(128)(4,1)}), s8[2097152]{0:T(1024)(128)(4,1)S(1)}, s32[]{:S(2)}) async-start(s8[6291456]{0:T(1024)(128)(4,1)} %bitcast.225), calls=%async_computation.6 | async-start | bytes 4194304
  512.7 22.0 %slice-start.3 = ((s8[6291456]{0:T(1024)(128)(4,1)}), s8[4194304]{0:T(1024)(128)(4,1)S(1)}, s32[]{:S(2)}) async-start(s8[6291456]{0:T(1024)(128)(4,1)} %bitcast.225), calls=%async_computation.7 | async-start | bytes 8388608
  541.7 4.3 collective-permute-start.4
  543.0 3.6 collective-permute-start.5
  549.1 27.2 %copy-start.47 = (bf16[8,2,48,768]{3,2,1,0:T(8,128)(2,1)S(1)}, bf16[8,2,48,768]{3,2,1,0:T(8,128)(2,1)}, u32[]{:S(2)}) copy-start(bf16[8,2,48,768]{3,2,1,0:T(8,128)(2,1)} %copy-done.46) | copy-start | bytes 3538948
  549.1 27.2 %copy-start.93 = (f32[512,768]{1,0:T(8,128)S(1)}, f32[512,768]{1,0:T(8,128)}, u32[]{:S(2)}) copy-start(f32[512,768]{1,0:T(8,128)} %copy-done.92) | copy-start | bytes 4718596
  576.3 51.1 %copy-start.10 = (f32[128,768]{1,0:T(8,128)}, f32[128,768]{1,0:T(8,128)S(1)}, u32[]{:S(2)}) copy-start(f32[128,768]{1,0:T(8,128)S(1)} %get-tuple-element.101.refs_4_.refs_8_) | copy-start | bytes 1179652
  578.9 25.8 %slice-start = ((s8[6291456]{0:T(1024)(128)(4,1)}), s8[2097152]{0:T(1024)(128)(4,1)S(1)}, s32[]{:S(2)}) async-start(s8[6291456]{0:T(1024)(128)(4,1)} %bitcast.223), calls=%async_computation.4 | async-start | bytes 4194304
  580.8 23.9 %slice-start.1 = ((s8[6291456]{0:T(1024)(128)(4,1)}), s8[4194304]{0:T(1024)(128)(4,1)S(1)}, s32[]{:S(2)}) async-start(s8[6291456]{0:T(1024)(128)(4,1)} %bitcast.223), calls=%async_computation.5 | async-start | bytes 8388608
  582.8 21.5 %copy-start.39 = (bf16[2,2,48,768]{3,2,1,0:T(8,128)(2,1)S(1)}, bf16[2,2,48,768]{3,2,1,0:T(8,128)(2,1)}, u32[]{:S(2)}) copy-start(bf16[2,2,48,768]{3,2,1,0:T(8,128)(2,1)} %copy-done.38) | copy-start | bytes 884740
  606.6 9.4 %copy-start.68 = (f32[1,1024,3,64]{1,3,2,0:T(8,128)}, f32[1,1024,3,64]{1,3,2,0:T(8,128)S(1)}, u32[]{:S(2)}) copy-start(f32[1,1024,3,64]{1,3,2,0:T(8,128)S(1)} %convolution_bitcast_fusion) | copy-start | bytes 2359300
  614.7 7.1 collective-permute-start.6
  616.7 6.4 collective-permute-start.7
  618.0 165.1 %all-reduce.13.cloned.1.call-start = ((), (), s32[]{:S(2)}) async-start(), calls=%async_computation.3 | async-start | bytes 3538944 | tf_op jit(solution)/shard_map/psum | solution.py:1316
  645.1 97.0 %copy-start.26 = (f32[1,768]{1,0:T(1,128)}, f32[1,768]{1,0:T(1,128)S(1)}, u32[]{:S(2)}) copy-start(f32[1,768]{1,0:T(1,128)S(1)} %get-tuple-element.102.refs_0_) | copy-start | bytes 9220
  742.1 26.4 %copy-start.2 = (bf16[24,48,768]{2,1,0:T(8,128)(2,1)S(1)}, bf16[24,48,768]{2,1,0:T(8,128)(2,1)}, u32[]{:S(2)}) copy-start(bf16[24,48,768]{2,1,0:T(8,128)(2,1)} %all-reduce.11.cloned.1.call-done.rest_1_) | copy-start | bytes 5308420
  783.1 19.6 %copy-start.3 = (bf16[24,48,768]{2,1,0:T(8,128)(2,1)S(1)}, bf16[24,48,768]{2,1,0:T(8,128)(2,1)}, u32[]{:S(2)}) copy-start(bf16[24,48,768]{2,1,0:T(8,128)(2,1)} %all-reduce.13.cloned.1.call-done.rest_0_) | copy-start | bytes 5308420
  807.2 47.5 %copy-start.85 = (f32[5,768]{1,0:T(8,128)S(1)}, f32[5,768]{1,0:T(8,128)}, u32[]{:S(2)}) copy-start(f32[5,768]{1,0:T(8,128)} %get-tuple-element.209) | copy-start | bytes 46084
  807.2 48.1 %copy-start.84 = (f32[5,768]{1,0:T(8,128)S(1)}, f32[5,768]{1,0:T(8,128)}, u32[]{:S(2)}) copy-start(f32[5,768]{1,0:T(8,128)} %get-tuple-element.210) | copy-start | bytes 46084
  807.2 48.7 %copy-start.83 = (f32[5,768]{1,0:T(8,128)S(1)}, f32[5,768]{1,0:T(8,128)}, u32[]{:S(2)}) copy-start(f32[5,768]{1,0:T(8,128)} %get-tuple-element.211) | copy-start | bytes 46084
  807.2 49.3 %copy-start.91 = (f32[1,5]{1,0:T(1,128)S(1)}, f32[1,5]{1,0:T(1,128)}, u32[]{:S(2)}) copy-start(f32[1,5]{1,0:T(1,128)} %get-tuple-element.125) | copy-start | bytes 64
  807.2 49.8 %copy-start.90 = (f32[1,5]{1,0:T(1,128)S(1)}, f32[1,5]{1,0:T(1,128)}, u32[]{:S(2)}) copy-start(f32[1,5]{1,0:T(1,128)} %get-tuple-element.126) | copy-start | bytes 64
  807.2 50.3 %copy-start.89 = (f32[1,5]{1,0:T(1,128)S(1)}, f32[1,5]{1,0:T(1,128)}, u32[]{:S(2)}) copy-start(f32[1,5]{1,0:T(1,128)} %get-tuple-element.127) | copy-start | bytes 64
  807.2 50.9 %copy-start.88 = (f32[1,128]{1,0:T(1,128)S(1)}, f32[1,128]{1,0:T(1,128)}, u32[]{:S(2)}) copy-start(f32[1,128]{1,0:T(1,128)} %get-tuple-element.116.refs_14_) | copy-start | bytes 1540
  (64 other events, 129.7 us)
Sparse Core Ops, SparseCore 0:
  21.8 90.9 all-reduce.6
  143.5 76.6 all-reduce.8
  618.1 76.4 all-reduce.10
  697.0 86.0 all-reduce.12

commit v3 on v2

--- a/solution.py
+++ b/solution.py
@@ -270,13 +270,168 @@
     )(*operands)
 
 
-def reduce_all(terms, collective_id):
+LINE_BLOCKS = 2
+
+
+class Line:
+    def __init__(self, rider, share):
+        self.groups = lax.axis_size("dp")
+        self.half = rider.shape
+        self.chunks = rider.shape[0] // LINE_BLOCKS
+        self.share = share
+        count, half_rows, _ = rider.shape
+        dma = pltpu.SemaphoreType.DMA
+        out = (count, 2, half_rows, D) if share else rider.shape
+        self.out_shape = jax.ShapeDtypeStruct(out, jnp.bfloat16)
+        self.out_spec = pl.BlockSpec(memory_space=pl.ANY if share else pltpu.VMEM)
+        self.scratch = [
+            pltpu.VMEM(self.half, jnp.bfloat16),
+            pltpu.VMEM((2,) + self.half, jnp.bfloat16),
+            pltpu.VMEM((2,) + self.half, jnp.bfloat16),
+            dma,
+            dma((2, self.chunks)),
+            dma((2, self.chunks)),
+        ]
+        if share:
+            self.scratch += [pltpu.VMEM(self.half, jnp.bfloat16)] + [dma((self.chunks,))] * 3
+
+    def neighbours(self, signal):
+        group = lax.axis_index("dp")
+
+        @pl.when(group > 0)
+        def _():
+            signal({"dp": group - 1})
+
+        @pl.when(group < self.groups - 1)
+        def _():
+            signal({"dp": group + 1})
+
+    def bind(self, rider_ref, out_ref, refs):
+        self.rider, self.out = rider_ref, out_ref
+        self.own, self.came, self.going, self.own_sem, self.send_sems, self.recv_sems = refs[:6]
+        self.total = out_ref
+        if self.share:
+            self.total, self.keep_sems, self.twin_send, self.twin_recv = refs[6:]
+        self.group = lax.axis_index("dp")
+        self.first = jnp.where(self.group < self.groups // 2, 0, 1)
+
+    def at(self, chunk):
+        return pl.ds(chunk * LINE_BLOCKS, LINE_BLOCKS)
+
+    def comes(self, way):
+        return jnp.where(way == 0, self.group > 0, self.group < self.groups - 1)
+
+    def goes(self, way):
+        return jnp.where(way == 0, self.group < self.groups - 1, self.group > 0)
+
+    def copy(self, source, way, chunk):
+        target = jnp.where(way == 0, self.group + 1, self.group - 1)
+        return pltpu.make_async_remote_copy(
+            src_ref=source,
+            dst_ref=self.came.at[way, self.at(chunk)],
+            send_sem=self.send_sems.at[way, chunk],
+            recv_sem=self.recv_sems.at[way, chunk],
+            device_id={"dp": target},
+            device_id_type=MESH,
+        )
+
+    def begin(self):
+        copy = pltpu.make_async_copy(self.rider, self.own, self.own_sem)
+        copy.start()
+        copy.wait()
+        for way in range(2):
+
+            @pl.when(jnp.logical_not(self.comes(way)))
+            def _():
+                self.came[way] = jnp.zeros(self.half, jnp.bfloat16)
+                self.going[way] = self.own[...]
+
+                def start(chunk, carry):
+                    self.copy(self.going.at[way, self.at(chunk)], way, chunk).start()
+                    return carry
+
+                lax.fori_loop(0, self.chunks, start, 0)
+
+    def twin_copy(self, chunk):
+        side = lax.axis_index("seq")
+        return pltpu.make_async_remote_copy(
+            src_ref=self.total.at[self.at(chunk)],
+            dst_ref=self.out.at[self.at(chunk), side],
+            send_sem=self.twin_send.at[chunk],
+            recv_sem=self.twin_recv.at[chunk],
+            device_id={"seq": 1 - side},
+            device_id_type=MESH,
+        )
+
+    def keep_copy(self, chunk):
+        return pltpu.make_async_copy(
+            self.total.at[self.at(chunk)],
+            self.out.at[self.at(chunk), lax.axis_index("seq")],
+            self.keep_sems.at[chunk],
+        )
+
+    def step(self, chunk):
+        rows = self.at(chunk)
+        own = self.own[rows].astype(jnp.float32)
+        for turn in range(2):
+            way = self.first if turn == 0 else 1 - self.first
+
+            @pl.when(self.comes(way))
+            def _():
+                copy = self.copy(self.going.at[way, rows], way, chunk)
+                copy.wait_recv()
+
+                @pl.when(self.goes(way))
+                def _():
+                    value = own + self.came[way, rows].astype(jnp.float32)
+                    self.going[way, rows] = value.astype(jnp.bfloat16)
+                    copy.start()
+
+        value = own + self.came[0, rows].astype(jnp.float32) + self.came[1, rows].astype(jnp.float32)
+        self.total[rows] = value.astype(jnp.bfloat16)
+        if self.share:
+            self.keep_copy(chunk).start()
+            self.twin_copy(chunk).start()
+
+    def steps(self, start, stop):
+        def one(chunk, carry):
+            self.step(chunk)
+            return carry
+
+        lax.fori_loop(start, stop, one, 0)
+
+    def end(self):
+        def one(chunk, carry):
+            for way in range(2):
+
+                @pl.when(self.goes(way))
+                def _():
+                    self.copy(self.going.at[way, self.at(chunk)], way, chunk).wait_send()
+
+            if self.share:
+                self.keep_copy(chunk).wait()
+                self.twin_copy(chunk).wait()
+            return carry
+
+        lax.fori_loop(0, self.chunks, one, 0)
+
+
+def reduce_all(terms, collective_id, rider=None):
     _, tensors, groups, count, _ = terms.shape
-
-    def kernel(
-        terms_ref, out_ref, near, own, mid, mid_in, far, far_in,
-        own_sems, near_send, near_recv, mid_send, mid_recv, far_send, far_recv,
-    ):
+    line = None if rider is None else Line(rider, True)
+
+    def kernel(*refs):
+        refs = list(refs)
+        terms_ref = refs.pop(0)
+        rider_ref = refs.pop(0) if line else None
+        out_ref = refs.pop(0)
+        joined_ref = refs.pop(0) if line else None
+        (
+            near, own, mid, mid_in, far, far_in,
+            own_sems, near_send, near_recv, mid_send, mid_recv, far_send, far_recv,
+        ) = refs[:13]
+        if line:
+            line.bind(rider_ref, joined_ref, refs[13:])
         group, part, side = lax.axis_index("dp"), lax.axis_index("tensor"), lax.axis_index("seq")
         twin = 1 - side
         parts = others("tensor")
@@ -302,6 +457,8 @@
             )
             copy.start()
             own_copies.append(copy)
+        if line:
+            line.begin()
         mid_copies = []
         for place in range(groups):
             near_copies[place].wait_recv()
@@ -324,6 +481,8 @@
             )
         far_copies = []
         for place, target in enumerate(order):
+            if line:
+                line.steps(line.chunks * place // groups, line.chunks * (place + 1) // groups)
             total = mid[place, part].astype(jnp.float32)
             for step in range(tensors - 1):
                 mid_copies[place][step].wait_recv()
@@ -345,15 +504,17 @@
         out_ref[...] = total
         for copy in near_copies + far_copies + [c for row in mid_copies for c in row]:
             copy.wait_send()
+        if line:
+            line.end()
 
     block = (count, D)
     dma = pltpu.SemaphoreType.DMA
     return pl.pallas_call(
         kernel,
         name="reduce_all",
-        out_shape=jax.ShapeDtypeStruct(block, jnp.float32),
-        in_specs=[pl.BlockSpec(memory_space=pl.ANY)],
-        out_specs=pl.BlockSpec(memory_space=pltpu.VMEM),
+        out_shape=[jax.ShapeDtypeStruct(block, jnp.float32)] + ([line.out_shape] if line else []),
+        in_specs=[pl.BlockSpec(memory_space=pl.ANY)] * (2 if line else 1),
+        out_specs=[pl.BlockSpec(memory_space=pltpu.VMEM)] + ([line.out_spec] if line else []),
         scratch_shapes=[pltpu.VMEM((groups, tensors) + block, jnp.bfloat16)] * 3
         + [
             pltpu.VMEM((groups, tensors - 1) + block, jnp.bfloat16),
@@ -366,17 +527,27 @@
             dma((groups, tensors - 1)),
             dma((groups,)),
             dma((groups,)),
-        ],
+        ]
+        + (line.scratch if line else []),
         compiler_params=pltpu.CompilerParams(
             collective_id=collective_id, has_side_effects=True, vmem_limit_bytes=56 << 20
         ),
-    )(terms)
-
-
-def gather_all(block, collective_id):
+    )(terms, *([rider] if line else []))
+
+
+def gather_all(block, collective_id, rider=None):
     tensors, groups = lax.axis_size("tensor"), lax.axis_size("dp")
-
-    def kernel(block_ref, out, own_sem, far_send, far_recv, mid_send, mid_recv, near_send, near_recv):
+    line = None if rider is None else Line(rider, False)
+
+    def kernel(*refs):
+        refs = list(refs)
+        block_ref = refs.pop(0)
+        rider_ref = refs.pop(0) if line else None
+        out = refs.pop(0)
+        summed_ref = refs.pop(0) if line else None
+        own_sem, far_send, far_recv, mid_send, mid_recv, near_send, near_recv = refs[:7]
+        if line:
+            line.bind(rider_ref, summed_ref, refs[7:])
         group, part, side = lax.axis_index("dp"), lax.axis_index("tensor"), lax.axis_index("seq")
         twin = 1 - side
         parts = others("tensor")
@@ -398,8 +569,14 @@
         own = pltpu.make_async_copy(block_ref, out.at[side, part, group], own_sem)
         own.start()
         own.wait()
+        if line:
+            line.begin()
         mid_copies, near_copies = [], []
         for place in range(groups):
+            if line and place:
+                line.steps(
+                    line.chunks * (place - 1) // groups // 2, line.chunks * place // groups // 2
+                )
             source = behind("dp", place)
             if place:
                 far_copies[place - 1].wait_recv()
@@ -413,7 +590,12 @@
             near_copies.append(
                 send(held, held, near_send.at[place, 0], near_recv.at[place, 0], {"seq": twin})
             )
+        if line:
+            done = line.chunks * (groups - 1) // groups // 2
         for place in range(groups):
+            if line:
+                left = line.chunks - done
+                line.steps(done + left * place // groups, done + left * (place + 1) // groups)
             source = behind("dp", place)
             for step in range(tensors - 1):
                 mid_copies[place][step].wait_recv()
@@ -431,14 +613,18 @@
             copy.wait_recv()
         for copy in near_copies + far_copies + [c for row in mid_copies for c in row]:
             copy.wait_send()
+        if line:
+            line.end()
 
     dma = pltpu.SemaphoreType.DMA
+    anywhere = pl.BlockSpec(memory_space=pl.ANY)
     return pl.pallas_call(
         kernel,
         name="gather_all",
-        out_shape=jax.ShapeDtypeStruct((2, tensors, groups) + block.shape, block.dtype),
-        in_specs=[pl.BlockSpec(memory_space=pl.ANY)],
-        out_specs=pl.BlockSpec(memory_space=pl.ANY),
+        out_shape=[jax.ShapeDtypeStruct((2, tensors, groups) + block.shape, block.dtype)]
+        + ([line.out_shape] if line else []),
+        in_specs=[anywhere] * (2 if line else 1),
+        out_specs=[anywhere] + ([line.out_spec] if line else []),
         scratch_shapes=[
             dma,
             dma((groups - 1,)),
@@ -447,20 +633,27 @@
             dma((groups, tensors - 1)),
             dma((groups, tensors)),
             dma((groups, tensors)),
-        ],
-        compiler_params=pltpu.CompilerParams(collective_id=collective_id, has_side_effects=True),
-    )(block)
-
-
-def reduce_rows(terms, collective_id):
+        ]
+        + (line.scratch if line else []),
+        compiler_params=pltpu.CompilerParams(
+            collective_id=collective_id, has_side_effects=True, vmem_limit_bytes=40 << 20
+        ),
+    )(block, *([rider] if line else []))
+
+
+def reduce_rows(terms, ids, rider=None):
     count, groups = terms.shape[3], terms.shape[2]
     pieces = max(1, groups // 4)
     part = count // pieces
-    sums = [
-        reduce_all(terms[:, :, :, i * part : (i + 1) * part] if pieces > 1 else terms, collective_id)
-        for i in range(pieces)
-    ]
-    return jnp.concatenate(sums, axis=0) if pieces > 1 else sums[0]
+    sums, joined = [], None
+    for i in range(pieces):
+        piece = terms[:, :, :, i * part : (i + 1) * part] if pieces > 1 else terms
+        if i == 0 and rider is not None:
+            total, joined = reduce_all(piece, ids[1], rider)
+        else:
+            (total,) = reduce_all(piece, ids[0])
+        sums.append(total)
+    return jnp.concatenate(sums, axis=0) if pieces > 1 else sums[0], joined
 
 
 def join_stats(stats, collective_id):
@@ -722,42 +915,69 @@
     )(*operands)
 
 
+SLOT_STEP = 4
+
+
 def update_slots(plan, factor, master, first, second, layer_grads, grad_table):
     slots, half_rows, _ = master.shape
+    steps = -(-slots // SLOT_STEP)
+    plan = jnp.pad(plan, ((0, 0), (0, steps * SLOT_STEP - slots)))
 
     def kernel(plan_ref, factor_ref, master_ref, first_ref, second_ref, *rest):
-        layer_refs, (table_ref, new_master, new_first, new_second) = rest[:LAYERS], rest[LAYERS:]
-        kind = plan_ref[0, pl.program_id(0)]
-        grad = table_ref[...]
-        for level in range(LAYERS):
-            grad = jnp.where(kind == level, layer_refs[level][0].astype(jnp.float32), grad)
-        grad = jnp.where(kind >= 0, grad * factor_ref[0:1, 0:1], 0.0)
-        values = adam_update(
-            master_ref[0], first_ref[0], second_ref[0], grad, RATE_MATRIX, DECAY_MATRIX
-        )
-        for ref, value in zip((new_master, new_first, new_second), values):
-            ref[0] = value
-
-    slot = pl.BlockSpec((1, half_rows, D), lambda step, plan: (step, 0, 0))
+        layer_refs = rest[: LAYERS * SLOT_STEP]
+        table_ref, new_master, new_first, new_second = rest[LAYERS * SLOT_STEP :]
+        for place in range(SLOT_STEP):
+            kind = plan_ref[0, pl.program_id(0) * SLOT_STEP + place]
+            grad = table_ref[place * half_rows : (place + 1) * half_rows, :]
+            for level in range(LAYERS):
+                layer = layer_refs[level * SLOT_STEP + place][0].astype(jnp.float32)
+                grad = jnp.where(kind == level, layer, grad)
+            grad = jnp.where(kind >= 0, grad * factor_ref[0:1, 0:1], 0.0)
+            values = adam_update(
+                master_ref[place],
+                first_ref[place],
+                second_ref[place],
+                grad,
+                RATE_MATRIX,
+                DECAY_MATRIX,
+            )
+            for ref, value in zip((new_master, new_first, new_second), values):
+                ref[place] = value
+
+    slot = pl.BlockSpec((SLOT_STEP, half_rows, D), lambda step, plan: (step, 0, 0))
     return pl.pallas_call(
         kernel,
         name="update_slots",
         grid_spec=pltpu.PrefetchScalarGridSpec(
             num_scalar_prefetch=1,
-            grid=(slots,),
+            grid=(steps,),
             in_specs=[pl.BlockSpec((8, LANES), lambda step, plan: (0, 0)), slot, slot, slot]
             + [
                 pl.BlockSpec(
-                    (1, half_rows, D), lambda step, plan, level=level: (plan[1 + level, step], 0, 0)
+                    (1, half_rows, D),
+                    lambda step, plan, level=level, place=place: (
+                        plan[1 + level, step * SLOT_STEP + place],
+                        0,
+                        0,
+                    ),
                 )
                 for level in range(LAYERS)
+                for place in range(SLOT_STEP)
             ]
-            + [pl.BlockSpec((half_rows, D), lambda step, plan: (step, 0))],
+            + [pl.BlockSpec((SLOT_STEP * half_rows, D), lambda step, plan: (step, 0))],
             out_specs=[slot] * 3,
         ),
         out_shape=[jax.ShapeDtypeStruct(master.shape, jnp.float32)] * 3,
-        compiler_params=pltpu.CompilerParams(vmem_limit_bytes=32 << 20),
-    )(plan, factor, master, first, second, *layer_grads, grad_table)
+        compiler_params=pltpu.CompilerParams(vmem_limit_bytes=48 << 20),
+    )(
+        plan,
+        factor,
+        master,
+        first,
+        second,
+        *[grads for grads in layer_grads for _ in range(SLOT_STEP)],
+        grad_table,
+    )
 
 
 def row_of(groups_ref):
@@ -1133,12 +1353,12 @@
     halves = []
     for level in range(LAYERS):
         chosen = slice(level * layer_blocks, (level + 1) * layer_blocks)
-        own = jnp.where(
-            mine[chosen][:, None, None], jnp.take(table_slots, slot_rank[chosen], axis=0), 0.0
-        ).astype(jnp.bfloat16)
-        if level:
-            own, halves[-1] = lax.optimization_barrier((own, halves[-1]))
-        halves.append(lax.psum(own, "dp"))
+        halves.append(
+            jnp.where(
+                mine[chosen][:, None, None], jnp.take(table_slots, slot_rank[chosen], axis=0), 0.0
+            ).astype(jnp.bfloat16)
+        )
+    halves[1:] = [lax.psum(half, "dp") for half in halves[1:]]
 
     def cut(joined):
         joined = joined.reshape(layer_rows, D)
@@ -1153,7 +1373,8 @@
     geometry = (cosine, sine, allowed, seq_count, half_len, local_heads)
 
     looked = look_up(span, row_ids, ids_all, table).reshape(order + (D,))
-    start = reduce_rows(looked, 0)
+    start, joined = reduce_rows(looked, (0, 14), halves[0])
+    weights_all = [cut(joined)]
     gain = [gains[i : i + 1] for i in range(2 * LAYERS + 1)]
     piece = ((share, D), jnp.float32)
 
@@ -1172,10 +1393,7 @@
             stream = stream + scalars[base + source] * state
         return (outcome, stream, layer_norm_parts(stream)[0] * gain_row)
 
-    normed, joined = tensor_step(
-        "normed", normed_of, None, (start, gain[0]), (), [], True, 1, "share", halves[0]
-    )
-    weights_all = [cut(joined)]
+    (normed,) = tensor_step("normed", normed_of, None, (start, gain[0]), (), [], True, 1)
     states, streams, inners, kept_all = [start], [start], [], []
     for level in range(LAYERS):
         qkv_w, out_w, up_w, down_w = weights_all[level]
@@ -1214,7 +1432,7 @@
         streams.append(results[1])
         normed = results[2]
 
-    final_all = gather_all(normed, 3 + LAYERS).reshape(-1, D)
+    final_all = gather_all(normed, 3 + LAYERS)[0].reshape(-1, D)
     powers, stats = head_forward(span, row_ids, labels_all, table, final_all)
     home, log_totals = join_stats(
         stats.reshape((2, tensors, groups, 8, LANES)), 4 + LAYERS
@@ -1230,7 +1448,7 @@
         final_all,
         powers,
     )
-    grad_final = reduce_rows(grad_final.reshape(order + (D,)), 0)
+    grad_final, _ = reduce_rows(grad_final.reshape(order + (D,)), (0, 14))
 
     row = ((1, D), jnp.float32)
 
@@ -1309,13 +1527,10 @@
             grads.reshape(layer_blocks, 2, half_rows, D),
         )
         grad_ys[level], grad_state, gain_grads[2 * level], grad_branch, folded = results
-        if level < LAYERS - 1:
-            folded, layer_grads[level + 1] = lax.optimization_barrier(
-                (folded, layer_grads[level + 1])
-            )
-        layer_grads[level] = lax.psum(folded, "dp")
-
-    grad_start_all = gather_all(grad_branch, 3 + LAYERS).reshape(-1, D)
+        layer_grads[level] = lax.psum(folded, "dp") if level else folded
+
+    grad_start_all, layer_grads[0] = gather_all(grad_branch, 13, layer_grads[0])
+    grad_start_all = grad_start_all.reshape(-1, D)
     grad_table, table_squares = look_back(span, row_ids, ids_all, grad_start_all, grad_table)
     layer_squares = jnp.zeros((), jnp.float32)
     for level in range(LAYERS):

time: 880 us -> 917 us (1.042); the launches traced: 866 us -> 919 us
  Pallas kernels: 612 us -> 725 us
  waiting for transfers between devices: 107 us -> 35.8 us
    pallas_call x4, Pallas kernels: 204 us -> 318 us  [the longest x2 166 us: reduce_all(): pl.pallas_call(kernel, name='reduce_all', out_shape=[jax.ShapeDtypeStruct...]
    psum x4 -> x2, waiting for transfers between devices: 107 us -> 35.7 us  [the longest x1 35.7 us: body(): halves[1:] = [lax.psum(half, 'dp') for half in halves[1:]]]
    pallas_call x1, Pallas kernels: 47.5 us -> 34.4 us  [update_slots(): pl.pallas_call(kernel, name='update_slots', grid_spec=pltpu.PrefetchScala...]
    unnamed x206 -> x250, local copies, waits for them, and re-layouts: 24.6 us -> 24.1 us
  transfers between devices with their start and end apart: 12 -> 10, of which waited for: 4 -> 1; matrix products, arithmetic and copies ran while one was open for 4% -> 4% of each run, Pallas kernels for 23% -> 19%
where the time goes in v3:
time: 917 us; the launch traced here: 919 us
  Pallas kernels  725 us (79%)
  local copies, waits for them, and re-layouts  47.2 us (5%)
  matrix products  45.4 us (5%)
  waiting for transfers between devices  35.8 us (4%)
  other arithmetic  31.4 us (3%)
  between operations  20.7 us (2%)
  starting transfers between devices  13 us (1%)
    pallas_call x10, Pallas kernels, tensor_step(): pl.pallas_call(kernel, name=name, out_shape=shapes, in_specs=in_specs, ou...  188 us
    pallas_call x2, Pallas kernels, reduce_all(): pl.pallas_call(kernel, name='reduce_all', out_shape=[jax.ShapeDtypeStruct...  166 us
    pallas_call x2, Pallas kernels, gather_all(): pl.pallas_call(kernel, name='gather_all', out_shape=[jax.ShapeDtypeStruct...  153 us
    pallas_call x4, Pallas kernels, local_call(): pl.pallas_call(kernel, name=name, grid_spec=pltpu.PrefetchScalarGridSpec(...  121 us
    psum x1, waiting for transfers between devices, body(): halves[1:] = [lax.psum(half, 'dp') for half in halves[1:]]  35.7 us
    pallas_call x1, Pallas kernels, update_slots(): pl.pallas_call(kernel, name='update_slots', grid_spec=pltpu.PrefetchScala...  34.4 us
    pallas_call x1, Pallas kernels, join_stats(): pl.pallas_call(kernel, name='join_stats', out_shape=[jax.ShapeDtypeStruct...  33.1 us
    unnamed x250, local copies, waits for them, and re-layouts  24.1 us
  transfers between devices with their start and end apart: 10, of which 1 were waited for; matrix products, arithmetic and copies ran while one was open for 4% of the time, Pallas kernels for 19%

profile of v3, /device:TPU:0, one launch (start us, length us, event | category | flops | bytes accessed | tf_op | source)
XLA Modules:
  0.0 918.9 jit_solution(14838886660069426184)
XLA Ops:
  13.5 9.1 spread_tokens.1
  22.6 4.4 convert_element_type.136
  28.9 2.8 pad.14
  31.8 3.2 gather_fusion
  36.6 24.9 %look_up.1 = bf16[4096,768]{1,0:T(8,128)(2,1)} custom-call(s32[2]{0:T(128)} %pad_add_fusion.2.span_ref, s32[3648,1]{1,0:T(8,128)} %pad.13.ids_ref, s32[4,8,128]{2,1,0:T(8,128)} %get-tuple-element.69.tokens_ref, bf16[3648,768]{1,0:T(8,128)(2,1)} %bitcast.221), custom_call_target="tpu_custom_call" | custom-call | tf_op jit(solution)/shard_map/look_up/pallas_call | solution.py:1010
  61.4 104.1 %reduce_all.2 = (f32[128,768]{1,0:T(8,128)}, bf16[24,2,48,768]{3,2,1,0:T(8,128)(2,1)}) custom-call(bf16[2,4,4,128,768]{4,3,2,1,0:T(8,128)(2,1)} %bitcast.228, bf16[24,48,768]{2,1,0:T(8,128)(2,1)} %select_select_fusion.1.refs_1_), custom_call_target="tpu_custom_call" | custom-call | tf_op jit(solution)/shard_map/reduce_all/pallas_call | solution.py:512
  166.9 14.1 %normed.1 = bf16[4,128,768]{2,1,0:T(8,128)(2,1)S(1)} custom-call(f32[128,768]{1,0:T(8,128)S(1)} %copy-done.2, f32[1,768]{1,0:T(1,128)S(1)} %get-tuple-element.168.refs_1_.refs_3_), custom_call_target="tpu_custom_call" | custom-call | tf_op jit(solution)/shard_map/normed/pallas_call | solution.py:260
  185.0 1.8 collective-permute-start
  186.8 2.0 collective-permute-start.1
  188.8 4.5 gather_fusion.1
  193.3 3.0 select_select_fusion
  197.6 3.3 fusion.67
  206.6 2.7 convolution_convert_fusion.9
  209.7 20.0 %inner.2 = (f32[128,768]{1,0:T(8,128)S(1)}, bf16[4,128,768]{2,1,0:T(8,128)(2,1)S(1)}) custom-call(f32[512,768]{1,0:T(8,128)S(1)} %fusion.74.refs_0_, f32[128,768]{1,0:T(8,128)S(1)} %copy-done.2, f32[1,768]{1,0:T(1,128)S(1)} %get-tuple-element.167.refs_2_.refs_3_), custom_call_target="tpu_custom_call" | custom-call | tf_op jit(solution)/shard_map/inner/pallas_call | solution.py:260
  231.8 2.2 fusion.64.refs_0_
  234.0 35.7 %all-reduce.6.cloned.1.call-done.refs_5_ = bf16[24,48,768]{2,1,0:T(8,128)(2,1)} async-done(((bf16[24,48,768]{2,1,0:T(8,128)(2,1)}), bf16[24,48,768]{2,1,0:T(8,128)(2,1)}) %all-reduce.6.cloned.1.call-update) | async-done | bytes 1769488 | tf_op jit(solution)/shard_map/psum | solution.py:1361
  272.6 21.6 %outcome_0.1 = (f32[128,768]{1,0:T(8,128)S(1)}, f32[128,768]{1,0:T(8,128)S(1)}, bf16[4,128,768]{2,1,0:T(8,128)(2,1)S(1)}, bf16[24,2,48,768]{3,2,1,0:T(8,128)(2,1)S(1)}) custom-call(f32[512,768]{1,0:T(8,128)S(1)} %copy-done.8, f32[128,768]{1,0:T(8,128)S(1)} %get-tuple-element.73.refs_1_.refs_2_, f32[1,768]{1,0:T(1,128)S(1)} %get-tuple-element.166.refs_2_.refs_3_, ...), custom_call_target="tpu_custom_call" | custom-call | tf_op jit(solution)/shard_map/outcome_0/pallas_call | solution.py:260
  296.0 1.9 collective-permute-start.2
  301.1 1.8 exponential_reduce_fusion
  306.2 21.9 %inner.3 = (f32[128,768]{1,0:T(8,128)S(1)}, bf16[4,128,768]{2,1,0:T(8,128)(2,1)S(1)}) custom-call(f32[512,768]{1,0:T(8,128)S(1)} %fusion.77.refs_0_, f32[128,768]{1,0:T(8,128)S(1)} %get-tuple-element.78.refs_1_.refs_2_, f32[1,768]{1,0:T(1,128)S(1)} %get-tuple-element.165.refs_2_.refs_3_), custom_call_target="tpu_custom_call" | custom-call | tf_op jit(solution)/shard_map/inner/pallas_call | solution.py:260
  330.2 13.0 %outcome_1.1 = (f32[128,768]{1,0:T(8,128)S(1)}, f32[128,768]{1,0:T(8,128)S(1)}, bf16[128,768]{1,0:T(8,128)(2,1)S(1)}) custom-call(f32[512,768]{1,0:T(8,128)S(1)} %fusion.65.refs_0_, f32[128,768]{1,0:T(8,128)S(1)} %get-tuple-element.80.refs_1_.refs_2_, f32[1,768]{1,0:T(1,128)S(1)} %get-tuple-element.164.refs_2_, f32[128,768]{1,0:T(8,128)S(1)} %copy-done.2, ...), custom_call_target="tpu_custom_call" | custom-call | tf_op jit(solution)/shard_map/outcome_1/pallas_call | solution.py:260
  343.9 39.0 %gather_all.2 = bf16[2,4,4,128,768]{4,3,2,1,0:T(8,128)(2,1)S(1)} custom-call(bf16[128,768]{1,0:T(8,128)(2,1)S(1)} %get-tuple-element.82.refs_0_), custom_call_target="tpu_custom_call" | custom-call | tf_op jit(solution)/shard_map/gather_all/pallas_call | solution.py:621
  382.9 2.7 copy-done
  385.6 27.3 %head_forward.1 = (bf16[3648,4096]{1,0:T(8,128)(2,1)}, f32[32,8,128]{2,1,0:T(8,128)}) custom-call(s32[2]{0:T(128)} %pad_add_fusion.2.span_ref, s32[3648,1]{1,0:T(8,128)} %pad.13.ids_ref, s32[4,8,128]{2,1,0:T(8,128)} %get-tuple-element.76.labels_ref, bf16[3648,768]{1,0:T(8,128)(2,1)} %bitcast.222, bf16[4096,768]{1,0:T(8,128)(2,1)} %bitcast.199), custom_call_target="tpu_custom_call" | custom-call | tf_op jit(solution)/shard_map/head_forward/pallas_call | solution.py:1010
  413.0 33.1 %join_stats.1 = (f32[8,128]{1,0:T(8,128)}, f32[2,4,4,8,128]{4,3,2,1,0:T(8,128)}) custom-call(f32[2,4,4,8,128]{4,3,2,1,0:T(8,128)} %bitcast.264), custom_call_target="tpu_custom_call" | custom-call | tf_op jit(solution)/shard_map/join_stats/pallas_call | solution.py:730
  446.0 42.3 %head_backward.1 = (bf16[4096,768]{1,0:T(8,128)(2,1)}, f32[3648,768]{1,0:T(8,128)}) custom-call(s32[2]{0:T(128)} %pad_add_fusion.2.span_ref, s32[3648,1]{1,0:T(8,128)} %pad.13.ids_ref, s32[4,8,128]{2,1,0:T(8,128)} %get-tuple-element.76.labels_ref, f32[4,8,128]{2,1,0:T(8,128)} %get-tuple-element.77.keep_ref, f32[32,8,128]{2,1,0:T(8,128)} %get-tuple-element.83.stats_ref, ...), custom_call_target="tpu_custom_call" | custom-call | tf_op jit(solution)/shard_map/head_backward/pallas_call | solution.py:1010
  488.4 61.4 %reduce_all.3.refs_0_ = f32[128,768]{1,0:T(8,128)} custom-call(bf16[2,4,4,128,768]{4,3,2,1,0:T(8,128)(2,1)} %bitcast.229), custom_call_target="tpu_custom_call" | custom-call | tf_op jit(solution)/shard_map/reduce_all/pallas_call | solution.py:512
  550.8 12.7 %top_back.1 = (f32[128,768]{1,0:T(8,128)S(1)}, f32[128,768]{1,0:T(8,128)S(1)}, f32[1,768]{1,0:T(1,128)S(1)}, bf16[4,128,768]{2,1,0:T(8,128)(2,1)S(1)}) custom-call(f32[128,768]{1,0:T(8,128)S(1)} %copy-done.9, f32[128,768]{1,0:T(8,128)S(1)} %copy-done.13, f32[1,768]{1,0:T(1,128)S(1)} %get-tuple-element.164.refs_2_, f32[5]{0:T(128)S(1)} %copy-done.18), custom_call_target="tpu_custom_call" | custom-call | tf_op jit(solution)/shard_map/top_back/pallas_call | solution.py:260
  564.2 3.1 fusion.17
  570.2 20.9 %inner_back.2 = (f32[128,768]{1,0:T(8,128)S(1)}, f32[1,768]{1,0:T(1,128)S(1)}, bf16[4,128,768]{2,1,0:T(8,128)(2,1)S(1)}) custom-call(f32[512,768]{1,0:T(8,128)S(1)} %fusion.79.refs_0_, f32[128,768]{1,0:T(8,128)S(1)} %get-tuple-element.89.refs_1_, f32[128,768]{1,0:T(8,128)S(1)} %get-tuple-element.80.refs_1_.refs_2_, ...), custom_call_target="tpu_custom_call" | custom-call | tf_op jit(solution)/shard_map/inner_back/pallas_call | solution.py:260
  591.6 1.8 convolution_bitcast_fusion.1
  593.5 2.5 multiply_reduce_fusion.1
  596.0 1.9 multiply_convert_fusion.1
  606.2 25.4 %stream_back_1.1 = (f32[128,768]{1,0:T(8,128)S(1)}, f32[128,768]{1,0:T(8,128)S(1)}, f32[1,768]{1,0:T(1,128)S(1)}, bf16[4,128,768]{2,1,0:T(8,128)(2,1)S(1)}, bf16[24,48,768]{2,1,0:T(8,128)(2,1)S(1)}) custom-call(f32[512,768]{1,0:T(8,128)S(1)} %fusion.29.refs_0_, f32[128,768]{1,0:T(8,128)S(1)} %get-tuple-element.91.refs_1_, ...), custom_call_target="tpu_custom_call" | custom-call | tf_op jit(solution)/shard_map/stream_back_1/pallas_call | solution.py:260
  634.8 1.8 convolution_convert_fusion.1
  636.7 2.0 convolution_convert_fusion
  638.7 21.5 %inner_back.3 = (f32[128,768]{1,0:T(8,128)S(1)}, f32[1,768]{1,0:T(1,128)S(1)}, bf16[4,128,768]{2,1,0:T(8,128)(2,1)S(1)}) custom-call(f32[512,768]{1,0:T(8,128)S(1)} %fusion.80.refs_0_, f32[128,768]{1,0:T(8,128)S(1)} %get-tuple-element.94.refs_1_, f32[128,768]{1,0:T(8,128)S(1)} %get-tuple-element.73.refs_1_.refs_2_, ...), custom_call_target="tpu_custom_call" | custom-call | tf_op jit(solution)/shard_map/inner_back/pallas_call | solution.py:260
  660.6 1.8 convolution_bitcast_fusion
  662.4 3.6 multiply_reduce_fusion
  666.1 1.9 multiply_convert_fusion
  674.2 3.0 fusion.20
  683.4 16.6 %stream_back_0.1 = (f32[128,768]{1,0:T(8,128)}, f32[128,768]{1,0:T(8,128)}, f32[1,768]{1,0:T(1,128)S(1)}, bf16[128,768]{1,0:T(8,128)(2,1)S(1)}, bf16[24,48,768]{2,1,0:T(8,128)(2,1)S(1)}) custom-call(f32[512,768]{1,0:T(8,128)S(1)} %fusion.28.refs_0_, f32[128,768]{1,0:T(8,128)S(1)} %get-tuple-element.96.refs_1_, f32[128,768]{1,0:T(8,128)S(1)} %copy-done.2, ...), custom_call_target="tpu_custom_call" | custom-call | tf_op jit(solution)/shard_map/stream_back_0/pallas_call | solution.py:260
  700.1 113.6 %gather_all.3 = (bf16[2,4,4,128,768]{4,3,2,1,0:T(8,128)(2,1)S(1)}, bf16[24,48,768]{2,1,0:T(8,128)(2,1)S(1)}) custom-call(bf16[128,768]{1,0:T(8,128)(2,1)S(1)} %get-tuple-element.105.refs_0_, bf16[24,48,768]{2,1,0:T(8,128)(2,1)S(1)} %get-tuple-element.106.refs_1_), custom_call_target="tpu_custom_call" | custom-call | tf_op jit(solution)/shard_map/gather_all/pallas_call | solution.py:621
  813.7 2.7 copy-done.3
  816.4 26.3 %look_back.1 = (f32[3648,768]{1,0:T(8,128)}, f32[8,768]{1,0:T(8,128)}) custom-call(s32[2]{0:T(128)} %pad_add_fusion.2.span_ref, s32[3648,1]{1,0:T(8,128)} %pad.13.ids_ref, s32[4,8,128]{2,1,0:T(8,128)} %get-tuple-element.69.tokens_ref, bf16[4096,768]{1,0:T(8,128)(2,1)} %bitcast.203, f32[3648,768]{1,0:T(8,128)} %get-tuple-element.108.table_ref), custom_call_target="tpu_custom_call" | custom-call | tf_op jit(solution)/shard_map/look_back/pallas_call | solution.py:1010
  844.3 3.2 select_reduce_fusion
  848.8 22.1 %finish.1 = (f32[5,768]{1,0:T(8,128)}, f32[5,768]{1,0:T(8,128)}, f32[5,768]{1,0:T(8,128)}, f32[1,5]{1,0:T(1,128)}, f32[1,5]{1,0:T(1,128)}, /*index=5*/f32[1,5]{1,0:T(1,128)}, f32[1,128]{1,0:T(1,128)}, f32[8,128]{1,0:T(8,128)}) custom-call(f32[1,768]{1,0:T(1,128)} %copy-done.26, f32[1,768]{1,0:T(1,128)} %copy-done.25, f32[1,768]{1,0:T(1,128)} %copy-done.24, ...), custom_call_target="tpu_custom_call" | custom-call | tf_op jit(solution)/shard_map/finish/pallas_call | solution.py:893
  872.9 34.4 %update_slots.1 = (f32[67,48,768]{2,1,0:T(8,128)}, f32[67,48,768]{2,1,0:T(8,128)}, f32[67,48,768]{2,1,0:T(8,128)}) custom-call(s32[3,68]{1,0:T(4,128)S(1)} %copy-done.20, f32[8,128]{1,0:T(8,128)S(1)} %copy-done.21, f32[67,48,768]{2,1,0:T(8,128)} %master_ref.1, f32[67,48,768]{2,1,0:T(8,128)} %first_ref.1, f32[67,48,768]{2,1,0:T(8,128)} %second_ref.1, ...), custom_call_target="tpu_custom_call" | custom-call | tf_op jit(solution)/shard_map/update_slots/pallas_call | solution.py:948
  (358 shorter events, 71.7 us)
Async XLA Ops:
  7.2 262.5 %all-reduce.6.cloned.1.call-start = ((), (), s32[]{:S(2)}) async-start(), calls=%async_computation | async-start | bytes 3538944 | tf_op jit(solution)/shard_map/psum | solution.py:1361
  9.6 25.4 %copy-start.106 = (pred[24]{0:T(512)(128)(4,1)}, pred[24]{0:T(512)(128)(4,1)S(1)}, u32[]{:S(2)}) copy-start(pred[24]{0:T(512)(128)(4,1)S(1)} %get-tuple-element.177) | copy-start | bytes 76
  9.6 183.7 %copy-start.104 = (pred[24]{0:T(512)(128)(4,1)}, pred[24]{0:T(512)(128)(4,1)S(1)}, u32[]{:S(2)}) copy-start(pred[24]{0:T(512)(128)(4,1)S(1)} %get-tuple-element.176) | copy-start | bytes 76
  27.0 139.9 %copy-start.14 = (f32[1,768]{1,0:T(1,128)}, f32[1,768]{1,0:T(1,128)S(1)}, u32[]{:S(2)}) copy-start(f32[1,768]{1,0:T(1,128)S(1)} %get-tuple-element.168.refs_1_.refs_3_) | copy-start | bytes 9220
  185.0 17.5 %collective-permute-start = (bf16[1,512,3,64]{1,3,2,0:T(8,128)(2,1)S(1)}, bf16[1,512,3,64]{1,3,2,0:T(8,128)(2,1)S(1)}, u32[]{:S(2)}, u32[]{:S(2)}) collective-permute-start(bf16[1,512,3,64]{1,3,2,0:T(8,128)(2,1)S(1)} %pad_maximum_fusion.8), channel_id=1, source_target_pairs={{0,1},{2,3},{4,5},{6,7},{8,9},{10,11},{12,13},{14,15},{16,17},{18,... | collective-permute-start | bytes 589832 | tf_op jit(solution)/shard_map/ppermute | solution.py:33
  186.8 18.9 %collective-permute-start.1 = (bf16[1,512,3,64]{1,3,2,0:T(8,128)(2,1)S(1)}, bf16[1,512,3,64]{1,3,2,0:T(8,128)(2,1)}, u32[]{:S(2)}, u32[]{:S(2)}) collective-permute-start(bf16[1,512,3,64]{1,3,2,0:T(8,128)(2,1)S(1)} %bitcast.258), channel_id=1, source_target_pairs={{0,1},{2,3},{4,5},{6,7},{8,9},{10,11},{12,13},{14,15},{16,17},{18,... | collective-permute-start | bytes 589832 | tf_op jit(solution)/shard_map/ppermute | solution.py:33
  196.4 647.9 %all-reduce.8.cloned.1.call-start = ((), (), s32[]{:S(2)}) async-start(), calls=%async_computation.1 | async-start | bytes 3538944 | tf_op jit(solution)/shard_map/psum | solution.py:1530
  202.5 100.4 %copy-start.34 = (pred[512,1024]{1,0:T(8,128)(4,1)}, pred[512,1024]{1,0:T(8,128)(4,1)S(1)}, u32[]{:S(2)}) copy-start(pred[512,1024]{1,0:T(8,128)(4,1)S(1)} %compare_and_fusion) | copy-start | bytes 1572868
  209.3 20.5 %copy-start.68 = (bf16[3,64,512]{2,1,0:T(8,128)(2,1)}, bf16[3,64,512]{2,1,0:T(8,128)(2,1)S(1)}, u32[]{:S(2)}) copy-start(bf16[3,64,512]{2,1,0:T(8,128)(2,1)S(1)} %convolution_convert_fusion.9) | copy-start | bytes 589828
  209.3 20.5 %copy-start.52 = (bf16[8,2,48,768]{3,2,1,0:T(8,128)(2,1)S(1)}, bf16[8,2,48,768]{3,2,1,0:T(8,128)(2,1)}, u32[]{:S(2)}) copy-start(bf16[8,2,48,768]{3,2,1,0:T(8,128)(2,1)} %get-tuple-element.135) | copy-start | bytes 3538948
  231.8 37.9 %copy-start.16 = (f32[5]{0:T(128)S(1)}, f32[5]{0:T(128)}, u32[]{:S(2)}) copy-start(f32[5]{0:T(128)} %refs_6_.1) | copy-start | bytes 64
  294.2 36.0 %copy-start.7 = (f32[128,768]{1,0:T(8,128)}, f32[128,768]{1,0:T(8,128)S(1)}, u32[]{:S(2)}) copy-start(f32[128,768]{1,0:T(8,128)S(1)} %get-tuple-element.81.refs_4_.refs_6_) | copy-start | bytes 1179652
  296.0 3.6 collective-permute-start.2
  297.9 5.0 collective-permute-start.3
  299.6 28.6 %copy-start.56 = (bf16[8,2,48,768]{3,2,1,0:T(8,128)(2,1)}, bf16[8,2,48,768]{3,2,1,0:T(8,128)(2,1)S(1)}, u32[]{:S(2)}) copy-start(bf16[8,2,48,768]{3,2,1,0:T(8,128)(2,1)S(1)} %get-tuple-element.133) | copy-start | bytes 3538948
  299.6 29.4 %copy-start.58 = (bf16[8,2,48,768]{3,2,1,0:T(8,128)(2,1)}, bf16[8,2,48,768]{3,2,1,0:T(8,128)(2,1)S(1)}, u32[]{:S(2)}) copy-start(bf16[8,2,48,768]{3,2,1,0:T(8,128)(2,1)S(1)} %get-tuple-element.132) | copy-start | bytes 3538948
  343.9 39.0 %copy-start.11 = (f32[128,768]{1,0:T(8,128)}, f32[128,768]{1,0:T(8,128)S(1)}, u32[]{:S(2)}) copy-start(f32[128,768]{1,0:T(8,128)S(1)} %get-tuple-element.103.refs_7_) | copy-start | bytes 1179652
  488.4 61.4 %copy-start.13 = (f32[128,768]{1,0:T(8,128)S(1)}, f32[128,768]{1,0:T(8,128)}, u32[]{:S(2)}) copy-start(f32[128,768]{1,0:T(8,128)} %copy-done.12) | copy-start | bytes 1179652
  488.4 61.4 %copy-start.18 = (f32[5]{0:T(128)S(1)}, f32[5]{0:T(128)}, u32[]{:S(2)}) copy-start(f32[5]{0:T(128)} %refs_6_.1) | copy-start | bytes 64
  488.4 75.7 %copy-start.59 = (bf16[8,2,48,768]{3,2,1,0:T(8,128)(2,1)S(1)}, bf16[8,2,48,768]{3,2,1,0:T(8,128)(2,1)}, u32[]{:S(2)}) copy-start(bf16[8,2,48,768]{3,2,1,0:T(8,128)(2,1)} %copy-done.58) | copy-start | bytes 3538948
  564.1 119.0 %copy-start.4 = (f32[128,768]{1,0:T(8,128)}, f32[128,768]{1,0:T(8,128)S(1)}, u32[]{:S(2)}) copy-start(f32[128,768]{1,0:T(8,128)S(1)} %get-tuple-element.92.refs_4_.refs_5_.refs_9_) | copy-start | bytes 1179652
  568.4 23.2 %slice-start.2 = ((s8[6291456]{0:T(1024)(128)(4,1)}), s8[4194304]{0:T(1024)(128)(4,1)S(1)}, s32[]{:S(2)}) async-start(s8[6291456]{0:T(1024)(128)(4,1)} %bitcast.226), calls=%async_computation.4 | async-start | bytes 8388608
  569.2 22.4 %slice-start.3 = ((s8[6291456]{0:T(1024)(128)(4,1)}), s8[2097152]{0:T(1024)(128)(4,1)S(1)}, s32[]{:S(2)}) async-start(s8[6291456]{0:T(1024)(128)(4,1)} %bitcast.226), calls=%async_computation.5 | async-start | bytes 4194304
  570.2 20.9 %copy-start.43 = (bf16[2,2,48,768]{3,2,1,0:T(8,128)(2,1)S(1)}, bf16[2,2,48,768]{3,2,1,0:T(8,128)(2,1)}, u32[]{:S(2)}) copy-start(bf16[2,2,48,768]{3,2,1,0:T(8,128)(2,1)} %copy-done.42) | copy-start | bytes 884740
  570.2 21.4 %copy-start.35 = (pred[512,1024]{1,0:T(8,128)(4,1)S(1)}, pred[512,1024]{1,0:T(8,128)(4,1)}, u32[]{:S(2)}) copy-start(pred[512,1024]{1,0:T(8,128)(4,1)} %copy-done.34) | copy-start | bytes 1572868
  570.2 21.4 %copy-start.99 = (f32[3,512]{1,0:T(4,128)S(1)}, f32[3,512]{1,0:T(4,128)}, u32[]{:S(2)}) copy-start(f32[3,512]{1,0:T(4,128)} %copy-done.98) | copy-start | bytes 18436
  598.6 4.4 collective-permute-start.4
  600.1 3.6 collective-permute-start.5
  606.2 25.5 %copy-start.55 = (bf16[8,2,48,768]{3,2,1,0:T(8,128)(2,1)S(1)}, bf16[8,2,48,768]{3,2,1,0:T(8,128)(2,1)}, u32[]{:S(2)}) copy-start(bf16[8,2,48,768]{3,2,1,0:T(8,128)(2,1)} %get-tuple-element.134) | copy-start | bytes 3538948
  606.2 25.5 %copy-start.115 = (f32[512,768]{1,0:T(8,128)S(1)}, f32[512,768]{1,0:T(8,128)}, u32[]{:S(2)}) copy-start(f32[512,768]{1,0:T(8,128)} %copy-done.114) | copy-start | bytes 4718596
  631.7 51.5 %copy-start.10 = (f32[128,768]{1,0:T(8,128)}, f32[128,768]{1,0:T(8,128)S(1)}, u32[]{:S(2)}) copy-start(f32[128,768]{1,0:T(8,128)S(1)} %get-tuple-element.97.refs_4_.refs_8_) | copy-start | bytes 1179652
  634.8 25.7 %slice-start = ((s8[6291456]{0:T(1024)(128)(4,1)}), s8[4194304]{0:T(1024)(128)(4,1)S(1)}, s32[]{:S(2)}) async-start(s8[6291456]{0:T(1024)(128)(4,1)} %bitcast.224), calls=%async_computation.2 | async-start | bytes 8388608
  636.7 23.9 %slice-start.1 = ((s8[6291456]{0:T(1024)(128)(4,1)}), s8[2097152]{0:T(1024)(128)(4,1)S(1)}, s32[]{:S(2)}) async-start(s8[6291456]{0:T(1024)(128)(4,1)} %bitcast.224), calls=%async_computation.3 | async-start | bytes 4194304
  638.7 21.5 %copy-start.41 = (bf16[2,2,48,768]{3,2,1,0:T(8,128)(2,1)S(1)}, bf16[2,2,48,768]{3,2,1,0:T(8,128)(2,1)}, u32[]{:S(2)}) copy-start(bf16[2,2,48,768]{3,2,1,0:T(8,128)(2,1)} %copy-done.40) | copy-start | bytes 884740
  638.7 21.9 %copy-start.97 = (f32[3,512]{1,0:T(4,128)S(1)}, f32[3,512]{1,0:T(4,128)}, u32[]{:S(2)}) copy-start(f32[3,512]{1,0:T(4,128)} %copy-done.96) | copy-start | bytes 18436
  670.6 7.0 collective-permute-start.6
  672.6 6.3 collective-permute-start.7
  700.0 113.6 %copy-start.26 = (f32[1,768]{1,0:T(1,128)}, f32[1,768]{1,0:T(1,128)S(1)}, u32[]{:S(2)}) copy-start(f32[1,768]{1,0:T(1,128)S(1)} %get-tuple-element.98.refs_0_) | copy-start | bytes 9220
  816.3 26.3 %copy-start.107 = (pred[24]{0:T(512)(128)(4,1)S(1)}, pred[24]{0:T(512)(128)(4,1)}, u32[]{:S(2)}) copy-start(pred[24]{0:T(512)(128)(4,1)} %copy-done.106) | copy-start | bytes 76
  844.2 27.9 %copy-start.20 = (s32[3,68]{1,0:T(4,128)S(1)}, s32[3,68]{1,0:T(4,128)}, u32[]{:S(2)}) copy-start(s32[3,68]{1,0:T(4,128)} %pad.12.plan_ref) | copy-start | bytes 2452
  844.3 27.9 %copy-start.1 = (bf16[24,48,768]{2,1,0:T(8,128)(2,1)S(1)}, bf16[24,48,768]{2,1,0:T(8,128)(2,1)}, u32[]{:S(2)}) copy-start(bf16[24,48,768]{2,1,0:T(8,128)(2,1)} %all-reduce.8.cloned.1.call-done.rest_4_.rest_5_.rest_6_.rest_7_) | copy-start | bytes 5308420
  872.8 34.5 %copy-start.103 = (f32[5,768]{1,0:T(8,128)S(1)}, f32[5,768]{1,0:T(8,128)}, u32[]{:S(2)}) copy-start(f32[5,768]{1,0:T(8,128)} %get-tuple-element.205) | copy-start | bytes 46084
  872.8 35.1 %copy-start.102 = (f32[5,768]{1,0:T(8,128)S(1)}, f32[5,768]{1,0:T(8,128)}, u32[]{:S(2)}) copy-start(f32[5,768]{1,0:T(8,128)} %get-tuple-element.206) | copy-start | bytes 46084
  872.8 35.7 %copy-start.101 = (f32[5,768]{1,0:T(8,128)S(1)}, f32[5,768]{1,0:T(8,128)}, u32[]{:S(2)}) copy-start(f32[5,768]{1,0:T(8,128)} %get-tuple-element.207) | copy-start | bytes 46084
  872.8 36.3 %copy-start.113 = (f32[1,5]{1,0:T(1,128)S(1)}, f32[1,5]{1,0:T(1,128)}, u32[]{:S(2)}) copy-start(f32[1,5]{1,0:T(1,128)} %get-tuple-element.121) | copy-start | bytes 64
  872.8 36.8 %copy-start.112 = (f32[1,5]{1,0:T(1,128)S(1)}, f32[1,5]{1,0:T(1,128)}, u32[]{:S(2)}) copy-start(f32[1,5]{1,0:T(1,128)} %get-tuple-element.122) | copy-start | bytes 64
  872.8 37.3 %copy-start.111 = (f32[1,5]{1,0:T(1,128)S(1)}, f32[1,5]{1,0:T(1,128)}, u32[]{:S(2)}) copy-start(f32[1,5]{1,0:T(1,128)} %get-tuple-element.123) | copy-start | bytes 64
  872.9 37.8 %copy-start.110 = (f32[1,128]{1,0:T(1,128)S(1)}, f32[1,128]{1,0:T(1,128)}, u32[]{:S(2)}) copy-start(f32[1,128]{1,0:T(1,128)} %get-tuple-element.112.refs_14_) | copy-start | bytes 1540
  (84 other events, 304.7 us)
Sparse Core Ops, SparseCore 0:
  196.5 73.2 all-reduce.5
  674.3 114.6 all-reduce.7

commit v4 on v3

--- a/solution.py
+++ b/solution.py
@@ -27,12 +27,6 @@
 DECAY_MATRIX = 0.1
 
 
-def from_behind(block, axis, distance):
-    devices = range(lax.axis_size(axis))
-    route = [(i - distance, i) for i in devices if i - distance in devices]
-    return lax.ppermute(block, axis, route)
-
-
 def contract_last(left, right):
     return lax.dot_general(
         left, right, (((1,), (1,)), ((), ())), preferred_element_type=jnp.float32
@@ -42,36 +36,6 @@
 def contract_first(left, right):
     return lax.dot_general(
         left, right, (((0,), (0,)), ((), ())), preferred_element_type=jnp.float32
-    )
-
-
-def normalize(stream):
-    center = stream - jnp.mean(stream, -1, keepdims=True)
-    inverse = lax.rsqrt(jnp.mean(center * center, -1, keepdims=True) + EPS_NORM)
-    return (center * inverse, inverse)
-
-
-def norm_back(grad_normed, gain, scaled, inverse):
-    grad_scaled = grad_normed * gain
-    grad_stream = inverse * (
-        grad_scaled
-        - jnp.mean(grad_scaled, -1, keepdims=True)
-        - scaled * jnp.mean(grad_scaled * scaled, -1, keepdims=True)
-    )
-    return (grad_stream, jnp.sum(grad_normed * scaled, axis=0))
-
-
-def rotary(positions):
-    steps_half = jnp.arange(HEAD_DIM // 2).astype(jnp.float32)
-    freqs = 10000.0 ** (-2.0 * steps_half / HEAD_DIM)
-    angles = positions.astype(jnp.float32)[:, None] * freqs[None, :]
-    return (jnp.cos(angles)[:, None, :], jnp.sin(angles)[:, None, :])
-
-
-def rotate(tensor, cosine, sine):
-    first, second = jnp.split(tensor, 2, axis=-1)
-    return jnp.concatenate(
-        [first * cosine - second * sine, second * cosine + first * sine], axis=-1
     )
 
 
@@ -79,13 +43,6 @@
     ranks = jnp.arange(owners.shape[0])
     same = (owners[None, :] == owners[:, None]) & (ranks[None, :] < ranks[:, None])
     return jnp.sum(jnp.where(same, 1, 0), axis=1).astype(jnp.int32)
-
-
-def attention_scores(queries, keys_all, allowed):
-    raw = jnp.einsum(
-        "bqhd,bkhd->bhqk", queries, keys_all, preferred_element_type=jnp.float32
-    ) * HEAD_DIM ** (-0.5)
-    return jnp.where(allowed[None, None], raw, -1e30)
 
 
 def adam_update(weight, first, second, grad, rate, decay):
@@ -101,6 +58,7 @@
 ROW_STEP = 400
 TILE_GROUPS = 8
 LANES = 128
+SHORT = pl.CostEstimate(flops=1000, bytes_accessed=1000, transcendentals=0)
 
 
 def meet(peers):
@@ -150,45 +108,47 @@
     return grad_stream, jnp.sum(grad_normed * scaled, axis=0, keepdims=True)
 
 
-def tensor_step(
-    name, function, partial, extras, scalars, outs, gather, collective_id, beside=None, rider=None
-):
+class Work:
+    def __init__(self, before, during, operands, specs, outs, scratch, after=None, twins=False):
+        self.before, self.during, self.after, self.twins = before, during, after, twins
+        self.operands, self.specs, self.outs, self.scratch = operands, specs, outs, scratch
+
+
+def tensor_step(name, function, work, extras, scalars, outs, gather, collective_id, rider=None):
     parts = lax.axis_size("tensor")
     share = extras[0].shape[0]
-    reduce = partial is not None
-    if beside:
-        count, half_rows = rider.shape[0], rider.shape[-2]
-        half = (count, half_rows, D)
+    reduce = work is not None
+    work = work or Work(None, None, [], [], [], [])
 
     def kernel(*refs):
         refs = list(refs)
-        partial_ref = refs.pop(0) if reduce else None
-        extra_refs = [refs.pop(0) for _ in extras]
-        scalar_refs = [refs.pop(0) for _ in scalars]
-        rider_ref = refs.pop(0) if beside else None
-        out_refs = [refs.pop(0) for _ in outs]
-        full = refs.pop(0) if gather else None
-        joined = refs.pop(0) if beside else None
-        outgoing = refs.pop(0) if reduce else None
-        arrived = refs.pop(0) if reduce else None
-        send_sems, recv_sems = refs[:2]
-        me = lax.axis_index("tensor")
+
+        def take(count):
+            return [refs.pop(0) for _ in range(count)]
+
+        work_refs = take(len(work.operands))
+        extra_refs = take(len(extras))
+        scalar_refs = take(len(scalars))
+        (rider_ref,) = take(1) if rider is not None else [None]
+        out_refs = take(len(outs))
+        (full,) = take(1) if gather else [None]
+        work_outs = take(len(work.outs))
+        (joined,) = take(1) if rider is not None else [None]
+        send_sems, recv_sems = take(2)
+        partial_ref, outgoing, arrived = take(3) if reduce else [None] * 3
+        own_sem, twin_send, twin_recv = take(3) if rider is not None else [None] * 3
+        me, side = lax.axis_index("tensor"), lax.axis_index("seq")
         peers = others("tensor")
-        side = lax.axis_index("seq")
-        twin = [{"seq": 1 - side}] if beside else []
-        meet([{"tensor": peer} for peer in peers] + twin)
-        if beside == "share":
-            _, _, own_sem, twin_send, twin_recv = refs
+        twin = {"seq": 1 - side}
+        twins = work.twins or rider is not None
+        meet([{"tensor": peer} for peer in peers] + [twin] * twins)
+        if rider is not None:
             own_copy = pltpu.make_async_copy(rider_ref, joined.at[:, side], own_sem)
             own_copy.start()
-            twin_copy = send(rider_ref, joined.at[:, side], twin_send, twin_recv, twin[0])
-        if beside == "fold":
-            _, _, own_sem, twin_send, twin_recv, near = refs
-            own_copy = pltpu.make_async_copy(rider_ref.at[:, side], joined, own_sem)
-            own_copy.start()
-            twin_copy = send(rider_ref.at[:, 1 - side], near, twin_send, twin_recv, twin[0])
+            twin_copy = send(rider_ref, joined.at[:, side], twin_send, twin_recv, twin)
         total = None
         if reduce:
+            work.before(work_refs, work_outs, refs, partial_ref)
             copies = []
             for step, peer in enumerate(peers):
                 rows = pl.ds(pl.multiple_of(peer * share, share), share)
@@ -202,6 +162,8 @@
                         {"tensor": peer},
                     )
                 )
+            if work.during:
+                work.during(work_refs, work_outs, refs)
             total = partial_ref[pl.ds(pl.multiple_of(me * share, share), share), :]
             for step, copy in enumerate(copies):
                 copy.wait()
@@ -221,17 +183,11 @@
                 )
                 for step, peer in enumerate(peers)
             ]
-        if beside:
+        if work.after:
+            work.after(work_refs, work_outs, refs)
+        if rider is not None:
             own_copy.wait()
             twin_copy.wait()
-        if beside == "fold":
-
-            def add_block(block, carry):
-                value = joined[block].astype(jnp.float32) + near[block].astype(jnp.float32)
-                joined[block] = value.astype(jnp.bfloat16)
-                return carry
-
-            lax.fori_loop(0, count, add_block, 0)
         if gather:
             for copy in copies:
                 copy.wait()
@@ -242,35 +198,325 @@
     shapes = [jax.ShapeDtypeStruct(shape, dtype) for shape, dtype in outs]
     if gather:
         shapes.append(jax.ShapeDtypeStruct((parts, share, D), jnp.bfloat16))
-    buffers = [pltpu.VMEM((parts - 1, share, D), jnp.bfloat16)] * (2 if reduce else 0)
-    operands = ([partial] if reduce else []) + list(extras) + list(scalars)
-    in_specs = [vmem] * (len(operands) - len(scalars)) + [smem] * len(scalars)
+    shapes += [jax.ShapeDtypeStruct(shape, dtype) for shape, dtype in work.outs]
     out_specs = [vmem] * len(shapes)
+    operands = list(work.operands) + list(extras) + list(scalars)
+    in_specs = list(work.specs) + [vmem] * len(extras) + [smem] * len(scalars)
     dma = pltpu.SemaphoreType.DMA
-    buffers += [dma((2, parts - 1))] * 2
-    if beside:
+    buffers = [dma((2, parts - 1))] * 2
+    if reduce:
+        buffers += [pltpu.VMEM((parts * share, D), jnp.float32)]
+        buffers += [pltpu.VMEM((parts - 1, share, D), jnp.bfloat16)] * 2
+    if rider is not None:
         operands.append(rider)
         in_specs.append(anywhere)
+        count, half_rows, _ = rider.shape
+        shapes.append(jax.ShapeDtypeStruct((count, 2, half_rows, D), jnp.bfloat16))
+        out_specs.append(anywhere)
         buffers += [dma] * 3
-        folds = beside == "fold"
-        kept = half if folds else (count, 2, half_rows, D)
-        shapes.append(jax.ShapeDtypeStruct(kept, jnp.bfloat16))
-        out_specs.append(vmem if folds else anywhere)
-        buffers += [pltpu.VMEM(half, jnp.bfloat16)] * folds
     return pl.pallas_call(
         kernel,
         name=name,
+        grid=(1,),
         out_shape=shapes,
         in_specs=in_specs,
         out_specs=out_specs,
-        scratch_shapes=buffers,
+        scratch_shapes=buffers + list(work.scratch),
+        cost_estimate=SHORT,
         compiler_params=pltpu.CompilerParams(
-            collective_id=collective_id, has_side_effects=True, vmem_limit_bytes=40 << 20
+            collective_id=collective_id, has_side_effects=True, vmem_limit_bytes=50 << 20
         ),
     )(*operands)
 
 
+VMEM_SPEC = pl.BlockSpec(memory_space=pltpu.VMEM)
+
+
+def part_spec(rows, index):
+    return pl.BlockSpec((rows, D), lambda step: (index, 0), pipeline_mode=pl.Buffered(1))
+
+
+def turn(block, cosine, sine):
+    half = HEAD_DIM // 2
+    first, second = block[:half], block[half:]
+    return jnp.concatenate(
+        [first * cosine - second * sine, second * cosine + first * sine], axis=0
+    )
+
+
+def times(left, right):
+    return jnp.dot(left, right, preferred_element_type=jnp.float32)
+
+
+def scores_of(keys_values, head, queries, side):
+    span = slice(head * HEAD_DIM, (head + 1) * HEAD_DIM)
+    count = queries.shape[1]
+    scale = HEAD_DIM ** (-0.5)
+    far = contract_first(keys_values[0, 0, span, :], queries) * scale
+    own = contract_first(keys_values[1, 0, span, :], queries) * scale
+    key = lax.broadcasted_iota(jnp.int32, (count, count), 0)
+    query = lax.broadcasted_iota(jnp.int32, (count, count), 1)
+    own = jnp.where(key <= query, own, -1e30)
+    far = jnp.where(query + side * (2 * count) >= 2 * count, far, -1e30)
+    return far, own
+
+
+def attention_work(normed, table, cosine, sine):
+    parts, share, _ = normed.shape
+    count = parts * share
+    width = D // parts
+    heads = width // HEAD_DIM
+
+    def before(ins, outs, scratch, partial_ref):
+        normed_ref, qkv_ref, out_ref, cosine_ref, sine_ref = ins
+        queries_ref, both, logs_ref, attended_ref = outs
+        send_sem, recv_sem = scratch
+        side = lax.axis_index("seq")
+        cosine, sine = cosine_ref[...], sine_ref[...]
+        rows = normed_ref[...].reshape(count, D)
+        joined = contract_last(qkv_ref[...], rows)
+        for head in range(heads):
+            span = slice(head * HEAD_DIM, (head + 1) * HEAD_DIM)
+            keys = joined[width + head * HEAD_DIM : width + (head + 1) * HEAD_DIM]
+            both[1, 0, span, :] = turn(keys, cosine, sine).astype(jnp.bfloat16)
+        both[1, 1] = joined[2 * width :].astype(jnp.bfloat16)
+        copy = pltpu.make_async_remote_copy(
+            src_ref=both.at[1],
+            dst_ref=both.at[0],
+            send_sem=send_sem,
+            recv_sem=recv_sem,
+            device_id={"seq": 1 - side},
+            device_id_type=MESH,
+        )
+
+        copy.start()
+        for head in range(heads):
+            span = slice(head * HEAD_DIM, (head + 1) * HEAD_DIM)
+            queries_ref[span, :] = turn(joined[span], cosine, sine).astype(jnp.bfloat16)
+
+        copy.wait()
+        for head in range(heads):
+            span = slice(head * HEAD_DIM, (head + 1) * HEAD_DIM)
+            far, own = scores_of(both, head, queries_ref[span, :], side)
+            peak = jnp.maximum(
+                jnp.max(far, axis=0, keepdims=True), jnp.max(own, axis=0, keepdims=True)
+            )
+            far, own = jnp.exp(far - peak), jnp.exp(own - peak)
+            total = jnp.sum(far, axis=0, keepdims=True) + jnp.sum(own, axis=0, keepdims=True)
+            logs_ref[head] = peak + jnp.log(total)
+            inverse = 1.0 / total
+            attended = times(both[0, 1, span, :], (far * inverse).astype(jnp.bfloat16))
+            attended += times(both[1, 1, span, :], (own * inverse).astype(jnp.bfloat16))
+            attended_ref[span, :] = attended.astype(jnp.bfloat16)
+        partial_ref[...] = contract_first(attended_ref[...], out_ref[...])
+
+    low = jnp.bfloat16
+    return Work(
+        before,
+        None,
+        [normed, table, table, cosine, sine],
+        [VMEM_SPEC, part_spec(3 * width, 0), part_spec(width, 3), VMEM_SPEC, VMEM_SPEC],
+        [
+            ((width, count), low),
+            ((2, 2, width, count), low),
+            ((heads, 1, count), jnp.float32),
+            ((width, count), low),
+        ],
+        [pltpu.SemaphoreType.DMA, pltpu.SemaphoreType.DMA],
+        twins=True,
+    )
+
+
+def attention_back_work(grad, normed, table, kept, cosine, sine, unit_grads):
+    parts, share, _ = normed.shape
+    count = parts * share
+    width = D // parts
+    heads = width // HEAD_DIM
+    queries, both, logs, attended = kept
+    half_rows = unit_grads[0].shape[2]
+    joined_blocks, out_blocks = 3 * width // (2 * half_rows), width // (2 * half_rows)
+    unit_blocks = unit_grads[0].shape[0]
+    starts = [0, joined_blocks, joined_blocks + out_blocks, joined_blocks + out_blocks + unit_blocks]
+    sizes = [joined_blocks, out_blocks, unit_blocks, unit_blocks]
+    blocks = sum(sizes)
+
+    def twin_copy(source, target, send_sem, recv_sem):
+        return pltpu.make_async_remote_copy(
+            src_ref=source,
+            dst_ref=target,
+            send_sem=send_sem,
+            recv_sem=recv_sem,
+            device_id={"seq": 1 - lax.axis_index("seq")},
+            device_id_type=MESH,
+        )
+
+    def fold_copy(index, source, refs):
+        near, fold_send, fold_recv = refs
+        side = lax.axis_index("seq")
+        rows = pl.ds(starts[index], sizes[index])
+        return twin_copy(
+            source.at[:, 1 - side], near.at[rows], fold_send.at[index], fold_recv.at[index]
+        )
+
+    def before(ins, outs, scratch, partial_ref):
+        grad_ref, _, qkv_ref, out_ref, queries_ref, both, logs_ref, _, cosine_ref, sine_ref = ins[:10]
+        back, came, grad_joined, send_sem, recv_sem = scratch[:5]
+        side = lax.axis_index("seq")
+        for index, source in zip((2, 3), ins[10:]):
+            fold_copy(index, source, scratch[7:]).start()
+        cosine, sine = cosine_ref[...], -sine_ref[...]
+        scale = HEAD_DIM ** (-0.5)
+        grads = contract_last(out_ref[...], grad_ref[...].reshape(count, D)).astype(jnp.bfloat16)
+        own_grads = []
+        for head in range(heads):
+            span = slice(head * HEAD_DIM, (head + 1) * HEAD_DIM)
+            head_queries, head_grads = queries_ref[span, :], grads[span]
+            far, own = scores_of(both, head, head_queries, side)
+            far, own = jnp.exp(far - logs_ref[head]), jnp.exp(own - logs_ref[head])
+            far_grad = contract_first(both[0, 1, span, :], head_grads)
+            own_grad = contract_first(both[1, 1, span, :], head_grads)
+            mean = jnp.sum(far * far_grad, axis=0, keepdims=True)
+            mean += jnp.sum(own * own_grad, axis=0, keepdims=True)
+            far_grad = (far * (far_grad - mean)).astype(jnp.bfloat16)
+            own_grad = (own * (own_grad - mean)).astype(jnp.bfloat16)
+            far, own = far.astype(jnp.bfloat16), own.astype(jnp.bfloat16)
+            back[0, span, :] = (contract_last(head_queries, far_grad) * scale).astype(jnp.bfloat16)
+            back[1, span, :] = contract_last(head_grads, far).astype(jnp.bfloat16)
+            query_grad = times(both[0, 0, span, :], far_grad) + times(both[1, 0, span, :], own_grad)
+            grad_joined[span, :] = turn(query_grad * scale, cosine, sine).astype(jnp.bfloat16)
+            own_grads.append(
+                (contract_last(head_queries, own_grad) * scale, contract_last(head_grads, own))
+            )
+        copy = twin_copy(back, came, send_sem, recv_sem)
+        copy.start()
+        copy.wait()
+        for head, (key_grad, value_grad) in enumerate(own_grads):
+            span = slice(head * HEAD_DIM, (head + 1) * HEAD_DIM)
+            key_grad = key_grad + came[0, span, :].astype(jnp.float32)
+            value_grad = value_grad + came[1, span, :].astype(jnp.float32)
+            start = width + head * HEAD_DIM
+            grad_joined[start : start + HEAD_DIM, :] = turn(key_grad, cosine, sine).astype(
+                jnp.bfloat16
+            )
+            start += width
+            grad_joined[start : start + HEAD_DIM, :] = value_grad.astype(jnp.bfloat16)
+        partial_ref[...] = contract_first(grad_joined[...], qkv_ref[...])
+
+    def during(ins, outs, scratch):
+        grad_ref, normed_ref, attended_ref = ins[0], ins[1], ins[7]
+        grad_joined, joined_part, out_part = scratch[2], scratch[5], scratch[6]
+        value = times(grad_joined[...], normed_ref[...].reshape(count, D))
+        joined_part[...] = value.astype(jnp.bfloat16).reshape(joined_part.shape)
+        fold_copy(0, joined_part, scratch[7:]).start()
+        value = times(attended_ref[...], grad_ref[...].reshape(count, D))
+        out_part[...] = value.astype(jnp.bfloat16).reshape(out_part.shape)
+        fold_copy(1, out_part, scratch[7:]).start()
+
+    def after(ins, outs, scratch):
+        side = lax.axis_index("seq")
+        (folded,) = outs
+        near = scratch[7]
+        sources = [scratch[5], scratch[6], ins[10], ins[11]]
+        for index in (2, 3, 0, 1):
+            source, start = sources[index], starts[index]
+            fold_copy(index, source, scratch[7:]).wait()
+
+            def add_block(block, carry):
+                value = source[block, side].astype(jnp.float32)
+                value = value + near[start + block].astype(jnp.float32)
+                folded[start + block] = value.astype(jnp.bfloat16)
+                return carry
+
+            lax.fori_loop(0, sizes[index], add_block, 0)
+
+    low = jnp.bfloat16
+    dma = pltpu.SemaphoreType.DMA
+    return Work(
+        before,
+        during,
+        [grad, normed, table, table, queries, both, logs, attended, cosine, sine] + list(unit_grads),
+        [VMEM_SPEC, VMEM_SPEC, part_spec(3 * width, 0), part_spec(width, 3)] + [VMEM_SPEC] * 8,
+        [((blocks, half_rows, D), low)],
+        [
+            pltpu.VMEM((2, width, count), low),
+            pltpu.VMEM((2, width, count), low),
+            pltpu.VMEM((3 * width, count), low),
+            dma,
+            dma,
+            pltpu.VMEM((joined_blocks, 2, half_rows, D), low),
+            pltpu.VMEM((out_blocks, 2, half_rows, D), low),
+            pltpu.VMEM((blocks, half_rows, D), low),
+            dma((4,)),
+            dma((4,)),
+        ],
+        after,
+        True,
+    )
+
+
+def gelu(hidden):
+    return jax.nn.gelu(hidden, approximate=True)
+
+
+def unit_work(normed, table):
+    parts, share, _ = normed.shape
+    count = parts * share
+    units = FF // parts
+
+    def before(ins, outs, scratch, partial_ref):
+        normed_ref, up_ref, down_ref = ins
+        hidden_ref, activated_ref = outs
+        hidden = contract_last(up_ref[...], normed_ref[...].reshape(count, D))
+        hidden_ref[...] = hidden
+        activated_ref[...] = gelu(hidden).astype(jnp.bfloat16)
+        partial_ref[...] = contract_first(activated_ref[...], down_ref[...])
+
+    return Work(
+        before,
+        None,
+        [normed, table, table],
+        [VMEM_SPEC, part_spec(units, 1), part_spec(units, 2)],
+        [((units, count), jnp.float32), ((units, count), jnp.bfloat16)],
+        [],
+    )
+
+
+def unit_back_work(grad, normed, table, kept, half_rows):
+    parts, share, _ = normed.shape
+    count = parts * share
+    units = FF // parts
+    hidden, activated = kept
+
+    def before(ins, outs, scratch, partial_ref):
+        grad_ref, _, up_ref, down_ref, hidden_ref, _ = ins
+        (grad_hidden,) = scratch
+        grad_act = contract_last(down_ref[...], grad_ref[...].reshape(count, D))
+        _, pull = jax.vjp(gelu, hidden_ref[...])
+        grad_hidden[...] = pull(grad_act)[0].astype(jnp.bfloat16)
+        partial_ref[...] = contract_first(grad_hidden[...], up_ref[...])
+
+    def during(ins, outs, scratch):
+        grad_ref, normed_ref, _, _, _, activated_ref = ins
+        up_grad, down_grad = outs
+        (grad_hidden,) = scratch
+        value = times(grad_hidden[...], normed_ref[...].reshape(count, D))
+        up_grad[...] = value.astype(jnp.bfloat16).reshape(up_grad.shape)
+        value = times(activated_ref[...], grad_ref[...].reshape(count, D))
+        down_grad[...] = value.astype(jnp.bfloat16).reshape(down_grad.shape)
+
+    grads = ((units // (2 * half_rows), 2, half_rows, D), jnp.bfloat16)
+    return Work(
+        before,
+        during,
+        [grad, normed, table, table, hidden, activated],
+        [VMEM_SPEC, VMEM_SPEC, part_spec(units, 1), part_spec(units, 2), VMEM_SPEC, VMEM_SPEC],
+        [grads, grads],
+        [pltpu.VMEM((units, count), jnp.bfloat16)],
+    )
+
+
 LINE_BLOCKS = 2
+LINE_LAG = 2
 
 
 class Line:
@@ -295,23 +541,13 @@
         if share:
             self.scratch += [pltpu.VMEM(self.half, jnp.bfloat16)] + [dma((self.chunks,))] * 3
 
-    def neighbours(self, signal):
-        group = lax.axis_index("dp")
-
-        @pl.when(group > 0)
-        def _():
-            signal({"dp": group - 1})
-
-        @pl.when(group < self.groups - 1)
-        def _():
-            signal({"dp": group + 1})
-
     def bind(self, rider_ref, out_ref, refs):
         self.rider, self.out = rider_ref, out_ref
         self.own, self.came, self.going, self.own_sem, self.send_sems, self.recv_sems = refs[:6]
         self.total = out_ref
         if self.share:
             self.total, self.keep_sems, self.twin_send, self.twin_recv = refs[6:]
+        self.done = 0
         self.group = lax.axis_index("dp")
         self.first = jnp.where(self.group < self.groups // 2, 0, 1)
 
@@ -370,35 +606,47 @@
             self.keep_sems.at[chunk],
         )
 
-    def step(self, chunk):
+    def pass_on(self, way, chunk):
         rows = self.at(chunk)
-        own = self.own[rows].astype(jnp.float32)
-        for turn in range(2):
-            way = self.first if turn == 0 else 1 - self.first
-
-            @pl.when(self.comes(way))
+
+        @pl.when(self.comes(way))
+        def _():
+            copy = self.copy(self.going.at[way, rows], way, chunk)
+            copy.wait_recv()
+
+            @pl.when(self.goes(way))
             def _():
-                copy = self.copy(self.going.at[way, rows], way, chunk)
-                copy.wait_recv()
-
-                @pl.when(self.goes(way))
-                def _():
-                    value = own + self.came[way, rows].astype(jnp.float32)
-                    self.going[way, rows] = value.astype(jnp.bfloat16)
-                    copy.start()
-
-        value = own + self.came[0, rows].astype(jnp.float32) + self.came[1, rows].astype(jnp.float32)
-        self.total[rows] = value.astype(jnp.bfloat16)
-        if self.share:
-            self.keep_copy(chunk).start()
-            self.twin_copy(chunk).start()
-
-    def steps(self, start, stop):
-        def one(chunk, carry):
-            self.step(chunk)
+                value = self.own[rows].astype(jnp.float32) + self.came[way, rows].astype(jnp.float32)
+                self.going[way, rows] = value.astype(jnp.bfloat16)
+                copy.start()
+
+    def step(self, index):
+        @pl.when(index < self.chunks)
+        def _():
+            self.pass_on(self.first, index)
+
+        @pl.when(index >= LINE_LAG)
+        def _():
+            chunk = index - LINE_LAG
+            rows = self.at(chunk)
+            self.pass_on(1 - self.first, chunk)
+            value = self.own[rows].astype(jnp.float32)
+            value = value + self.came[0, rows].astype(jnp.float32)
+            value = value + self.came[1, rows].astype(jnp.float32)
+            self.total[rows] = value.astype(jnp.bfloat16)
+            if self.share:
+                self.keep_copy(chunk).start()
+                self.twin_copy(chunk).start()
+
+    def steps(self, count=None):
+        stop = self.chunks + LINE_LAG if count is None else self.done + count
+
+        def one(index, carry):
+            self.step(index)
             return carry
 
-        lax.fori_loop(start, stop, one, 0)
+        lax.fori_loop(self.done, stop, one, 0)
+        self.done = stop
 
     def end(self):
         def one(chunk, carry):
@@ -463,6 +711,8 @@
         for place in range(groups):
             near_copies[place].wait_recv()
             own_copies[place].wait()
+            if line and place < 4:
+                line.steps(1)
             for slot in range(tensors):
                 mid[place, slot] = (
                     own[place, slot].astype(jnp.float32) + near[place, slot].astype(jnp.float32)
@@ -481,8 +731,8 @@
             )
         far_copies = []
         for place, target in enumerate(order):
-            if line:
-                line.steps(line.chunks * place // groups, line.chunks * (place + 1) // groups)
+            if line and place < 4:
+                line.steps(2)
             total = mid[place, part].astype(jnp.float32)
             for step in range(tensors - 1):
                 mid_copies[place][step].wait_recv()
@@ -498,6 +748,8 @@
                         {"dp": target},
                     )
                 )
+        if line:
+            line.steps()
         for place, copy in enumerate(far_copies):
             copy.wait_recv()
             total = total + far_in[place].astype(jnp.float32)
@@ -529,6 +781,7 @@
             dma((groups,)),
         ]
         + (line.scratch if line else []),
+        cost_estimate=SHORT,
         compiler_params=pltpu.CompilerParams(
             collective_id=collective_id, has_side_effects=True, vmem_limit_bytes=56 << 20
         ),
@@ -573,10 +826,8 @@
             line.begin()
         mid_copies, near_copies = [], []
         for place in range(groups):
-            if line and place:
-                line.steps(
-                    line.chunks * (place - 1) // groups // 2, line.chunks * place // groups // 2
-                )
+            if line and 0 < place < 4:
+                line.steps(1)
             source = behind("dp", place)
             if place:
                 far_copies[place - 1].wait_recv()
@@ -590,12 +841,9 @@
             near_copies.append(
                 send(held, held, near_send.at[place, 0], near_recv.at[place, 0], {"seq": twin})
             )
-        if line:
-            done = line.chunks * (groups - 1) // groups // 2
         for place in range(groups):
-            if line:
-                left = line.chunks - done
-                line.steps(done + left * place // groups, done + left * (place + 1) // groups)
+            if line and place < 4:
+                line.steps(2)
             source = behind("dp", place)
             for step in range(tensors - 1):
                 mid_copies[place][step].wait_recv()
@@ -609,6 +857,8 @@
                         {"seq": twin},
                     )
                 )
+        if line:
+            line.steps()
         for copy in near_copies:
             copy.wait_recv()
         for copy in near_copies + far_copies + [c for row in mid_copies for c in row]:
@@ -635,6 +885,7 @@
             dma((groups, tensors)),
         ]
         + (line.scratch if line else []),
+        cost_estimate=SHORT,
         compiler_params=pltpu.CompilerParams(
             collective_id=collective_id, has_side_effects=True, vmem_limit_bytes=40 << 20
         ),
@@ -749,6 +1000,7 @@
             dma((2, groups - 1)),
             dma((2, groups - 1)),
         ],
+        cost_estimate=SHORT,
         compiler_params=pltpu.CompilerParams(collective_id=collective_id, has_side_effects=True),
     )(stats)
 
@@ -807,6 +1059,7 @@
             dma((2 * groups - 1,)),
             dma((2 * groups - 1,)),
         ],
+        cost_estimate=SHORT,
         compiler_params=pltpu.CompilerParams(collective_id=collective_id, has_side_effects=True),
     )(block)
 
@@ -911,6 +1164,7 @@
             dma((groups - 1,)),
             dma((groups - 1,)),
         ],
+        cost_estimate=SHORT,
         compiler_params=pltpu.CompilerParams(collective_id=collective_id, has_side_effects=True),
     )(*operands)
 
@@ -968,6 +1222,7 @@
             out_specs=[slot] * 3,
         ),
         out_shape=[jax.ShapeDtypeStruct(master.shape, jnp.float32)] * 3,
+        cost_estimate=SHORT,
         compiler_params=pltpu.CompilerParams(vmem_limit_bytes=48 << 20),
     )(
         plan,
@@ -1018,6 +1273,7 @@
             scratch_shapes=scratch,
         ),
         out_shape=out_shape,
+        cost_estimate=SHORT,
         compiler_params=pltpu.CompilerParams(vmem_limit_bytes=60 << 20),
     )(span, *operands)
 
@@ -1203,78 +1459,6 @@
         [whole((rows, D)), whole((8, D))],
         [],
     )
-
-
-def attend(joined, geometry):
-    cosine, sine, allowed, seq_count, half_len, local_heads = geometry
-    width = local_heads * HEAD_DIM
-    shape_four = (seq_count, half_len, local_heads, HEAD_DIM)
-    queries = (
-        rotate(joined[:, :width].reshape(-1, local_heads, HEAD_DIM), cosine, sine)
-        .astype(jnp.bfloat16)
-        .reshape(shape_four)
-    )
-    own_keys = (
-        rotate(joined[:, width : 2 * width].reshape(-1, local_heads, HEAD_DIM), cosine, sine)
-        .astype(jnp.bfloat16)
-        .reshape(shape_four)
-    )
-    own_values = joined[:, 2 * width :].astype(jnp.bfloat16).reshape(shape_four)
-    far_keys, far_values = from_behind((own_keys, own_values), "seq", 1)
-    keys_all = jnp.concatenate([far_keys, own_keys], axis=1)
-    values_all = jnp.concatenate([far_values, own_values], axis=1)
-    scores = attention_scores(queries, keys_all, allowed)
-    peak = jnp.max(scores, -1, keepdims=True)
-    log_total = peak + jnp.log(jnp.sum(jnp.exp(scores - peak), -1, keepdims=True))
-    probs = jnp.exp(scores - log_total).astype(jnp.bfloat16)
-    attended = jnp.einsum("bhqk,bkhd->bqhd", probs, values_all, preferred_element_type=jnp.float32)
-    attended = attended.astype(jnp.bfloat16).reshape(-1, width)
-    return attended, (queries, keys_all, values_all, log_total)
-
-
-def attend_back(grad_attended, kept, geometry):
-    queries, keys_all, values_all, log_total = kept
-    cosine, sine, allowed, seq_count, half_len, local_heads = geometry
-    width = local_heads * HEAD_DIM
-    grad_attended = grad_attended.reshape(seq_count, half_len, local_heads, HEAD_DIM)
-    probs = jnp.exp(attention_scores(queries, keys_all, allowed) - log_total)
-    grad_probs = jnp.einsum(
-        "bqhd,bkhd->bhqk", grad_attended, values_all, preferred_element_type=jnp.float32
-    )
-    grad_scores = (probs * (grad_probs - jnp.sum(probs * grad_probs, -1, keepdims=True))).astype(
-        jnp.bfloat16
-    )
-    scale = HEAD_DIM ** (-0.5)
-    grad_queries = (
-        jnp.einsum("bhqk,bkhd->bqhd", grad_scores, keys_all, preferred_element_type=jnp.float32)
-        * scale
-    )
-    grad_keys = (
-        jnp.einsum("bhqk,bqhd->bkhd", grad_scores, queries, preferred_element_type=jnp.float32)
-        * scale
-    )
-    grad_values = jnp.einsum(
-        "bhqk,bqhd->bkhd",
-        probs.astype(jnp.bfloat16),
-        grad_attended,
-        preferred_element_type=jnp.float32,
-    )
-    back_keys, back_values = (
-        from_behind(grad_keys[:, :half_len].astype(jnp.bfloat16), "seq", -1).astype(jnp.float32),
-        from_behind(grad_values[:, :half_len].astype(jnp.bfloat16), "seq", -1).astype(jnp.float32),
-    )
-    grad_keys = grad_keys[:, half_len:] + back_keys
-    grad_values = grad_values[:, half_len:] + back_values
-    return jnp.concatenate(
-        [
-            rotate(grad_queries.reshape(-1, local_heads, HEAD_DIM), cosine, -sine).reshape(
-                -1, width
-            ),
-            rotate(grad_keys.reshape(-1, local_heads, HEAD_DIM), cosine, -sine).reshape(-1, width),
-            grad_values.reshape(-1, width),
-        ],
-        axis=1,
-    ).astype(jnp.bfloat16)
 
 
 def body(
@@ -1350,31 +1534,21 @@
     table_slots = jnp.pad(master.astype(jnp.bfloat16), ((0, spare), (0, 0), (0, 0)))
     table = table_slots.reshape(-1, D)
 
-    halves = []
-    for level in range(LAYERS):
-        chosen = slice(level * layer_blocks, (level + 1) * layer_blocks)
-        halves.append(
-            jnp.where(
-                mine[chosen][:, None, None], jnp.take(table_slots, slot_rank[chosen], axis=0), 0.0
-            ).astype(jnp.bfloat16)
-        )
+    halves = jnp.where(
+        mine[:blocks][:, None, None], jnp.take(table_slots, slot_rank[:blocks], axis=0), 0.0
+    ).astype(jnp.bfloat16)
+    halves = [halves[i * layer_blocks : (i + 1) * layer_blocks] for i in range(LAYERS)]
     halves[1:] = [lax.psum(half, "dp") for half in halves[1:]]
 
-    def cut(joined):
-        joined = joined.reshape(layer_rows, D)
-        cut_one, cut_two = head_rows + out_rows, head_rows + out_rows + unit_rows
-        return (joined[:head_rows], joined[head_rows:cut_one], joined[cut_one:cut_two], joined[cut_two:])
-
     positions = seq_part * half_len + jnp.arange(row_count) % half_len
-    cosine, sine = rotary(positions)
-    query_pos = seq_part * half_len + jnp.arange(half_len)
-    key_pos = jnp.concatenate([(seq_part - 1) * half_len + jnp.arange(half_len), query_pos])
-    allowed = (key_pos[None, :] <= query_pos[:, None]) & (key_pos[None, :] >= 0)
-    geometry = (cosine, sine, allowed, seq_count, half_len, local_heads)
+    steps_half = jnp.arange(HEAD_DIM // 2).astype(jnp.float32)
+    freqs = 10000.0 ** (-2.0 * steps_half / HEAD_DIM)
+    angles = freqs[:, None] * positions.astype(jnp.float32)[None, :]
+    cosine, sine = jnp.cos(angles), jnp.sin(angles)
 
     looked = look_up(span, row_ids, ids_all, table).reshape(order + (D,))
     start, joined = reduce_rows(looked, (0, 14), halves[0])
-    weights_all = [cut(joined)]
+    tables = [joined.reshape(layer_rows, D)]
     gain = [gains[i : i + 1] for i in range(2 * LAYERS + 1)]
     piece = ((share, D), jnp.float32)
 
@@ -1396,41 +1570,34 @@
     (normed,) = tensor_step("normed", normed_of, None, (start, gain[0]), (), [], True, 1)
     states, streams, inners, kept_all = [start], [start], [], []
     for level in range(LAYERS):
-        qkv_w, out_w, up_w, down_w = weights_all[level]
-        normed = normed.reshape(row_count, D)
-        attended, kept = attend(contract_last(normed, qkv_w), geometry)
-        inner, normed_two = tensor_step(
-            "inner",
+        inner, normed_two, *kept = tensor_step(
+            f"inner_{level}",
             inner_of,
-            jnp.dot(attended, out_w, preferred_element_type=jnp.float32),
+            attention_work(normed, tables[level], cosine, sine),
             (streams[level], gain[2 * level + 1]),
             (),
             [piece],
             True,
-            2,
+            2 if level == 0 else 15 + level,
         )
-        normed_two = normed_two.reshape(row_count, D)
-        hidden = contract_last(normed_two, up_w)
-        activated = jax.nn.gelu(hidden, approximate=True).astype(jnp.bfloat16)
         last = level == LAYERS - 1
-        results = tensor_step(
+        outcome, stream, normed_next, hidden, activated, *joined = tensor_step(
             f"outcome_{level}",
             partial(outcome_of, (level + 1) * (level + 2) // 2 - 1),
-            jnp.dot(activated, down_w, preferred_element_type=jnp.float32),
+            unit_work(normed_two, tables[level]),
             [inner, gain[2 * level + 2]] + states,
             (mix,),
             [piece, piece] + ([((share, D), jnp.bfloat16)] if last else []),
             not last,
             3 + level,
-            *((None, None) if last else ("share", halves[level + 1])),
+            None if last else halves[level + 1],
         )
-        if not last:
-            weights_all.append(cut(results[3]))
+        tables += [table_next.reshape(layer_rows, D) for table_next in joined]
         inners.append(inner)
-        kept_all.append((normed, kept, attended, normed_two, hidden, activated))
-        states.append(results[0])
-        streams.append(results[1])
-        normed = results[2]
+        kept_all.append((normed, kept, normed_two, (hidden, activated)))
+        states.append(outcome)
+        streams.append(stream)
+        normed = normed_next
 
     final_all = gather_all(normed, 3 + LAYERS)[0].reshape(-1, D)
     powers, stats = head_forward(span, row_ids, labels_all, table, final_all)
@@ -1486,47 +1653,29 @@
         5 + LAYERS,
     )
     for level in reversed(range(LAYERS)):
-        qkv_w, out_w, up_w, down_w = weights_all[level]
-        normed, kept, attended, normed_two, hidden, activated = kept_all[level]
-        grad_branch = grad_branch.reshape(row_count, D)
-        grad_act = contract_last(grad_branch, down_w)
-        _, gelu_pull = jax.vjp(partial(jax.nn.gelu, approximate=True), hidden)
-        grad_hidden = gelu_pull(grad_act)[0].astype(jnp.bfloat16)
-        grad_inner, gain_grads[2 * level + 1], grad_attn = tensor_step(
-            "inner_back",
+        normed, kept, normed_two, unit_kept = kept_all[level]
+        grad_inner, gain_grads[2 * level + 1], grad_attn, *unit_grads = tensor_step(
+            f"inner_back_{level}",
             inner_back,
-            jnp.dot(grad_hidden, up_w, preferred_element_type=jnp.float32),
+            unit_back_work(grad_branch, normed_two, tables[level], unit_kept, half_rows),
             (grad_state, inners[level], gain[2 * level + 1]),
             (),
             [piece, row],
             True,
-            6 + LAYERS,
+            6 + LAYERS if level == 0 else 19 + level,
         )
-        grad_attn = grad_attn.reshape(row_count, D)
-        grad_attended = contract_last(grad_attn, out_w).astype(jnp.bfloat16)
-        grad_joined = attend_back(grad_attended, kept, geometry)
-        grads = jnp.concatenate(
-            [
-                contract_first(grad_joined, normed),
-                contract_first(attended, grad_attn),
-                contract_first(grad_hidden, normed_two),
-                contract_first(activated, grad_branch),
-            ],
-            axis=0,
-        ).astype(jnp.bfloat16)
-        results = tensor_step(
+        grad_ys[level], grad_state, gain_grads[2 * level], grad_branch, folded = tensor_step(
             f"stream_back_{level}",
             partial(stream_back, level),
-            jnp.dot(grad_joined, qkv_w, preferred_element_type=jnp.float32),
+            attention_back_work(
+                grad_attn, normed, tables[level], kept, cosine, sine, unit_grads
+            ),
             [grad_inner, streams[level], gain[2 * level]] + grad_ys[level + 1 :],
             (mix,),
             [piece, piece, row] + ([] if level else [((share, D), jnp.bfloat16)]),
             level > 0,
             7 + LAYERS + level,
-            "fold",
-            grads.reshape(layer_blocks, 2, half_rows, D),
         )
-        grad_ys[level], grad_state, gain_grads[2 * level], grad_branch, folded = results
         layer_grads[level] = lax.psum(folded, "dp") if level else folded
 
     grad_start_all, layer_grads[0] = gather_all(grad_branch, 13, layer_grads[0])

time: 917 us -> 857 us (0.935)
  Pallas kernels: 725 us -> 780 us
  matrix products: 45.4 us -> 0 us
  waiting for transfers between devices: 35.8 us -> 0.04 us
  other arithmetic: 31.4 us -> 15.4 us
  starting transfers between devices: 13 us -> 0.08 us
  local copies, waits for them, and re-layouts: 47.2 us -> 34.7 us
    pallas_call x10, Pallas kernels: 188 us -> 286 us  [tensor_step(): pl.pallas_call(kernel, name=name, grid=(1,), out_shape=shapes, in_specs=i...]
    dot_general x36 -> x0, matrix products: 45.4 us -> none  [the longest x8 8.34 us: contract_last(): lax.dot_general(left, right, (((1,), (1,)), ((), ())), preferred_element_...]
    psum x1, waiting for transfers between devices: 35.7 us -> 0.01 us  [body(): halves[1:] = [lax.psum(half, 'dp') for half in halves[1:]]]
    pallas_call x2, Pallas kernels: 153 us -> 120 us  [gather_all(): pl.pallas_call(kernel, name='gather_all', out_shape=[jax.ShapeDtypeStruct...]
    ppermute x8 -> x0, starting transfers between devices: 12.8 us -> none  [from_behind(): return lax.ppermute(block, axis, route)]
    unnamed x250 -> x138, local copies, waits for them, and re-layouts: 24.1 us -> 21.7 us
  transfers between devices with their start and end apart: 10 -> 2, of which waited for: 1 -> 0; matrix products, arithmetic and copies ran while one was open for 4% -> 1% of each run, Pallas kernels for 19% -> 40%
where the time goes in v4:
time: 857 us; the launch traced here: 850 us
  Pallas kernels  780 us (91%)
  local copies, waits for them, and re-layouts  34.7 us (4%)
  between operations  19.8 us (2%)
  other arithmetic  15.4 us (2%)
    pallas_call x10, Pallas kernels, tensor_step(): pl.pallas_call(kernel, name=name, grid=(1,), out_shape=shapes, in_specs=i...  286 us
    pallas_call x2, Pallas kernels, reduce_all(): pl.pallas_call(kernel, name='reduce_all', out_shape=[jax.ShapeDtypeStruct...  161 us
    pallas_call x4, Pallas kernels, local_call(): pl.pallas_call(kernel, name=name, grid_spec=pltpu.PrefetchScalarGridSpec(...  120 us
    pallas_call x2, Pallas kernels, gather_all(): pl.pallas_call(kernel, name='gather_all', out_shape=[jax.ShapeDtypeStruct...  120 us
    pallas_call x1, Pallas kernels, update_slots(): pl.pallas_call(kernel, name='update_slots', grid_spec=pltpu.PrefetchScala...  34.4 us
    pallas_call x1, Pallas kernels, join_stats(): pl.pallas_call(kernel, name='join_stats', out_shape=[jax.ShapeDtypeStruct...  28.4 us
    unnamed x138, local copies, waits for them, and re-layouts  21.7 us
    pallas_call x1, Pallas kernels, finish(): pl.pallas_call(kernel, name='finish', out_shape=[jax.ShapeDtypeStruct(val...  20.1 us
  transfers between devices with their start and end apart: 2, of which 0 were waited for; matrix products, arithmetic and copies ran while one was open for 1% of the time, Pallas kernels for 40%

profile of v4, /device:TPU:0, one launch (start us, length us, event | category | flops | bytes accessed | tf_op | source)
XLA Modules:
  0.0 849.9 jit_solution(10467081255805860371)
XLA Ops:
  7.2 0.9 select_reduce_fusion.2
  8.2 1.3 fusion.7
  9.5 4.4 convert_element_type.27
  14.4 2.8 pad.14
  17.2 3.4 gather_fusion
  20.6 1.2 select_select_fusion
  21.8 2.1 fusion.9
  24.7 0.7 add_add_fusion.block_ref
  25.3 9.2 %spread_tokens.1 = (s32[4,8,128]{2,1,0:T(8,128)}, s32[4,8,128]{2,1,0:T(8,128)}, f32[4,8,128]{2,1,0:T(8,128)}, f32[1,128]{1,0:T(1,128)}) custom-call(s32[16,128]{1,0:T(8,128)} %add_add_fusion.block_ref), custom_call_target="tpu_custom_call" | custom-call | flops 1000 | bytes 1000 | tf_op jit(solution)/shard_map/spread_tokens/pallas_call | solution.py:1045
  35.3 0.8 select_n.148
  37.4 1.4 pad.13.ids_ref
  39.4 24.9 %look_up.1 = bf16[4096,768]{1,0:T(8,128)(2,1)} custom-call(s32[2]{0:T(128)} %pad_add_fusion.1.span_ref, s32[3648,1]{1,0:T(8,128)} %pad.13.ids_ref, s32[4,8,128]{2,1,0:T(8,128)} %get-tuple-element.86.tokens_ref, bf16[3648,768]{1,0:T(8,128)(2,1)} %bitcast.68), custom_call_target="tpu_custom_call" | custom-call | flops 1000 | bytes 1000 | tf_op jit(solution)/shard_map/look_up/pallas_call | solution.py:1265
  64.3 106.6 %reduce_all.2 = (f32[128,768]{1,0:T(8,128)}, bf16[24,2,48,768]{3,2,1,0:T(8,128)(2,1)}) custom-call(bf16[2,4,4,128,768]{4,3,2,1,0:T(8,128)(2,1)} %bitcast.71, bf16[24,48,768]{2,1,0:T(8,128)(2,1)} %get-tuple-element.162.refs_1_), custom_call_target="tpu_custom_call" | custom-call | flops 1000 | bytes 1000 | tf_op jit(solution)/shard_map/reduce_all/pallas_call | solution.py:764
  171.5 1.0 copy-done.2
  172.5 12.7 %normed.1.refs_0_.refs_1_ = bf16[4,128,768]{2,1,0:T(8,128)(2,1)S(1)} custom-call(f32[128,768]{1,0:T(8,128)S(1)} %copy-done.2, f32[1,768]{1,0:T(1,128)S(1)} %get-tuple-element.167.refs_1_.refs_14_), custom_call_target="tpu_custom_call" | custom-call | flops 1000 | bytes 1000 | tf_op jit(solution)/shard_map/normed/pallas_call | solution.py:217
  185.5 1.0 copy-done.3
  186.5 30.4 %inner_0.1 = (f32[128,768]{1,0:T(8,128)S(1)}, bf16[4,128,768]{2,1,0:T(8,128)(2,1)S(1)}, bf16[192,512]{1,0:T(8,128)(2,1)S(1)}, bf16[2,2,192,512]{3,2,1,0:T(8,128)...) custom-call(bf16[4,128,768]{2,1,0:T(8,128)(2,1)S(1)} %normed.1.refs_0_.refs_1_, ...), custom_call_target="tpu_custom_call" | custom-call | flops 1000 | bytes 1000 | tf_op jit(solution)/shard_map/inner_0/pallas_call | solution.py:217
  218.2 0.9 copy-done.23
  219.1 0.7 copy-done.32
  219.8 0.7 copy-done.34
  220.5 59.3 %outcome_0.1 = (f32[128,768]{1,0:T(8,128)S(1)}, f32[128,768]{1,0:T(8,128)S(1)}, bf16[4,128,768]{2,1,0:T(8,128)(2,1)S(1)}, f32[768,512]{1,0:T(8,128)}, bf16[768,5...) custom-call(bf16[4,128,768]{2,1,0:T(8,128)(2,1)S(1)} %get-tuple-element.89.refs_0_.refs_1_, ...), custom_call_target="tpu_custom_call" | custom-call | flops 1000 | bytes 1000 | tf_op jit(solution)/shard_map/outcome_0/pallas_call | solution.py:217
  280.0 30.5 %inner_1.1 = (f32[128,768]{1,0:T(8,128)S(1)}, bf16[4,128,768]{2,1,0:T(8,128)(2,1)S(1)}, bf16[192,512]{1,0:T(8,128)(2,1)S(1)}, bf16[2,2,192,512]{3,2,1,0:T(8,128)...) custom-call(bf16[4,128,768]{2,1,0:T(8,128)(2,1)S(1)} %get-tuple-element.91.refs_0_.refs_1_, ...), custom_call_target="tpu_custom_call" | custom-call | flops 1000 | bytes 1000 | tf_op jit(solution)/shard_map/inner_1/pallas_call | solution.py:217
  310.5 0.9 copy-done.25
  311.4 0.7 copy-done.36
  312.1 23.9 %outcome_1.1 = (f32[128,768]{1,0:T(8,128)S(1)}, f32[128,768]{1,0:T(8,128)S(1)}, bf16[128,768]{1,0:T(8,128)(2,1)S(1)}, f32[768,512]{1,0:T(8,128)}, bf16[768,512]{1,0:T(8,128)(2,1)S(1)}) custom-call(bf16[4,128,768]{2,1,0:T(8,128)(2,1)S(1)} %get-tuple-element.94.refs_0_.refs_1_, bf16[2304,768]{1,0:T(8,128)(2,1)} %bitcast.62, bf16[2304,768]{1,0:T(8,128)(2,1)} %bitcast.63, ...), custom_call_target="tpu_custom_call" | custom-call | flops 1000 | bytes 1000 | tf_op jit(solution)/shard_map/outcome_1/pallas_call | solution.py:217
  336.1 42.7 %gather_all.2 = bf16[2,4,4,128,768]{4,3,2,1,0:T(8,128)(2,1)S(1)} custom-call(bf16[128,768]{1,0:T(8,128)(2,1)S(1)} %get-tuple-element.97.refs_0_), custom_call_target="tpu_custom_call" | custom-call | flops 1000 | bytes 1000 | tf_op jit(solution)/shard_map/gather_all/pallas_call | solution.py:871
  378.8 2.7 copy-done
  381.5 27.3 %head_forward.1 = (bf16[3648,4096]{1,0:T(8,128)(2,1)}, f32[32,8,128]{2,1,0:T(8,128)}) custom-call(s32[2]{0:T(128)} %pad_add_fusion.1.span_ref, s32[3648,1]{1,0:T(8,128)} %pad.13.ids_ref, s32[4,8,128]{2,1,0:T(8,128)} %get-tuple-element.84.labels_ref, bf16[3648,768]{1,0:T(8,128)(2,1)} %bitcast.69, bf16[4096,768]{1,0:T(8,128)(2,1)} %bitcast.48), custom_call_target="tpu_custom_call" | custom-call | flops 1000 | bytes 1000 | tf_op jit(solution)/shard_map/head_forward/pallas_call | solution.py:1265
  408.8 28.4 %join_stats.1 = (f32[8,128]{1,0:T(8,128)}, f32[2,4,4,8,128]{4,3,2,1,0:T(8,128)}) custom-call(f32[2,4,4,8,128]{4,3,2,1,0:T(8,128)} %bitcast.73), custom_call_target="tpu_custom_call" | custom-call | flops 1000 | bytes 1000 | tf_op jit(solution)/shard_map/join_stats/pallas_call | solution.py:981
  437.2 41.9 %head_backward.1 = (bf16[4096,768]{1,0:T(8,128)(2,1)}, f32[3648,768]{1,0:T(8,128)}) custom-call(s32[2]{0:T(128)} %pad_add_fusion.1.span_ref, s32[3648,1]{1,0:T(8,128)} %pad.13.ids_ref, s32[4,8,128]{2,1,0:T(8,128)} %get-tuple-element.84.labels_ref, f32[4,8,128]{2,1,0:T(8,128)} %get-tuple-element.85.keep_ref, f32[32,8,128]{2,1,0:T(8,128)} %get-tuple-element.98.stats_ref, ...), custom_call_target="tpu_custom_call" | custom-call | flops 1000 | bytes 1000 | tf_op jit(solution)/shard_map/head_backward/pallas_call | solution.py:1265
  479.1 54.2 %reduce_all.3.refs_0_ = f32[128,768]{1,0:T(8,128)} custom-call(bf16[2,4,4,128,768]{4,3,2,1,0:T(8,128)(2,1)} %bitcast.72), custom_call_target="tpu_custom_call" | custom-call | flops 1000 | bytes 1000 | tf_op jit(solution)/shard_map/reduce_all/pallas_call | solution.py:764
  533.4 1.0 copy-done.22
  534.3 12.8 %top_back.1 = (f32[128,768]{1,0:T(8,128)S(1)}, f32[128,768]{1,0:T(8,128)S(1)}, f32[1,768]{1,0:T(1,128)S(1)}, bf16[4,128,768]{2,1,0:T(8,128)(2,1)S(1)}) custom-call(f32[128,768]{1,0:T(8,128)S(1)} %copy-done.22, f32[128,768]{1,0:T(8,128)S(1)} %copy-done.31, f32[1,768]{1,0:T(1,128)S(1)} %copy-done.40, f32[5]{0:T(128)S(1)} %copy-done.42), custom_call_target="tpu_custom_call" | custom-call | flops 1000 | bytes 1000 | tf_op jit(solution)/shard_map/top_back/pallas_call | solution.py:217
  547.2 27.2 %inner_back_1.1 = (f32[128,768]{1,0:T(8,128)S(1)}, f32[1,768]{1,0:T(1,128)S(1)}, bf16[4,128,768]{2,1,0:T(8,128)(2,1)S(1)}, bf16[8,2,48,768]{3,2,1,0:T(8,128)(2,1)}, bf16[8,2,48,768]{3,2,1,0:T(8,128)(2,1)}) custom-call(bf16[4,128,768]{2,1,0:T(8,128)(2,1)S(1)} %get-tuple-element.103.refs_0_, bf16[4,128,768]{2,1,0:T(8,128)(2,1)S(1)} %get-tuple-element.94.refs_0_.refs_1_, ...), custom_call_target="tpu_custom_call" | custom-call | flops 1000 | bytes 1000 | tf_op jit(solution)/shard_map/inner_back_1/pallas_call | solution.py:217
  574.5 35.9 %stream_back_1.1 = (f32[128,768]{1,0:T(8,128)S(1)}, f32[128,768]{1,0:T(8,128)S(1)}, f32[1,768]{1,0:T(1,128)S(1)}, bf16[4,128,768]{2,1,0:T(8,128)(2,1)S(1)}, bf16[24,48,768]{2,1,0:T(8,128)(2,1)}) custom-call(bf16[4,128,768]{2,1,0:T(8,128)(2,1)S(1)} %get-tuple-element.107.refs_0_, bf16[4,128,768]{2,1,0:T(8,128)(2,1)} %copy-done.8, bf16[2304,768]{1,0:T(8,128)(2,1)} %bitcast.66, ...), custom_call_target="tpu_custom_call" | custom-call | flops 1000 | bytes 1000 | tf_op jit(solution)/shard_map/stream_back_1/pallas_call | solution.py:217
  610.4 0.9 copy-done.26
  612.5 1.1 copy-done.27
  613.6 27.5 %inner_back_0.1 = (f32[128,768]{1,0:T(8,128)S(1)}, f32[1,768]{1,0:T(1,128)S(1)}, bf16[4,128,768]{2,1,0:T(8,128)(2,1)S(1)}, bf16[8,2,48,768]{3,2,1,0:T(8,128)(2,1)}, bf16[8,2,48,768]{3,2,1,0:T(8,128)(2,1)}) custom-call(bf16[4,128,768]{2,1,0:T(8,128)(2,1)S(1)} %copy-done.27, bf16[4,128,768]{2,1,0:T(8,128)(2,1)S(1)} %get-tuple-element.89.refs_0_.refs_1_, ...), custom_call_target="tpu_custom_call" | custom-call | flops 1000 | bytes 1000 | tf_op jit(solution)/shard_map/inner_back_0/pallas_call | solution.py:217
  641.2 26.0 %stream_back_0.1 = (f32[128,768]{1,0:T(8,128)}, f32[128,768]{1,0:T(8,128)}, f32[1,768]{1,0:T(1,128)S(1)}, bf16[128,768]{1,0:T(8,128)(2,1)S(1)}, bf16[24,48,768]{2,1,0:T(8,128)(2,1)}) custom-call(bf16[4,128,768]{2,1,0:T(8,128)(2,1)S(1)} %get-tuple-element.120.refs_0_, bf16[4,128,768]{2,1,0:T(8,128)(2,1)} %copy-done.5, bf16[2304,768]{1,0:T(8,128)(2,1)} %bitcast.58, ...), custom_call_target="tpu_custom_call" | custom-call | flops 1000 | bytes 1000 | tf_op jit(solution)/shard_map/stream_back_0/pallas_call | solution.py:217
  667.3 1.5 copy-done.9
  668.7 77.7 %gather_all.3 = (bf16[2,4,4,128,768]{4,3,2,1,0:T(8,128)(2,1)S(1)}, bf16[24,48,768]{2,1,0:T(8,128)(2,1)S(1)}) custom-call(bf16[128,768]{1,0:T(8,128)(2,1)S(1)} %get-tuple-element.136.refs_0_, bf16[24,48,768]{2,1,0:T(8,128)(2,1)S(1)} %copy-done.9), custom_call_target="tpu_custom_call" | custom-call | flops 1000 | bytes 1000 | tf_op jit(solution)/shard_map/gather_all/pallas_call | solution.py:871
  746.4 2.7 copy-done.6
  749.1 26.3 %look_back.1 = (f32[3648,768]{1,0:T(8,128)}, f32[8,768]{1,0:T(8,128)}) custom-call(s32[2]{0:T(128)} %pad_add_fusion.1.span_ref, s32[3648,1]{1,0:T(8,128)} %pad.13.ids_ref, s32[4,8,128]{2,1,0:T(8,128)} %get-tuple-element.86.tokens_ref, bf16[4096,768]{1,0:T(8,128)(2,1)} %bitcast.50, f32[3648,768]{1,0:T(8,128)} %get-tuple-element.139.table_ref), custom_call_target="tpu_custom_call" | custom-call | flops 1000 | bytes 1000 | tf_op jit(solution)/shard_map/look_back/pallas_call | solution.py:1265
  775.4 1.6 select_reduce_fusion.1
  777.0 3.2 select_reduce_fusion
  781.5 20.1 %finish.1 = (f32[5,768]{1,0:T(8,128)}, f32[5,768]{1,0:T(8,128)}, f32[5,768]{1,0:T(8,128)}, f32[1,5]{1,0:T(1,128)}, f32[1,5]{1,0:T(1,128)}, /*index=5*/f32[1,5]{1,0:T(1,128)}, f32[1,128]{1,0:T(1,128)}, f32[8,128]{1,0:T(8,128)}) custom-call(f32[1,768]{1,0:T(1,128)} %copy-done.50, f32[1,768]{1,0:T(1,128)} %copy-done.49, f32[1,768]{1,0:T(1,128)} %copy-done.48, ...), custom_call_target="tpu_custom_call" | custom-call | flops 1000 | bytes 1000 | tf_op jit(solution)/shard_map/finish/pallas_call | solution.py:1146
  801.6 1.3 fusion.11
  803.7 34.4 %update_slots.1 = (f32[67,48,768]{2,1,0:T(8,128)}, f32[67,48,768]{2,1,0:T(8,128)}, f32[67,48,768]{2,1,0:T(8,128)}) custom-call(s32[3,68]{1,0:T(4,128)S(1)} %pad.12.plan_ref, f32[8,128]{1,0:T(8,128)S(1)} %copy-done.45, f32[67,48,768]{2,1,0:T(8,128)} %master_ref.1, f32[67,48,768]{2,1,0:T(8,128)} %first_ref.1, f32[67,48,768]{2,1,0:T(8,128)} %second_ref.1, ...), custom_call_target="tpu_custom_call" | custom-call | flops 1000 | bytes 1000 | tf_op jit(solution)/shard_map/update_slots/pallas_call | solution.py:1202
  (149 shorter events, 9.6 us)
Async XLA Ops:
  7.2 213.3 %all-reduce.6.cloned.1.call-start = ((), (), s32[]{:S(2)}) async-start(), calls=%async_computation | async-start | bytes 3538944 | tf_op jit(solution)/shard_map/psum | solution.py:1541
  9.5 25.1 %copy-start.55 = (pred[179]{0:T(512)(128)(4,1)}, pred[179]{0:T(512)(128)(4,1)S(1)}, u32[]{:S(2)}) copy-start(pred[179]{0:T(512)(128)(4,1)S(1)} %get-tuple-element.160) | copy-start | bytes 541
  23.9 753.1 %all-reduce.8.cloned.1.call-start = ((), (), s32[]{:S(2)}) async-start(), calls=%async_computation.1 | async-start | bytes 3538944 | tf_op jit(solution)/shard_map/psum | solution.py:1679
  64.3 106.6 %copy-start.51 = (f32[5,768]{1,0:T(8,128)S(1)}, f32[5,768]{1,0:T(8,128)}, u32[]{:S(2)}) copy-start(f32[5,768]{1,0:T(8,128)} %refs_15_.1) | copy-start | bytes 46084
  185.2 31.7 %copy-start.5 = (bf16[4,128,768]{2,1,0:T(8,128)(2,1)}, bf16[4,128,768]{2,1,0:T(8,128)(2,1)S(1)}, u32[]{:S(2)}) copy-start(bf16[4,128,768]{2,1,0:T(8,128)(2,1)S(1)} %normed.1.refs_0_.refs_1_) | copy-start | bytes 2359300
  186.5 34.0 %copy-start.4 = (f32[128,768]{1,0:T(8,128)S(1)}, f32[128,768]{1,0:T(8,128)}, u32[]{:S(2)}) copy-start(f32[128,768]{1,0:T(8,128)} %get-tuple-element.87.refs_0_.refs_5_.refs_13_) | copy-start | bytes 1179652
  186.5 34.0 %copy-start.41 = (f32[5]{0:T(128)S(1)}, f32[5]{0:T(128)}, u32[]{:S(2)}) copy-start(f32[5]{0:T(128)} %refs_17_.2) | copy-start | bytes 64
  220.5 59.4 %copy-start.14 = (f32[128,768]{1,0:T(8,128)}, f32[128,768]{1,0:T(8,128)S(1)}, u32[]{:S(2)}) copy-start(f32[128,768]{1,0:T(8,128)S(1)} %get-tuple-element.90.refs_3_.refs_7_) | copy-start | bytes 1179652
  220.5 59.4 %copy-start.43 = (f32[3,1,512]{2,1,0:T(1,128)}, f32[3,1,512]{2,1,0:T(1,128)S(1)}, u32[]{:S(2)}) copy-start(f32[3,1,512]{2,1,0:T(1,128)S(1)} %get-tuple-element.123.refs_6_) | copy-start | bytes 18436
  220.5 59.4 %copy-start.11 = (f32[32,512]{1,0:T(8,128)S(1)}, f32[32,512]{1,0:T(8,128)}, u32[]{:S(2)}) copy-start(f32[32,512]{1,0:T(8,128)} %copy-done.10) | copy-start | bytes 196612
  220.5 59.4 %copy-start.13 = (f32[32,512]{1,0:T(8,128)S(1)}, f32[32,512]{1,0:T(8,128)}, u32[]{:S(2)}) copy-start(f32[32,512]{1,0:T(8,128)} %copy-done.12) | copy-start | bytes 196612
  279.9 30.6 %copy-start.8 = (bf16[4,128,768]{2,1,0:T(8,128)(2,1)}, bf16[4,128,768]{2,1,0:T(8,128)(2,1)S(1)}, u32[]{:S(2)}) copy-start(bf16[4,128,768]{2,1,0:T(8,128)(2,1)S(1)} %get-tuple-element.91.refs_0_.refs_1_) | copy-start | bytes 2359300
  279.9 30.6 %copy-start.16 = (f32[128,768]{1,0:T(8,128)}, f32[128,768]{1,0:T(8,128)S(1)}, u32[]{:S(2)}) copy-start(f32[128,768]{1,0:T(8,128)S(1)} %get-tuple-element.93.refs_5_.refs_13_) | copy-start | bytes 1179652
  279.9 30.6 %copy-start.24 = (bf16[768,512]{1,0:T(8,128)(2,1)}, bf16[768,512]{1,0:T(8,128)(2,1)S(1)}, u32[]{:S(2)}) copy-start(bf16[768,512]{1,0:T(8,128)(2,1)S(1)} %get-tuple-element.118.refs_5_) | copy-start | bytes 2359300
  279.9 32.2 %copy-start.20 = (f32[128,768]{1,0:T(8,128)}, f32[128,768]{1,0:T(8,128)S(1)}, u32[]{:S(2)}) copy-start(f32[128,768]{1,0:T(8,128)S(1)} %get-tuple-element.96.refs_6_) | copy-start | bytes 1179652
  279.9 32.2 %copy-start.40 = (f32[1,768]{1,0:T(1,128)S(1)}, f32[1,768]{1,0:T(1,128)}, u32[]{:S(2)}) copy-start(f32[1,768]{1,0:T(1,128)} %get-tuple-element.163.refs_4_.refs_2_) | copy-start | bytes 9220
  279.9 32.2 %copy-start.42 = (f32[5]{0:T(128)S(1)}, f32[5]{0:T(128)}, u32[]{:S(2)}) copy-start(f32[5]{0:T(128)} %refs_17_.2) | copy-start | bytes 64
  312.1 23.9 %copy-start.38 = (bf16[192,512]{1,0:T(8,128)(2,1)}, bf16[192,512]{1,0:T(8,128)(2,1)S(1)}, u32[]{:S(2)}) copy-start(bf16[192,512]{1,0:T(8,128)(2,1)S(1)} %get-tuple-element.111.refs_7_) | copy-start | bytes 589828
  336.0 42.7 %copy-start.29 = (f32[128,768]{1,0:T(8,128)}, f32[128,768]{1,0:T(8,128)S(1)}, u32[]{:S(2)}) copy-start(f32[128,768]{1,0:T(8,128)S(1)} %get-tuple-element.134.refs_7_) | copy-start | bytes 1179652
  336.0 45.4 %copy-start.30 = (f32[128,768]{1,0:T(8,128)}, f32[128,768]{1,0:T(8,128)S(1)}, u32[]{:S(2)}) copy-start(f32[128,768]{1,0:T(8,128)S(1)} %get-tuple-element.102.refs_1_) | copy-start | bytes 1179652
  336.1 72.8 %copy-start.28 = (bf16[768,512]{1,0:T(8,128)(2,1)}, bf16[768,512]{1,0:T(8,128)(2,1)S(1)}, u32[]{:S(2)}) copy-start(bf16[768,512]{1,0:T(8,128)(2,1)S(1)} %get-tuple-element.105.refs_5_) | copy-start | bytes 2359300
  479.1 54.2 %copy-start.31 = (f32[128,768]{1,0:T(8,128)S(1)}, f32[128,768]{1,0:T(8,128)}, u32[]{:S(2)}) copy-start(f32[128,768]{1,0:T(8,128)} %copy-done.30) | copy-start | bytes 1179652
  479.1 68.1 %copy-start.19 = (f32[128,768]{1,0:T(8,128)S(1)}, f32[128,768]{1,0:T(8,128)}, u32[]{:S(2)}) copy-start(f32[128,768]{1,0:T(8,128)} %copy-done.18) | copy-start | bytes 1179652
  547.2 27.2 %copy-start.46 = (f32[1,768]{1,0:T(1,128)}, f32[1,768]{1,0:T(1,128)S(1)}, u32[]{:S(2)}) copy-start(f32[1,768]{1,0:T(1,128)S(1)} %get-tuple-element.133.refs_4_) | copy-start | bytes 9220
  547.2 94.0 %copy-start.7 = (f32[128,768]{1,0:T(8,128)}, f32[128,768]{1,0:T(8,128)S(1)}, u32[]{:S(2)}) copy-start(f32[128,768]{1,0:T(8,128)S(1)} %get-tuple-element.115.refs_15_.refs_16_.refs_9_) | copy-start | bytes 1179652
  547.2 27.2 %copy-start.17 = (f32[128,768]{1,0:T(8,128)S(1)}, f32[128,768]{1,0:T(8,128)}, u32[]{:S(2)}) copy-start(f32[128,768]{1,0:T(8,128)} %copy-done.16) | copy-start | bytes 1179652
  547.2 27.2 %copy-start.37 = (bf16[192,512]{1,0:T(8,128)(2,1)S(1)}, bf16[192,512]{1,0:T(8,128)(2,1)}, u32[]{:S(2)}) copy-start(bf16[192,512]{1,0:T(8,128)(2,1)} %copy-done.36) | copy-start | bytes 589828
  547.2 27.2 %copy-start.39 = (bf16[192,512]{1,0:T(8,128)(2,1)S(1)}, bf16[192,512]{1,0:T(8,128)(2,1)}, u32[]{:S(2)}) copy-start(bf16[192,512]{1,0:T(8,128)(2,1)} %copy-done.38) | copy-start | bytes 589828
  574.4 35.9 %copy-start.47 = (f32[1,768]{1,0:T(1,128)}, f32[1,768]{1,0:T(1,128)S(1)}, u32[]{:S(2)}) copy-start(f32[1,768]{1,0:T(1,128)S(1)} %get-tuple-element.132.refs_3_) | copy-start | bytes 9220
  574.5 36.8 %copy-start.58 = (s32[67]{0:T(128)S(1)}, s32[67]{0:T(128)}, u32[]{:S(2)}) copy-start(s32[67]{0:T(128)} %copy-done.57) | copy-start | bytes 808
  574.5 37.4 %copy-start.56 = (pred[179]{0:T(512)(128)(4,1)S(1)}, pred[179]{0:T(512)(128)(4,1)}, u32[]{:S(2)}) copy-start(pred[179]{0:T(512)(128)(4,1)} %copy-done.55) | copy-start | bytes 541
  574.5 38.0 %copy-start.15 = (f32[128,768]{1,0:T(8,128)S(1)}, f32[128,768]{1,0:T(8,128)}, u32[]{:S(2)}) copy-start(f32[128,768]{1,0:T(8,128)} %copy-done.14) | copy-start | bytes 1179652
  611.2 29.9 %copy-start.48 = (f32[1,768]{1,0:T(1,128)}, f32[1,768]{1,0:T(1,128)S(1)}, u32[]{:S(2)}) copy-start(f32[1,768]{1,0:T(1,128)S(1)} %get-tuple-element.131.refs_2_) | copy-start | bytes 9220
  611.3 29.9 %copy-start.21 = (f32[128,768]{1,0:T(8,128)}, f32[128,768]{1,0:T(8,128)S(1)}, u32[]{:S(2)}) copy-start(f32[128,768]{1,0:T(8,128)S(1)} %get-tuple-element.128.refs_15_.refs_8_) | copy-start | bytes 1179652
  613.6 27.6 %copy-start.33 = (bf16[192,512]{1,0:T(8,128)(2,1)S(1)}, bf16[192,512]{1,0:T(8,128)(2,1)}, u32[]{:S(2)}) copy-start(bf16[192,512]{1,0:T(8,128)(2,1)} %copy-done.32) | copy-start | bytes 589828
  613.6 27.6 %copy-start.35 = (bf16[192,512]{1,0:T(8,128)(2,1)S(1)}, bf16[192,512]{1,0:T(8,128)(2,1)}, u32[]{:S(2)}) copy-start(bf16[192,512]{1,0:T(8,128)(2,1)} %copy-done.34) | copy-start | bytes 589828
  613.6 27.6 %copy-start.44 = (f32[3,1,512]{2,1,0:T(1,128)S(1)}, f32[3,1,512]{2,1,0:T(1,128)}, u32[]{:S(2)}) copy-start(f32[3,1,512]{2,1,0:T(1,128)} %copy-done.43) | copy-start | bytes 18436
  641.2 26.1 %copy-start.49 = (f32[1,768]{1,0:T(1,128)}, f32[1,768]{1,0:T(1,128)S(1)}, u32[]{:S(2)}) copy-start(f32[1,768]{1,0:T(1,128)S(1)} %get-tuple-element.130.refs_1_) | copy-start | bytes 9220
  667.3 79.2 %copy-start.50 = (f32[1,768]{1,0:T(1,128)}, f32[1,768]{1,0:T(1,128)S(1)}, u32[]{:S(2)}) copy-start(f32[1,768]{1,0:T(1,128)S(1)} %get-tuple-element.129.refs_0_) | copy-start | bytes 9220
  749.1 27.9 %copy-start.59 = (pred[24]{0:T(512)(128)(4,1)S(1)}, pred[24]{0:T(512)(128)(4,1)}, u32[]{:S(2)}) copy-start(pred[24]{0:T(512)(128)(4,1)} %get-tuple-element.172) | copy-start | bytes 76
  777.0 26.0 %copy-start.1 = (bf16[24,48,768]{2,1,0:T(8,128)(2,1)S(1)}, bf16[24,48,768]{2,1,0:T(8,128)(2,1)}, u32[]{:S(2)}) copy-start(bf16[24,48,768]{2,1,0:T(8,128)(2,1)} %all-reduce.8.cloned.1.call-done.rest_4_.rest_5_.rest_6_.rest_7_) | copy-start | bytes 5308420
  803.6 34.5 %copy-start.54 = (f32[5,768]{1,0:T(8,128)S(1)}, f32[5,768]{1,0:T(8,128)}, u32[]{:S(2)}) copy-start(f32[5,768]{1,0:T(8,128)} %get-tuple-element.193) | copy-start | bytes 46084
  803.6 35.1 %copy-start.53 = (f32[5,768]{1,0:T(8,128)S(1)}, f32[5,768]{1,0:T(8,128)}, u32[]{:S(2)}) copy-start(f32[5,768]{1,0:T(8,128)} %get-tuple-element.194) | copy-start | bytes 46084
  803.6 35.7 %copy-start.52 = (f32[5,768]{1,0:T(8,128)S(1)}, f32[5,768]{1,0:T(8,128)}, u32[]{:S(2)}) copy-start(f32[5,768]{1,0:T(8,128)} %get-tuple-element.195) | copy-start | bytes 46084
  803.7 36.3 %copy-start.65 = (f32[1,5]{1,0:T(1,128)S(1)}, f32[1,5]{1,0:T(1,128)}, u32[]{:S(2)}) copy-start(f32[1,5]{1,0:T(1,128)} %get-tuple-element.152) | copy-start | bytes 64
  803.7 36.8 %copy-start.64 = (f32[1,5]{1,0:T(1,128)S(1)}, f32[1,5]{1,0:T(1,128)}, u32[]{:S(2)}) copy-start(f32[1,5]{1,0:T(1,128)} %get-tuple-element.153) | copy-start | bytes 64
  803.7 37.3 %copy-start.63 = (f32[1,5]{1,0:T(1,128)S(1)}, f32[1,5]{1,0:T(1,128)}, u32[]{:S(2)}) copy-start(f32[1,5]{1,0:T(1,128)} %get-tuple-element.154) | copy-start | bytes 64
  803.7 37.8 %copy-start.62 = (f32[1,128]{1,0:T(1,128)S(1)}, f32[1,128]{1,0:T(1,128)}, u32[]{:S(2)}) copy-start(f32[1,128]{1,0:T(1,128)} %get-tuple-element.143.refs_14_) | copy-start | bytes 1540
  (20 other events, 47.9 us)
Sparse Core Ops, SparseCore 0:
  24.0 95.8 all-reduce.5
  611.4 88.4 all-reduce.7

commit v5 on v4

--- a/solution.py
+++ b/solution.py
@@ -114,7 +114,7 @@
         self.operands, self.specs, self.outs, self.scratch = operands, specs, outs, scratch
 
 
-def tensor_step(name, function, work, extras, scalars, outs, gather, collective_id, rider=None):
+def tensor_step(name, function, work, extras, scalars, outs, gather, collective_id, line=None):
     parts = lax.axis_size("tensor")
     share = extras[0].shape[0]
     reduce = work is not None
@@ -129,26 +129,35 @@
         work_refs = take(len(work.operands))
         extra_refs = take(len(extras))
         scalar_refs = take(len(scalars))
-        (rider_ref,) = take(1) if rider is not None else [None]
+        source_refs = take(len(line.operands)) if line else []
         out_refs = take(len(outs))
         (full,) = take(1) if gather else [None]
         work_outs = take(len(work.outs))
-        (joined,) = take(1) if rider is not None else [None]
+        (joined,) = take(1) if line else [None]
         send_sems, recv_sems = take(2)
         partial_ref, outgoing, arrived = take(3) if reduce else [None] * 3
-        own_sem, twin_send, twin_recv = take(3) if rider is not None else [None] * 3
+        if line:
+            line.bind(source_refs, joined, take(len(line.scratch)))
+            line.load()
+
+        def tick(count=1):
+            if line:
+                line.steps(count)
+
         me, side = lax.axis_index("tensor"), lax.axis_index("seq")
         peers = others("tensor")
         twin = {"seq": 1 - side}
-        twins = work.twins or rider is not None
-        meet([{"tensor": peer} for peer in peers] + [twin] * twins)
-        if rider is not None:
-            own_copy = pltpu.make_async_copy(rider_ref, joined.at[:, side], own_sem)
-            own_copy.start()
-            twin_copy = send(rider_ref, joined.at[:, side], twin_send, twin_recv, twin)
+        twins = work.twins or (line and line.share)
+        meet(
+            [{"tensor": peer} for peer in peers]
+            + [twin] * bool(twins)
+            + ([{"dp": peer} for peer in others("dp")] if line else [])
+        )
+        if line:
+            line.begin()
         total = None
         if reduce:
-            work.before(work_refs, work_outs, refs, partial_ref)
+            work.before(work_refs, work_outs, refs, partial_ref, tick)
             copies = []
             for step, peer in enumerate(peers):
                 rows = pl.ds(pl.multiple_of(peer * share, share), share)
@@ -164,6 +173,7 @@
                 )
             if work.during:
                 work.during(work_refs, work_outs, refs)
+            tick(4)
             total = partial_ref[pl.ds(pl.multiple_of(me * share, share), share), :]
             for step, copy in enumerate(copies):
                 copy.wait()
@@ -185,15 +195,14 @@
             ]
         if work.after:
             work.after(work_refs, work_outs, refs)
-        if rider is not None:
-            own_copy.wait()
-            twin_copy.wait()
+        tick(None)
         if gather:
             for copy in copies:
                 copy.wait()
+        if line:
+            line.end()
 
     vmem = pl.BlockSpec(memory_space=pltpu.VMEM)
-    anywhere = pl.BlockSpec(memory_space=pl.ANY)
     smem = pl.BlockSpec(memory_space=pltpu.SMEM)
     shapes = [jax.ShapeDtypeStruct(shape, dtype) for shape, dtype in outs]
     if gather:
@@ -207,13 +216,12 @@
     if reduce:
         buffers += [pltpu.VMEM((parts * share, D), jnp.float32)]
         buffers += [pltpu.VMEM((parts - 1, share, D), jnp.bfloat16)] * 2
-    if rider is not None:
-        operands.append(rider)
-        in_specs.append(anywhere)
-        count, half_rows, _ = rider.shape
-        shapes.append(jax.ShapeDtypeStruct((count, 2, half_rows, D), jnp.bfloat16))
-        out_specs.append(anywhere)
-        buffers += [dma] * 3
+    if line:
+        operands += line.operands
+        in_specs += line.in_specs
+        shapes.append(line.out_shape)
+        out_specs.append(line.out_spec)
+        buffers += line.scratch
     return pl.pallas_call(
         kernel,
         name=name,
@@ -267,7 +275,7 @@
     width = D // parts
     heads = width // HEAD_DIM
 
-    def before(ins, outs, scratch, partial_ref):
+    def before(ins, outs, scratch, partial_ref, tick):
         normed_ref, qkv_ref, out_ref, cosine_ref, sine_ref = ins
         queries_ref, both, logs_ref, attended_ref = outs
         send_sem, recv_sem = scratch
@@ -308,6 +316,7 @@
             attended = times(both[0, 1, span, :], (far * inverse).astype(jnp.bfloat16))
             attended += times(both[1, 1, span, :], (own * inverse).astype(jnp.bfloat16))
             attended_ref[span, :] = attended.astype(jnp.bfloat16)
+            tick()
         partial_ref[...] = contract_first(attended_ref[...], out_ref[...])
 
     low = jnp.bfloat16
@@ -327,43 +336,41 @@
     )
 
 
-def attention_back_work(grad, normed, table, kept, cosine, sine, unit_grads):
+def fold_copy(own, near, send_sems, recv_sems, index):
+    side = lax.axis_index("seq")
+    return pltpu.make_async_remote_copy(
+        src_ref=own.at[index, :, 1 - side],
+        dst_ref=near.at[index],
+        send_sem=send_sems.at[index],
+        recv_sem=recv_sems.at[index],
+        device_id={"seq": 1 - side},
+        device_id_type=MESH,
+    )
+
+
+def add_halves(own, near, out, start):
+    side = lax.axis_index("seq")
+
+    def one(block, carry):
+        value = own[block, side].astype(jnp.float32) + near[block].astype(jnp.float32)
+        out[start + block] = value.astype(jnp.bfloat16)
+        return carry
+
+    lax.fori_loop(0, near.shape[0], one, 0)
+
+
+def attention_back_work(grad, normed, table, kept, cosine, sine, half_rows):
     parts, share, _ = normed.shape
     count = parts * share
     width = D // parts
     heads = width // HEAD_DIM
     queries, both, logs, attended = kept
-    half_rows = unit_grads[0].shape[2]
-    joined_blocks, out_blocks = 3 * width // (2 * half_rows), width // (2 * half_rows)
-    unit_blocks = unit_grads[0].shape[0]
-    starts = [0, joined_blocks, joined_blocks + out_blocks, joined_blocks + out_blocks + unit_blocks]
-    sizes = [joined_blocks, out_blocks, unit_blocks, unit_blocks]
-    blocks = sum(sizes)
-
-    def twin_copy(source, target, send_sem, recv_sem):
-        return pltpu.make_async_remote_copy(
-            src_ref=source,
-            dst_ref=target,
-            send_sem=send_sem,
-            recv_sem=recv_sem,
-            device_id={"seq": 1 - lax.axis_index("seq")},
-            device_id_type=MESH,
-        )
-
-    def fold_copy(index, source, refs):
-        near, fold_send, fold_recv = refs
-        side = lax.axis_index("seq")
-        rows = pl.ds(starts[index], sizes[index])
-        return twin_copy(
-            source.at[:, 1 - side], near.at[rows], fold_send.at[index], fold_recv.at[index]
-        )
-
-    def before(ins, outs, scratch, partial_ref):
-        grad_ref, _, qkv_ref, out_ref, queries_ref, both, logs_ref, _, cosine_ref, sine_ref = ins[:10]
+    blocks = 4 * width // (2 * half_rows)
+
+    def before(ins, outs, scratch, partial_ref, tick):
+        grad_ref, _, qkv_ref, out_ref, queries_ref, both, logs_ref, _, cosine_ref, sine_ref = ins
         back, came, grad_joined, send_sem, recv_sem = scratch[:5]
         side = lax.axis_index("seq")
-        for index, source in zip((2, 3), ins[10:]):
-            fold_copy(index, source, scratch[7:]).start()
         cosine, sine = cosine_ref[...], -sine_ref[...]
         scale = HEAD_DIM ** (-0.5)
         grads = contract_last(out_ref[...], grad_ref[...].reshape(count, D)).astype(jnp.bfloat16)
@@ -387,8 +394,8 @@
             own_grads.append(
                 (contract_last(head_queries, own_grad) * scale, contract_last(head_grads, own))
             )
-        copy = twin_copy(back, came, send_sem, recv_sem)
-        copy.start()
+            tick()
+        copy = send(back, came, send_sem, recv_sem, {"seq": 1 - side})
         copy.wait()
         for head, (key_grad, value_grad) in enumerate(own_grads):
             span = slice(head * HEAD_DIM, (head + 1) * HEAD_DIM)
@@ -404,38 +411,27 @@
 
     def during(ins, outs, scratch):
         grad_ref, normed_ref, attended_ref = ins[0], ins[1], ins[7]
-        grad_joined, joined_part, out_part = scratch[2], scratch[5], scratch[6]
-        value = times(grad_joined[...], normed_ref[...].reshape(count, D))
-        joined_part[...] = value.astype(jnp.bfloat16).reshape(joined_part.shape)
-        fold_copy(0, joined_part, scratch[7:]).start()
-        value = times(attended_ref[...], grad_ref[...].reshape(count, D))
-        out_part[...] = value.astype(jnp.bfloat16).reshape(out_part.shape)
-        fold_copy(1, out_part, scratch[7:]).start()
+        grad_joined = scratch[2]
+        own, near, fold_send, fold_recv = scratch[5:]
+        value = times(grad_joined[...], normed_ref[...].reshape(count, D)).astype(jnp.bfloat16)
+        part = 3 * blocks // 4
+        own[0, :part] = value.reshape(part, 2, half_rows, D)
+        value = times(attended_ref[...], grad_ref[...].reshape(count, D)).astype(jnp.bfloat16)
+        own[0, part:] = value.reshape(blocks - part, 2, half_rows, D)
+        fold_copy(own, near, fold_send, fold_recv, 0).start()
 
     def after(ins, outs, scratch):
-        side = lax.axis_index("seq")
-        (folded,) = outs
-        near = scratch[7]
-        sources = [scratch[5], scratch[6], ins[10], ins[11]]
-        for index in (2, 3, 0, 1):
-            source, start = sources[index], starts[index]
-            fold_copy(index, source, scratch[7:]).wait()
-
-            def add_block(block, carry):
-                value = source[block, side].astype(jnp.float32)
-                value = value + near[start + block].astype(jnp.float32)
-                folded[start + block] = value.astype(jnp.bfloat16)
-                return carry
-
-            lax.fori_loop(0, sizes[index], add_block, 0)
+        own, near, fold_send, fold_recv = scratch[5:]
+        fold_copy(own, near, fold_send, fold_recv, 0).wait()
+        add_halves(own.at[0], near.at[0], outs[0], 0)
 
     low = jnp.bfloat16
     dma = pltpu.SemaphoreType.DMA
     return Work(
         before,
         during,
-        [grad, normed, table, table, queries, both, logs, attended, cosine, sine] + list(unit_grads),
-        [VMEM_SPEC, VMEM_SPEC, part_spec(3 * width, 0), part_spec(width, 3)] + [VMEM_SPEC] * 8,
+        [grad, normed, table, table, queries, both, logs, attended, cosine, sine],
+        [VMEM_SPEC, VMEM_SPEC, part_spec(3 * width, 0), part_spec(width, 3)] + [VMEM_SPEC] * 6,
         [((blocks, half_rows, D), low)],
         [
             pltpu.VMEM((2, width, count), low),
@@ -443,11 +439,10 @@
             pltpu.VMEM((3 * width, count), low),
             dma,
             dma,
-            pltpu.VMEM((joined_blocks, 2, half_rows, D), low),
-            pltpu.VMEM((out_blocks, 2, half_rows, D), low),
-            pltpu.VMEM((blocks, half_rows, D), low),
-            dma((4,)),
-            dma((4,)),
+            pltpu.VMEM((1, blocks, 2, half_rows, D), low),
+            pltpu.VMEM((1, blocks, half_rows, D), low),
+            dma((1,)),
+            dma((1,)),
         ],
         after,
         True,
@@ -458,60 +453,79 @@
     return jax.nn.gelu(hidden, approximate=True)
 
 
-def unit_work(normed, table):
+def unit_work(normed, up, down):
     parts, share, _ = normed.shape
     count = parts * share
     units = FF // parts
 
-    def before(ins, outs, scratch, partial_ref):
+    def before(ins, outs, scratch, partial_ref, tick):
         normed_ref, up_ref, down_ref = ins
         hidden_ref, activated_ref = outs
         hidden = contract_last(up_ref[...], normed_ref[...].reshape(count, D))
         hidden_ref[...] = hidden
         activated_ref[...] = gelu(hidden).astype(jnp.bfloat16)
+        tick(2)
         partial_ref[...] = contract_first(activated_ref[...], down_ref[...])
 
     return Work(
         before,
         None,
-        [normed, table, table],
-        [VMEM_SPEC, part_spec(units, 1), part_spec(units, 2)],
+        [normed, up[0], down[0]],
+        [VMEM_SPEC, part_spec(units, up[1]), part_spec(units, down[1])],
         [((units, count), jnp.float32), ((units, count), jnp.bfloat16)],
         [],
     )
 
 
-def unit_back_work(grad, normed, table, kept, half_rows):
+def unit_back_work(grad, normed, up, down, kept, half_rows):
     parts, share, _ = normed.shape
     count = parts * share
     units = FF // parts
     hidden, activated = kept
-
-    def before(ins, outs, scratch, partial_ref):
+    blocks = units // (2 * half_rows)
+
+    def before(ins, outs, scratch, partial_ref, tick):
         grad_ref, _, up_ref, down_ref, hidden_ref, _ = ins
-        (grad_hidden,) = scratch
+        grad_hidden = scratch[0]
         grad_act = contract_last(down_ref[...], grad_ref[...].reshape(count, D))
         _, pull = jax.vjp(gelu, hidden_ref[...])
         grad_hidden[...] = pull(grad_act)[0].astype(jnp.bfloat16)
+        tick(2)
         partial_ref[...] = contract_first(grad_hidden[...], up_ref[...])
 
     def during(ins, outs, scratch):
         grad_ref, normed_ref, _, _, _, activated_ref = ins
-        up_grad, down_grad = outs
-        (grad_hidden,) = scratch
+        grad_hidden, own, near, fold_send, fold_recv = scratch
         value = times(grad_hidden[...], normed_ref[...].reshape(count, D))
-        up_grad[...] = value.astype(jnp.bfloat16).reshape(up_grad.shape)
+        own[0] = value.astype(jnp.bfloat16).reshape(own.shape[1:])
+        fold_copy(own, near, fold_send, fold_recv, 0).start()
         value = times(activated_ref[...], grad_ref[...].reshape(count, D))
-        down_grad[...] = value.astype(jnp.bfloat16).reshape(down_grad.shape)
-
-    grads = ((units // (2 * half_rows), 2, half_rows, D), jnp.bfloat16)
+        own[1] = value.astype(jnp.bfloat16).reshape(own.shape[1:])
+        fold_copy(own, near, fold_send, fold_recv, 1).start()
+
+    def after(ins, outs, scratch):
+        _, own, near, fold_send, fold_recv = scratch
+        for index in range(2):
+            fold_copy(own, near, fold_send, fold_recv, index).wait()
+            add_halves(own.at[index], near.at[index], outs[0], index * blocks)
+
+    low, dma = jnp.bfloat16, pltpu.SemaphoreType.DMA
     return Work(
         before,
         during,
-        [grad, normed, table, table, hidden, activated],
-        [VMEM_SPEC, VMEM_SPEC, part_spec(units, 1), part_spec(units, 2), VMEM_SPEC, VMEM_SPEC],
-        [grads, grads],
-        [pltpu.VMEM((units, count), jnp.bfloat16)],
+        [grad, normed, up[0], down[0], hidden, activated],
+        [VMEM_SPEC, VMEM_SPEC, part_spec(units, up[1]), part_spec(units, down[1])]
+        + [VMEM_SPEC] * 2,
+        [((2 * blocks, half_rows, D), low)],
+        [
+            pltpu.VMEM((units, count), low),
+            pltpu.VMEM((2, blocks, 2, half_rows, D), low),
+            pltpu.VMEM((2, blocks, half_rows, D), low),
+            dma((2,)),
+            dma((2,)),
+        ],
+        after,
+        True,
     )
 
 
@@ -520,30 +534,33 @@
 
 
 class Line:
-    def __init__(self, rider, share):
+    def __init__(self, sources, share):
         self.groups = lax.axis_size("dp")
-        self.half = rider.shape
-        self.chunks = rider.shape[0] // LINE_BLOCKS
-        self.share = share
-        count, half_rows, _ = rider.shape
+        self.sources, self.share = sources, share
+        count = sum(size for _, _, size in sources)
+        _, half_rows, _ = sources[0][0].shape
+        self.half = (count, half_rows, D)
+        self.chunks = count // LINE_BLOCKS
+        self.operands = [array for array, _, _ in sources]
+        self.in_specs = [pl.BlockSpec(memory_space=pl.ANY)] * len(sources)
         dma = pltpu.SemaphoreType.DMA
-        out = (count, 2, half_rows, D) if share else rider.shape
+        out = (count, 2, half_rows, D) if share else self.half
         self.out_shape = jax.ShapeDtypeStruct(out, jnp.bfloat16)
         self.out_spec = pl.BlockSpec(memory_space=pl.ANY if share else pltpu.VMEM)
         self.scratch = [
             pltpu.VMEM(self.half, jnp.bfloat16),
             pltpu.VMEM((2,) + self.half, jnp.bfloat16),
             pltpu.VMEM((2,) + self.half, jnp.bfloat16),
-            dma,
+            dma((len(sources),)),
             dma((2, self.chunks)),
             dma((2, self.chunks)),
         ]
         if share:
             self.scratch += [pltpu.VMEM(self.half, jnp.bfloat16)] + [dma((self.chunks,))] * 3
 
-    def bind(self, rider_ref, out_ref, refs):
-        self.rider, self.out = rider_ref, out_ref
-        self.own, self.came, self.going, self.own_sem, self.send_sems, self.recv_sems = refs[:6]
+    def bind(self, source_refs, out_ref, refs):
+        self.source_refs, self.out = source_refs, out_ref
+        self.own, self.came, self.going, self.own_sems, self.send_sems, self.recv_sems = refs[:6]
         self.total = out_ref
         if self.share:
             self.total, self.keep_sems, self.twin_send, self.twin_recv = refs[6:]
@@ -571,10 +588,19 @@
             device_id_type=MESH,
         )
 
+    def load(self):
+        self.loads, place = [], 0
+        for index, (ref, (_, start, size)) in enumerate(zip(self.source_refs, self.sources)):
+            copy = pltpu.make_async_copy(
+                ref.at[pl.ds(start, size)], self.own.at[pl.ds(place, size)], self.own_sems.at[index]
+            )
+            copy.start()
+            self.loads.append(copy)
+            place += size
+
     def begin(self):
-        copy = pltpu.make_async_copy(self.rider, self.own, self.own_sem)
-        copy.start()
-        copy.wait()
+        for copy in self.loads:
+            copy.wait()
         for way in range(2):
 
             @pl.when(jnp.logical_not(self.comes(way)))
@@ -639,7 +665,8 @@
                 self.twin_copy(chunk).start()
 
     def steps(self, count=None):
-        stop = self.chunks + LINE_LAG if count is None else self.done + count
+        last = self.chunks + LINE_LAG
+        stop = last if count is None else min(self.done + count, last)
 
         def one(index, carry):
             self.step(index)
@@ -664,22 +691,23 @@
         lax.fori_loop(0, self.chunks, one, 0)
 
 
-def reduce_all(terms, collective_id, rider=None):
+def reduce_all(terms, collective_id, line=None):
     _, tensors, groups, count, _ = terms.shape
-    line = None if rider is None else Line(rider, True)
+    half = count // 2
 
     def kernel(*refs):
         refs = list(refs)
         terms_ref = refs.pop(0)
-        rider_ref = refs.pop(0) if line else None
+        source_refs = [refs.pop(0) for _ in line.operands] if line else []
         out_ref = refs.pop(0)
         joined_ref = refs.pop(0) if line else None
         (
-            near, own, mid, mid_in, far, far_in,
+            near, own, mid, sums, mid_in, far, far_in,
             own_sems, near_send, near_recv, mid_send, mid_recv, far_send, far_recv,
-        ) = refs[:13]
+        ) = refs[:14]
         if line:
-            line.bind(rider_ref, joined_ref, refs[13:])
+            line.bind(source_refs, joined_ref, refs[14:])
+            line.load()
         group, part, side = lax.axis_index("dp"), lax.axis_index("tensor"), lax.axis_index("seq")
         twin = 1 - side
         parts = others("tensor")
@@ -707,7 +735,21 @@
             own_copies.append(copy)
         if line:
             line.begin()
-        mid_copies = []
+        beside = lax.rem(part + 1, 2) + part - lax.rem(part, 2)
+        across = lax.rem(part + 2, 4)
+        corner = 3 - part
+        upper, lower = pl.ds(0, half), pl.ds(half, half)
+        first_copies, second_copies = [], []
+
+        def hand(place, index, source, target):
+            return send(
+                source,
+                mid_in.at[place, index],
+                mid_send.at[place, index],
+                mid_recv.at[place, index],
+                {"tensor": target},
+            )
+
         for place in range(groups):
             near_copies[place].wait_recv()
             own_copies[place].wait()
@@ -717,26 +759,38 @@
                 mid[place, slot] = (
                     own[place, slot].astype(jnp.float32) + near[place, slot].astype(jnp.float32)
                 ).astype(jnp.bfloat16)
-            mid_copies.append(
+            first_copies.append(
                 [
-                    send(
-                        mid.at[place, peer],
-                        mid_in.at[place, step],
-                        mid_send.at[place, step],
-                        mid_recv.at[place, step],
-                        {"tensor": peer},
-                    )
-                    for step, peer in enumerate(parts)
+                    hand(place, 0, mid.at[place, corner, upper], beside),
+                    hand(place, 1, mid.at[place, corner, lower], across),
+                    hand(place, 2, mid.at[place, beside, upper], beside),
+                    hand(place, 3, mid.at[place, across, lower], across),
                 ]
             )
+        for place in range(groups):
+            if line and place < 4:
+                line.steps(1)
+            copies = []
+            for index, slot, rows, target in ((0, across, upper, across), (1, beside, lower, beside)):
+                first_copies[place][index].wait_recv()
+                value = mid[place, slot, rows].astype(jnp.float32)
+                value = value + mid_in[place, index].astype(jnp.float32)
+                sums[place, index] = value.astype(jnp.bfloat16)
+                copies.append(hand(place, 4 + index, sums.at[place, index], target))
+            second_copies.append(copies)
         far_copies = []
         for place, target in enumerate(order):
             if line and place < 4:
-                line.steps(2)
-            total = mid[place, part].astype(jnp.float32)
-            for step in range(tensors - 1):
-                mid_copies[place][step].wait_recv()
-                total = total + mid_in[place, step].astype(jnp.float32)
+                line.steps(1)
+            copies = first_copies[place][2:] + second_copies[place]
+            for copy in copies:
+                copy.wait_recv()
+
+            def joined(index):
+                return mid_in[place, index].astype(jnp.float32)
+
+            halves = [joined(2) + joined(4), joined(3) + joined(5)]
+            total = mid[place, part].astype(jnp.float32) + jnp.concatenate(halves, axis=0)
             if place < groups - 1:
                 far[place] = total.astype(jnp.bfloat16)
                 far_copies.append(
@@ -754,7 +808,9 @@
             copy.wait_recv()
             total = total + far_in[place].astype(jnp.float32)
         out_ref[...] = total
-        for copy in near_copies + far_copies + [c for row in mid_copies for c in row]:
+        for copy in near_copies + far_copies + [
+            copy for row in first_copies + second_copies for copy in row
+        ]:
             copy.wait_send()
         if line:
             line.end()
@@ -765,18 +821,19 @@
         kernel,
         name="reduce_all",
         out_shape=[jax.ShapeDtypeStruct(block, jnp.float32)] + ([line.out_shape] if line else []),
-        in_specs=[pl.BlockSpec(memory_space=pl.ANY)] * (2 if line else 1),
+        in_specs=[pl.BlockSpec(memory_space=pl.ANY)] + (line.in_specs if line else []),
         out_specs=[pl.BlockSpec(memory_space=pltpu.VMEM)] + ([line.out_spec] if line else []),
         scratch_shapes=[pltpu.VMEM((groups, tensors) + block, jnp.bfloat16)] * 3
         + [
-            pltpu.VMEM((groups, tensors - 1) + block, jnp.bfloat16),
+            pltpu.VMEM((groups, 2, half, D), jnp.bfloat16),
+            pltpu.VMEM((groups, 6, half, D), jnp.bfloat16),
             pltpu.VMEM((groups,) + block, jnp.bfloat16),
             pltpu.VMEM((groups,) + block, jnp.bfloat16),
             dma((groups,)),
             dma((groups,)),
             dma((groups,)),
-            dma((groups, tensors - 1)),
-            dma((groups, tensors - 1)),
+            dma((groups, 6)),
+            dma((groups, 6)),
             dma((groups,)),
             dma((groups,)),
         ]
@@ -785,28 +842,28 @@
         compiler_params=pltpu.CompilerParams(
             collective_id=collective_id, has_side_effects=True, vmem_limit_bytes=56 << 20
         ),
-    )(terms, *([rider] if line else []))
-
-
-def gather_all(block, collective_id, rider=None):
+    )(terms, *(line.operands if line else []))
+
+
+def gather_all(block, collective_id, line=None):
     tensors, groups = lax.axis_size("tensor"), lax.axis_size("dp")
-    line = None if rider is None else Line(rider, False)
+    half = block.shape[0] // 2
 
     def kernel(*refs):
         refs = list(refs)
         block_ref = refs.pop(0)
-        rider_ref = refs.pop(0) if line else None
+        source_refs = [refs.pop(0) for _ in line.operands] if line else []
         out = refs.pop(0)
         summed_ref = refs.pop(0) if line else None
         own_sem, far_send, far_recv, mid_send, mid_recv, near_send, near_recv = refs[:7]
         if line:
-            line.bind(rider_ref, summed_ref, refs[7:])
+            line.bind(source_refs, summed_ref, refs[7:])
+            line.load()
         group, part, side = lax.axis_index("dp"), lax.axis_index("tensor"), lax.axis_index("seq")
         twin = 1 - side
-        parts = others("tensor")
         meet(
             [{"seq": twin}]
-            + [{"tensor": peer} for peer in parts]
+            + [{"tensor": peer} for peer in others("tensor")]
             + [{"dp": peer} for peer in others("dp")]
         )
         far_copies = [
@@ -821,33 +878,64 @@
         ]
         own = pltpu.make_async_copy(block_ref, out.at[side, part, group], own_sem)
         own.start()
-        own.wait()
         if line:
             line.begin()
-        mid_copies, near_copies = [], []
+        beside = lax.rem(part + 1, 2) + part - lax.rem(part, 2)
+        across = lax.rem(part + 2, 4)
+        corner = 3 - part
+        upper, lower = pl.ds(0, half), pl.ds(half, half)
+        first_copies, second_copies, near_copies = [], [], []
         for place in range(groups):
-            if line and 0 < place < 4:
-                line.steps(1)
             source = behind("dp", place)
             if place:
+                if line and place < 4:
+                    line.steps(1)
                 far_copies[place - 1].wait_recv()
-            held = out.at[side, part, source]
-            mid_copies.append(
-                [
-                    send(held, held, mid_send.at[place, step], mid_recv.at[place, step], {"tensor": peer})
-                    for step, peer in enumerate(parts)
-                ]
+            held = out.at[side, part, source] if place else block_ref
+
+            def hand(index, piece, slot, rows, target):
+                return send(
+                    piece,
+                    out.at[side, slot, source, rows],
+                    mid_send.at[place, index],
+                    mid_recv.at[place, index],
+                    {"tensor": target},
+                )
+
+            first = [
+                hand(0, held.at[upper], part, upper, beside),
+                hand(1, held.at[lower], part, lower, across),
+                hand(2, held.at[lower], part, lower, beside),
+                hand(3, held.at[upper], part, upper, across),
+            ]
+            near_copies.append(
+                send(
+                    held,
+                    out.at[side, part, source],
+                    near_send.at[place, 0],
+                    near_recv.at[place, 0],
+                    {"seq": twin},
+                )
             )
-            near_copies.append(
-                send(held, held, near_send.at[place, 0], near_recv.at[place, 0], {"seq": twin})
-            )
+            first[0].wait_recv()
+            second = [hand(4, out.at[side, beside, source, upper], beside, upper, across)]
+            first[1].wait_recv()
+            second.append(hand(5, out.at[side, across, source, lower], across, lower, beside))
+            first_copies.append(first)
+            second_copies.append(second)
         for place in range(groups):
             if line and place < 4:
                 line.steps(2)
             source = behind("dp", place)
-            for step in range(tensors - 1):
-                mid_copies[place][step].wait_recv()
-                held = out.at[side, behind("tensor", step + 1), source]
+            ready = [
+                (beside, first_copies[place][2:3]),
+                (across, first_copies[place][3:4]),
+                (corner, second_copies[place]),
+            ]
+            for step, (slot, copies) in enumerate(ready):
+                for copy in copies:
+                    copy.wait_recv()
+                held = out.at[side, slot, source]
                 near_copies.append(
                     send(
                         held,
@@ -861,8 +949,11 @@
             line.steps()
         for copy in near_copies:
             copy.wait_recv()
-        for copy in near_copies + far_copies + [c for row in mid_copies for c in row]:
+        for copy in near_copies + far_copies + [
+            copy for row in first_copies + second_copies for copy in row
+        ]:
             copy.wait_send()
+        own.wait()
         if line:
             line.end()
 
@@ -873,14 +964,14 @@
         name="gather_all",
         out_shape=[jax.ShapeDtypeStruct((2, tensors, groups) + block.shape, block.dtype)]
         + ([line.out_shape] if line else []),
-        in_specs=[anywhere] * (2 if line else 1),
+        in_specs=[VMEM_SPEC] + (line.in_specs if line else []),
         out_specs=[anywhere] + ([line.out_spec] if line else []),
         scratch_shapes=[
             dma,
             dma((groups - 1,)),
             dma((groups - 1,)),
-            dma((groups, tensors - 1)),
-            dma((groups, tensors - 1)),
+            dma((groups, 6)),
+            dma((groups, 6)),
             dma((groups, tensors)),
             dma((groups, tensors)),
         ]
@@ -889,18 +980,18 @@
         compiler_params=pltpu.CompilerParams(
             collective_id=collective_id, has_side_effects=True, vmem_limit_bytes=40 << 20
         ),
-    )(block, *([rider] if line else []))
-
-
-def reduce_rows(terms, ids, rider=None):
+    )(block, *(line.operands if line else []))
+
+
+def reduce_rows(terms, ids, line=None):
     count, groups = terms.shape[3], terms.shape[2]
     pieces = max(1, groups // 4)
     part = count // pieces
     sums, joined = [], None
     for i in range(pieces):
         piece = terms[:, :, :, i * part : (i + 1) * part] if pieces > 1 else terms
-        if i == 0 and rider is not None:
-            total, joined = reduce_all(piece, ids[1], rider)
+        if i == 0 and line:
+            total, joined = reduce_all(piece, ids[1], line)
         else:
             (total,) = reduce_all(piece, ids[0])
         sums.append(total)
@@ -1178,14 +1269,12 @@
     plan = jnp.pad(plan, ((0, 0), (0, steps * SLOT_STEP - slots)))
 
     def kernel(plan_ref, factor_ref, master_ref, first_ref, second_ref, *rest):
-        layer_refs = rest[: LAYERS * SLOT_STEP]
-        table_ref, new_master, new_first, new_second = rest[LAYERS * SLOT_STEP :]
+        layer_refs = rest[:SLOT_STEP]
+        table_ref, new_master, new_first, new_second = rest[SLOT_STEP:]
         for place in range(SLOT_STEP):
             kind = plan_ref[0, pl.program_id(0) * SLOT_STEP + place]
             grad = table_ref[place * half_rows : (place + 1) * half_rows, :]
-            for level in range(LAYERS):
-                layer = layer_refs[level * SLOT_STEP + place][0].astype(jnp.float32)
-                grad = jnp.where(kind == level, layer, grad)
+            grad = jnp.where(kind == 0, layer_refs[place][0].astype(jnp.float32), grad)
             grad = jnp.where(kind >= 0, grad * factor_ref[0:1, 0:1], 0.0)
             values = adam_update(
                 master_ref[place],
@@ -1209,13 +1298,8 @@
             + [
                 pl.BlockSpec(
                     (1, half_rows, D),
-                    lambda step, plan, level=level, place=place: (
-                        plan[1 + level, step * SLOT_STEP + place],
-                        0,
-                        0,
-                    ),
+                    lambda step, plan, place=place: (plan[1, step * SLOT_STEP + place], 0, 0),
                 )
-                for level in range(LAYERS)
                 for place in range(SLOT_STEP)
             ]
             + [pl.BlockSpec((SLOT_STEP * half_rows, D), lambda step, plan: (step, 0))],
@@ -1230,7 +1314,7 @@
         master,
         first,
         second,
-        *[grads for grads in layer_grads for _ in range(SLOT_STEP)],
+        *[layer_grads] * SLOT_STEP,
         grad_table,
     )
 
@@ -1511,12 +1595,10 @@
     held = jnp.sum(jnp.where(mine, 1, 0)) * half_rows
     first_held = jnp.sum(jnp.where(mine & (block_ids < blocks), 1, 0)) * half_rows
     span = jnp.stack([first_held, held]).astype(jnp.int32)
-    level_of = jnp.where(slot_block < 0, -1, jnp.minimum(slot_block // layer_blocks, LAYERS))
     plan = jnp.stack(
-        [level_of]
-        + [
-            jnp.where(level_of == level, slot_block - level * layer_blocks, 0)
-            for level in range(LAYERS)
+        [
+            jnp.where(slot_block < 0, -1, jnp.where(slot_block < blocks, 0, 1)),
+            jnp.where(slot_block < blocks, jnp.maximum(slot_block, 0), 0),
         ]
     ).astype(jnp.int32)
 
@@ -1537,8 +1619,13 @@
     halves = jnp.where(
         mine[:blocks][:, None, None], jnp.take(table_slots, slot_rank[:blocks], axis=0), 0.0
     ).astype(jnp.bfloat16)
-    halves = [halves[i * layer_blocks : (i + 1) * layer_blocks] for i in range(LAYERS)]
-    halves[1:] = [lax.psum(half, "dp") for half in halves[1:]]
+    third = layer_blocks // 3
+
+    def weights_line(start, size):
+        return Line([(halves, start * third, size * third)], True)
+
+    def as_table(joined):
+        return joined.reshape(-1, D)
 
     positions = seq_part * half_len + jnp.arange(row_count) % half_len
     steps_half = jnp.arange(HEAD_DIM // 2).astype(jnp.float32)
@@ -1547,8 +1634,10 @@
     cosine, sine = jnp.cos(angles), jnp.sin(angles)
 
     looked = look_up(span, row_ids, ids_all, table).reshape(order + (D,))
-    start, joined = reduce_rows(looked, (0, 14), halves[0])
-    tables = [joined.reshape(layer_rows, D)]
+    start, joined = reduce_rows(looked, (0, 14), weights_line(0, 2))
+    table_one = as_table(joined)
+    attention_table, up = table_one, (table_one, 1)
+    tables = []
     gain = [gains[i : i + 1] for i in range(2 * LAYERS + 1)]
     piece = ((share, D), jnp.float32)
 
@@ -1570,29 +1659,39 @@
     (normed,) = tensor_step("normed", normed_of, None, (start, gain[0]), (), [], True, 1)
     states, streams, inners, kept_all = [start], [start], [], []
     for level in range(LAYERS):
-        inner, normed_two, *kept = tensor_step(
+        here = 3 * level
+        inner, normed_two, queries, both, logs, attended, joined = tensor_step(
             f"inner_{level}",
             inner_of,
-            attention_work(normed, tables[level], cosine, sine),
+            attention_work(normed, attention_table, cosine, sine),
             (streams[level], gain[2 * level + 1]),
             (),
             [piece],
             True,
             2 if level == 0 else 15 + level,
+            weights_line(here + 1, 2) if level else weights_line(here + 2, 1),
         )
+        kept = (queries, both, logs, attended)
+        joined = as_table(joined)
+        if level:
+            up, down = (joined, 0), (joined, 1)
+        else:
+            down = (joined, 0)
+        tables.append((attention_table, up, down))
         last = level == LAYERS - 1
         outcome, stream, normed_next, hidden, activated, *joined = tensor_step(
             f"outcome_{level}",
             partial(outcome_of, (level + 1) * (level + 2) // 2 - 1),
-            unit_work(normed_two, tables[level]),
+            unit_work(normed_two, up, down),
             [inner, gain[2 * level + 2]] + states,
             (mix,),
             [piece, piece] + ([((share, D), jnp.bfloat16)] if last else []),
             not last,
             3 + level,
-            None if last else halves[level + 1],
+            None if last else weights_line(here + 3, 1),
         )
-        tables += [table_next.reshape(layer_rows, D) for table_next in joined]
+        if not last:
+            attention_table = as_table(joined[0])
         inners.append(inner)
         kept_all.append((normed, kept, normed_two, (hidden, activated)))
         states.append(outcome)
@@ -1641,7 +1740,7 @@
 
     grad_ys = [None] * (LAYERS + 1)
     gain_grads = [None] * (2 * LAYERS + 1)
-    layer_grads = [None] * LAYERS
+    layer_grads, attention_grads = [None] * (3 * LAYERS), None
     grad_ys[LAYERS], grad_state, gain_grads[2 * LAYERS], grad_branch = tensor_step(
         "top_back",
         top_of,
@@ -1654,38 +1753,47 @@
     )
     for level in reversed(range(LAYERS)):
         normed, kept, normed_two, unit_kept = kept_all[level]
-        grad_inner, gain_grads[2 * level + 1], grad_attn, *unit_grads = tensor_step(
+        attention_table, up, down = tables[level]
+        grad_inner, gain_grads[2 * level + 1], grad_attn, unit_grads, *summed = tensor_step(
             f"inner_back_{level}",
             inner_back,
-            unit_back_work(grad_branch, normed_two, tables[level], unit_kept, half_rows),
+            unit_back_work(grad_branch, normed_two, up, down, unit_kept, half_rows),
             (grad_state, inners[level], gain[2 * level + 1]),
             (),
             [piece, row],
             True,
             6 + LAYERS if level == 0 else 19 + level,
+            None if attention_grads is None else Line([(attention_grads, 0, third)], False),
         )
-        grad_ys[level], grad_state, gain_grads[2 * level], grad_branch, folded = tensor_step(
-            f"stream_back_{level}",
-            partial(stream_back, level),
-            attention_back_work(
-                grad_attn, normed, tables[level], kept, cosine, sine, unit_grads
-            ),
-            [grad_inner, streams[level], gain[2 * level]] + grad_ys[level + 1 :],
-            (mix,),
-            [piece, piece, row] + ([] if level else [((share, D), jnp.bfloat16)]),
-            level > 0,
-            7 + LAYERS + level,
+        if summed:
+            layer_grads[3 * (level + 1)] = summed[0]
+        carried = 1 if level == 0 else 2
+        grad_ys[level], grad_state, gain_grads[2 * level], grad_branch, attention_grads, summed = (
+            tensor_step(
+                f"stream_back_{level}",
+                partial(stream_back, level),
+                attention_back_work(
+                    grad_attn, normed, attention_table, kept, cosine, sine, half_rows
+                ),
+                [grad_inner, streams[level], gain[2 * level]] + grad_ys[level + 1 :],
+                (mix,),
+                [piece, piece, row] + ([] if level else [((share, D), jnp.bfloat16)]),
+                level > 0,
+                7 + LAYERS + level,
+                Line([(unit_grads, 0, carried * third)], False),
+            )
         )
-        layer_grads[level] = lax.psum(folded, "dp") if level else folded
-
-    grad_start_all, layer_grads[0] = gather_all(grad_branch, 13, layer_grads[0])
+        layer_grads[3 * level + 1] = summed
+
+    grad_start_all, summed = gather_all(
+        grad_branch, 13, Line([(attention_grads, 0, third), (unit_grads, third, third)], False)
+    )
+    layer_grads[0], layer_grads[2] = summed[:third], summed[third:]
+    layer_grads = jnp.concatenate([grads for grads in layer_grads if grads is not None], axis=0)
     grad_start_all = grad_start_all.reshape(-1, D)
     grad_table, table_squares = look_back(span, row_ids, ids_all, grad_start_all, grad_table)
-    layer_squares = jnp.zeros((), jnp.float32)
-    for level in range(LAYERS):
-        chosen = slice(level * layer_blocks, (level + 1) * layer_blocks)
-        values = layer_grads[level].astype(jnp.float32)
-        layer_squares += jnp.sum(jnp.where(mine[chosen][:, None, None], values * values, 0.0))
+    values = layer_grads.astype(jnp.float32)
+    layer_squares = jnp.sum(jnp.where(mine[:blocks][:, None, None], values * values, 0.0))
     keep = jnp.where(
         tensor_part * share + jnp.arange(share) < real_counts[0], 1.0, 0.0
     ).astype(jnp.float32)

time: 857 us -> 833 us (0.972)
  between operations: 19.8 us -> 4.77 us
  Pallas kernels: 780 us -> 771 us
    pallas_call x4, Pallas kernels: 120 us -> 181 us  [local_call(): pl.pallas_call(kernel, name=name, grid_spec=pltpu.PrefetchScalarGridSpec(...]
    pallas_call x2, Pallas kernels: 161 us -> 103 us  [reduce_all(): pl.pallas_call(kernel, name='reduce_all', out_shape=[jax.ShapeDtypeStruct...]
    pallas_call x10, Pallas kernels: 286 us -> 316 us  [tensor_step(): pl.pallas_call(kernel, name=name, grid=(1,), out_shape=shapes, in_specs=i...]
    pallas_call x2, Pallas kernels: 120 us -> 95.2 us  [gather_all(): pl.pallas_call(kernel, name='gather_all', out_shape=[jax.ShapeDtypeStruct...]
    pallas_call x1, Pallas kernels: 28.4 us -> 18.8 us  [join_stats(): pl.pallas_call(kernel, name='join_stats', out_shape=[jax.ShapeDtypeStruct...]
    unnamed x138 -> x88, local copies, waits for them, and re-layouts: 21.7 us -> 21.2 us
  transfers between devices with their start and end apart: 2 -> 0, of which waited for: 0 -> 0; matrix products, arithmetic and copies ran while one was open for 1% -> 0% of each run, Pallas kernels for 40% -> 0%
where the time goes in v5:
time: 833 us; the launch traced here: 826 us
  Pallas kernels  771 us (93%)
  local copies, waits for them, and re-layouts  33.9 us (4%)
  other arithmetic  16.5 us (2%)
    pallas_call x10, Pallas kernels, tensor_step(): pl.pallas_call(kernel, name=name, grid=(1,), out_shape=shapes, in_specs=i...  316 us
    pallas_call x4, Pallas kernels, local_call(): pl.pallas_call(kernel, name=name, grid_spec=pltpu.PrefetchScalarGridSpec(...  181 us
    pallas_call x2, Pallas kernels, reduce_all(): pl.pallas_call(kernel, name='reduce_all', out_shape=[jax.ShapeDtypeStruct...  103 us
    pallas_call x2, Pallas kernels, gather_all(): pl.pallas_call(kernel, name='gather_all', out_shape=[jax.ShapeDtypeStruct...  95.2 us
    pallas_call x1, Pallas kernels, update_slots(): pl.pallas_call(kernel, name='update_slots', grid_spec=pltpu.PrefetchScala...  34.1 us
    unnamed x88, local copies, waits for them, and re-layouts  21.2 us
    pallas_call x1, Pallas kernels, join_stats(): pl.pallas_call(kernel, name='join_stats', out_shape=[jax.ShapeDtypeStruct...  18.8 us

profile of v5, /device:TPU:0, one launch (start us, length us, event | category | flops | bytes accessed | tf_op | source)
XLA Modules:
  0.0 826.2 jit_solution(2020210806961891299)
XLA Ops:
  1.9 0.9 select_reduce_fusion.1
  2.9 1.3 fusion.7
  6.3 1.4 add_add_fusion.block_ref
  7.6 0.9 fusion.10
  8.7 9.1 %spread_tokens.1 = (s32[4,8,128]{2,1,0:T(8,128)}, s32[4,8,128]{2,1,0:T(8,128)}, f32[4,8,128]{2,1,0:T(8,128)}, f32[1,128]{1,0:T(1,128)}) custom-call(s32[16,128]{1,0:T(8,128)} %add_add_fusion.block_ref), custom_call_target="tpu_custom_call" | custom-call | flops 1000 | bytes 1000 | tf_op jit(solution)/shard_map/spread_tokens/pallas_call | solution.py:1136
  18.1 0.8 select_n.125
  18.9 1.4 pad.13.ids_ref
  20.3 4.4 convert_element_type.24
  24.7 2.8 pad.14
  27.5 5.3 gather_fusion
  32.8 4.3 select_select_fusion.refs_1_.refs_7_
  37.1 38.7 %look_up.1 = bf16[4096,768]{1,0:T(8,128)(2,1)} custom-call(s32[2]{0:T(128)} %pad_add_fusion.1.span_ref, s32[3648,1]{1,0:T(8,128)} %pad.13.ids_ref, s32[4,8,128]{2,1,0:T(8,128)} %get-tuple-element.89.tokens_ref, bf16[3648,768]{1,0:T(8,128)(2,1)} %bitcast.38), custom_call_target="tpu_custom_call" | custom-call | flops 1000 | bytes 1000 | tf_op jit(solution)/shard_map/look_up/pallas_call | solution.py:1349
  75.7 60.8 %reduce_all.2 = (f32[128,768]{1,0:T(8,128)}, bf16[16,2,48,768]{3,2,1,0:T(8,128)(2,1)}) custom-call(bf16[2,4,4,128,768]{4,3,2,1,0:T(8,128)(2,1)} %bitcast.51, bf16[48,48,768]{2,1,0:T(8,128)(2,1)} %select_select_fusion.refs_1_.refs_7_), custom_call_target="tpu_custom_call" | custom-call | flops 1000 | bytes 1000 | tf_op jit(solution)/shard_map/reduce_all/pallas_call | solution.py:820
  136.5 1.0 copy-done.1
  137.5 10.4 %normed.1.refs_0_.refs_1_ = bf16[4,128,768]{2,1,0:T(8,128)(2,1)S(1)} custom-call(f32[128,768]{1,0:T(8,128)S(1)} %copy-done.1, f32[1,768]{1,0:T(1,128)S(1)} %get-tuple-element.171.refs_1_.refs_12_), custom_call_target="tpu_custom_call" | custom-call | flops 1000 | bytes 1000 | tf_op jit(solution)/shard_map/normed/pallas_call | solution.py:225
  147.9 39.7 %inner_0.1 = (f32[128,768]{1,0:T(8,128)S(1)}, bf16[4,128,768]{2,1,0:T(8,128)(2,1)S(1)}, bf16[192,512]{1,0:T(8,128)(2,1)S(1)}, bf16[2,2,192,512]{3,2,1,0:T(8,128)...) custom-call(bf16[4,128,768]{2,1,0:T(8,128)(2,1)S(1)} %normed.1.refs_0_.refs_1_, ...), custom_call_target="tpu_custom_call" | custom-call | flops 1000 | bytes 1000 | tf_op jit(solution)/shard_map/inner_0/pallas_call | solution.py:225
  187.6 0.9 copy-done.13
  188.5 39.9 %outcome_0.1 = (f32[128,768]{1,0:T(8,128)S(1)}, f32[128,768]{1,0:T(8,128)S(1)}, bf16[4,128,768]{2,1,0:T(8,128)(2,1)S(1)}, f32[768,512]{1,0:T(8,128)}, bf16[768,5...) custom-call(bf16[4,128,768]{2,1,0:T(8,128)(2,1)S(1)} %get-tuple-element.92.refs_0_.refs_1_, ...), custom_call_target="tpu_custom_call" | custom-call | flops 1000 | bytes 1000 | tf_op jit(solution)/shard_map/outcome_0/pallas_call | solution.py:225
  228.4 0.9 copy-done.14
  229.3 42.7 %inner_1.1 = (f32[128,768]{1,0:T(8,128)S(1)}, bf16[4,128,768]{2,1,0:T(8,128)(2,1)S(1)}, bf16[192,512]{1,0:T(8,128)(2,1)S(1)}, bf16[2,2,192,512]{3,2,1,0:T(8,128)...) custom-call(bf16[4,128,768]{2,1,0:T(8,128)(2,1)S(1)} %get-tuple-element.95.refs_, ...), custom_call_target="tpu_custom_call" | custom-call | flops 1000 | bytes 1000 | tf_op jit(solution)/shard_map/inner_1/pallas_call | solution.py:225
  272.0 0.9 copy-done.15
  272.9 17.6 %outcome_1.1 = (f32[128,768]{1,0:T(8,128)S(1)}, f32[128,768]{1,0:T(8,128)S(1)}, bf16[128,768]{1,0:T(8,128)(2,1)S(1)}, f32[768,512]{1,0:T(8,128)}, bf16[768,512]{1,0:T(8,128)(2,1)S(1)}) custom-call(bf16[4,128,768]{2,1,0:T(8,128)(2,1)S(1)} %get-tuple-element.98.refs_0_.refs_1_, bf16[1536,768]{1,0:T(8,128)(2,1)} %bitcast.47, bf16[1536,768]{1,0:T(8,128)(2,1)} %bitcast.48, ...), custom_call_target="tpu_custom_call" | custom-call | flops 1000 | bytes 1000 | tf_op jit(solution)/shard_map/outcome_1/pallas_call | solution.py:225
  290.5 33.4 %gather_all.2 = bf16[2,4,4,128,768]{4,3,2,1,0:T(8,128)(2,1)S(1)} custom-call(bf16[128,768]{1,0:T(8,128)(2,1)S(1)} %get-tuple-element.102.refs_0_), custom_call_target="tpu_custom_call" | custom-call | flops 1000 | bytes 1000 | tf_op jit(solution)/shard_map/gather_all/pallas_call | solution.py:962
  324.0 2.7 copy-done
  326.7 42.0 %head_forward.1 = (bf16[3648,4096]{1,0:T(8,128)(2,1)}, f32[32,8,128]{2,1,0:T(8,128)}) custom-call(s32[2]{0:T(128)} %pad_add_fusion.1.span_ref, s32[3648,1]{1,0:T(8,128)} %pad.13.ids_ref, s32[4,8,128]{2,1,0:T(8,128)} %get-tuple-element.87.labels_ref, bf16[3648,768]{1,0:T(8,128)(2,1)} %bitcast.39, bf16[4096,768]{1,0:T(8,128)(2,1)} %bitcast.34), custom_call_target="tpu_custom_call" | custom-call | flops 1000 | bytes 1000 | tf_op jit(solution)/shard_map/head_forward/pallas_call | solution.py:1349
  368.6 18.8 %join_stats.1 = (f32[8,128]{1,0:T(8,128)}, f32[2,4,4,8,128]{4,3,2,1,0:T(8,128)}) custom-call(f32[2,4,4,8,128]{4,3,2,1,0:T(8,128)} %bitcast.59), custom_call_target="tpu_custom_call" | custom-call | flops 1000 | bytes 1000 | tf_op jit(solution)/shard_map/join_stats/pallas_call | solution.py:1072
  387.5 63.1 %head_backward.1 = (bf16[4096,768]{1,0:T(8,128)(2,1)}, f32[3648,768]{1,0:T(8,128)}) custom-call(s32[2]{0:T(128)} %pad_add_fusion.1.span_ref, s32[3648,1]{1,0:T(8,128)} %pad.13.ids_ref, s32[4,8,128]{2,1,0:T(8,128)} %get-tuple-element.87.labels_ref, f32[4,8,128]{2,1,0:T(8,128)} %get-tuple-element.88.keep_ref, f32[32,8,128]{2,1,0:T(8,128)} %get-tuple-element.103.stats_ref, ...), custom_call_target="tpu_custom_call" | custom-call | flops 1000 | bytes 1000 | tf_op jit(solution)/shard_map/head_backward/pallas_call | solution.py:1349
  450.5 42.7 %reduce_all.3.refs_0_ = f32[128,768]{1,0:T(8,128)} custom-call(bf16[2,4,4,128,768]{4,3,2,1,0:T(8,128)(2,1)} %bitcast.56), custom_call_target="tpu_custom_call" | custom-call | flops 1000 | bytes 1000 | tf_op jit(solution)/shard_map/reduce_all/pallas_call | solution.py:820
  493.2 1.0 copy-done.10
  494.2 12.3 %top_back.1 = (f32[128,768]{1,0:T(8,128)S(1)}, f32[128,768]{1,0:T(8,128)S(1)}, f32[1,768]{1,0:T(1,128)S(1)}, bf16[4,128,768]{2,1,0:T(8,128)(2,1)S(1)}) custom-call(f32[128,768]{1,0:T(8,128)S(1)} %copy-done.10, f32[128,768]{1,0:T(8,128)S(1)} %get-tuple-element.107.refs_1_, f32[1,768]{1,0:T(1,128)S(1)} %get-tuple-element.167.refs_4_.refs_2_, f32[5]{0:T(128)S(1)} %copy-done.24), custom_call_target="tpu_custom_call" | custom-call | flops 1000 | bytes 1000 | tf_op jit(solution)/shard_map/top_back/pallas_call | solution.py:225
  506.6 26.7 %inner_back_1.1 = (f32[128,768]{1,0:T(8,128)S(1)}, f32[1,768]{1,0:T(1,128)S(1)}, bf16[4,128,768]{2,1,0:T(8,128)(2,1)S(1)}, bf16[16,48,768]{2,1,0:T(8,128)(2,1)}) custom-call(bf16[4,128,768]{2,1,0:T(8,128)(2,1)S(1)} %get-tuple-element.108.refs_0_, bf16[4,128,768]{2,1,0:T(8,128)(2,1)S(1)} %get-tuple-element.98.refs_0_.refs_1_, bf16[1536,768]{1,0:T(8,128)(2,1)} %bitcast.49, ...), custom_call_target="tpu_custom_call" | custom-call | flops 1000 | bytes 1000 | tf_op jit(solution)/shard_map/inner_back_1/pallas_call | solution.py:225
  533.3 0.9 copy-done.17
  534.2 51.3 %stream_back_1.1 = (f32[128,768]{1,0:T(8,128)S(1)}, f32[128,768]{1,0:T(8,128)S(1)}, f32[1,768]{1,0:T(1,128)S(1)}, bf16[4,128,768]{2,1,0:T(8,128)(2,1)S(1)}, bf16...) custom-call(bf16[4,128,768]{2,1,0:T(8,128)(2,1)} %copy-done.17, bf16[4,128,768]{2,1,0:T(8,128)(2,1)} %copy-done.7, ...), custom_call_target="tpu_custom_call" | custom-call | flops 1000 | bytes 1000 | tf_op jit(solution)/shard_map/stream_back_1/pallas_call | solution.py:225
  585.6 38.6 %inner_back_0.1 = (f32[128,768]{1,0:T(8,128)S(1)}, f32[1,768]{1,0:T(1,128)S(1)}, bf16[4,128,768]{2,1,0:T(8,128)(2,1)S(1)}, bf16[16,48,768]{2,1,0:T(8,128)(2,1)}, bf16[8,48,768]{2,1,0:T(8,128)(2,1)S(1)}) custom-call(bf16[4,128,768]{2,1,0:T(8,128)(2,1)S(1)} %get-tuple-element.120.refs_0_, bf16[4,128,768]{2,1,0:T(8,128)(2,1)} %copy-done.8, ...), custom_call_target="tpu_custom_call" | custom-call | flops 1000 | bytes 1000 | tf_op jit(solution)/shard_map/inner_back_0/pallas_call | solution.py:225
  624.2 0.9 copy-done.16
  625.1 0.8 copy-done.19
  625.9 36.7 %stream_back_0.1 = (f32[128,768]{1,0:T(8,128)}, f32[128,768]{1,0:T(8,128)}, f32[1,768]{1,0:T(1,128)S(1)}, bf16[128,768]{1,0:T(8,128)(2,1)S(1)}, bf16[8,48,768]{2...) custom-call(bf16[4,128,768]{2,1,0:T(8,128)(2,1)} %copy-done.16, bf16[4,128,768]{2,1,0:T(8,128)(2,1)} %copy-done.3, ...), custom_call_target="tpu_custom_call" | custom-call | flops 1000 | bytes 1000 | tf_op jit(solution)/shard_map/stream_back_0/pallas_call | solution.py:225
  662.7 61.8 %gather_all.3 = (bf16[2,4,4,128,768]{4,3,2,1,0:T(8,128)(2,1)S(1)}, bf16[16,48,768]{2,1,0:T(8,128)(2,1)S(1)}) custom-call(bf16[128,768]{1,0:T(8,128)(2,1)S(1)} %get-tuple-element.140.refs_0_, bf16[8,48,768]{2,1,0:T(8,128)(2,1)S(1)} %get-tuple-element.141.refs_1_, bf16[16,48,768]{2,1,0:T(8,128)(2,1)S(1)} %copy-done.5), custom_call_target="tpu_custom_call" | custom-call | flops 1000 | bytes 1000 | tf_op jit(solution)/shard_map/gather_all/pallas_call | solution.py:962
  724.5 2.7 copy-done.4
  727.2 1.0 copy-done.12
  728.2 37.2 %look_back.1 = (f32[3648,768]{1,0:T(8,128)}, f32[8,768]{1,0:T(8,128)}) custom-call(s32[2]{0:T(128)} %pad_add_fusion.1.span_ref, s32[3648,1]{1,0:T(8,128)} %pad.13.ids_ref, s32[4,8,128]{2,1,0:T(8,128)} %get-tuple-element.89.tokens_ref, bf16[4096,768]{1,0:T(8,128)(2,1)} %bitcast.36, f32[3648,768]{1,0:T(8,128)} %get-tuple-element.143.table_ref), custom_call_target="tpu_custom_call" | custom-call | flops 1000 | bytes 1000 | tf_op jit(solution)/shard_map/look_back/pallas_call | solution.py:1349
  765.4 1.2 slice_dynamic-update-slice_fusion.1
  766.7 1.1 constant_dynamic-update-slice_fusion.2
  767.8 1.1 slice_dynamic-update-slice_fusion
  769.0 2.5 select_reduce_fusion
  771.5 13.6 %finish.1 = (f32[5,768]{1,0:T(8,128)}, f32[5,768]{1,0:T(8,128)}, f32[5,768]{1,0:T(8,128)}, f32[1,5]{1,0:T(1,128)}, f32[1,5]{1,0:T(1,128)}, /*index=5*/f32[1,5]{1,0:T(1,128)}, f32[1,128]{1,0:T(1,128)}, f32[8,128]{1,0:T(8,128)}) custom-call(f32[1,768]{1,0:T(1,128)} %copy-done.30, f32[1,768]{1,0:T(1,128)} %copy-done.29, f32[1,768]{1,0:T(1,128)} %copy-done.28, ...), custom_call_target="tpu_custom_call" | custom-call | flops 1000 | bytes 1000 | tf_op jit(solution)/shard_map/finish/pallas_call | solution.py:1237
  785.2 1.2 fusion.11
  787.1 34.1 %update_slots.1 = (f32[67,48,768]{2,1,0:T(8,128)}, f32[67,48,768]{2,1,0:T(8,128)}, f32[67,48,768]{2,1,0:T(8,128)}) custom-call(s32[2,68]{1,0:T(2,128)S(1)} %pad.12.plan_ref, f32[8,128]{1,0:T(8,128)S(1)} %copy-done.25, f32[67,48,768]{2,1,0:T(8,128)} %master_ref.1, f32[67,48,768]{2,1,0:T(8,128)} %first_ref.1, f32[67,48,768]{2,1,0:T(8,128)} %second_ref.1, ...), custom_call_target="tpu_custom_call" | custom-call | flops 1000 | bytes 1000 | tf_op jit(solution)/shard_map/update_slots/pallas_call | solution.py:1291
  (90 shorter events, 6.1 us)
Async XLA Ops:
  136.5 1.0 copy-start.1
  147.9 39.7 %copy-start.3 = (bf16[4,128,768]{2,1,0:T(8,128)(2,1)}, bf16[4,128,768]{2,1,0:T(8,128)(2,1)S(1)}, u32[]{:S(2)}) copy-start(bf16[4,128,768]{2,1,0:T(8,128)(2,1)S(1)} %normed.1.refs_0_.refs_1_) | copy-start | bytes 2359300
  147.9 40.6 %copy-start.24 = (f32[5]{0:T(128)S(1)}, f32[5]{0:T(128)}, u32[]{:S(2)}) copy-start(f32[5]{0:T(128)} %refs_15_.2) | copy-start | bytes 64
  187.6 0.9 copy-start.13
  188.5 39.9 %copy-start.8 = (bf16[4,128,768]{2,1,0:T(8,128)(2,1)}, bf16[4,128,768]{2,1,0:T(8,128)(2,1)S(1)}, u32[]{:S(2)}) copy-start(bf16[4,128,768]{2,1,0:T(8,128)(2,1)S(1)} %get-tuple-element.92.refs_0_.refs_1_) | copy-start | bytes 2359300
  228.4 0.9 copy-start.14
  229.3 42.7 %copy-start.7 = (bf16[4,128,768]{2,1,0:T(8,128)(2,1)}, bf16[4,128,768]{2,1,0:T(8,128)(2,1)S(1)}, u32[]{:S(2)}) copy-start(bf16[4,128,768]{2,1,0:T(8,128)(2,1)S(1)} %get-tuple-element.95.refs_0_.refs_1_) | copy-start | bytes 2359300
  229.3 43.6 %copy-start.11 = (f32[128,768]{1,0:T(8,128)}, f32[128,768]{1,0:T(8,128)S(1)}, u32[]{:S(2)}) copy-start(f32[128,768]{1,0:T(8,128)S(1)} %get-tuple-element.101.refs_6_) | copy-start | bytes 1179652
  229.3 43.6 %copy-start.2 = (f32[128,768]{1,0:T(8,128)S(1)}, f32[128,768]{1,0:T(8,128)}, u32[]{:S(2)}) copy-start(f32[128,768]{1,0:T(8,128)} %get-tuple-element.90.refs_0_.refs_5_.refs_11_) | copy-start | bytes 1179652
  272.0 0.9 copy-start.15
  272.9 51.0 %copy-start.22 = (bf16[192,512]{1,0:T(8,128)(2,1)}, bf16[192,512]{1,0:T(8,128)(2,1)S(1)}, u32[]{:S(2)}) copy-start(bf16[192,512]{1,0:T(8,128)(2,1)S(1)} %get-tuple-element.116.refs_7_) | copy-start | bytes 589828
  290.5 33.5 %copy-start.18 = (bf16[768,512]{1,0:T(8,128)(2,1)}, bf16[768,512]{1,0:T(8,128)(2,1)S(1)}, u32[]{:S(2)}) copy-start(bf16[768,512]{1,0:T(8,128)(2,1)S(1)} %get-tuple-element.110.refs_5_) | copy-start | bytes 2359300
  290.5 33.5 %copy-start.21 = (f32[128,768]{1,0:T(8,128)}, f32[128,768]{1,0:T(8,128)S(1)}, u32[]{:S(2)}) copy-start(f32[128,768]{1,0:T(8,128)S(1)} %get-tuple-element.138.refs_7_) | copy-start | bytes 1179652
  324.0 2.7 copy-start
  493.2 1.0 copy-start.10
  506.6 26.7 %copy-start.26 = (f32[1,768]{1,0:T(1,128)}, f32[1,768]{1,0:T(1,128)S(1)}, u32[]{:S(2)}) copy-start(f32[1,768]{1,0:T(1,128)S(1)} %get-tuple-element.137.refs_4_) | copy-start | bytes 9220
  506.6 119.4 %copy-start.6 = (f32[128,768]{1,0:T(8,128)}, f32[128,768]{1,0:T(8,128)S(1)}, u32[]{:S(2)}) copy-start(f32[128,768]{1,0:T(8,128)S(1)} %get-tuple-element.118.refs_13_.refs_14_.refs_9_) | copy-start | bytes 1179652
  506.6 27.6 %copy-start.23 = (bf16[192,512]{1,0:T(8,128)(2,1)S(1)}, bf16[192,512]{1,0:T(8,128)(2,1)}, u32[]{:S(2)}) copy-start(bf16[192,512]{1,0:T(8,128)(2,1)} %copy-done.22) | copy-start | bytes 589828
  533.3 0.9 copy-start.17
  534.2 51.4 %copy-start.27 = (f32[1,768]{1,0:T(1,128)}, f32[1,768]{1,0:T(1,128)S(1)}, u32[]{:S(2)}) copy-start(f32[1,768]{1,0:T(1,128)S(1)} %get-tuple-element.136.refs_3_) | copy-start | bytes 9220
  585.5 38.7 %copy-start.28 = (f32[1,768]{1,0:T(1,128)}, f32[1,768]{1,0:T(1,128)S(1)}, u32[]{:S(2)}) copy-start(f32[1,768]{1,0:T(1,128)S(1)} %get-tuple-element.135.refs_2_) | copy-start | bytes 9220
  585.6 40.4 %copy-start.9 = (f32[128,768]{1,0:T(8,128)}, f32[128,768]{1,0:T(8,128)S(1)}, u32[]{:S(2)}) copy-start(f32[128,768]{1,0:T(8,128)S(1)} %get-tuple-element.131.refs_13_.refs_8_) | copy-start | bytes 1179652
  624.2 0.9 copy-start.16
  625.1 0.8 copy-start.19
  625.9 36.7 %copy-start.29 = (f32[1,768]{1,0:T(1,128)}, f32[1,768]{1,0:T(1,128)S(1)}, u32[]{:S(2)}) copy-start(f32[1,768]{1,0:T(1,128)S(1)} %get-tuple-element.134.refs_1_) | copy-start | bytes 9220
  625.9 36.7 %copy-start.5 = (bf16[16,48,768]{2,1,0:T(8,128)(2,1)S(1)}, bf16[16,48,768]{2,1,0:T(8,128)(2,1)}, u32[]{:S(2)}) copy-start(bf16[16,48,768]{2,1,0:T(8,128)(2,1)} %get-tuple-element.132.refs_16_.refs_2_) | copy-start | bytes 3538948
  662.7 102.7 %copy-start.30 = (f32[1,768]{1,0:T(1,128)}, f32[1,768]{1,0:T(1,128)S(1)}, u32[]{:S(2)}) copy-start(f32[1,768]{1,0:T(1,128)S(1)} %get-tuple-element.133.refs_0_) | copy-start | bytes 9220
  724.5 2.7 copy-start.4
  727.2 1.0 copy-start.12
  765.4 3.5 copy-start.20
  765.4 3.5 copy-start.31
  786.4 0.7 copy-start.25
  787.1 34.1 %copy-start.34 = (f32[5,768]{1,0:T(8,128)S(1)}, f32[5,768]{1,0:T(8,128)}, u32[]{:S(2)}) copy-start(f32[5,768]{1,0:T(8,128)} %get-tuple-element.195) | copy-start | bytes 46084
  787.1 34.7 %copy-start.33 = (f32[5,768]{1,0:T(8,128)S(1)}, f32[5,768]{1,0:T(8,128)}, u32[]{:S(2)}) copy-start(f32[5,768]{1,0:T(8,128)} %get-tuple-element.196) | copy-start | bytes 46084
  787.1 35.3 %copy-start.32 = (f32[5,768]{1,0:T(8,128)S(1)}, f32[5,768]{1,0:T(8,128)}, u32[]{:S(2)}) copy-start(f32[5,768]{1,0:T(8,128)} %get-tuple-element.197) | copy-start | bytes 46084
  787.1 36.0 %copy-start.38 = (f32[1,5]{1,0:T(1,128)S(1)}, f32[1,5]{1,0:T(1,128)}, u32[]{:S(2)}) copy-start(f32[1,5]{1,0:T(1,128)} %get-tuple-element.158) | copy-start | bytes 64
  787.1 36.5 %copy-start.37 = (f32[1,5]{1,0:T(1,128)S(1)}, f32[1,5]{1,0:T(1,128)}, u32[]{:S(2)}) copy-start(f32[1,5]{1,0:T(1,128)} %get-tuple-element.159) | copy-start | bytes 64
  787.1 37.0 %copy-start.36 = (f32[1,5]{1,0:T(1,128)S(1)}, f32[1,5]{1,0:T(1,128)}, u32[]{:S(2)}) copy-start(f32[1,5]{1,0:T(1,128)} %get-tuple-element.160) | copy-start | bytes 64
  787.1 37.5 %copy-start.35 = (f32[1,128]{1,0:T(1,128)S(1)}, f32[1,128]{1,0:T(1,128)}, u32[]{:S(2)}) copy-start(f32[1,128]{1,0:T(1,128)} %get-tuple-element.149.refs_14_) | copy-start | bytes 1540

commit v6 on v5

--- a/solution.py
+++ b/solution.py
@@ -173,7 +173,7 @@
                 )
             if work.during:
                 work.during(work_refs, work_outs, refs)
-            tick(4)
+            tick(6)
             total = partial_ref[pl.ds(pl.multiple_of(me * share, share), share), :]
             for step, copy in enumerate(copies):
                 copy.wait()
@@ -316,7 +316,7 @@
             attended = times(both[0, 1, span, :], (far * inverse).astype(jnp.bfloat16))
             attended += times(both[1, 1, span, :], (own * inverse).astype(jnp.bfloat16))
             attended_ref[span, :] = attended.astype(jnp.bfloat16)
-            tick()
+            tick(2)
         partial_ref[...] = contract_first(attended_ref[...], out_ref[...])
 
     low = jnp.bfloat16
@@ -394,7 +394,7 @@
             own_grads.append(
                 (contract_last(head_queries, own_grad) * scale, contract_last(head_grads, own))
             )
-            tick()
+            tick(2)
         copy = send(back, came, send_sem, recv_sem, {"seq": 1 - side})
         copy.wait()
         for head, (key_grad, value_grad) in enumerate(own_grads):
@@ -529,8 +529,8 @@
     )
 
 
-LINE_BLOCKS = 2
-LINE_LAG = 2
+LINE_BLOCKS = 1
+LINE_LAG = 3
 
 
 class Line:
@@ -606,10 +606,9 @@
             @pl.when(jnp.logical_not(self.comes(way)))
             def _():
                 self.came[way] = jnp.zeros(self.half, jnp.bfloat16)
-                self.going[way] = self.own[...]
 
                 def start(chunk, carry):
-                    self.copy(self.going.at[way, self.at(chunk)], way, chunk).start()
+                    self.copy(self.own.at[self.at(chunk)], way, chunk).start()
                     return carry
 
                 lax.fori_loop(0, self.chunks, start, 0)
@@ -753,8 +752,6 @@
         for place in range(groups):
             near_copies[place].wait_recv()
             own_copies[place].wait()
-            if line and place < 4:
-                line.steps(1)
             for slot in range(tensors):
                 mid[place, slot] = (
                     own[place, slot].astype(jnp.float32) + near[place, slot].astype(jnp.float32)
@@ -768,8 +765,8 @@
                 ]
             )
         for place in range(groups):
-            if line and place < 4:
-                line.steps(1)
+            if line and 0 < place < 4:
+                line.steps(2)
             copies = []
             for index, slot, rows, target in ((0, across, upper, across), (1, beside, lower, beside)):
                 first_copies[place][index].wait_recv()
@@ -781,7 +778,7 @@
         far_copies = []
         for place, target in enumerate(order):
             if line and place < 4:
-                line.steps(1)
+                line.steps(2)
             copies = first_copies[place][2:] + second_copies[place]
             for copy in copies:
                 copy.wait_recv()
@@ -888,8 +885,6 @@
         for place in range(groups):
             source = behind("dp", place)
             if place:
-                if line and place < 4:
-                    line.steps(1)
                 far_copies[place - 1].wait_recv()
             held = out.at[side, part, source] if place else block_ref
 
@@ -965,7 +960,7 @@
         out_shape=[jax.ShapeDtypeStruct((2, tensors, groups) + block.shape, block.dtype)]
         + ([line.out_shape] if line else []),
         in_specs=[VMEM_SPEC] + (line.in_specs if line else []),
-        out_specs=[anywhere] + ([line.out_spec] if line else []),
+        out_specs=[pl.BlockSpec(memory_space=pltpu.HBM)] + ([line.out_spec] if line else []),
         scratch_shapes=[
             dma,
             dma((groups - 1,)),
@@ -1621,8 +1616,8 @@
     ).astype(jnp.bfloat16)
     third = layer_blocks // 3
 
-    def weights_line(start, size):
-        return Line([(halves, start * third, size * third)], True)
+    def weights_line(*starts):
+        return Line([(halves, start * third, third) for start in starts], True)
 
     def as_table(joined):
         return joined.reshape(-1, D)
@@ -1634,7 +1629,7 @@
     cosine, sine = jnp.cos(angles), jnp.sin(angles)
 
     looked = look_up(span, row_ids, ids_all, table).reshape(order + (D,))
-    start, joined = reduce_rows(looked, (0, 14), weights_line(0, 2))
+    start, joined = reduce_rows(looked, (0, 14), weights_line(0, 1))
     table_one = as_table(joined)
     attention_table, up = table_one, (table_one, 1)
     tables = []
@@ -1659,7 +1654,9 @@
     (normed,) = tensor_step("normed", normed_of, None, (start, gain[0]), (), [], True, 1)
     states, streams, inners, kept_all = [start], [start], [], []
     for level in range(LAYERS):
-        here = 3 * level
+        here, last = 3 * level, level == LAYERS - 1
+        carried = [] if last else [here + 3]
+        carried += [here + 1, here + 2] if level else [here + 2]
         inner, normed_two, queries, both, logs, attended, joined = tensor_step(
             f"inner_{level}",
             inner_of,
@@ -1669,17 +1666,15 @@
             [piece],
             True,
             2 if level == 0 else 15 + level,
-            weights_line(here + 1, 2) if level else weights_line(here + 2, 1),
+            weights_line(*carried),
         )
         kept = (queries, both, logs, attended)
         joined = as_table(joined)
-        if level:
-            up, down = (joined, 0), (joined, 1)
-        else:
-            down = (joined, 0)
+        down = (joined, len(carried) - 1)
+        up = (joined, len(carried) - 2) if level else up
         tables.append((attention_table, up, down))
-        last = level == LAYERS - 1
-        outcome, stream, normed_next, hidden, activated, *joined = tensor_step(
+        attention_table = joined
+        outcome, stream, normed_next, hidden, activated = tensor_step(
             f"outcome_{level}",
             partial(outcome_of, (level + 1) * (level + 2) // 2 - 1),
             unit_work(normed_two, up, down),
@@ -1688,10 +1683,7 @@
             [piece, piece] + ([((share, D), jnp.bfloat16)] if last else []),
             not last,
             3 + level,
-            None if last else weights_line(here + 3, 1),
         )
-        if not last:
-            attention_table = as_table(joined[0])
         inners.append(inner)
         kept_all.append((normed, kept, normed_two, (hidden, activated)))
         states.append(outcome)
@@ -1767,7 +1759,6 @@
         )
         if summed:
             layer_grads[3 * (level + 1)] = summed[0]
-        carried = 1 if level == 0 else 2
         grad_ys[level], grad_state, gain_grads[2 * level], grad_branch, attention_grads, summed = (
             tensor_step(
                 f"stream_back_{level}",
@@ -1780,15 +1771,14 @@
                 [piece, piece, row] + ([] if level else [((share, D), jnp.bfloat16)]),
                 level > 0,
                 7 + LAYERS + level,
-                Line([(unit_grads, 0, carried * third)], False),
+                Line([(unit_grads, 0, 2 * third)], False),
             )
         )
         layer_grads[3 * level + 1] = summed
 
-    grad_start_all, summed = gather_all(
-        grad_branch, 13, Line([(attention_grads, 0, third), (unit_grads, third, third)], False)
-    )
-    layer_grads[0], layer_grads[2] = summed[:third], summed[third:]
+    grad_start_all, layer_grads[0] = gather_all(
+        grad_branch, 13, Line([(attention_grads, 0, third)], False)
+    )
     layer_grads = jnp.concatenate([grads for grads in layer_grads if grads is not None], axis=0)
     grad_start_all = grad_start_all.reshape(-1, D)
     grad_table, table_squares = look_back(span, row_ids, ids_all, grad_start_all, grad_table)

time: 833 us -> 785 us (0.942)
  Pallas kernels: 771 us -> 722 us
    pallas_call x4, Pallas kernels: 181 us -> 121 us  [local_call(): pl.pallas_call(kernel, name=name, grid_spec=pltpu.PrefetchScalarGridSpec(...]
    pallas_call x2, Pallas kernels: 103 us -> 129 us  [reduce_all(): pl.pallas_call(kernel, name='reduce_all', out_shape=[jax.ShapeDtypeStruct...]
    pallas_call x2, Pallas kernels: 95.2 us -> 76.6 us  [gather_all(): pl.pallas_call(kernel, name='gather_all', out_shape=[jax.ShapeDtypeStruct...]
    pallas_call x10, Pallas kernels: 316 us -> 306 us  [tensor_step(): pl.pallas_call(kernel, name=name, grid=(1,), out_shape=shapes, in_specs=i...]
    pallas_call x1, Pallas kernels: 18.8 us -> 27.2 us  [join_stats(): pl.pallas_call(kernel, name='join_stats', out_shape=[jax.ShapeDtypeStruct...]
    unnamed x88 -> x89, local copies, waits for them, and re-layouts: 21.2 us -> 21.5 us
where the time goes in v6:
time: 785 us; the launch traced here: 777 us
  Pallas kernels  722 us (92%)
  local copies, waits for them, and re-layouts  34.3 us (4%)
  other arithmetic  16.5 us (2%)
    pallas_call x10, Pallas kernels, tensor_step(): pl.pallas_call(kernel, name=name, grid=(1,), out_shape=shapes, in_specs=i...  306 us
    pallas_call x2, Pallas kernels, reduce_all(): pl.pallas_call(kernel, name='reduce_all', out_shape=[jax.ShapeDtypeStruct...  129 us
    pallas_call x4, Pallas kernels, local_call(): pl.pallas_call(kernel, name=name, grid_spec=pltpu.PrefetchScalarGridSpec(...  121 us
    pallas_call x2, Pallas kernels, gather_all(): pl.pallas_call(kernel, name='gather_all', out_shape=[jax.ShapeDtypeStruct...  76.6 us
    pallas_call x1, Pallas kernels, update_slots(): pl.pallas_call(kernel, name='update_slots', grid_spec=pltpu.PrefetchScala...  34.1 us
    pallas_call x1, Pallas kernels, join_stats(): pl.pallas_call(kernel, name='join_stats', out_shape=[jax.ShapeDtypeStruct...  27.2 us
    unnamed x89, local copies, waits for them, and re-layouts  21.5 us
    pallas_call x1, Pallas kernels, finish(): pl.pallas_call(kernel, name='finish', out_shape=[jax.ShapeDtypeStruct(val...  19.3 us

profile of v6, /device:TPU:0, one launch (start us, length us, event | category | flops | bytes accessed | tf_op | source)
XLA Modules:
  0.0 777.5 jit_solution(16514392277924107894)
XLA Ops:
  1.9 0.9 select_reduce_fusion.1
  2.9 1.3 fusion.7
  6.3 1.4 add_add_fusion.block_ref
  7.6 0.9 fusion.10
  8.7 9.1 %spread_tokens.1 = (s32[4,8,128]{2,1,0:T(8,128)}, s32[4,8,128]{2,1,0:T(8,128)}, f32[4,8,128]{2,1,0:T(8,128)}, f32[1,128]{1,0:T(1,128)}) custom-call(s32[16,128]{1,0:T(8,128)} %add_add_fusion.block_ref), custom_call_target="tpu_custom_call" | custom-call | flops 1000 | bytes 1000 | tf_op jit(solution)/shard_map/spread_tokens/pallas_call | solution.py:1131
  18.1 0.8 select_n.125
  18.9 1.4 pad.13.ids_ref
  20.3 4.4 convert_element_type.24
  24.7 2.8 pad.14
  27.5 5.3 gather_fusion
  32.8 4.3 select_select_fusion.refs_1_.refs_2_.refs_7_.refs_8_
  37.1 24.9 %look_up.1 = bf16[4096,768]{1,0:T(8,128)(2,1)} custom-call(s32[2]{0:T(128)} %pad_add_fusion.1.span_ref, s32[3648,1]{1,0:T(8,128)} %pad.13.ids_ref, s32[4,8,128]{2,1,0:T(8,128)} %get-tuple-element.88.tokens_ref, bf16[3648,768]{1,0:T(8,128)(2,1)} %bitcast.37), custom_call_target="tpu_custom_call" | custom-call | flops 1000 | bytes 1000 | tf_op jit(solution)/shard_map/look_up/pallas_call | solution.py:1344
  61.9 73.3 %reduce_all.2 = (f32[128,768]{1,0:T(8,128)}, bf16[16,2,48,768]{3,2,1,0:T(8,128)(2,1)}) custom-call(bf16[2,4,4,128,768]{4,3,2,1,0:T(8,128)(2,1)} %bitcast.56, bf16[48,48,768]{2,1,0:T(8,128)(2,1)} %select_select_fusion.refs_1_.refs_2_.refs_7_.refs_8_, bf16[48,48,768]{2,1,0:T(8,128)(2,1)} %select_select_fusion.refs_1_.refs_2_.refs_7_.refs_8_), custom_call_target="tpu_custom_call" | custom-call | flops 1000 | bytes 1000 | tf_op jit(solution)/shard_map/reduce_all/pallas_call | solution.py:817
  135.2 1.0 copy-done.1
  136.2 12.7 %normed.1.refs_0_.refs_1_ = bf16[4,128,768]{2,1,0:T(8,128)(2,1)S(1)} custom-call(f32[128,768]{1,0:T(8,128)S(1)} %copy-done.1, f32[1,768]{1,0:T(1,128)S(1)} %get-tuple-element.169.refs_1_.refs_12_), custom_call_target="tpu_custom_call" | custom-call | flops 1000 | bytes 1000 | tf_op jit(solution)/shard_map/normed/pallas_call | solution.py:225
  148.9 41.3 %inner_0.1 = (f32[128,768]{1,0:T(8,128)S(1)}, bf16[4,128,768]{2,1,0:T(8,128)(2,1)S(1)}, bf16[192,512]{1,0:T(8,128)(2,1)S(1)}, bf16[2,2,192,512]{3,2,1,0:T(8,128)...) custom-call(bf16[4,128,768]{2,1,0:T(8,128)(2,1)S(1)} %normed.1.refs_0_.refs_1_, ...), custom_call_target="tpu_custom_call" | custom-call | flops 1000 | bytes 1000 | tf_op jit(solution)/shard_map/inner_0/pallas_call | solution.py:225
  190.2 0.9 copy-done.15
  191.1 27.8 %outcome_0.1 = (f32[128,768]{1,0:T(8,128)S(1)}, f32[128,768]{1,0:T(8,128)S(1)}, bf16[4,128,768]{2,1,0:T(8,128)(2,1)S(1)}, f32[768,512]{1,0:T(8,128)}, bf16[768,512]{1,0:T(8,128)(2,1)S(1)}) custom-call(bf16[4,128,768]{2,1,0:T(8,128)(2,1)S(1)} %get-tuple-element.91.refs_0_.refs_1_, bf16[1536,768]{1,0:T(8,128)(2,1)} %bitcast.42, bf16[1536,768]{1,0:T(8,128)(2,1)} %bitcast.46, ...), custom_call_target="tpu_custom_call" | custom-call | flops 1000 | bytes 1000 | tf_op jit(solution)/shard_map/outcome_0/pallas_call | solution.py:225
  218.9 0.9 copy-done.16
  219.8 40.1 %inner_1.1 = (f32[128,768]{1,0:T(8,128)S(1)}, bf16[4,128,768]{2,1,0:T(8,128)(2,1)S(1)}, bf16[192,512]{1,0:T(8,128)(2,1)S(1)}, bf16[2,2,192,512]{3,2,1,0:T(8,128)...) custom-call(bf16[4,128,768]{2,1,0:T(8,128)(2,1)S(1)} %get-tuple-element.94.refs_, ...), custom_call_target="tpu_custom_call" | custom-call | flops 1000 | bytes 1000 | tf_op jit(solution)/shard_map/inner_1/pallas_call | solution.py:225
  259.9 0.9 copy-done.17
  260.8 16.8 %outcome_1.1 = (f32[128,768]{1,0:T(8,128)S(1)}, f32[128,768]{1,0:T(8,128)S(1)}, bf16[128,768]{1,0:T(8,128)(2,1)S(1)}, f32[768,512]{1,0:T(8,128)}, bf16[768,512]{1,0:T(8,128)(2,1)S(1)}) custom-call(bf16[4,128,768]{2,1,0:T(8,128)(2,1)S(1)} %get-tuple-element.96.refs_0_.refs_1_, bf16[1536,768]{1,0:T(8,128)(2,1)} %bitcast.52, bf16[1536,768]{1,0:T(8,128)(2,1)} %bitcast.53, ...), custom_call_target="tpu_custom_call" | custom-call | flops 1000 | bytes 1000 | tf_op jit(solution)/shard_map/outcome_1/pallas_call | solution.py:225
  277.7 0.7 copy-done.24
  278.4 33.6 %gather_all.2 = bf16[2,4,4,128,768]{4,3,2,1,0:T(8,128)(2,1)S(1)} custom-call(bf16[128,768]{1,0:T(8,128)(2,1)S(1)} %get-tuple-element.100.refs_0_), custom_call_target="tpu_custom_call" | custom-call | flops 1000 | bytes 1000 | tf_op jit(solution)/shard_map/gather_all/pallas_call | solution.py:957
  312.0 2.7 copy-done
  314.7 27.3 %head_forward.1 = (bf16[3648,4096]{1,0:T(8,128)(2,1)}, f32[32,8,128]{2,1,0:T(8,128)}) custom-call(s32[2]{0:T(128)} %pad_add_fusion.1.span_ref, s32[3648,1]{1,0:T(8,128)} %pad.13.ids_ref, s32[4,8,128]{2,1,0:T(8,128)} %get-tuple-element.86.labels_ref, bf16[3648,768]{1,0:T(8,128)(2,1)} %bitcast.38, bf16[4096,768]{1,0:T(8,128)(2,1)} %bitcast.33), custom_call_target="tpu_custom_call" | custom-call | flops 1000 | bytes 1000 | tf_op jit(solution)/shard_map/head_forward/pallas_call | solution.py:1344
  342.0 27.2 %join_stats.1 = (f32[8,128]{1,0:T(8,128)}, f32[2,4,4,8,128]{4,3,2,1,0:T(8,128)}) custom-call(f32[2,4,4,8,128]{4,3,2,1,0:T(8,128)} %bitcast.58), custom_call_target="tpu_custom_call" | custom-call | flops 1000 | bytes 1000 | tf_op jit(solution)/shard_map/join_stats/pallas_call | solution.py:1067
  369.3 42.3 %head_backward.1 = (bf16[4096,768]{1,0:T(8,128)(2,1)}, f32[3648,768]{1,0:T(8,128)}) custom-call(s32[2]{0:T(128)} %pad_add_fusion.1.span_ref, s32[3648,1]{1,0:T(8,128)} %pad.13.ids_ref, s32[4,8,128]{2,1,0:T(8,128)} %get-tuple-element.86.labels_ref, f32[4,8,128]{2,1,0:T(8,128)} %get-tuple-element.87.keep_ref, f32[32,8,128]{2,1,0:T(8,128)} %get-tuple-element.101.stats_ref, ...), custom_call_target="tpu_custom_call" | custom-call | flops 1000 | bytes 1000 | tf_op jit(solution)/shard_map/head_backward/pallas_call | solution.py:1344
  411.6 55.6 %reduce_all.3.refs_0_ = f32[128,768]{1,0:T(8,128)} custom-call(bf16[2,4,4,128,768]{4,3,2,1,0:T(8,128)(2,1)} %bitcast.57), custom_call_target="tpu_custom_call" | custom-call | flops 1000 | bytes 1000 | tf_op jit(solution)/shard_map/reduce_all/pallas_call | solution.py:817
  467.1 1.0 copy-done.13
  468.1 12.4 %top_back.1 = (f32[128,768]{1,0:T(8,128)S(1)}, f32[128,768]{1,0:T(8,128)S(1)}, f32[1,768]{1,0:T(1,128)S(1)}, bf16[4,128,768]{2,1,0:T(8,128)(2,1)S(1)}) custom-call(f32[128,768]{1,0:T(8,128)S(1)} %copy-done.13, f32[128,768]{1,0:T(8,128)S(1)} %get-tuple-element.105.refs_1_, f32[1,768]{1,0:T(1,128)S(1)} %get-tuple-element.165.refs_4_.refs_2_, f32[5]{0:T(128)S(1)} %copy-done.25), custom_call_target="tpu_custom_call" | custom-call | flops 1000 | bytes 1000 | tf_op jit(solution)/shard_map/top_back/pallas_call | solution.py:225
  481.1 26.5 %inner_back_1.1 = (f32[128,768]{1,0:T(8,128)S(1)}, f32[1,768]{1,0:T(1,128)S(1)}, bf16[4,128,768]{2,1,0:T(8,128)(2,1)S(1)}, bf16[16,48,768]{2,1,0:T(8,128)(2,1)}) custom-call(bf16[4,128,768]{2,1,0:T(8,128)(2,1)S(1)} %get-tuple-element.106.refs_0_, bf16[4,128,768]{2,1,0:T(8,128)(2,1)S(1)} %get-tuple-element.96.refs_0_.refs_1_, bf16[1536,768]{1,0:T(8,128)(2,1)} %bitcast.54, ...), custom_call_target="tpu_custom_call" | custom-call | flops 1000 | bytes 1000 | tf_op jit(solution)/shard_map/inner_back_1/pallas_call | solution.py:225
  507.6 0.9 copy-done.19
  508.5 49.2 %stream_back_1.1 = (f32[128,768]{1,0:T(8,128)S(1)}, f32[128,768]{1,0:T(8,128)S(1)}, f32[1,768]{1,0:T(1,128)S(1)}, bf16[4,128,768]{2,1,0:T(8,128)(2,1)S(1)}, bf16...) custom-call(bf16[4,128,768]{2,1,0:T(8,128)(2,1)} %copy-done.19, bf16[4,128,768]{2,1,0:T(8,128)(2,1)} %copy-done.7, ...), custom_call_target="tpu_custom_call" | custom-call | flops 1000 | bytes 1000 | tf_op jit(solution)/shard_map/stream_back_1/pallas_call | solution.py:225
  557.7 34.2 %inner_back_0.1 = (f32[128,768]{1,0:T(8,128)S(1)}, f32[1,768]{1,0:T(1,128)S(1)}, bf16[4,128,768]{2,1,0:T(8,128)(2,1)S(1)}, bf16[16,48,768]{2,1,0:T(8,128)(2,1)}, bf16[8,48,768]{2,1,0:T(8,128)(2,1)S(1)}) custom-call(bf16[4,128,768]{2,1,0:T(8,128)(2,1)S(1)} %get-tuple-element.118.refs_0_, bf16[4,128,768]{2,1,0:T(8,128)(2,1)} %copy-done.6, ...), custom_call_target="tpu_custom_call" | custom-call | flops 1000 | bytes 1000 | tf_op jit(solution)/shard_map/inner_back_0/pallas_call | solution.py:225
  592.0 0.9 copy-done.18
  592.8 0.8 copy-done.21
  593.7 45.6 %stream_back_0.1 = (f32[128,768]{1,0:T(8,128)}, f32[128,768]{1,0:T(8,128)}, f32[1,768]{1,0:T(1,128)S(1)}, bf16[128,768]{1,0:T(8,128)(2,1)S(1)}, bf16[8,48,768]{2...) custom-call(bf16[4,128,768]{2,1,0:T(8,128)(2,1)} %copy-done.18, bf16[4,128,768]{2,1,0:T(8,128)(2,1)} %copy-done.3, ...), custom_call_target="tpu_custom_call" | custom-call | flops 1000 | bytes 1000 | tf_op jit(solution)/shard_map/stream_back_0/pallas_call | solution.py:225
  639.3 43.0 %gather_all.3 = (bf16[2,4,4,128,768]{4,3,2,1,0:T(8,128)(2,1)S(1)}, bf16[8,48,768]{2,1,0:T(8,128)(2,1)S(1)}) custom-call(bf16[128,768]{1,0:T(8,128)(2,1)S(1)} %get-tuple-element.138.refs_0_, bf16[8,48,768]{2,1,0:T(8,128)(2,1)S(1)} %get-tuple-element.139.refs_1_), custom_call_target="tpu_custom_call" | custom-call | flops 1000 | bytes 1000 | tf_op jit(solution)/shard_map/gather_all/pallas_call | solution.py:957
  682.3 2.7 copy-done.4
  685.0 0.8 copy-done.23
  685.8 26.2 %look_back.1 = (f32[3648,768]{1,0:T(8,128)}, f32[8,768]{1,0:T(8,128)}) custom-call(s32[2]{0:T(128)} %pad_add_fusion.1.span_ref, s32[3648,1]{1,0:T(8,128)} %pad.13.ids_ref, s32[4,8,128]{2,1,0:T(8,128)} %get-tuple-element.88.tokens_ref, bf16[4096,768]{1,0:T(8,128)(2,1)} %bitcast.35, f32[3648,768]{1,0:T(8,128)} %get-tuple-element.141.table_ref), custom_call_target="tpu_custom_call" | custom-call | flops 1000 | bytes 1000 | tf_op jit(solution)/shard_map/look_back/pallas_call | solution.py:1344
  712.0 1.2 constant_dynamic-update-slice_fusion.3
  713.2 1.3 constant_dynamic-update-slice_fusion.2
  714.7 2.5 select_reduce_fusion
  717.2 19.3 %finish.1 = (f32[5,768]{1,0:T(8,128)}, f32[5,768]{1,0:T(8,128)}, f32[5,768]{1,0:T(8,128)}, f32[1,5]{1,0:T(1,128)}, f32[1,5]{1,0:T(1,128)}, /*index=5*/f32[1,5]{1,0:T(1,128)}, f32[1,128]{1,0:T(1,128)}, f32[8,128]{1,0:T(8,128)}) custom-call(f32[1,768]{1,0:T(1,128)} %copy-done.31, f32[1,768]{1,0:T(1,128)} %copy-done.30, f32[1,768]{1,0:T(1,128)} %copy-done.29, ...), custom_call_target="tpu_custom_call" | custom-call | flops 1000 | bytes 1000 | tf_op jit(solution)/shard_map/finish/pallas_call | solution.py:1232
  736.5 1.3 fusion.11
  738.6 34.1 %update_slots.1 = (f32[67,48,768]{2,1,0:T(8,128)}, f32[67,48,768]{2,1,0:T(8,128)}, f32[67,48,768]{2,1,0:T(8,128)}) custom-call(s32[2,68]{1,0:T(2,128)S(1)} %pad.12.plan_ref, f32[8,128]{1,0:T(8,128)S(1)} %copy-done.26, f32[67,48,768]{2,1,0:T(8,128)} %master_ref.1, f32[67,48,768]{2,1,0:T(8,128)} %first_ref.1, f32[67,48,768]{2,1,0:T(8,128)} %second_ref.1, ...), custom_call_target="tpu_custom_call" | custom-call | flops 1000 | bytes 1000 | tf_op jit(solution)/shard_map/update_slots/pallas_call | solution.py:1286
  (91 shorter events, 6.6 us)
Async XLA Ops:
  135.2 1.0 copy-start.1
  148.9 41.3 %copy-start.3 = (bf16[4,128,768]{2,1,0:T(8,128)(2,1)}, bf16[4,128,768]{2,1,0:T(8,128)(2,1)S(1)}, u32[]{:S(2)}) copy-start(bf16[4,128,768]{2,1,0:T(8,128)(2,1)S(1)} %normed.1.refs_0_.refs_1_) | copy-start | bytes 2359300
  148.9 42.2 %copy-start.25 = (f32[5]{0:T(128)S(1)}, f32[5]{0:T(128)}, u32[]{:S(2)}) copy-start(f32[5]{0:T(128)} %refs_15_.2) | copy-start | bytes 64
  190.2 0.9 copy-start.15
  191.1 68.8 %copy-start.6 = (bf16[4,128,768]{2,1,0:T(8,128)(2,1)}, bf16[4,128,768]{2,1,0:T(8,128)(2,1)S(1)}, u32[]{:S(2)}) copy-start(bf16[4,128,768]{2,1,0:T(8,128)(2,1)S(1)} %get-tuple-element.91.refs_0_.refs_1_) | copy-start | bytes 2359300
  191.1 68.8 %copy-start.8 = (f32[128,768]{1,0:T(8,128)}, f32[128,768]{1,0:T(8,128)S(1)}, u32[]{:S(2)}) copy-start(f32[128,768]{1,0:T(8,128)S(1)} %get-tuple-element.93.refs_3_.refs_7_) | copy-start | bytes 1179652
  218.9 0.9 copy-start.16
  219.8 40.1 %copy-start.7 = (bf16[4,128,768]{2,1,0:T(8,128)(2,1)}, bf16[4,128,768]{2,1,0:T(8,128)(2,1)S(1)}, u32[]{:S(2)}) copy-start(bf16[4,128,768]{2,1,0:T(8,128)(2,1)S(1)} %get-tuple-element.94.refs_0_.refs_1_) | copy-start | bytes 2359300
  219.8 41.1 %copy-start.14 = (f32[128,768]{1,0:T(8,128)}, f32[128,768]{1,0:T(8,128)S(1)}, u32[]{:S(2)}) copy-start(f32[128,768]{1,0:T(8,128)S(1)} %get-tuple-element.99.refs_6_) | copy-start | bytes 1179652
  219.8 41.1 %copy-start.2 = (f32[128,768]{1,0:T(8,128)S(1)}, f32[128,768]{1,0:T(8,128)}, u32[]{:S(2)}) copy-start(f32[128,768]{1,0:T(8,128)} %get-tuple-element.89.refs_0_.refs_5_.refs_11_) | copy-start | bytes 1179652
  259.9 0.9 copy-start.17
  260.8 51.1 %copy-start.11 = (f32[128,768]{1,0:T(8,128)}, f32[128,768]{1,0:T(8,128)S(1)}, u32[]{:S(2)}) copy-start(f32[128,768]{1,0:T(8,128)S(1)} %get-tuple-element.98.refs_3_.refs_7_) | copy-start | bytes 1179652
  277.7 0.7 copy-start.24
  278.4 33.6 %copy-start.20 = (bf16[768,512]{1,0:T(8,128)(2,1)}, bf16[768,512]{1,0:T(8,128)(2,1)S(1)}, u32[]{:S(2)}) copy-start(bf16[768,512]{1,0:T(8,128)(2,1)S(1)} %get-tuple-element.108.refs_5_) | copy-start | bytes 2359300
  312.0 2.7 copy-start
  411.6 69.6 %copy-start.12 = (f32[128,768]{1,0:T(8,128)S(1)}, f32[128,768]{1,0:T(8,128)}, u32[]{:S(2)}) copy-start(f32[128,768]{1,0:T(8,128)} %copy-done.11) | copy-start | bytes 1179652
  467.1 1.0 copy-start.13
  480.5 0.6 copy-start.27
  481.1 112.5 %copy-start.5 = (f32[128,768]{1,0:T(8,128)}, f32[128,768]{1,0:T(8,128)S(1)}, u32[]{:S(2)}) copy-start(f32[128,768]{1,0:T(8,128)S(1)} %get-tuple-element.116.refs_13_.refs_14_.refs_9_) | copy-start | bytes 1179652
  507.6 0.9 copy-start.19
  508.5 49.2 %copy-start.28 = (f32[1,768]{1,0:T(1,128)}, f32[1,768]{1,0:T(1,128)S(1)}, u32[]{:S(2)}) copy-start(f32[1,768]{1,0:T(1,128)S(1)} %get-tuple-element.134.refs_3_) | copy-start | bytes 9220
  508.5 49.2 %copy-start.9 = (f32[128,768]{1,0:T(8,128)S(1)}, f32[128,768]{1,0:T(8,128)}, u32[]{:S(2)}) copy-start(f32[128,768]{1,0:T(8,128)} %copy-done.8) | copy-start | bytes 1179652
  557.7 34.3 %copy-start.29 = (f32[1,768]{1,0:T(1,128)}, f32[1,768]{1,0:T(1,128)S(1)}, u32[]{:S(2)}) copy-start(f32[1,768]{1,0:T(1,128)S(1)} %get-tuple-element.133.refs_2_) | copy-start | bytes 9220
  557.7 36.0 %copy-start.10 = (f32[128,768]{1,0:T(8,128)}, f32[128,768]{1,0:T(8,128)S(1)}, u32[]{:S(2)}) copy-start(f32[128,768]{1,0:T(8,128)S(1)} %get-tuple-element.129.refs_13_.refs_8_) | copy-start | bytes 1179652
  592.0 0.9 copy-start.18
  592.8 0.8 copy-start.21
  593.7 45.6 %copy-start.30 = (f32[1,768]{1,0:T(1,128)}, f32[1,768]{1,0:T(1,128)S(1)}, u32[]{:S(2)}) copy-start(f32[1,768]{1,0:T(1,128)S(1)} %get-tuple-element.132.refs_1_) | copy-start | bytes 9220
  639.2 72.7 %copy-start.31 = (f32[1,768]{1,0:T(1,128)}, f32[1,768]{1,0:T(1,128)S(1)}, u32[]{:S(2)}) copy-start(f32[1,768]{1,0:T(1,128)S(1)} %get-tuple-element.131.refs_0_) | copy-start | bytes 9220
  682.3 2.7 copy-start.4
  685.0 0.8 copy-start.23
  712.0 2.6 copy-start.22
  712.0 2.7 copy-start.32
  737.9 0.7 copy-start.26
  738.5 34.1 %copy-start.35 = (f32[5,768]{1,0:T(8,128)S(1)}, f32[5,768]{1,0:T(8,128)}, u32[]{:S(2)}) copy-start(f32[5,768]{1,0:T(8,128)} %get-tuple-element.193) | copy-start | bytes 46084
  738.5 34.7 %copy-start.34 = (f32[5,768]{1,0:T(8,128)S(1)}, f32[5,768]{1,0:T(8,128)}, u32[]{:S(2)}) copy-start(f32[5,768]{1,0:T(8,128)} %get-tuple-element.194) | copy-start | bytes 46084
  738.5 35.3 %copy-start.33 = (f32[5,768]{1,0:T(8,128)S(1)}, f32[5,768]{1,0:T(8,128)}, u32[]{:S(2)}) copy-start(f32[5,768]{1,0:T(8,128)} %get-tuple-element.195) | copy-start | bytes 46084
  738.5 36.0 %copy-start.39 = (f32[1,5]{1,0:T(1,128)S(1)}, f32[1,5]{1,0:T(1,128)}, u32[]{:S(2)}) copy-start(f32[1,5]{1,0:T(1,128)} %get-tuple-element.156) | copy-start | bytes 64
  738.5 36.5 %copy-start.38 = (f32[1,5]{1,0:T(1,128)S(1)}, f32[1,5]{1,0:T(1,128)}, u32[]{:S(2)}) copy-start(f32[1,5]{1,0:T(1,128)} %get-tuple-element.157) | copy-start | bytes 64
  738.5 37.0 %copy-start.37 = (f32[1,5]{1,0:T(1,128)S(1)}, f32[1,5]{1,0:T(1,128)}, u32[]{:S(2)}) copy-start(f32[1,5]{1,0:T(1,128)} %get-tuple-element.158) | copy-start | bytes 64
  738.6 37.5 %copy-start.36 = (f32[1,128]{1,0:T(1,128)S(1)}, f32[1,128]{1,0:T(1,128)}, u32[]{:S(2)}) copy-start(f32[1,128]{1,0:T(1,128)} %get-tuple-element.147.refs_14_) | copy-start | bytes 1540

commit v7 on v6

--- a/solution.py
+++ b/solution.py
@@ -1119,15 +1119,14 @@
                 total = total + limit
                 for part in range(tensors):
                     row = (half * tensors + part) * groups + source
-                    tile, place = row // TILE_GROUPS, slice(row % TILE_GROUPS, row % TILE_GROUPS + 1)
-                    ids[tile, place, :] = held[source, half, part : part + 1, :]
-                    targets[tile, place, :] = held[source, half, tensors + part : tensors + part + 1, :]
-                    kept[tile, place, :] = jnp.where(lane + part * LANES < limit, 1.0, 0.0)
+                    ids[row] = held[source, half, part : part + 1, :]
+                    targets[row] = held[source, half, tensors + part : tensors + part + 1, :]
+                    kept[row] = jnp.where(lane + part * LANES < limit, 1.0, 0.0)
         count[...] = total.astype(jnp.float32)
 
     dma = pltpu.SemaphoreType.DMA
     vmem = pl.BlockSpec(memory_space=pltpu.VMEM)
-    shape = (rows // TILE_GROUPS, TILE_GROUPS, LANES)
+    shape = (rows, 1, LANES)
     return pl.pallas_call(
         kernel,
         name="spread_tokens",
@@ -1179,7 +1178,7 @@
             grad = grad_refs[later - 1][...]
             for level in range(later + 1):
                 values.append(jnp.sum(grad * state_refs[level][...], keepdims=True))
-        loss = (home_ref[0:1, :] - home_ref[1:2, :]) * keep_ref[...]
+        loss = jnp.where(keep_ref[...] > 0.0, home_ref[0:1, :] - home_ref[1:2, :], 0.0)
         values.append(jnp.sum(loss, keepdims=True))
         values.append(jnp.sum(table_ref[...], keepdims=True) + layer_ref[...])
         lane = lax.broadcasted_iota(jnp.int32, (1, D), 1)
@@ -1314,33 +1313,65 @@
     )
 
 
-def row_of(groups_ref):
-    return jnp.concatenate([groups_ref[0, g : g + 1, :] for g in range(TILE_GROUPS)], axis=1)
-
-
-def stat_row(stat_ref, row):
-    return jnp.concatenate([stat_ref[g, row : row + 1, :] for g in range(TILE_GROUPS)], axis=1)
-
-
-def chunk_of(span_ref, step):
-    return pl.ds(pl.multiple_of(span_ref[0] + step * ROW_STEP, 16), ROW_STEP)
-
-
-def chunks_of(span_ref):
-    return (span_ref[1] - span_ref[0] + ROW_STEP - 1) // ROW_STEP
+TILE = TILE_GROUPS * LANES
+PICKED = 768
+
+
+def row_of(values_ref, groups, place=0):
+    rows = [values_ref[group, place : place + 1, :] for group in groups]
+    return jnp.concatenate(rows, axis=1)
+
+
+def tile_row(values_ref, tile):
+    start = tile * TILE_GROUPS
+    return row_of(values_ref, [start + place for place in range(TILE_GROUPS)])
+
+
+PLAN_GROUPS = 4
+
+
+def chunk_of(plan_ref, step):
+    return pl.ds(pl.multiple_of(plan_ref[0] + step * ROW_STEP, 16), ROW_STEP)
+
+
+def chunks_of(plan_ref):
+    return (plan_ref[1] - plan_ref[0] + ROW_STEP - 1) // ROW_STEP
 
 
 def whole(shape):
-    return pl.BlockSpec(shape, lambda step, span: (0,) * len(shape), pipeline_mode=pl.Buffered(1))
-
-
-TILE = TILE_GROUPS * LANES
-TOKENS_SPEC = pl.BlockSpec((1, TILE_GROUPS, LANES), lambda step, span: (step, 0, 0))
-STATS_SPEC = pl.BlockSpec((TILE_GROUPS, 8, LANES), lambda step, span: (step, 0, 0))
-ROWS_SPEC = pl.BlockSpec((TILE, D), lambda step, span: (step, 0))
-
-
-def local_call(name, kernel, steps, span, operands, in_specs, out_shape, out_specs, scratch):
+    return pl.BlockSpec(shape, lambda step, plan: (0,) * len(shape), pipeline_mode=pl.Buffered(1))
+
+
+def last_tile(plan):
+    return (plan[2] - 1) // TILE_GROUPS
+
+
+def group_specs():
+    return [
+        pl.BlockSpec(
+            (LANES, D),
+            lambda step, plan, place=place: (
+                plan[PLAN_GROUPS + jnp.minimum(step, last_tile(plan)) * TILE_GROUPS + place],
+                0,
+            ),
+        )
+        for place in range(TILE_GROUPS)
+    ]
+
+
+def powers_spec(rows):
+    return pl.BlockSpec((rows, TILE), lambda step, plan: (0, jnp.minimum(step, last_tile(plan))))
+
+
+def groups_of(plan_ref):
+    start = PLAN_GROUPS + pl.program_id(0) * TILE_GROUPS
+    return [plan_ref[start + place] for place in range(TILE_GROUPS)]
+
+
+ROWS_SPEC = pl.BlockSpec((TILE, D), lambda step, plan: (step, 0))
+
+
+def local_call(name, kernel, steps, plan, operands, in_specs, out_shape, out_specs, scratch):
     return pl.pallas_call(
         kernel,
         name=name,
@@ -1354,189 +1385,350 @@
         out_shape=out_shape,
         cost_estimate=SHORT,
         compiler_params=pltpu.CompilerParams(vmem_limit_bytes=60 << 20),
-    )(span, *operands)
-
-
-def look_up(span, row_ids, tokens, table):
-    rows = table.shape[0]
-    steps = tokens.shape[0]
-
-    def kernel(span_ref, ids_ref, tokens_ref, table_ref, out_ref, acc):
-        acc[...] = jnp.zeros_like(acc)
-        wanted = row_of(tokens_ref)
-
-        def one(step, carry):
-            chunk = chunk_of(span_ref, step)
-            hits = jnp.where(ids_ref[chunk, :] == wanted, 1.0, 0.0).astype(jnp.bfloat16)
-            acc[...] += contract_first(hits, table_ref[chunk, :])
-            return carry
-
-        lax.fori_loop(0, chunks_of(span_ref), one, 0)
-        out_ref[...] = acc[...].astype(jnp.bfloat16)
-
+    )(plan, *operands)
+
+
+def ones_where(condition):
+    return jnp.where(condition, 1.0, 0.0).astype(jnp.bfloat16)
+
+
+def picks(rank_row):
+    return ones_where(lax.broadcasted_iota(jnp.int32, (PICKED, TILE), 0) == rank_row)
+
+
+def rows_picked(plan_ref, step, place_row):
+    start = plan_ref[0] + step * ROW_STEP
+    row = lax.broadcasted_iota(jnp.int32, (ROW_STEP, PICKED), 0) + start
+    return ones_where(row == place_row)
+
+
+def look_up(plan, row_ids, tokens, places, table):
+    rows, groups = table.shape[0], tokens.shape[0]
+    steps = groups // TILE_GROUPS
+
+    def kernel(
+        plan_ref, ids_ref, tokens_ref, places_ref, table_ref, out_ref, ranks_ref, picked_ref, acc, picked
+    ):
+        tile = pl.program_id(0)
+        few = plan_ref[3] <= PICKED
+
+        @pl.when(tile == 0)
+        def _():
+            held = places_ref[...].reshape(groups, LANES) >= 0
+            ones = ones_where(held)
+            lane = (LANES, LANES)
+            before = ones_where(
+                lax.broadcasted_iota(jnp.int32, lane, 0) < lax.broadcasted_iota(jnp.int32, lane, 1)
+            )
+            group = (groups, groups)
+            above = ones_where(
+                lax.broadcasted_iota(jnp.int32, group, 1) < lax.broadcasted_iota(jnp.int32, group, 0)
+            )
+            totals = jnp.sum(ones.astype(jnp.float32), axis=1, keepdims=True)
+            totals = jnp.broadcast_to(totals, (groups, LANES)).astype(jnp.bfloat16)
+            ranks = (times(ones, before) + times(above, totals)).astype(jnp.int32)
+            ranks_ref[...] = jnp.where(held, ranks, -1).reshape(groups, 1, LANES)
+
+        @pl.when((tile == 0) & few)
+        def _():
+            def digits_of(step, total):
+                place = tile_row(places_ref, step)
+                high = lax.shift_right_arithmetic(place, 6)
+                digits = jnp.concatenate([high, place - high * 64] * 4, axis=0)
+                digits = digits.astype(jnp.float32).astype(jnp.bfloat16)
+                return total + contract_last(digits, picks(tile_row(ranks_ref, step)))
+
+            digits = lax.fori_loop(0, steps, digits_of, jnp.zeros((8, PICKED), jnp.float32))
+            place = (digits[0:1] * 64.0 + digits[1:2]).astype(jnp.int32)
+            index = lax.broadcasted_iota(jnp.int32, (1, PICKED), 1)
+            place = jnp.where(index < plan_ref[3], place, -1)
+            picked_ref[...] = jnp.broadcast_to(place, (8, PICKED))
+            acc[:PICKED, :] = jnp.zeros((PICKED, D), jnp.float32)
+
+            def one(step, carry):
+                hits = rows_picked(plan_ref, step, place)
+                acc[:PICKED, :] += contract_first(hits, table_ref[chunk_of(plan_ref, step), :])
+                return carry
+
+            lax.fori_loop(0, chunks_of(plan_ref), one, 0)
+            picked[...] = acc[:PICKED, :].astype(jnp.bfloat16)
+
+        @pl.when(few)
+        def _():
+            hits = picks(tile_row(ranks_ref, tile))
+            out_ref[...] = contract_first(hits, picked[...]).astype(jnp.bfloat16)
+
+        @pl.when(jnp.logical_not(few))
+        def _():
+            acc[...] = jnp.zeros_like(acc)
+            wanted = tile_row(tokens_ref, tile)
+
+            def one(step, carry):
+                chunk = chunk_of(plan_ref, step)
+                hits = ones_where(ids_ref[chunk, :] == wanted)
+                acc[...] += contract_first(hits, table_ref[chunk, :])
+                return carry
+
+            lax.fori_loop(0, chunks_of(plan_ref), one, 0)
+            out_ref[...] = acc[...].astype(jnp.bfloat16)
+
+    lanes = (groups, 1, LANES)
     return local_call(
         "look_up",
         kernel,
         steps,
-        span,
-        (row_ids, tokens, table),
-        [whole((rows, 1)), TOKENS_SPEC, whole((rows, D))],
-        jax.ShapeDtypeStruct((steps * TILE, D), jnp.bfloat16),
-        ROWS_SPEC,
-        [pltpu.VMEM((TILE, D), jnp.float32)],
-    )
-
-
-def head_forward(span, row_ids, labels, table, final):
-    rows = table.shape[0]
-    steps = labels.shape[0]
-
-    def kernel(span_ref, ids_ref, labels_ref, table_ref, final_ref, powers_ref, stats_ref, scores):
-        wanted = row_of(labels_ref)
-        hidden = final_ref[...]
-
-        def first(step, carry):
-            top, target = carry
-            chunk = chunk_of(span_ref, step)
-            ids = ids_ref[chunk, :]
-            raw = contract_last(table_ref[chunk, :], hidden)
-            raw = jnp.where(ids >= 0, raw, -1e30)
-            scores[chunk, :] = raw
-            top = jnp.maximum(top, jnp.max(raw, axis=0, keepdims=True))
-            target = target + jnp.sum(jnp.where(ids == wanted, raw, 0.0), axis=0, keepdims=True)
-            return (top, target)
-
+        plan,
+        (row_ids, tokens, places, table),
+        [whole((rows, 1)), whole(lanes), whole(lanes), whole((rows, D))],
+        [
+            jax.ShapeDtypeStruct((groups * LANES, D), jnp.bfloat16),
+            jax.ShapeDtypeStruct(lanes, jnp.int32),
+            jax.ShapeDtypeStruct((8, PICKED), jnp.int32),
+        ],
+        [ROWS_SPEC, whole(lanes), whole((8, PICKED))],
+        [pltpu.VMEM((TILE, D), jnp.float32), pltpu.VMEM((PICKED, D), jnp.bfloat16)],
+    )
+
+
+def head_forward(plan, row_ids, labels, table, final):
+    rows, groups = table.shape[0], labels.shape[0]
+    steps = groups // TILE_GROUPS
+
+    def kernel(plan_ref, ids_ref, labels_ref, table_ref, *rest):
+        final_refs, (powers_ref, stats_ref, scores, hidden) = rest[:TILE_GROUPS], rest[TILE_GROUPS:]
         blank = jnp.zeros((1, TILE), jnp.float32)
-        top, target = lax.fori_loop(0, chunks_of(span_ref), first, (blank - 1e30, blank))
-
-        def second(step, total):
-            chunk = chunk_of(span_ref, step)
-            powers = jnp.exp(scores[chunk, :] - top)
-            powers_ref[chunk, :] = powers.astype(jnp.bfloat16)
-            return total + jnp.sum(powers, axis=0, keepdims=True)
-
-        total = lax.fori_loop(0, chunks_of(span_ref), second, blank)
-        rest = jnp.zeros((5, LANES), jnp.float32)
-        for g in range(TILE_GROUPS):
-            lanes = slice(g * LANES, (g + 1) * LANES)
-            stats_ref[g] = jnp.concatenate(
-                [top[:, lanes], total[:, lanes], target[:, lanes], rest], axis=0
-            )
+        active = pl.program_id(0) <= last_tile(plan_ref)
+
+        def put(top, total, target):
+            pad = jnp.zeros((5, LANES), jnp.float32)
+            for place in range(TILE_GROUPS):
+                lanes = slice(place * LANES, (place + 1) * LANES)
+                stats_ref[place] = jnp.concatenate(
+                    [top[:, lanes], total[:, lanes], target[:, lanes], pad], axis=0
+                )
+
+        @pl.when(jnp.logical_not(active))
+        def _():
+            put(blank - 1e30, blank, blank)
+
+        @pl.when(active)
+        def _():
+            wanted = row_of(labels_ref, groups_of(plan_ref))
+            for place, ref in enumerate(final_refs):
+                hidden[place * LANES : (place + 1) * LANES, :] = ref[...]
+
+            def first(step, carry):
+                top, target = carry
+                chunk = chunk_of(plan_ref, step)
+                ids = ids_ref[chunk, :]
+                raw = contract_last(table_ref[chunk, :], hidden[...])
+                raw = jnp.where(ids >= 0, raw, -1e30)
+                scores[chunk, :] = raw
+                top = jnp.maximum(top, jnp.max(raw, axis=0, keepdims=True))
+                target = target + jnp.sum(
+                    jnp.where(ids == wanted, raw, 0.0), axis=0, keepdims=True
+                )
+                return (top, target)
+
+            top, target = lax.fori_loop(0, chunks_of(plan_ref), first, (blank - 1e30, blank))
+
+            def second(step, total):
+                chunk = chunk_of(plan_ref, step)
+                powers = jnp.exp(scores[chunk, :] - top)
+                powers_ref[chunk, :] = powers.astype(jnp.bfloat16)
+                return total + jnp.sum(powers, axis=0, keepdims=True)
+
+            put(top, lax.fori_loop(0, chunks_of(plan_ref), second, blank), target)
 
     return local_call(
         "head_forward",
         kernel,
         steps,
-        span,
-        (row_ids, labels, table, final),
-        [whole((rows, 1)), TOKENS_SPEC, whole((rows, D)), ROWS_SPEC],
+        plan,
+        (row_ids, labels, table) + (final,) * TILE_GROUPS,
+        [whole((rows, 1)), whole((groups, 1, LANES)), whole((rows, D))] + group_specs(),
         [
-            jax.ShapeDtypeStruct((rows, steps * TILE), jnp.bfloat16),
-            jax.ShapeDtypeStruct((steps * TILE_GROUPS, 8, LANES), jnp.float32),
+            jax.ShapeDtypeStruct((rows, groups * LANES), jnp.bfloat16),
+            jax.ShapeDtypeStruct((groups, 8, LANES), jnp.float32),
         ],
-        [pl.BlockSpec((rows, TILE), lambda step, span: (0, step)), STATS_SPEC],
-        [pltpu.VMEM((rows, TILE), jnp.float32)],
-    )
-
-
-def head_backward(span, row_ids, labels, keep, stats, log_totals, table, final, powers):
-    rows = table.shape[0]
-    steps = labels.shape[0]
-
-    def kernel(
-        span_ref, ids_ref, labels_ref, keep_ref, stats_ref, logs_ref, table_ref, final_ref,
-        powers_ref, grad_final_ref, grad_table_ref, acc,
-    ):
-        @pl.when(pl.program_id(0) == 0)
+        [
+            powers_spec(rows),
+            pl.BlockSpec((TILE_GROUPS, 8, LANES), lambda step, plan: (step, 0, 0)),
+        ],
+        [pltpu.VMEM((rows, TILE), jnp.float32), pltpu.VMEM((TILE, D), jnp.bfloat16)],
+    )
+
+
+def head_backward(plan, row_ids, labels, keep, stats, log_totals, table, final, powers):
+    rows, groups = table.shape[0], labels.shape[0]
+    steps = groups // TILE_GROUPS
+
+    def kernel(plan_ref, ids_ref, labels_ref, keep_ref, stats_ref, logs_ref, table_ref, powers_ref, *rest):
+        final_refs = rest[:TILE_GROUPS]
+        grad_final_ref, grad_table_ref, acc, hidden, low, sems = rest[TILE_GROUPS:]
+        tile = pl.program_id(0)
+        slot = lax.rem(tile, 2)
+        active = tile <= last_tile(plan_ref)
+
+        def copies(step):
+            start, side = PLAN_GROUPS + step * TILE_GROUPS, lax.rem(step, 2)
+            return [
+                pltpu.make_async_copy(
+                    low.at[side, place],
+                    grad_final_ref.at[plan_ref[start + place]],
+                    sems.at[side, place],
+                )
+                for place in range(TILE_GROUPS)
+            ]
+
+        @pl.when(tile == 0)
         def _():
             grad_table_ref[...] = jnp.zeros_like(grad_table_ref)
 
+        @pl.when(tile >= 2)
+        def _():
+            for copy in copies(tile - 2):
+                copy.wait()
+
         acc[...] = jnp.zeros_like(acc)
-        wanted, kept = row_of(labels_ref), row_of(keep_ref)
-        scale = jnp.exp(stat_row(stats_ref, 0) - stat_row(logs_ref, 0)) * kept
-        hidden = final_ref[...]
-
-        def one(step, carry):
-            chunk = chunk_of(span_ref, step)
-            grads = powers_ref[chunk, :].astype(jnp.float32) * scale
-            grads = grads - jnp.where(ids_ref[chunk, :] == wanted, kept, 0.0)
-            grads = grads.astype(jnp.bfloat16)
-            grad_table_ref[chunk, :] += jnp.dot(grads, hidden, preferred_element_type=jnp.float32)
-            acc[...] += contract_first(grads, table_ref[chunk, :])
-            return carry
-
-        lax.fori_loop(0, chunks_of(span_ref), one, 0)
-        grad_final_ref[...] = acc[...].astype(jnp.bfloat16)
-
+
+        @pl.when(active)
+        def _():
+            own = groups_of(plan_ref)
+            wanted, kept = row_of(labels_ref, own), row_of(keep_ref, own)
+            tops = row_of(stats_ref, range(TILE_GROUPS))
+            scale = jnp.exp(tops - row_of(logs_ref, own)) * kept
+            for place, ref in enumerate(final_refs):
+                hidden[place * LANES : (place + 1) * LANES, :] = ref[...]
+
+            def one(step, carry):
+                chunk = chunk_of(plan_ref, step)
+                grads = powers_ref[chunk, :].astype(jnp.float32) * scale
+                grads = grads - jnp.where(ids_ref[chunk, :] == wanted, kept, 0.0)
+                grads = grads.astype(jnp.bfloat16)
+                grad_table_ref[chunk, :] += times(grads, hidden[...])
+                acc[...] += contract_first(grads, table_ref[chunk, :])
+                return carry
+
+            lax.fori_loop(0, chunks_of(plan_ref), one, 0)
+
+        low[slot] = acc[...].astype(jnp.bfloat16).reshape(TILE_GROUPS, LANES, D)
+        for copy in copies(tile):
+            copy.start()
+
+        @pl.when(tile == steps - 1)
+        def _():
+            for step in range(max(0, steps - 2), steps):
+                for copy in copies(step):
+                    copy.wait()
+
+    lanes = (groups, 1, LANES)
     return local_call(
         "head_backward",
         kernel,
         steps,
-        span,
-        (row_ids, labels, keep, stats, log_totals, table, final, powers),
+        plan,
+        (row_ids, labels, keep, stats, log_totals, table, powers) + (final,) * TILE_GROUPS,
         [
             whole((rows, 1)),
-            TOKENS_SPEC,
-            TOKENS_SPEC,
-            STATS_SPEC,
-            STATS_SPEC,
+            whole(lanes),
+            whole(lanes),
+            pl.BlockSpec((TILE_GROUPS, 8, LANES), lambda step, plan: (step, 0, 0)),
+            whole((groups, 8, LANES)),
             whole((rows, D)),
-            ROWS_SPEC,
-            pl.BlockSpec((rows, TILE), lambda step, span: (0, step)),
-        ],
+            powers_spec(rows),
+        ]
+        + group_specs(),
         [
-            jax.ShapeDtypeStruct((steps * TILE, D), jnp.bfloat16),
+            jax.ShapeDtypeStruct((groups, LANES, D), jnp.bfloat16),
             jax.ShapeDtypeStruct((rows, D), jnp.float32),
         ],
-        [ROWS_SPEC, whole((rows, D))],
-        [pltpu.VMEM((TILE, D), jnp.float32)],
-    )
-
-
-def look_back(span, row_ids, tokens, grad_start, grad_table):
-    rows = grad_table.shape[0]
-    steps = tokens.shape[0]
-
-    def kernel(span_ref, ids_ref, tokens_ref, grad_ref, table_ref, out_ref, squares_ref):
-        @pl.when(pl.program_id(0) == 0)
+        [pl.BlockSpec(memory_space=pl.ANY), whole((rows, D))],
+        [
+            pltpu.VMEM((TILE, D), jnp.float32),
+            pltpu.VMEM((TILE, D), jnp.bfloat16),
+            pltpu.VMEM((2, TILE_GROUPS, LANES, D), jnp.bfloat16),
+            pltpu.SemaphoreType.DMA((2, TILE_GROUPS)),
+        ],
+    )
+
+
+def look_back(plan, row_ids, tokens, ranks, picked, grad_start, grad_table):
+    rows, groups = grad_table.shape[0], tokens.shape[0]
+    steps = groups // TILE_GROUPS
+
+    def kernel(
+        plan_ref, ids_ref, tokens_ref, ranks_ref, picked_ref, grad_ref, table_ref, out_ref, squares_ref, acc
+    ):
+        tile = pl.program_id(0)
+        few = plan_ref[3] <= PICKED
+
+        @pl.when(tile == 0)
         def _():
+            acc[...] = jnp.zeros_like(acc)
             out_ref[...] = table_ref[...]
 
-        wanted = row_of(tokens_ref)
-        grads = grad_ref[...]
-
-        def one(step, carry):
-            chunk = chunk_of(span_ref, step)
-            hits = jnp.where(ids_ref[chunk, :] == wanted, 1.0, 0.0).astype(jnp.bfloat16)
-            out_ref[chunk, :] += jnp.dot(hits, grads, preferred_element_type=jnp.float32)
-            return carry
-
-        lax.fori_loop(0, chunks_of(span_ref), one, 0)
-
-        @pl.when(pl.program_id(0) == steps - 1)
+        @pl.when(few)
+        def _():
+            acc[...] += times(picks(tile_row(ranks_ref, tile)), grad_ref[...])
+
+        @pl.when(jnp.logical_not(few))
+        def _():
+            wanted = tile_row(tokens_ref, tile)
+            grads = grad_ref[...]
+
+            def one(step, carry):
+                chunk = chunk_of(plan_ref, step)
+                out_ref[chunk, :] += times(ones_where(ids_ref[chunk, :] == wanted), grads)
+                return carry
+
+            lax.fori_loop(0, chunks_of(plan_ref), one, 0)
+
+        @pl.when(few & (tile == steps - 1))
+        def _():
+            grads = acc[...].astype(jnp.bfloat16)
+            place = picked_ref[0:1, :]
+
+            def one(step, carry):
+                out_ref[chunk_of(plan_ref, step), :] += times(
+                    rows_picked(plan_ref, step, place), grads
+                )
+                return carry
+
+            lax.fori_loop(0, chunks_of(plan_ref), one, 0)
+
+        @pl.when(tile == steps - 1)
         def _():
             def square(step, total):
-                values = out_ref[chunk_of(span_ref, step), :]
+                values = out_ref[chunk_of(plan_ref, step), :]
                 values = (values * values).reshape(ROW_STEP // 8, 8, D).sum(axis=0)
                 return total + values
 
             squares_ref[...] = lax.fori_loop(
-                0, chunks_of(span_ref), square, jnp.zeros((8, D), jnp.float32)
+                0, chunks_of(plan_ref), square, jnp.zeros((8, D), jnp.float32)
             )
 
+    lanes = (groups, 1, LANES)
     return local_call(
         "look_back",
         kernel,
         steps,
-        span,
-        (row_ids, tokens, grad_start, grad_table),
-        [whole((rows, 1)), TOKENS_SPEC, ROWS_SPEC, whole((rows, D))],
+        plan,
+        (row_ids, tokens, ranks, picked, grad_start, grad_table),
+        [
+            whole((rows, 1)),
+            whole(lanes),
+            whole(lanes),
+            whole((8, PICKED)),
+            ROWS_SPEC,
+            whole((rows, D)),
+        ],
         [
             jax.ShapeDtypeStruct((rows, D), jnp.float32),
             jax.ShapeDtypeStruct((8, D), jnp.float32),
         ],
         [whole((rows, D)), whole((8, D))],
-        [],
+        [pltpu.VMEM((PICKED, D), jnp.float32)],
     )
 
 
@@ -1589,8 +1781,7 @@
     row_ids = jnp.pad(row_ids, ((0, spare * half_rows), (0, 0)), constant_values=-1)
     held = jnp.sum(jnp.where(mine, 1, 0)) * half_rows
     first_held = jnp.sum(jnp.where(mine & (block_ids < blocks), 1, 0)) * half_rows
-    span = jnp.stack([first_held, held]).astype(jnp.int32)
-    plan = jnp.stack(
+    slot_plan = jnp.stack(
         [
             jnp.where(slot_block < 0, -1, jnp.where(slot_block < blocks, 0, 1)),
             jnp.where(slot_block < blocks, jnp.maximum(slot_block, 0), 0),
@@ -1607,6 +1798,39 @@
     )
     ids_all, labels_all, keep_all, count = spread_tokens(packed, 15)
     order = (2, tensors, groups, share)
+    local_ids = ids_all - tensor_part * vocab_rows
+    inside = (local_ids >= 0) & (local_ids < vocab_rows)
+    block_of, within = local_ids // (2 * half_rows) + blocks, local_ids % (2 * half_rows)
+    inside = inside & (within // half_rows == seq_part)
+    same = block_of.reshape(1, -1) == jnp.where(slot_block < 0, -1, slot_block)[:, None]
+    slot_of = jnp.sum(jnp.where(same, jnp.arange(1, slots + 1)[:, None], 0), axis=0)
+    slot_of = slot_of.reshape(ids_all.shape) - 1
+    places = jnp.where(inside & (slot_of >= 0), slot_of * half_rows + within % half_rows, -1)
+    active = keep_all[:, 0, 0] > 0.0
+    group_ids = jnp.arange(active.shape[0])
+    earlier = group_ids[None, :] < group_ids[:, None]
+    turn_of = jnp.where(
+        active,
+        jnp.sum(jnp.where(earlier & active[None, :], 1, 0), axis=1),
+        jnp.sum(jnp.where(active, 1, 0))
+        + jnp.sum(jnp.where(earlier & ~active[None, :], 1, 0), axis=1),
+    )
+    group_order = jnp.sum(
+        jnp.where(turn_of[None, :] == group_ids[:, None], group_ids[None, :], 0), axis=1
+    )
+    plan = jnp.concatenate(
+        [
+            jnp.stack(
+                [
+                    first_held,
+                    held,
+                    jnp.sum(jnp.where(active, 1, 0)),
+                    jnp.sum(jnp.where(places >= 0, 1, 0)),
+                ]
+            ),
+            group_order,
+        ]
+    ).astype(jnp.int32)
 
     table_slots = jnp.pad(master.astype(jnp.bfloat16), ((0, spare), (0, 0), (0, 0)))
     table = table_slots.reshape(-1, D)
@@ -1628,7 +1852,8 @@
     angles = freqs[:, None] * positions.astype(jnp.float32)[None, :]
     cosine, sine = jnp.cos(angles), jnp.sin(angles)
 
-    looked = look_up(span, row_ids, ids_all, table).reshape(order + (D,))
+    looked, ranks, picked = look_up(plan, row_ids, ids_all, places, table)
+    looked = looked.reshape(order + (D,))
     start, joined = reduce_rows(looked, (0, 14), weights_line(0, 1))
     table_one = as_table(joined)
     attention_table, up = table_one, (table_one, 1)
@@ -1691,12 +1916,12 @@
         normed = normed_next
 
     final_all = gather_all(normed, 3 + LAYERS)[0].reshape(-1, D)
-    powers, stats = head_forward(span, row_ids, labels_all, table, final_all)
+    powers, stats = head_forward(plan, row_ids, labels_all, table, final_all)
     home, log_totals = join_stats(
-        stats.reshape((2, tensors, groups, 8, LANES)), 4 + LAYERS
+        jnp.take(stats, turn_of, axis=0).reshape((2, tensors, groups, 8, LANES)), 4 + LAYERS
     )
     grad_final, grad_table = head_backward(
-        span,
+        plan,
         row_ids,
         labels_all,
         keep_all,
@@ -1781,7 +2006,9 @@
     )
     layer_grads = jnp.concatenate([grads for grads in layer_grads if grads is not None], axis=0)
     grad_start_all = grad_start_all.reshape(-1, D)
-    grad_table, table_squares = look_back(span, row_ids, ids_all, grad_start_all, grad_table)
+    grad_table, table_squares = look_back(
+        plan, row_ids, ids_all, ranks, picked, grad_start_all, grad_table
+    )
     values = layer_grads.astype(jnp.float32)
     layer_squares = jnp.sum(jnp.where(mine[:blocks][:, None, None], values * values, 0.0))
     keep = jnp.where(
@@ -1804,7 +2031,7 @@
     loss_sum, clip_norm = news[6][0, 0], news[6][0, 1]
     token_count = count[0, 0]
     new_master, new_first, new_second = update_slots(
-        plan, news[7], master, first_moment, second_moment, layer_grads, grad_table
+        slot_plan, news[7], master, first_moment, second_moment, layer_grads, grad_table
     )
     return (
         new_master,

time: 785 us -> 743 us (0.946)
  Pallas kernels: 722 us -> 673 us
    pallas_call x2, Pallas kernels: 129 us -> 107 us  [reduce_all(): pl.pallas_call(kernel, name='reduce_all', out_shape=[jax.ShapeDtypeStruct...]
    pallas_call x4, Pallas kernels: 121 us -> 107 us  [local_call(): pl.pallas_call(kernel, name=name, grid_spec=pltpu.PrefetchScalarGridSpec(...]
    pallas_call x1, Pallas kernels: 27.2 us -> 18.8 us  [join_stats(): pl.pallas_call(kernel, name='join_stats', out_shape=[jax.ShapeDtypeStruct...]
where the time goes in v7:
time: 743 us; the launch traced here: 739 us
  Pallas kernels  673 us (91%)
  local copies, waits for them, and re-layouts  37.8 us (5%)
  other arithmetic  22.8 us (3%)
    pallas_call x10, Pallas kernels, tensor_step(): pl.pallas_call(kernel, name=name, grid=(1,), out_shape=shapes, in_specs=i...  307 us
    pallas_call x4, Pallas kernels, local_call(): pl.pallas_call(kernel, name=name, grid_spec=pltpu.PrefetchScalarGridSpec(...  107 us
    pallas_call x2, Pallas kernels, reduce_all(): pl.pallas_call(kernel, name='reduce_all', out_shape=[jax.ShapeDtypeStruct...  107 us
    pallas_call x2, Pallas kernels, gather_all(): pl.pallas_call(kernel, name='gather_all', out_shape=[jax.ShapeDtypeStruct...  77.1 us
    pallas_call x1, Pallas kernels, update_slots(): pl.pallas_call(kernel, name='update_slots', grid_spec=pltpu.PrefetchScala...  34.1 us
    unnamed x89, local copies, waits for them, and re-layouts  21.5 us
    pallas_call x1, Pallas kernels, join_stats(): pl.pallas_call(kernel, name='join_stats', out_shape=[jax.ShapeDtypeStruct...  18.8 us

profile of v7, /device:TPU:0, one launch (start us, length us, event | category | flops | bytes accessed | tf_op | source)
XLA Modules:
  0.0 738.7 jit_solution(4166078780155222212)
XLA Ops:
  1.9 0.9 select_reduce_fusion.2
  2.9 1.3 select_reduce_fusion.7
  5.7 1.4 add_add_fusion.block_ref
  7.1 0.9 fusion.18
  8.1 9.1 %spread_tokens.1 = (s32[32,1,128]{2,1,0:T(1,128)}, s32[32,1,128]{2,1,0:T(1,128)}, f32[32,1,128]{2,1,0:T(1,128)}, f32[1,128]{1,0:T(1,128)}) custom-call(s32[16,128]{1,0:T(8,128)} %add_add_fusion.block_ref), custom_call_target="tpu_custom_call" | custom-call | flops 1000 | bytes 1000 | tf_op jit(solution)/shard_map/spread_tokens/pallas_call | solution.py:1130
  17.2 1.4 compare_reduce_fusion
  21.5 2.2 fusion.6
  23.7 1.9 concatenate.10.plan_ref
  26.7 1.4 pad.13.ids_ref
  28.1 4.4 convert_element_type.24
  32.4 2.8 pad.14
  35.3 5.3 gather_fusion
  40.5 4.3 select_select_fusion.refs_1_.refs_2_.refs_7_.refs_8_
  44.9 19.7 %look_up.1 = (bf16[4096,768]{1,0:T(8,128)(2,1)}, s32[32,1,128]{2,1,0:T(1,128)}, s32[8,768]{1,0:T(8,128)}) custom-call(s32[36]{0:T(128)} %concatenate.10.plan_ref, s32[3648,1]{1,0:T(8,128)} %pad.13.ids_ref, s32[32,1,128]{2,1,0:T(1,128)} %get-tuple-element.90.tokens_ref, s32[32,1,128]{2,1,0:T(1,128)} %get-tuple-element.173.places_ref, bf16[3648,768]{1,0:T(8,128)(2,1)} %bitcast.73), custom_call_target="tpu_custom_call" | custom-call | flops 1000 | bytes 1000 | tf_op jit(solution)/shard_map/look_up/pallas_call | solution.py:1375
  64.5 64.4 %reduce_all.2 = (f32[128,768]{1,0:T(8,128)}, bf16[16,2,48,768]{3,2,1,0:T(8,128)(2,1)}) custom-call(bf16[2,4,4,128,768]{4,3,2,1,0:T(8,128)(2,1)} %bitcast.93, bf16[48,48,768]{2,1,0:T(8,128)(2,1)} %select_select_fusion.refs_1_.refs_2_.refs_7_.refs_8_, bf16[48,48,768]{2,1,0:T(8,128)(2,1)} %select_select_fusion.refs_1_.refs_2_.refs_7_.refs_8_), custom_call_target="tpu_custom_call" | custom-call | flops 1000 | bytes 1000 | tf_op jit(solution)/shard_map/reduce_all/pallas_call | solution.py:817
  129.0 1.0 copy-done.1
  130.0 12.6 %normed.1.refs_0_.refs_1_ = bf16[4,128,768]{2,1,0:T(8,128)(2,1)S(1)} custom-call(f32[128,768]{1,0:T(8,128)S(1)} %copy-done.1, f32[1,768]{1,0:T(1,128)S(1)} %get-tuple-element.179.refs_1_.refs_12_), custom_call_target="tpu_custom_call" | custom-call | flops 1000 | bytes 1000 | tf_op jit(solution)/shard_map/normed/pallas_call | solution.py:225
  142.6 40.4 %inner_0.1 = (f32[128,768]{1,0:T(8,128)S(1)}, bf16[4,128,768]{2,1,0:T(8,128)(2,1)S(1)}, bf16[192,512]{1,0:T(8,128)(2,1)S(1)}, bf16[2,2,192,512]{3,2,1,0:T(8,128)...) custom-call(bf16[4,128,768]{2,1,0:T(8,128)(2,1)S(1)} %normed.1.refs_0_.refs_1_, ...), custom_call_target="tpu_custom_call" | custom-call | flops 1000 | bytes 1000 | tf_op jit(solution)/shard_map/inner_0/pallas_call | solution.py:225
  183.0 0.9 copy-done.15
  183.9 28.0 %outcome_0.1 = (f32[128,768]{1,0:T(8,128)S(1)}, f32[128,768]{1,0:T(8,128)S(1)}, bf16[4,128,768]{2,1,0:T(8,128)(2,1)S(1)}, f32[768,512]{1,0:T(8,128)}, bf16[768,512]{1,0:T(8,128)(2,1)S(1)}) custom-call(bf16[4,128,768]{2,1,0:T(8,128)(2,1)S(1)} %get-tuple-element.95.refs_0_.refs_1_, bf16[1536,768]{1,0:T(8,128)(2,1)} %bitcast.78, bf16[1536,768]{1,0:T(8,128)(2,1)} %bitcast.82, ...), custom_call_target="tpu_custom_call" | custom-call | flops 1000 | bytes 1000 | tf_op jit(solution)/shard_map/outcome_0/pallas_call | solution.py:225
  211.9 0.9 copy-done.16
  212.8 40.6 %inner_1.1 = (f32[128,768]{1,0:T(8,128)S(1)}, bf16[4,128,768]{2,1,0:T(8,128)(2,1)S(1)}, bf16[192,512]{1,0:T(8,128)(2,1)S(1)}, bf16[2,2,192,512]{3,2,1,0:T(8,128)...) custom-call(bf16[4,128,768]{2,1,0:T(8,128)(2,1)S(1)} %get-tuple-element.98.refs_, ...), custom_call_target="tpu_custom_call" | custom-call | flops 1000 | bytes 1000 | tf_op jit(solution)/shard_map/inner_1/pallas_call | solution.py:225
  253.4 0.9 copy-done.17
  254.3 17.0 %outcome_1.1 = (f32[128,768]{1,0:T(8,128)S(1)}, f32[128,768]{1,0:T(8,128)S(1)}, bf16[128,768]{1,0:T(8,128)(2,1)S(1)}, f32[768,512]{1,0:T(8,128)}, bf16[768,512]{1,0:T(8,128)(2,1)S(1)}) custom-call(bf16[4,128,768]{2,1,0:T(8,128)(2,1)S(1)} %get-tuple-element.100.refs_0_.refs_1_, bf16[1536,768]{1,0:T(8,128)(2,1)} %bitcast.88, bf16[1536,768]{1,0:T(8,128)(2,1)} %bitcast.89, ...), custom_call_target="tpu_custom_call" | custom-call | flops 1000 | bytes 1000 | tf_op jit(solution)/shard_map/outcome_1/pallas_call | solution.py:225
  272.1 34.0 %gather_all.2 = bf16[2,4,4,128,768]{4,3,2,1,0:T(8,128)(2,1)S(1)} custom-call(bf16[128,768]{1,0:T(8,128)(2,1)S(1)} %get-tuple-element.104.refs_0_), custom_call_target="tpu_custom_call" | custom-call | flops 1000 | bytes 1000 | tf_op jit(solution)/shard_map/gather_all/pallas_call | solution.py:957
  306.1 2.7 copy-done
  308.8 25.0 %head_forward.1 = (bf16[3648,4096]{1,0:T(8,128)(2,1)}, f32[32,8,128]{2,1,0:T(8,128)}) custom-call(s32[36]{0:T(128)} %concatenate.10.plan_ref, s32[3648,1]{1,0:T(8,128)} %pad.13.ids_ref, s32[32,1,128]{2,1,0:T(1,128)} %get-tuple-element.91.labels_ref, bf16[3648,768]{1,0:T(8,128)(2,1)} %bitcast.74, bf16[4096,768]{1,0:T(8,128)(2,1)} %bitcast.55, ...), custom_call_target="tpu_custom_call" | custom-call | flops 1000 | bytes 1000 | tf_op jit(solution)/shard_map/head_forward/pallas_call | solution.py:1375
  333.8 1.5 gather_fusion.1
  336.0 18.8 %join_stats.1 = (f32[8,128]{1,0:T(8,128)}, f32[2,4,4,8,128]{4,3,2,1,0:T(8,128)}) custom-call(f32[2,4,4,8,128]{4,3,2,1,0:T(8,128)} %broadcast_select_fusion.stats_ref), custom_call_target="tpu_custom_call" | custom-call | flops 1000 | bytes 1000 | tf_op jit(solution)/shard_map/join_stats/pallas_call | solution.py:1067
  354.9 40.2 %head_backward.1 = (bf16[32,128,768]{2,1,0:T(8,128)(2,1)}, f32[3648,768]{1,0:T(8,128)}) custom-call(s32[36]{0:T(128)} %concatenate.10.plan_ref, s32[3648,1]{1,0:T(8,128)} %pad.13.ids_ref, s32[32,1,128]{2,1,0:T(1,128)} %get-tuple-element.91.labels_ref, f32[32,1,128]{2,1,0:T(1,128)} %get-tuple-element.89.keep_ref, f32[32,8,128]{2,1,0:T(8,128)} %get-tuple-element.105.stats_ref, ...), custom_call_target="tpu_custom_call" | custom-call | flops 1000 | bytes 1000 | tf_op jit(solution)/shard_map/head_backward/pallas_call | solution.py:1375
  395.1 42.1 %reduce_all.3.refs_0_ = f32[128,768]{1,0:T(8,128)} custom-call(bf16[2,4,4,128,768]{4,3,2,1,0:T(8,128)(2,1)} %bitcast.92), custom_call_target="tpu_custom_call" | custom-call | flops 1000 | bytes 1000 | tf_op jit(solution)/shard_map/reduce_all/pallas_call | solution.py:817
  437.2 1.0 copy-done.13
  438.2 12.8 %top_back.1 = (f32[128,768]{1,0:T(8,128)S(1)}, f32[128,768]{1,0:T(8,128)S(1)}, f32[1,768]{1,0:T(1,128)S(1)}, bf16[4,128,768]{2,1,0:T(8,128)(2,1)S(1)}) custom-call(f32[128,768]{1,0:T(8,128)S(1)} %copy-done.13, f32[128,768]{1,0:T(8,128)S(1)} %get-tuple-element.109.refs_1_, f32[1,768]{1,0:T(1,128)S(1)} %get-tuple-element.175.refs_4_.refs_2_, f32[5]{0:T(128)S(1)} %copy-done.25), custom_call_target="tpu_custom_call" | custom-call | flops 1000 | bytes 1000 | tf_op jit(solution)/shard_map/top_back/pallas_call | solution.py:225
  451.6 26.4 %inner_back_1.1 = (f32[128,768]{1,0:T(8,128)S(1)}, f32[1,768]{1,0:T(1,128)S(1)}, bf16[4,128,768]{2,1,0:T(8,128)(2,1)S(1)}, bf16[16,48,768]{2,1,0:T(8,128)(2,1)}) custom-call(bf16[4,128,768]{2,1,0:T(8,128)(2,1)S(1)} %get-tuple-element.110.refs_0_, bf16[4,128,768]{2,1,0:T(8,128)(2,1)S(1)} %get-tuple-element.100.refs_0_.refs_1_, bf16[1536,768]{1,0:T(8,128)(2,1)} %bitcast.90, ...), custom_call_target="tpu_custom_call" | custom-call | flops 1000 | bytes 1000 | tf_op jit(solution)/shard_map/inner_back_1/pallas_call | solution.py:225
  478.0 0.9 copy-done.19
  478.9 49.1 %stream_back_1.1 = (f32[128,768]{1,0:T(8,128)S(1)}, f32[128,768]{1,0:T(8,128)S(1)}, f32[1,768]{1,0:T(1,128)S(1)}, bf16[4,128,768]{2,1,0:T(8,128)(2,1)S(1)}, bf16...) custom-call(bf16[4,128,768]{2,1,0:T(8,128)(2,1)} %copy-done.19, bf16[4,128,768]{2,1,0:T(8,128)(2,1)} %copy-done.7, ...), custom_call_target="tpu_custom_call" | custom-call | flops 1000 | bytes 1000 | tf_op jit(solution)/shard_map/stream_back_1/pallas_call | solution.py:225
  528.0 33.8 %inner_back_0.1 = (f32[128,768]{1,0:T(8,128)S(1)}, f32[1,768]{1,0:T(1,128)S(1)}, bf16[4,128,768]{2,1,0:T(8,128)(2,1)S(1)}, bf16[16,48,768]{2,1,0:T(8,128)(2,1)}, bf16[8,48,768]{2,1,0:T(8,128)(2,1)S(1)}) custom-call(bf16[4,128,768]{2,1,0:T(8,128)(2,1)S(1)} %get-tuple-element.122.refs_0_, bf16[4,128,768]{2,1,0:T(8,128)(2,1)} %copy-done.6, ...), custom_call_target="tpu_custom_call" | custom-call | flops 1000 | bytes 1000 | tf_op jit(solution)/shard_map/inner_back_0/pallas_call | solution.py:225
  561.9 0.9 copy-done.18
  563.6 46.1 %stream_back_0.1 = (f32[128,768]{1,0:T(8,128)}, f32[128,768]{1,0:T(8,128)}, f32[1,768]{1,0:T(1,128)S(1)}, bf16[128,768]{1,0:T(8,128)(2,1)S(1)}, bf16[8,48,768]{2...) custom-call(bf16[4,128,768]{2,1,0:T(8,128)(2,1)} %copy-done.18, bf16[4,128,768]{2,1,0:T(8,128)(2,1)} %copy-done.3, ...), custom_call_target="tpu_custom_call" | custom-call | flops 1000 | bytes 1000 | tf_op jit(solution)/shard_map/stream_back_0/pallas_call | solution.py:225
  609.7 43.1 %gather_all.3 = (bf16[2,4,4,128,768]{4,3,2,1,0:T(8,128)(2,1)S(1)}, bf16[8,48,768]{2,1,0:T(8,128)(2,1)S(1)}) custom-call(bf16[128,768]{1,0:T(8,128)(2,1)S(1)} %get-tuple-element.144.refs_0_, bf16[8,48,768]{2,1,0:T(8,128)(2,1)S(1)} %get-tuple-element.145.refs_1_), custom_call_target="tpu_custom_call" | custom-call | flops 1000 | bytes 1000 | tf_op jit(solution)/shard_map/gather_all/pallas_call | solution.py:957
  652.9 2.7 copy-done.4
  656.4 22.4 %look_back.1 = (f32[3648,768]{1,0:T(8,128)}, f32[8,768]{1,0:T(8,128)}) custom-call(s32[36]{0:T(128)} %concatenate.10.plan_ref, s32[3648,1]{1,0:T(8,128)} %pad.13.ids_ref, s32[32,1,128]{2,1,0:T(1,128)} %get-tuple-element.90.tokens_ref, s32[32,1,128]{2,1,0:T(1,128)} %get-tuple-element.142.ranks_ref, s32[8,768]{1,0:T(8,128)} %get-tuple-element.143.picked_ref, ...), custom_call_target="tpu_custom_call" | custom-call | flops 1000 | bytes 1000 | tf_op jit(solution)/shard_map/look_back/pallas_call | solution.py:1375
  678.7 1.2 constant_dynamic-update-slice_fusion.3
  680.0 1.3 constant_dynamic-update-slice_fusion.2
  681.5 2.5 select_reduce_fusion
  684.0 13.6 %finish.1 = (f32[5,768]{1,0:T(8,128)}, f32[5,768]{1,0:T(8,128)}, f32[5,768]{1,0:T(8,128)}, f32[1,5]{1,0:T(1,128)}, f32[1,5]{1,0:T(1,128)}, /*index=5*/f32[1,5]{1,0:T(1,128)}, f32[1,128]{1,0:T(1,128)}, f32[8,128]{1,0:T(8,128)}) custom-call(f32[1,768]{1,0:T(1,128)} %copy-done.31, f32[1,768]{1,0:T(1,128)} %copy-done.30, f32[1,768]{1,0:T(1,128)} %copy-done.29, ...), custom_call_target="tpu_custom_call" | custom-call | flops 1000 | bytes 1000 | tf_op jit(solution)/shard_map/finish/pallas_call | solution.py:1231
  697.6 1.3 fusion.19
  699.6 34.1 %update_slots.1 = (f32[67,48,768]{2,1,0:T(8,128)}, f32[67,48,768]{2,1,0:T(8,128)}, f32[67,48,768]{2,1,0:T(8,128)}) custom-call(s32[2,68]{1,0:T(2,128)S(1)} %pad.12.plan_ref, f32[8,128]{1,0:T(8,128)S(1)} %copy-done.26, f32[67,48,768]{2,1,0:T(8,128)} %master_ref.1, f32[67,48,768]{2,1,0:T(8,128)} %first_ref.1, f32[67,48,768]{2,1,0:T(8,128)} %second_ref.1, ...), custom_call_target="tpu_custom_call" | custom-call | flops 1000 | bytes 1000 | tf_op jit(solution)/shard_map/update_slots/pallas_call | solution.py:1285
  (111 shorter events, 12.9 us)
Async XLA Ops:
  129.0 1.0 copy-start.1
  142.6 40.4 %copy-start.3 = (bf16[4,128,768]{2,1,0:T(8,128)(2,1)}, bf16[4,128,768]{2,1,0:T(8,128)(2,1)S(1)}, u32[]{:S(2)}) copy-start(bf16[4,128,768]{2,1,0:T(8,128)(2,1)S(1)} %normed.1.refs_0_.refs_1_) | copy-start | bytes 2359300
  142.6 41.3 %copy-start.25 = (f32[5]{0:T(128)S(1)}, f32[5]{0:T(128)}, u32[]{:S(2)}) copy-start(f32[5]{0:T(128)} %refs_15_.2) | copy-start | bytes 64
  183.0 0.9 copy-start.15
  183.9 69.5 %copy-start.6 = (bf16[4,128,768]{2,1,0:T(8,128)(2,1)}, bf16[4,128,768]{2,1,0:T(8,128)(2,1)S(1)}, u32[]{:S(2)}) copy-start(bf16[4,128,768]{2,1,0:T(8,128)(2,1)S(1)} %get-tuple-element.95.refs_0_.refs_1_) | copy-start | bytes 2359300
  183.9 69.5 %copy-start.8 = (f32[128,768]{1,0:T(8,128)}, f32[128,768]{1,0:T(8,128)S(1)}, u32[]{:S(2)}) copy-start(f32[128,768]{1,0:T(8,128)S(1)} %get-tuple-element.97.refs_3_.refs_7_) | copy-start | bytes 1179652
  211.9 0.9 copy-start.16
  212.8 40.7 %copy-start.7 = (bf16[4,128,768]{2,1,0:T(8,128)(2,1)}, bf16[4,128,768]{2,1,0:T(8,128)(2,1)S(1)}, u32[]{:S(2)}) copy-start(bf16[4,128,768]{2,1,0:T(8,128)(2,1)S(1)} %get-tuple-element.98.refs_0_.refs_1_) | copy-start | bytes 2359300
  212.8 41.6 %copy-start.14 = (f32[128,768]{1,0:T(8,128)}, f32[128,768]{1,0:T(8,128)S(1)}, u32[]{:S(2)}) copy-start(f32[128,768]{1,0:T(8,128)S(1)} %get-tuple-element.103.refs_6_) | copy-start | bytes 1179652
  212.8 41.6 %copy-start.2 = (f32[128,768]{1,0:T(8,128)S(1)}, f32[128,768]{1,0:T(8,128)}, u32[]{:S(2)}) copy-start(f32[128,768]{1,0:T(8,128)} %get-tuple-element.93.refs_0_.refs_5_.refs_11_) | copy-start | bytes 1179652
  253.4 0.9 copy-start.17
  254.3 51.8 %copy-start.11 = (f32[128,768]{1,0:T(8,128)}, f32[128,768]{1,0:T(8,128)S(1)}, u32[]{:S(2)}) copy-start(f32[128,768]{1,0:T(8,128)S(1)} %get-tuple-element.102.refs_3_.refs_7_) | copy-start | bytes 1179652
  271.3 0.8 copy-start.24
  272.1 34.0 %copy-start.20 = (bf16[768,512]{1,0:T(8,128)(2,1)}, bf16[768,512]{1,0:T(8,128)(2,1)S(1)}, u32[]{:S(2)}) copy-start(bf16[768,512]{1,0:T(8,128)(2,1)S(1)} %get-tuple-element.112.refs_5_) | copy-start | bytes 2359300
  306.1 2.7 copy-start
  395.1 56.5 %copy-start.12 = (f32[128,768]{1,0:T(8,128)S(1)}, f32[128,768]{1,0:T(8,128)}, u32[]{:S(2)}) copy-start(f32[128,768]{1,0:T(8,128)} %copy-done.11) | copy-start | bytes 1179652
  437.2 1.0 copy-start.13
  451.0 0.6 copy-start.27
  451.6 112.0 %copy-start.5 = (f32[128,768]{1,0:T(8,128)}, f32[128,768]{1,0:T(8,128)S(1)}, u32[]{:S(2)}) copy-start(f32[128,768]{1,0:T(8,128)S(1)} %get-tuple-element.120.refs_13_.refs_14_.refs_9_) | copy-start | bytes 1179652
  478.0 0.9 copy-start.19
  478.9 49.1 %copy-start.28 = (f32[1,768]{1,0:T(1,128)}, f32[1,768]{1,0:T(1,128)S(1)}, u32[]{:S(2)}) copy-start(f32[1,768]{1,0:T(1,128)S(1)} %get-tuple-element.138.refs_3_) | copy-start | bytes 9220
  478.9 49.1 %copy-start.9 = (f32[128,768]{1,0:T(8,128)S(1)}, f32[128,768]{1,0:T(8,128)}, u32[]{:S(2)}) copy-start(f32[128,768]{1,0:T(8,128)} %copy-done.8) | copy-start | bytes 1179652
  528.0 33.9 %copy-start.29 = (f32[1,768]{1,0:T(1,128)}, f32[1,768]{1,0:T(1,128)S(1)}, u32[]{:S(2)}) copy-start(f32[1,768]{1,0:T(1,128)S(1)} %get-tuple-element.137.refs_2_) | copy-start | bytes 9220
  528.0 35.6 %copy-start.10 = (f32[128,768]{1,0:T(8,128)}, f32[128,768]{1,0:T(8,128)S(1)}, u32[]{:S(2)}) copy-start(f32[128,768]{1,0:T(8,128)S(1)} %get-tuple-element.133.refs_13_.refs_8_) | copy-start | bytes 1179652
  561.9 0.9 copy-start.18
  562.8 0.8 copy-start.21
  563.6 46.1 %copy-start.30 = (f32[1,768]{1,0:T(1,128)}, f32[1,768]{1,0:T(1,128)S(1)}, u32[]{:S(2)}) copy-start(f32[1,768]{1,0:T(1,128)S(1)} %get-tuple-element.136.refs_1_) | copy-start | bytes 9220
  609.7 69.0 %copy-start.31 = (f32[1,768]{1,0:T(1,128)}, f32[1,768]{1,0:T(1,128)S(1)}, u32[]{:S(2)}) copy-start(f32[1,768]{1,0:T(1,128)S(1)} %get-tuple-element.135.refs_0_) | copy-start | bytes 9220
  652.8 2.7 copy-start.4
  655.5 0.8 copy-start.23
  678.7 2.6 copy-start.22
  678.7 2.7 copy-start.32
  698.9 0.7 copy-start.26
  699.6 34.1 %copy-start.35 = (f32[5,768]{1,0:T(8,128)S(1)}, f32[5,768]{1,0:T(8,128)}, u32[]{:S(2)}) copy-start(f32[5,768]{1,0:T(8,128)} %get-tuple-element.206) | copy-start | bytes 46084
  699.6 34.7 %copy-start.34 = (f32[5,768]{1,0:T(8,128)S(1)}, f32[5,768]{1,0:T(8,128)}, u32[]{:S(2)}) copy-start(f32[5,768]{1,0:T(8,128)} %get-tuple-element.207) | copy-start | bytes 46084
  699.6 35.4 %copy-start.33 = (f32[5,768]{1,0:T(8,128)S(1)}, f32[5,768]{1,0:T(8,128)}, u32[]{:S(2)}) copy-start(f32[5,768]{1,0:T(8,128)} %get-tuple-element.208) | copy-start | bytes 46084
  699.6 36.0 %copy-start.39 = (f32[1,5]{1,0:T(1,128)S(1)}, f32[1,5]{1,0:T(1,128)}, u32[]{:S(2)}) copy-start(f32[1,5]{1,0:T(1,128)} %get-tuple-element.162) | copy-start | bytes 64
  699.6 36.5 %copy-start.38 = (f32[1,5]{1,0:T(1,128)S(1)}, f32[1,5]{1,0:T(1,128)}, u32[]{:S(2)}) copy-start(f32[1,5]{1,0:T(1,128)} %get-tuple-element.163) | copy-start | bytes 64
  699.6 37.0 %copy-start.37 = (f32[1,5]{1,0:T(1,128)S(1)}, f32[1,5]{1,0:T(1,128)}, u32[]{:S(2)}) copy-start(f32[1,5]{1,0:T(1,128)} %get-tuple-element.164) | copy-start | bytes 64
  699.6 37.5 %copy-start.36 = (f32[1,128]{1,0:T(1,128)S(1)}, f32[1,128]{1,0:T(1,128)}, u32[]{:S(2)}) copy-start(f32[1,128]{1,0:T(1,128)} %get-tuple-element.153.refs_14_) | copy-start | bytes 1540

commit v8 on v7

--- a/solution.py
+++ b/solution.py
@@ -690,16 +690,23 @@
         lax.fori_loop(0, self.chunks, one, 0)
 
 
-def reduce_all(terms, collective_id, line=None):
+def reduce_all(terms, collective_id, line=None, tail=None):
     _, tensors, groups, count, _ = terms.shape
     half = count // 2
+    function, extras, scalars, outs = tail or (None, [], [], [])
+    extra_specs = [VMEM_SPEC] * len(extras)
+    extra_specs += [pl.BlockSpec(memory_space=pltpu.SMEM)] * len(scalars)
+    extras = list(extras) + list(scalars)
 
     def kernel(*refs):
         refs = list(refs)
         terms_ref = refs.pop(0)
         source_refs = [refs.pop(0) for _ in line.operands] if line else []
-        out_ref = refs.pop(0)
+        extra_refs = [refs.pop(0) for _ in extras]
+        out_refs = [refs.pop(0) for _ in range(len(outs) or 1)]
+        full = refs.pop(0) if tail else None
         joined_ref = refs.pop(0) if line else None
+        tail_sems = [refs.pop(0) for _ in range(2)] if tail else None
         (
             near, own, mid, sums, mid_in, far, far_in,
             own_sems, near_send, near_recv, mid_send, mid_recv, far_send, far_recv,
@@ -804,7 +811,25 @@
         for place, copy in enumerate(far_copies):
             copy.wait_recv()
             total = total + far_in[place].astype(jnp.float32)
-        out_ref[...] = total
+        if tail:
+            results = function(total, *extra_refs)
+            for ref, value in zip(out_refs, results):
+                ref[...] = value
+            full[part] = results[len(outs)].astype(jnp.bfloat16)
+            last_copies = [
+                send(
+                    full.at[part],
+                    full.at[part],
+                    tail_sems[0].at[step],
+                    tail_sems[1].at[step],
+                    {"tensor": peer},
+                )
+                for step, peer in enumerate(parts)
+            ]
+            for copy in last_copies:
+                copy.wait()
+        else:
+            out_refs[0][...] = total
         for copy in near_copies + far_copies + [
             copy for row in first_copies + second_copies for copy in row
         ]:
@@ -814,13 +839,19 @@
 
     block = (count, D)
     dma = pltpu.SemaphoreType.DMA
+    results = [jax.ShapeDtypeStruct(*out) for out in outs]
+    if tail:
+        results.append(jax.ShapeDtypeStruct((tensors,) + block, jnp.bfloat16))
+    else:
+        results.append(jax.ShapeDtypeStruct(block, jnp.float32))
     return pl.pallas_call(
         kernel,
         name="reduce_all",
-        out_shape=[jax.ShapeDtypeStruct(block, jnp.float32)] + ([line.out_shape] if line else []),
-        in_specs=[pl.BlockSpec(memory_space=pl.ANY)] + (line.in_specs if line else []),
-        out_specs=[pl.BlockSpec(memory_space=pltpu.VMEM)] + ([line.out_spec] if line else []),
-        scratch_shapes=[pltpu.VMEM((groups, tensors) + block, jnp.bfloat16)] * 3
+        out_shape=results + ([line.out_shape] if line else []),
+        in_specs=[pl.BlockSpec(memory_space=pl.ANY)] + (line.in_specs if line else []) + extra_specs,
+        out_specs=[VMEM_SPEC] * len(results) + ([line.out_spec] if line else []),
+        scratch_shapes=[dma((tensors - 1,))] * (2 if tail else 0)
+        + [pltpu.VMEM((groups, tensors) + block, jnp.bfloat16)] * 3
         + [
             pltpu.VMEM((groups, 2, half, D), jnp.bfloat16),
             pltpu.VMEM((groups, 6, half, D), jnp.bfloat16),
@@ -839,7 +870,7 @@
         compiler_params=pltpu.CompilerParams(
             collective_id=collective_id, has_side_effects=True, vmem_limit_bytes=56 << 20
         ),
-    )(terms, *(line.operands if line else []))
+    )(terms, *(line.operands if line else []), *extras)
 
 
 def gather_all(block, collective_id, line=None):
@@ -973,24 +1004,35 @@
         + (line.scratch if line else []),
         cost_estimate=SHORT,
         compiler_params=pltpu.CompilerParams(
-            collective_id=collective_id, has_side_effects=True, vmem_limit_bytes=40 << 20
+            collective_id=collective_id, has_side_effects=True, vmem_limit_bytes=60 << 20
         ),
     )(block, *(line.operands if line else []))
 
 
-def reduce_rows(terms, ids, line=None):
+def reduce_rows(name, terms, ids, line, function, extras, scalars, outs):
     count, groups = terms.shape[3], terms.shape[2]
     pieces = max(1, groups // 4)
+    if pieces == 1:
+        return reduce_all(terms, ids[0], line, (function, extras, scalars, outs))
     part = count // pieces
-    sums, joined = [], None
+    sums, joined = [], []
     for i in range(pieces):
-        piece = terms[:, :, :, i * part : (i + 1) * part] if pieces > 1 else terms
-        if i == 0 and line:
-            total, joined = reduce_all(piece, ids[1], line)
-        else:
-            (total,) = reduce_all(piece, ids[0])
+        piece = terms[:, :, :, i * part : (i + 1) * part]
+        total, *joined_now = reduce_all(piece, ids[1 if i and line else 0], None if i else line)
         sums.append(total)
-    return jnp.concatenate(sums, axis=0) if pieces > 1 else sums[0], joined
+        joined += joined_now
+    total = jnp.concatenate(sums, axis=0)
+    results = tensor_step(
+        name,
+        lambda _, total_ref, *refs: function(total_ref, *refs),
+        None,
+        [total] + list(extras),
+        scalars,
+        outs,
+        True,
+        ids[2],
+    )
+    return list(results) + joined
 
 
 def join_stats(stats, collective_id):
@@ -1149,12 +1191,12 @@
     )(block)
 
 
-def finish(gain_grads, states, grad_ys, home, keep, table_squares, layer_squares, count, smalls, collective_id):
+def finish(gain_grads, states, grad_ys, home, keep, table_squares, count, smalls, collective_id):
     tensors, groups = lax.axis_size("tensor"), lax.axis_size("dp")
     block = (8, D)
     gain_rows = 2 * LAYERS + 1
     operands = list(gain_grads) + list(states) + list(grad_ys) + [
-        home, keep, table_squares, layer_squares, count
+        home, keep, table_squares, count
     ] + list(smalls)
 
     def kernel(*refs):
@@ -1162,7 +1204,7 @@
         gain_refs = [refs.pop(0) for _ in gain_grads]
         state_refs = [refs.pop(0) for _ in states]
         grad_refs = [refs.pop(0) for _ in grad_ys]
-        home_ref, keep_ref, table_ref, layer_ref, count_ref = [refs.pop(0) for _ in range(5)]
+        home_ref, keep_ref, table_ref, count_ref = [refs.pop(0) for _ in range(4)]
         small_refs = [refs.pop(0) for _ in smalls]
         out_refs = [refs.pop(0) for _ in range(8)]
         near, mid, far, near_send, near_recv, mid_send, mid_recv, far_send, far_recv = refs
@@ -1180,7 +1222,7 @@
                 values.append(jnp.sum(grad * state_refs[level][...], keepdims=True))
         loss = jnp.where(keep_ref[...] > 0.0, home_ref[0:1, :] - home_ref[1:2, :], 0.0)
         values.append(jnp.sum(loss, keepdims=True))
-        values.append(jnp.sum(table_ref[...], keepdims=True) + layer_ref[...])
+        values.append(jnp.sum(table_ref[...], keepdims=True))
         lane = lax.broadcasted_iota(jnp.int32, (1, D), 1)
         row = jnp.zeros((1, D), jnp.float32)
         for place, value in enumerate(values):
@@ -1254,63 +1296,57 @@
     )(*operands)
 
 
-SLOT_STEP = 4
-
-
-def update_slots(plan, factor, master, first, second, layer_grads, grad_table):
+SLOT_STEP = 8
+PREPARE_STEP = 20
+
+
+def prepare(slot_block, master, blocks):
     slots, half_rows, _ = master.shape
-    steps = -(-slots // SLOT_STEP)
-    plan = jnp.pad(plan, ((0, 0), (0, steps * SLOT_STEP - slots)))
-
-    def kernel(plan_ref, factor_ref, master_ref, first_ref, second_ref, *rest):
-        layer_refs = rest[:SLOT_STEP]
-        table_ref, new_master, new_first, new_second = rest[SLOT_STEP:]
-        for place in range(SLOT_STEP):
-            kind = plan_ref[0, pl.program_id(0) * SLOT_STEP + place]
-            grad = table_ref[place * half_rows : (place + 1) * half_rows, :]
-            grad = jnp.where(kind == 0, layer_refs[place][0].astype(jnp.float32), grad)
-            grad = jnp.where(kind >= 0, grad * factor_ref[0:1, 0:1], 0.0)
-            values = adam_update(
-                master_ref[place],
-                first_ref[place],
-                second_ref[place],
-                grad,
-                RATE_MATRIX,
-                DECAY_MATRIX,
-            )
-            for ref, value in zip((new_master, new_first, new_second), values):
-                ref[place] = value
-
-    slot = pl.BlockSpec((SLOT_STEP, half_rows, D), lambda step, plan: (step, 0, 0))
+    total = slot_block.shape[0]
+    steps = -(-total // PREPARE_STEP)
+    slot_block = jnp.pad(slot_block, (0, steps * PREPARE_STEP - total), constant_values=-1)
+    rows = PREPARE_STEP * half_rows
+
+    def kernel(plan_ref, master_ref, table_ref, halves_ref):
+        @pl.when(pl.program_id(0) == 0)
+        def _():
+            halves_ref[...] = jnp.zeros_like(halves_ref)
+
+        for place in range(PREPARE_STEP):
+            slot = pl.program_id(0) * PREPARE_STEP + place
+            value = jnp.where(slot < slots, master_ref[place], 0.0).astype(jnp.bfloat16)
+            table_ref[place * half_rows : (place + 1) * half_rows, :] = value
+
+            block = plan_ref[slot]
+
+            @pl.when((block >= 0) & (block < blocks))
+            def _():
+                halves_ref[block] = value
+
+    last = (slots - 1) // PREPARE_STEP
     return pl.pallas_call(
         kernel,
-        name="update_slots",
+        name="prepare",
         grid_spec=pltpu.PrefetchScalarGridSpec(
             num_scalar_prefetch=1,
             grid=(steps,),
-            in_specs=[pl.BlockSpec((8, LANES), lambda step, plan: (0, 0)), slot, slot, slot]
-            + [
+            in_specs=[
                 pl.BlockSpec(
-                    (1, half_rows, D),
-                    lambda step, plan, place=place: (plan[1, step * SLOT_STEP + place], 0, 0),
+                    (PREPARE_STEP, half_rows, D), lambda step, plan: (jnp.minimum(step, last), 0, 0)
                 )
-                for place in range(SLOT_STEP)
-            ]
-            + [pl.BlockSpec((SLOT_STEP * half_rows, D), lambda step, plan: (step, 0))],
-            out_specs=[slot] * 3,
+            ],
+            out_specs=[
+                pl.BlockSpec((rows, D), lambda step, plan: (step, 0)),
+                pl.BlockSpec((blocks, half_rows, D), lambda step, plan: (0, 0, 0)),
+            ],
         ),
-        out_shape=[jax.ShapeDtypeStruct(master.shape, jnp.float32)] * 3,
+        out_shape=[
+            jax.ShapeDtypeStruct((total * half_rows, D), jnp.bfloat16),
+            jax.ShapeDtypeStruct((blocks, half_rows, D), jnp.bfloat16),
+        ],
         cost_estimate=SHORT,
-        compiler_params=pltpu.CompilerParams(vmem_limit_bytes=48 << 20),
-    )(
-        plan,
-        factor,
-        master,
-        first,
-        second,
-        *[layer_grads] * SLOT_STEP,
-        grad_table,
-    )
+        compiler_params=pltpu.CompilerParams(vmem_limit_bytes=60 << 20),
+    )(slot_block, master)
 
 
 TILE = TILE_GROUPS * LANES
@@ -1653,83 +1689,135 @@
     )
 
 
-def look_back(plan, row_ids, tokens, ranks, picked, grad_start, grad_table):
+def look_back(
+    plan, slot_plan, slots, row_ids, tokens, ranks, picked, grad_start, grad_table, layer_grads
+):
     rows, groups = grad_table.shape[0], tokens.shape[0]
     steps = groups // TILE_GROUPS
-
-    def kernel(
-        plan_ref, ids_ref, tokens_ref, ranks_ref, picked_ref, grad_ref, table_ref, out_ref, squares_ref, acc
-    ):
-        tile = pl.program_id(0)
+    half_rows = layer_grads[0].shape[1]
+    block = SLOT_STEP * half_rows
+    kinds = len(layer_grads)
+
+    def kernel(plan_ref, slot_ref, ids_ref, tokens_ref, ranks_ref, picked_ref, grad_ref, table_ref, *rest):
+        layer_refs = rest[:kinds]
+        slots_ref, squares_ref, acc, held, out_ref = rest[kinds:]
+        step = pl.program_id(0)
         few = plan_ref[3] <= PICKED
 
-        @pl.when(tile == 0)
+        @pl.when(step == 0)
         def _():
             acc[...] = jnp.zeros_like(acc)
-            out_ref[...] = table_ref[...]
-
-        @pl.when(few)
+            squares_ref[...] = jnp.zeros_like(squares_ref)
+
+        @pl.when((step < steps) & few)
         def _():
-            acc[...] += times(picks(tile_row(ranks_ref, tile)), grad_ref[...])
-
-        @pl.when(jnp.logical_not(few))
+            acc[...] += times(picks(tile_row(ranks_ref, step)), grad_ref[...])
+
+        @pl.when((step < steps) & jnp.logical_not(few))
         def _():
-            wanted = tile_row(tokens_ref, tile)
-            grads = grad_ref[...]
-
-            def one(step, carry):
-                chunk = chunk_of(plan_ref, step)
-                out_ref[chunk, :] += times(ones_where(ids_ref[chunk, :] == wanted), grads)
-                return carry
-
-            lax.fori_loop(0, chunks_of(plan_ref), one, 0)
-
-        @pl.when(few & (tile == steps - 1))
+            held[step] = grad_ref[...]
+
+        @pl.when(step >= steps)
         def _():
-            grads = acc[...].astype(jnp.bfloat16)
-            place = picked_ref[0:1, :]
-
-            def one(step, carry):
-                out_ref[chunk_of(plan_ref, step), :] += times(
-                    rows_picked(plan_ref, step, place), grads
-                )
-                return carry
-
-            lax.fori_loop(0, chunks_of(plan_ref), one, 0)
-
-        @pl.when(tile == steps - 1)
-        def _():
-            def square(step, total):
-                values = out_ref[chunk_of(plan_ref, step), :]
-                values = (values * values).reshape(ROW_STEP // 8, 8, D).sum(axis=0)
-                return total + values
-
-            squares_ref[...] = lax.fori_loop(
-                0, chunks_of(plan_ref), square, jnp.zeros((8, D), jnp.float32)
-            )
+            start = (step - steps) * block
+
+            @pl.when(few)
+            def _():
+                row = lax.broadcasted_iota(jnp.int32, (block, PICKED), 0) + start
+                hits = ones_where(row == picked_ref[0:1, :])
+                out_ref[...] = table_ref[...] + times(hits, acc[...].astype(jnp.bfloat16))
+
+            @pl.when(jnp.logical_not(few))
+            def _():
+                out_ref[...] = table_ref[...]
+                ids = ids_ref[pl.ds(pl.multiple_of(start, 16), block), :]
+
+                def one(tile, carry):
+                    hits = ones_where(ids == tile_row(tokens_ref, tile))
+                    out_ref[...] += times(hits, held[tile])
+                    return carry
+
+                lax.fori_loop(0, steps, one, 0)
+
+            for place in range(SLOT_STEP):
+                slot = (step - steps) * SLOT_STEP + place
+                kind = slot_ref[0, slot]
+                part = slice(place * half_rows, (place + 1) * half_rows)
+
+                for index in range(kinds):
+
+                    @pl.when(kind == index)
+                    def _():
+                        layer = layer_refs[index][slot_ref[1 + index, slot]]
+                        out_ref[part, :] = layer.astype(jnp.float32)
+
+                @pl.when(kind < 0)
+                def _():
+                    out_ref[part, :] = jnp.zeros((half_rows, D), jnp.float32)
+
+                slots_ref[place] = out_ref[part, :]
+
+            values = out_ref[...]
+            squares_ref[...] += (values * values).reshape(block // 8, 8, D).sum(axis=0)
+
+    def fixed(shape):
+        return pl.BlockSpec(
+            shape, lambda step, plan, slot: (0,) * len(shape), pipeline_mode=pl.Buffered(1)
+        )
 
     lanes = (groups, 1, LANES)
-    return local_call(
-        "look_back",
+    row_spec = pl.BlockSpec((block, D), lambda step, plan, slot: (jnp.maximum(step - steps, 0), 0))
+    return pl.pallas_call(
         kernel,
-        steps,
-        plan,
-        (row_ids, tokens, ranks, picked, grad_start, grad_table),
-        [
-            whole((rows, 1)),
-            whole(lanes),
-            whole(lanes),
-            whole((8, PICKED)),
-            ROWS_SPEC,
-            whole((rows, D)),
-        ],
-        [
-            jax.ShapeDtypeStruct((rows, D), jnp.float32),
+        name="look_back",
+        grid_spec=pltpu.PrefetchScalarGridSpec(
+            num_scalar_prefetch=2,
+            grid=(steps + -(-slots // SLOT_STEP),),
+            in_specs=[
+                fixed((rows, 1)),
+                fixed(lanes),
+                fixed(lanes),
+                fixed((8, PICKED)),
+                pl.BlockSpec((TILE, D), lambda step, plan, slot: (jnp.minimum(step, steps - 1), 0)),
+                row_spec,
+            ]
+            + [fixed(grads.shape) for grads in layer_grads],
+            out_specs=[
+                pl.BlockSpec(
+                    (SLOT_STEP, half_rows, D),
+                    lambda step, plan, slot: (jnp.maximum(step - steps, 0), 0, 0),
+                ),
+                fixed((8, D)),
+            ],
+            scratch_shapes=[
+                pltpu.VMEM((PICKED, D), jnp.float32),
+                pltpu.VMEM((steps, TILE, D), jnp.bfloat16),
+                pltpu.VMEM((block, D), jnp.float32),
+            ],
+        ),
+        out_shape=[
+            jax.ShapeDtypeStruct((slots, half_rows, D), jnp.float32),
             jax.ShapeDtypeStruct((8, D), jnp.float32),
         ],
-        [whole((rows, D)), whole((8, D))],
-        [pltpu.VMEM((PICKED, D), jnp.float32)],
-    )
+        cost_estimate=SHORT,
+        compiler_params=pltpu.CompilerParams(vmem_limit_bytes=60 << 20),
+    )(
+        plan,
+        slot_plan,
+        row_ids,
+        tokens,
+        ranks,
+        picked,
+        grad_start,
+        grad_table,
+        *layer_grads,
+    )
+
+
+def grads_home(level):
+    if level == 0:
+        return [(0, 1), (1, 0), (0, 0)]
+    return [(2 * level, 0), (2 * level + 1, 0), (2 * level + 1, 1)]
 
 
 def body(
@@ -1778,14 +1866,22 @@
     )
     row_ids = jnp.where(slot_block[:, None] >= blocks, row_ids, -1).reshape(-1, 1)
     spare = -(-ROW_STEP // half_rows)
+    spare += -(slots + spare) % SLOT_STEP
     row_ids = jnp.pad(row_ids, ((0, spare * half_rows), (0, 0)), constant_values=-1)
     held = jnp.sum(jnp.where(mine, 1, 0)) * half_rows
     first_held = jnp.sum(jnp.where(mine & (block_ids < blocks), 1, 0)) * half_rows
+    slot_block_all = jnp.pad(slot_block, (0, spare), constant_values=-1).astype(jnp.int32)
+    third = layer_blocks // 3
+    which, within = slot_block_all // third, slot_block_all % third
+    homes = [home for level in range(LAYERS) for home in grads_home(level)]
+    arrays = 1 + max(array for array, _ in homes)
+    kind, index = jnp.full(which.shape, -1), jnp.zeros_like(which)
+    for place, (array, part) in enumerate(homes):
+        kind = jnp.where(which == place, array, kind)
+        index = jnp.where(which == place, within + part * third, index)
+    kind = jnp.where(slot_block_all >= blocks, arrays, jnp.where(slot_block_all < 0, -1, kind))
     slot_plan = jnp.stack(
-        [
-            jnp.where(slot_block < 0, -1, jnp.where(slot_block < blocks, 0, 1)),
-            jnp.where(slot_block < blocks, jnp.maximum(slot_block, 0), 0),
-        ]
+        [kind] + [jnp.where(kind == array, index, 0) for array in range(arrays)]
     ).astype(jnp.int32)
 
     packed = jnp.concatenate(
@@ -1832,13 +1928,7 @@
         ]
     ).astype(jnp.int32)
 
-    table_slots = jnp.pad(master.astype(jnp.bfloat16), ((0, spare), (0, 0), (0, 0)))
-    table = table_slots.reshape(-1, D)
-
-    halves = jnp.where(
-        mine[:blocks][:, None, None], jnp.take(table_slots, slot_rank[:blocks], axis=0), 0.0
-    ).astype(jnp.bfloat16)
-    third = layer_blocks // 3
+    table, halves = prepare(slot_block_all, master, blocks)
 
     def weights_line(*starts):
         return Line([(halves, start * third, third) for start in starts], True)
@@ -1854,15 +1944,11 @@
 
     looked, ranks, picked = look_up(plan, row_ids, ids_all, places, table)
     looked = looked.reshape(order + (D,))
-    start, joined = reduce_rows(looked, (0, 14), weights_line(0, 1))
-    table_one = as_table(joined)
-    attention_table, up = table_one, (table_one, 1)
-    tables = []
     gain = [gains[i : i + 1] for i in range(2 * LAYERS + 1)]
     piece = ((share, D), jnp.float32)
 
-    def normed_of(total, stream, gain_row):
-        return (layer_norm_parts(stream)[0] * gain_row,)
+    def normed_of(total, gain_row):
+        return (total[...], layer_norm_parts(total[...])[0] * gain_row[...])
 
     def inner_of(total, stream, gain_row):
         inner = stream + total
@@ -1876,12 +1962,16 @@
             stream = stream + scalars[base + source] * state
         return (outcome, stream, layer_norm_parts(stream)[0] * gain_row)
 
-    (normed,) = tensor_step("normed", normed_of, None, (start, gain[0]), (), [], True, 1)
+    start, normed, joined = reduce_rows(
+        "normed", looked, (14, 18, 1), weights_line(0, 1), normed_of, [gain[0]], [], [piece]
+    )
+    table_one = as_table(joined)
+    attention_table, up = table_one, (table_one, 1)
+    tables = []
     states, streams, inners, kept_all = [start], [start], [], []
     for level in range(LAYERS):
         here, last = 3 * level, level == LAYERS - 1
-        carried = [] if last else [here + 3]
-        carried += [here + 1, here + 2] if level else [here + 2]
+        carried = [here + 1, here + 2] if level else [here + 2]
         inner, normed_two, queries, both, logs, attended, joined = tensor_step(
             f"inner_{level}",
             inner_of,
@@ -1898,8 +1988,7 @@
         down = (joined, len(carried) - 1)
         up = (joined, len(carried) - 2) if level else up
         tables.append((attention_table, up, down))
-        attention_table = joined
-        outcome, stream, normed_next, hidden, activated = tensor_step(
+        outcome, stream, normed_next, hidden, activated, *joined = tensor_step(
             f"outcome_{level}",
             partial(outcome_of, (level + 1) * (level + 2) // 2 - 1),
             unit_work(normed_two, up, down),
@@ -1908,7 +1997,9 @@
             [piece, piece] + ([((share, D), jnp.bfloat16)] if last else []),
             not last,
             3 + level,
+            None if last else weights_line(here + 3),
         )
+        attention_table = None if last else as_table(joined[0])
         inners.append(inner)
         kept_all.append((normed, kept, normed_two, (hidden, activated)))
         states.append(outcome)
@@ -1931,12 +2022,12 @@
         final_all,
         powers,
     )
-    grad_final, _ = reduce_rows(grad_final.reshape(order + (D,)), (0, 14))
+    grad_final = grad_final.reshape(order + (D,))
 
     row = ((1, D), jnp.float32)
 
-    def top_of(total, grad, stream, gain_row, scalars):
-        grad_top, grad_gain = norm_pull(grad, gain_row, stream)
+    def top_of(total, stream, gain_row, scalars):
+        grad_top, grad_gain = norm_pull(total[...], gain_row[...], stream[...])
         grad_state = scalars[MIX_WEIGHTS - 1] * grad_top
         return (grad_top, grad_state, grad_gain, grad_state)
 
@@ -1957,16 +2048,16 @@
 
     grad_ys = [None] * (LAYERS + 1)
     gain_grads = [None] * (2 * LAYERS + 1)
-    layer_grads, attention_grads = [None] * (3 * LAYERS), None
-    grad_ys[LAYERS], grad_state, gain_grads[2 * LAYERS], grad_branch = tensor_step(
+    layer_grads, attention_grads = [None] * (2 * LAYERS), None
+    grad_ys[LAYERS], grad_state, gain_grads[2 * LAYERS], grad_branch = reduce_rows(
         "top_back",
+        grad_final,
+        (0, 0, 5 + LAYERS),
+        None,
         top_of,
-        None,
-        (grad_final, streams[LAYERS], gain[2 * LAYERS]),
-        (mix,),
+        [streams[LAYERS], gain[2 * LAYERS]],
+        [mix],
         [piece, piece, row],
-        True,
-        5 + LAYERS,
     )
     for level in reversed(range(LAYERS)):
         normed, kept, normed_two, unit_kept = kept_all[level]
@@ -1983,7 +2074,7 @@
             None if attention_grads is None else Line([(attention_grads, 0, third)], False),
         )
         if summed:
-            layer_grads[3 * (level + 1)] = summed[0]
+            layer_grads[2 * (level + 1)] = summed[0]
         grad_ys[level], grad_state, gain_grads[2 * level], grad_branch, attention_grads, summed = (
             tensor_step(
                 f"stream_back_{level}",
@@ -1996,21 +2087,27 @@
                 [piece, piece, row] + ([] if level else [((share, D), jnp.bfloat16)]),
                 level > 0,
                 7 + LAYERS + level,
-                Line([(unit_grads, 0, 2 * third)], False),
+                Line([(unit_grads, 0, 2 * third if level else third)], False),
             )
         )
-        layer_grads[3 * level + 1] = summed
+        layer_grads[2 * level + 1] = summed
 
     grad_start_all, layer_grads[0] = gather_all(
-        grad_branch, 13, Line([(attention_grads, 0, third)], False)
-    )
-    layer_grads = jnp.concatenate([grads for grads in layer_grads if grads is not None], axis=0)
+        grad_branch, 13, Line([(unit_grads, third, third), (attention_grads, 0, third)], False)
+    )
     grad_start_all = grad_start_all.reshape(-1, D)
-    grad_table, table_squares = look_back(
-        plan, row_ids, ids_all, ranks, picked, grad_start_all, grad_table
-    )
-    values = layer_grads.astype(jnp.float32)
-    layer_squares = jnp.sum(jnp.where(mine[:blocks][:, None, None], values * values, 0.0))
+    owned, table_squares = look_back(
+        plan,
+        slot_plan,
+        slots,
+        row_ids,
+        ids_all,
+        ranks,
+        picked,
+        grad_start_all,
+        grad_table,
+        layer_grads,
+    )
     keep = jnp.where(
         tensor_part * share + jnp.arange(share) < real_counts[0], 1.0, 0.0
     ).astype(jnp.float32)
@@ -2021,7 +2118,6 @@
         home,
         keep[None],
         table_squares,
-        layer_squares.reshape(1, 1),
         count,
         (gains, gains_first, gains_second, mix[None], mix_first[None], mix_second[None]),
         7 + 2 * LAYERS,
@@ -2030,8 +2126,9 @@
     new_mix, new_mix_first, new_mix_second = [value[0] for value in news[3:6]]
     loss_sum, clip_norm = news[6][0, 0], news[6][0, 1]
     token_count = count[0, 0]
-    new_master, new_first, new_second = update_slots(
-        slot_plan, news[7], master, first_moment, second_moment, layer_grads, grad_table
+    owned = owned * news[7][0, 0]
+    new_master, new_first, new_second = adam_update(
+        master, first_moment, second_moment, owned, RATE_MATRIX, DECAY_MATRIX
     )
     return (
         new_master,

time: 743 us -> 736 us (level)
  Pallas kernels: 673 us -> 653 us
  other arithmetic: 22.8 us -> 38.7 us
  local copies, waits for them, and re-layouts: 37.8 us -> 30.1 us
    pallas_call x4 -> x3, Pallas kernels: 107 us -> 58.8 us  [local_call(): pl.pallas_call(kernel, name=name, grid_spec=pltpu.PrefetchScalarGridSpec(...]
    pallas_call x3 -> x4, Pallas kernels: 141 us -> 175 us  [the longest x2 142 us: reduce_all(): pl.pallas_call(kernel, name='reduce_all', out_shape=results + ([line.out_...]
    pallas_call x10 -> x8, Pallas kernels: 307 us -> 273 us  [tensor_step(): pl.pallas_call(kernel, name=name, grid=(1,), out_shape=shapes, in_specs=i...]
    sub x0 -> x1, other arithmetic: none -> 26.5 us  [adam_update(): weight - rate * (first_hat / (jnp.sqrt(second_hat) + ADAM_EPS) + decay *...]
    pallas_call x2, Pallas kernels: 77.1 us -> 94.7 us  [gather_all(): pl.pallas_call(kernel, name='gather_all', out_shape=[jax.ShapeDtypeStruct...]
    pallas_call x1, Pallas kernels: 18.8 us -> 29.3 us  [join_stats(): pl.pallas_call(kernel, name='join_stats', out_shape=[jax.ShapeDtypeStruct...]
    unnamed x89 -> x110, local copies, waits for them, and re-layouts: 21.5 us -> 21.3 us
where the time goes in v8:
time: 736 us; the launch traced here: 727 us
  Pallas kernels  653 us (89%)
  other arithmetic  38.7 us (5%)
  local copies, waits for them, and re-layouts  30.1 us (4%)
    pallas_call x8, Pallas kernels, tensor_step(): pl.pallas_call(kernel, name=name, grid=(1,), out_shape=shapes, in_specs=i...  273 us
    pallas_call x2, Pallas kernels, reduce_all(): pl.pallas_call(kernel, name='reduce_all', out_shape=results + ([line.out_...  142 us
    pallas_call x2, Pallas kernels, gather_all(): pl.pallas_call(kernel, name='gather_all', out_shape=[jax.ShapeDtypeStruct...  94.7 us
    pallas_call x3, Pallas kernels, local_call(): pl.pallas_call(kernel, name=name, grid_spec=pltpu.PrefetchScalarGridSpec(...  58.8 us
    pallas_call x1, Pallas kernels, join_stats(): pl.pallas_call(kernel, name='join_stats', out_shape=[jax.ShapeDtypeStruct...  29.3 us
    sub x1, other arithmetic, adam_update(): weight - rate * (first_hat / (jnp.sqrt(second_hat) + ADAM_EPS) + decay *...  26.5 us
    pallas_call x1, Pallas kernels, look_back(): pl.pallas_call(kernel, name='look_back', grid_spec=pltpu.PrefetchScalarGr...  23.2 us
    unnamed x110, local copies, waits for them, and re-layouts  21.3 us

profile of v8, /device:TPU:0, one launch (start us, length us, event | category | flops | bytes accessed | tf_op | source)
XLA Modules:
  0.0 726.8 jit_solution(13609566793043657388)
XLA Ops:
  1.4 1.4 add_add_fusion.block_ref
  2.7 9.1 %spread_tokens.1 = (s32[32,1,128]{2,1,0:T(1,128)}, s32[32,1,128]{2,1,0:T(1,128)}, f32[32,1,128]{2,1,0:T(1,128)}, f32[1,128]{1,0:T(1,128)}) custom-call(s32[16,128]{1,0:T(8,128)} %add_add_fusion.block_ref), custom_call_target="tpu_custom_call" | custom-call | flops 1000 | bytes 1000 | tf_op jit(solution)/shard_map/spread_tokens/pallas_call | solution.py:1172
  11.8 1.4 compare_reduce_fusion
  14.8 1.3 select_reduce_fusion.6
  16.1 0.9 select_reduce_fusion.1
  17.2 0.8 fusion.8
  18.2 2.2 fusion.7
  21.8 1.9 concatenate.7.plan_ref
  23.7 0.8 select_n.261
  24.6 1.4 pad.9.ids_ref
  26.5 9.2 %prepare.1 = (bf16[3840,768]{1,0:T(8,128)(2,1)}, bf16[48,48,768]{2,1,0:T(8,128)(2,1)}) custom-call(s32[80]{0:T(128)} %get-tuple-element.193.plan_ref, f32[67,48,768]{2,1,0:T(8,128)} %master_ref.1), custom_call_target="tpu_custom_call" | custom-call | flops 1000 | bytes 1000 | tf_op jit(solution)/shard_map/prepare/pallas_call | solution.py:1327
  35.7 16.4 %look_up.1 = (bf16[4096,768]{1,0:T(8,128)(2,1)}, s32[32,1,128]{2,1,0:T(1,128)}, s32[8,768]{1,0:T(8,128)}) custom-call(s32[36]{0:T(128)} %concatenate.7.plan_ref, s32[3840,1]{1,0:T(8,128)} %pad.9.ids_ref, s32[32,1,128]{2,1,0:T(1,128)} %get-tuple-element.91.tokens_ref, s32[32,1,128]{2,1,0:T(1,128)} %get-tuple-element.179.places_ref, ...), custom_call_target="tpu_custom_call" | custom-call | flops 1000 | bytes 1000 | tf_op jit(solution)/shard_map/look_up/pallas_call | solution.py:1411
  52.7 78.5 %reduce_all.2 = (f32[128,768]{1,0:T(8,128)}, bf16[4,128,768]{2,1,0:T(8,128)(2,1)}, bf16[16,2,48,768]{3,2,1,0:T(8,128)(2,1)}) custom-call(bf16[2,4,4,128,768]{4,3,2,1,0:T(8,128)(2,1)} %bitcast.90, bf16[48,48,768]{2,1,0:T(8,128)(2,1)} %get-tuple-element.97.refs_1_.refs_2_.refs_7_.refs_8_, ...), custom_call_target="tpu_custom_call" | custom-call | flops 1000 | bytes 1000 | tf_op jit(solution)/shard_map/reduce_all/pallas_call | solution.py:847
  131.6 1.0 copy-done
  132.6 1.1 copy-done.5
  133.7 37.2 %inner_0.1 = (f32[128,768]{1,0:T(8,128)S(1)}, bf16[4,128,768]{2,1,0:T(8,128)(2,1)S(1)}, bf16[192,512]{1,0:T(8,128)(2,1)S(1)}, bf16[2,2,192,512]{3,2,1,0:T(8,128)...) custom-call(bf16[4,128,768]{2,1,0:T(8,128)(2,1)S(1)} %copy-done.5, ...), custom_call_target="tpu_custom_call" | custom-call | flops 1000 | bytes 1000 | tf_op jit(solution)/shard_map/inner_0/pallas_call | solution.py:225
  170.9 0.9 copy-done.15
  171.8 32.7 %outcome_0.1 = (f32[128,768]{1,0:T(8,128)S(1)}, f32[128,768]{1,0:T(8,128)S(1)}, bf16[4,128,768]{2,1,0:T(8,128)(2,1)S(1)}, f32[768,512]{1,0:T(8,128)}, bf16[768,5...) custom-call(bf16[4,128,768]{2,1,0:T(8,128)(2,1)S(1)} %get-tuple-element.101.refs_0_.refs_1_, ...), custom_call_target="tpu_custom_call" | custom-call | flops 1000 | bytes 1000 | tf_op jit(solution)/shard_map/outcome_0/pallas_call | solution.py:225
  204.6 0.9 copy-done.16
  205.5 40.5 %inner_1.1 = (f32[128,768]{1,0:T(8,128)S(1)}, bf16[4,128,768]{2,1,0:T(8,128)(2,1)S(1)}, bf16[192,512]{1,0:T(8,128)(2,1)S(1)}, bf16[2,2,192,512]{3,2,1,0:T(8,128)...) custom-call(bf16[4,128,768]{2,1,0:T(8,128)(2,1)S(1)} %get-tuple-element.104.refs, ...), custom_call_target="tpu_custom_call" | custom-call | flops 1000 | bytes 1000 | tf_op jit(solution)/shard_map/inner_1/pallas_call | solution.py:225
  246.0 0.9 copy-done.17
  248.2 18.0 %outcome_1.1 = (f32[128,768]{1,0:T(8,128)S(1)}, f32[128,768]{1,0:T(8,128)S(1)}, bf16[128,768]{1,0:T(8,128)(2,1)S(1)}, f32[768,512]{1,0:T(8,128)}, bf16[768,512]{1,0:T(8,128)(2,1)S(1)}) custom-call(bf16[4,128,768]{2,1,0:T(8,128)(2,1)S(1)} %get-tuple-element.107.refs_0_.refs_1_, bf16[1536,768]{1,0:T(8,128)(2,1)} %bitcast.82, bf16[1536,768]{1,0:T(8,128)(2,1)} %bitcast.83, ...), custom_call_target="tpu_custom_call" | custom-call | flops 1000 | bytes 1000 | tf_op jit(solution)/shard_map/outcome_1/pallas_call | solution.py:225
  267.1 0.9 copy-done.20
  267.9 0.8 copy-done.25
  268.7 0.8 copy-done.26
  270.1 35.6 %gather_all.2 = bf16[2,4,4,128,768]{4,3,2,1,0:T(8,128)(2,1)} custom-call(bf16[128,768]{1,0:T(8,128)(2,1)} %copy-done.27), custom_call_target="tpu_custom_call" | custom-call | flops 1000 | bytes 1000 | tf_op jit(solution)/shard_map/gather_all/pallas_call | solution.py:988
  305.8 15.9 %head_forward.1 = (bf16[3840,4096]{1,0:T(8,128)(2,1)}, f32[32,8,128]{2,1,0:T(8,128)}) custom-call(s32[36]{0:T(128)} %concatenate.7.plan_ref, s32[3840,1]{1,0:T(8,128)} %pad.9.ids_ref, s32[32,1,128]{2,1,0:T(1,128)} %get-tuple-element.95.labels_ref, bf16[3840,768]{1,0:T(8,128)(2,1)} %get-tuple-element.92.table_ref, bf16[4096,768]{1,0:T(8,128)(2,1)} %bitcast.60, ...), custom_call_target="tpu_custom_call" | custom-call | flops 1000 | bytes 1000 | tf_op jit(solution)/shard_map/head_forward/pallas_call | solution.py:1411
  321.7 1.5 gather_fusion
  323.4 0.8 broadcast_select_fusion.stats_ref
  324.2 29.3 %join_stats.1 = (f32[8,128]{1,0:T(8,128)}, f32[2,4,4,8,128]{4,3,2,1,0:T(8,128)}) custom-call(f32[2,4,4,8,128]{4,3,2,1,0:T(8,128)} %broadcast_select_fusion.stats_ref), custom_call_target="tpu_custom_call" | custom-call | flops 1000 | bytes 1000 | tf_op jit(solution)/shard_map/join_stats/pallas_call | solution.py:1109
  353.5 26.6 %head_backward.1 = (bf16[32,128,768]{2,1,0:T(8,128)(2,1)}, f32[3840,768]{1,0:T(8,128)}) custom-call(s32[36]{0:T(128)} %concatenate.7.plan_ref, s32[3840,1]{1,0:T(8,128)} %pad.9.ids_ref, s32[32,1,128]{2,1,0:T(1,128)} %get-tuple-element.95.labels_ref, f32[32,1,128]{2,1,0:T(1,128)} %get-tuple-element.90.keep_ref, f32[32,8,128]{2,1,0:T(8,128)} %get-tuple-element.112.stats_ref, ...), custom_call_target="tpu_custom_call" | custom-call | flops 1000 | bytes 1000 | tf_op jit(solution)/shard_map/head_backward/pallas_call | solution.py:1411
  380.2 63.9 %reduce_all.3 = (f32[128,768]{1,0:T(8,128)}, f32[128,768]{1,0:T(8,128)}, f32[1,768]{1,0:T(1,128)}, bf16[4,128,768]{2,1,0:T(8,128)(2,1)}) custom-call(bf16[2,4,4,128,768]{4,3,2,1,0:T(8,128)(2,1)} %bitcast.91, f32[128,768]{1,0:T(8,128)} %copy-done.26, f32[1,768]{1,0:T(1,128)} %copy-done.36, f32[5]{0:T(128)} %refs_15_.2), custom_call_target="tpu_custom_call" | custom-call | flops 1000 | bytes 1000 | tf_op jit(solution)/shard_map/reduce_all/pallas_call | solution.py:847
  444.2 1.2 copy-done.21
  445.4 1.0 copy-done.24
  446.3 26.7 %inner_back_1.1 = (f32[128,768]{1,0:T(8,128)S(1)}, f32[1,768]{1,0:T(1,128)S(1)}, bf16[4,128,768]{2,1,0:T(8,128)(2,1)S(1)}, bf16[16,48,768]{2,1,0:T(8,128)(2,1)}) custom-call(bf16[4,128,768]{2,1,0:T(8,128)(2,1)S(1)} %copy-done.21, bf16[4,128,768]{2,1,0:T(8,128)(2,1)S(1)} %get-tuple-element.107.refs_0_.refs_1_, bf16[1536,768]{1,0:T(8,128)(2,1)} %bitcast.84, ...), custom_call_target="tpu_custom_call" | custom-call | flops 1000 | bytes 1000 | tf_op jit(solution)/shard_map/inner_back_1/pallas_call | solution.py:225
  473.1 0.9 copy-done.19
  474.0 1.0 copy-done.2
  475.0 49.3 %stream_back_1.1 = (f32[128,768]{1,0:T(8,128)S(1)}, f32[128,768]{1,0:T(8,128)S(1)}, f32[1,768]{1,0:T(1,128)S(1)}, bf16[4,128,768]{2,1,0:T(8,128)(2,1)S(1)}, bf16...) custom-call(bf16[4,128,768]{2,1,0:T(8,128)(2,1)} %copy-done.19, bf16[4,128,768]{2,1,0:T(8,128)(2,1)} %copy-done.4, ...), custom_call_target="tpu_custom_call" | custom-call | flops 1000 | bytes 1000 | tf_op jit(solution)/shard_map/stream_back_1/pallas_call | solution.py:225
  524.3 33.9 %inner_back_0.1 = (f32[128,768]{1,0:T(8,128)S(1)}, f32[1,768]{1,0:T(1,128)S(1)}, bf16[4,128,768]{2,1,0:T(8,128)(2,1)S(1)}, bf16[16,48,768]{2,1,0:T(8,128)(2,1)}, bf16[8,48,768]{2,1,0:T(8,128)(2,1)S(1)}) custom-call(bf16[4,128,768]{2,1,0:T(8,128)(2,1)S(1)} %get-tuple-element.129.refs_0_, bf16[4,128,768]{2,1,0:T(8,128)(2,1)} %copy-done.6, ...), custom_call_target="tpu_custom_call" | custom-call | flops 1000 | bytes 1000 | tf_op jit(solution)/shard_map/inner_back_0/pallas_call | solution.py:225
  558.2 0.9 copy-done.18
  559.1 0.8 copy-done.22
  559.9 35.1 %stream_back_0.1 = (f32[128,768]{1,0:T(8,128)}, f32[128,768]{1,0:T(8,128)}, f32[1,768]{1,0:T(1,128)S(1)}, bf16[128,768]{1,0:T(8,128)(2,1)S(1)}, bf16[8,48,768]{2...) custom-call(bf16[4,128,768]{2,1,0:T(8,128)(2,1)} %copy-done.18, bf16[4,128,768]{2,1,0:T(8,128)(2,1)} %get-tuple-element.98.refs_0_.refs_1_, ...), custom_call_target="tpu_custom_call" | custom-call | flops 1000 | bytes 1000 | tf_op jit(solution)/shard_map/stream_back_0/pallas_call | solution.py:225
  595.0 0.8 copy-done.23
  597.0 59.1 %gather_all.3 = (bf16[2,4,4,128,768]{4,3,2,1,0:T(8,128)(2,1)}, bf16[16,48,768]{2,1,0:T(8,128)(2,1)}) custom-call(bf16[128,768]{1,0:T(8,128)(2,1)} %copy-done.34, bf16[16,48,768]{2,1,0:T(8,128)(2,1)} %get-tuple-element.141.refs_16_.refs_1_, bf16[8,48,768]{2,1,0:T(8,128)(2,1)} %copy-done.23), custom_call_target="tpu_custom_call" | custom-call | flops 1000 | bytes 1000 | tf_op jit(solution)/shard_map/gather_all/pallas_call | solution.py:988
  656.8 23.2 %look_back.1 = (f32[67,48,768]{2,1,0:T(8,128)}, f32[8,768]{1,0:T(8,128)}) custom-call(s32[36]{0:T(128)} %concatenate.7.plan_ref, s32[5,80]{1,0:T(8,128)} %stack.39.slot_ref, s32[3840,1]{1,0:T(8,128)} %pad.9.ids_ref, s32[32,1,128]{2,1,0:T(1,128)} %get-tuple-element.91.tokens_ref, s32[32,1,128]{2,1,0:T(1,128)} %get-tuple-element.93.ranks_ref, ...), custom_call_target="tpu_custom_call" | custom-call | flops 1000 | bytes 1000 | tf_op jit(solution)/shard_map/look_back/pallas_call | solution.py:1770
  680.6 12.9 %finish.1 = (f32[5,768]{1,0:T(8,128)}, f32[5,768]{1,0:T(8,128)}, f32[5,768]{1,0:T(8,128)}, f32[1,5]{1,0:T(1,128)}, f32[1,5]{1,0:T(1,128)}, /*index=5*/f32[1,5]{1,0:T(1,128)}, f32[1,128]{1,0:T(1,128)}, f32[8,128]{1,0:T(8,128)}) custom-call(f32[1,768]{1,0:T(1,128)} %copy-done.42, f32[1,768]{1,0:T(1,128)} %copy-done.41, f32[1,768]{1,0:T(1,128)} %copy-done.40, ...), custom_call_target="tpu_custom_call" | custom-call | flops 1000 | bytes 1000 | tf_op jit(solution)/shard_map/finish/pallas_call | solution.py:1273
  693.4 1.2 slice.36
  694.7 26.5 %multiply_subtract_fusion = (f32[67,48,768]{2,1,0:T(8,128)}, f32[67,48,768]{2,1,0:T(8,128)}, f32[67,48,768]{2,1,0:T(8,128)}) fusion(f32[67,48,768]{2,1,0:T(8,128)} %master_ref.1, f32[67,48,768]{2,1,0:T(8,128)} %get-tuple-element.150, f32[]{:T(128)} %bitcast.31, f32[67,48,768]{2,1,0:T(8,128)} %param.18, f32[67,48,768]{2,1,0:T(8,128)} %param.19), kind=kLoop, calls=%fused_computation.3 | loop fusion | flops 39518208 | bytes 69156864 | tf_op jit(solution)/shard_map/sub | solution.py:53
  (125 shorter events, 13.0 us)
Async XLA Ops:
  24.6 27.5 %copy-start.43 = (f32[5,768]{1,0:T(8,128)S(1)}, f32[5,768]{1,0:T(8,128)}, u32[]{:S(2)}) copy-start(f32[5,768]{1,0:T(8,128)} %refs_14_.3) | copy-start | bytes 46084
  52.7 195.5 %copy-start.36 = (f32[1,768]{1,0:T(1,128)}, f32[1,768]{1,0:T(1,128)S(1)}, u32[]{:S(2)}) copy-start(f32[1,768]{1,0:T(1,128)S(1)} %get-tuple-element.181.refs_4_.refs_2_) | copy-start | bytes 9220
  52.7 119.1 %copy-start.37 = (f32[5]{0:T(128)S(1)}, f32[5]{0:T(128)}, u32[]{:S(2)}) copy-start(f32[5]{0:T(128)} %refs_15_.2) | copy-start | bytes 64
  131.6 1.0 copy-start
  132.6 1.1 copy-start.5
  170.9 0.9 copy-start.15
  171.8 33.6 %copy-start.10 = (f32[128,768]{1,0:T(8,128)}, f32[128,768]{1,0:T(8,128)S(1)}, u32[]{:S(2)}) copy-start(f32[128,768]{1,0:T(8,128)S(1)} %get-tuple-element.103.refs_3_.refs_7_) | copy-start | bytes 1179652
  171.8 33.6 %copy-start.28 = (bf16[192,512]{1,0:T(8,128)(2,1)}, bf16[192,512]{1,0:T(8,128)(2,1)S(1)}, u32[]{:S(2)}) copy-start(bf16[192,512]{1,0:T(8,128)(2,1)S(1)} %get-tuple-element.138.refs_7_) | copy-start | bytes 589828
  171.8 94.5 %copy-start.6 = (bf16[4,128,768]{2,1,0:T(8,128)(2,1)}, bf16[4,128,768]{2,1,0:T(8,128)(2,1)S(1)}, u32[]{:S(2)}) copy-start(bf16[4,128,768]{2,1,0:T(8,128)(2,1)S(1)} %get-tuple-element.101.refs_0_.refs_1_) | copy-start | bytes 2359300
  171.8 76.4 %copy-start.1 = (f32[128,768]{1,0:T(8,128)S(1)}, f32[128,768]{1,0:T(8,128)}, u32[]{:S(2)}) copy-start(f32[128,768]{1,0:T(8,128)} %get-tuple-element.100.refs_5_.refs_11_) | copy-start | bytes 1179652
  204.5 0.9 copy-start.16
  205.5 60.8 %copy-start.14 = (f32[128,768]{1,0:T(8,128)}, f32[128,768]{1,0:T(8,128)S(1)}, u32[]{:S(2)}) copy-start(f32[128,768]{1,0:T(8,128)S(1)} %get-tuple-element.110.refs_6_) | copy-start | bytes 1179652
  205.5 100.3 %copy-start.4 = (bf16[4,128,768]{2,1,0:T(8,128)(2,1)}, bf16[4,128,768]{2,1,0:T(8,128)(2,1)S(1)}, u32[]{:S(2)}) copy-start(bf16[4,128,768]{2,1,0:T(8,128)(2,1)S(1)} %get-tuple-element.104.refs_0_.refs_1_) | copy-start | bytes 2359300
  205.5 100.3 %copy-start.7 = (f32[128,768]{1,0:T(8,128)}, f32[128,768]{1,0:T(8,128)S(1)}, u32[]{:S(2)}) copy-start(f32[128,768]{1,0:T(8,128)S(1)} %get-tuple-element.106.refs_5_.refs_11_) | copy-start | bytes 1179652
  246.0 0.9 copy-start.17
  246.9 0.7 copy-start.30
  266.3 0.8 copy-start.12
  267.1 0.9 copy-start.20
  267.9 0.8 copy-start.25
  268.7 0.8 copy-start.26
  353.5 90.6 %copy-start.13 = (f32[128,768]{1,0:T(8,128)S(1)}, f32[128,768]{1,0:T(8,128)}, u32[]{:S(2)}) copy-start(f32[128,768]{1,0:T(8,128)} %copy-done.12) | copy-start | bytes 1179652
  380.2 93.8 %copy-start.8 = (f32[128,768]{1,0:T(8,128)S(1)}, f32[128,768]{1,0:T(8,128)}, u32[]{:S(2)}) copy-start(f32[128,768]{1,0:T(8,128)} %copy-done.7) | copy-start | bytes 1179652
  380.2 93.8 %copy-start.31 = (bf16[192,512]{1,0:T(8,128)(2,1)S(1)}, bf16[192,512]{1,0:T(8,128)(2,1)}, u32[]{:S(2)}) copy-start(bf16[192,512]{1,0:T(8,128)(2,1)} %copy-done.30) | copy-start | bytes 589828
  380.2 93.8 %copy-start.33 = (bf16[192,512]{1,0:T(8,128)(2,1)S(1)}, bf16[192,512]{1,0:T(8,128)(2,1)}, u32[]{:S(2)}) copy-start(bf16[192,512]{1,0:T(8,128)(2,1)} %copy-done.32) | copy-start | bytes 589828
  380.2 93.8 %copy-start.38 = (f32[5]{0:T(128)S(1)}, f32[5]{0:T(128)}, u32[]{:S(2)}) copy-start(f32[5]{0:T(128)} %refs_15_.2) | copy-start | bytes 64
  444.1 80.1 %copy-start.11 = (f32[128,768]{1,0:T(8,128)S(1)}, f32[128,768]{1,0:T(8,128)}, u32[]{:S(2)}) copy-start(f32[128,768]{1,0:T(8,128)} %copy-done.10) | copy-start | bytes 1179652
  444.2 1.2 copy-start.21
  445.3 1.0 copy-start.24
  446.3 113.5 %copy-start.3 = (f32[128,768]{1,0:T(8,128)S(1)}, f32[128,768]{1,0:T(8,128)}, u32[]{:S(2)}) copy-start(f32[128,768]{1,0:T(8,128)} %get-tuple-element.127.refs_13_.refs_14_.refs_9_) | copy-start | bytes 1179652
  446.3 113.5 %copy-start.29 = (bf16[192,512]{1,0:T(8,128)(2,1)S(1)}, bf16[192,512]{1,0:T(8,128)(2,1)}, u32[]{:S(2)}) copy-start(bf16[192,512]{1,0:T(8,128)(2,1)} %copy-done.28) | copy-start | bytes 589828
  473.0 0.9 copy-start.19
  473.9 121.0 %copy-start.39 = (f32[1,768]{1,0:T(1,128)}, f32[1,768]{1,0:T(1,128)S(1)}, u32[]{:S(2)}) copy-start(f32[1,768]{1,0:T(1,128)S(1)} %get-tuple-element.154.refs_3_) | copy-start | bytes 9220
  473.9 86.0 %copy-start.35 = (f32[1,768]{1,0:T(1,128)S(1)}, f32[1,768]{1,0:T(1,128)}, u32[]{:S(2)}) copy-start(f32[1,768]{1,0:T(1,128)} %get-tuple-element.185.refs_3_.refs_12_) | copy-start | bytes 9220
  474.0 1.0 copy-start.2
  524.2 131.9 %copy-start.9 = (f32[128,768]{1,0:T(8,128)}, f32[128,768]{1,0:T(8,128)S(1)}, u32[]{:S(2)}) copy-start(f32[128,768]{1,0:T(8,128)S(1)} %get-tuple-element.140.refs_13_.refs_8_) | copy-start | bytes 1179652
  524.2 131.9 %copy-start.40 = (f32[1,768]{1,0:T(1,128)}, f32[1,768]{1,0:T(1,128)S(1)}, u32[]{:S(2)}) copy-start(f32[1,768]{1,0:T(1,128)S(1)} %get-tuple-element.153.refs_2_) | copy-start | bytes 9220
  558.2 0.9 copy-start.18
  559.1 0.8 copy-start.22
  559.9 120.2 %copy-start.41 = (f32[1,768]{1,0:T(1,128)}, f32[1,768]{1,0:T(1,128)S(1)}, u32[]{:S(2)}) copy-start(f32[1,768]{1,0:T(1,128)S(1)} %get-tuple-element.152.refs_1_) | copy-start | bytes 9220
  595.0 0.8 copy-start.23
  694.6 26.6 %copy-start.47 = (f32[1,128]{1,0:T(1,128)S(1)}, f32[1,128]{1,0:T(1,128)}, u32[]{:S(2)}) copy-start(f32[1,128]{1,0:T(1,128)} %get-tuple-element.167) | copy-start | bytes 1540
  694.6 27.2 %copy-start.46 = (f32[5,768]{1,0:T(8,128)S(1)}, f32[5,768]{1,0:T(8,128)}, u32[]{:S(2)}) copy-start(f32[5,768]{1,0:T(8,128)} %get-tuple-element.215) | copy-start | bytes 46084
  694.6 27.8 %copy-start.45 = (f32[5,768]{1,0:T(8,128)S(1)}, f32[5,768]{1,0:T(8,128)}, u32[]{:S(2)}) copy-start(f32[5,768]{1,0:T(8,128)} %get-tuple-element.216) | copy-start | bytes 46084
  694.6 28.4 %copy-start.44 = (f32[5,768]{1,0:T(8,128)S(1)}, f32[5,768]{1,0:T(8,128)}, u32[]{:S(2)}) copy-start(f32[5,768]{1,0:T(8,128)} %get-tuple-element.217) | copy-start | bytes 46084
  694.6 29.0 %copy-start.51 = (f32[1,5]{1,0:T(1,128)S(1)}, f32[1,5]{1,0:T(1,128)}, u32[]{:S(2)}) copy-start(f32[1,5]{1,0:T(1,128)} %get-tuple-element.164) | copy-start | bytes 64
  694.6 29.5 %copy-start.50 = (f32[1,5]{1,0:T(1,128)S(1)}, f32[1,5]{1,0:T(1,128)}, u32[]{:S(2)}) copy-start(f32[1,5]{1,0:T(1,128)} %get-tuple-element.165) | copy-start | bytes 64
  694.7 30.0 %copy-start.49 = (f32[1,5]{1,0:T(1,128)S(1)}, f32[1,5]{1,0:T(1,128)}, u32[]{:S(2)}) copy-start(f32[1,5]{1,0:T(1,128)} %get-tuple-element.166) | copy-start | bytes 64
  694.7 30.5 %copy-start.48 = (f32[1,128]{1,0:T(1,128)S(1)}, f32[1,128]{1,0:T(1,128)}, u32[]{:S(2)}) copy-start(f32[1,128]{1,0:T(1,128)} %get-tuple-element.159.refs_13_) | copy-start | bytes 1540
  (4 other events, 2.6 us)

commit v9 on v8

--- a/solution.py
+++ b/solution.py
@@ -232,7 +232,7 @@
         scratch_shapes=buffers + list(work.scratch),
         cost_estimate=SHORT,
         compiler_params=pltpu.CompilerParams(
-            collective_id=collective_id, has_side_effects=True, vmem_limit_bytes=50 << 20
+            collective_id=collective_id, has_side_effects=True, vmem_limit_bytes=60 << 20
         ),
     )(*operands)
 
@@ -256,16 +256,18 @@
     return jnp.dot(left, right, preferred_element_type=jnp.float32)
 
 
-def scores_of(keys_values, head, queries, side):
-    span = slice(head * HEAD_DIM, (head + 1) * HEAD_DIM)
-    count = queries.shape[1]
-    scale = HEAD_DIM ** (-0.5)
-    far = contract_first(keys_values[0, 0, span, :], queries) * scale
-    own = contract_first(keys_values[1, 0, span, :], queries) * scale
+def masks_of(count, side):
     key = lax.broadcasted_iota(jnp.int32, (count, count), 0)
     query = lax.broadcasted_iota(jnp.int32, (count, count), 1)
-    own = jnp.where(key <= query, own, -1e30)
-    far = jnp.where(query + side * (2 * count) >= 2 * count, far, -1e30)
+    far = jnp.where(side == 0, -1e30, 0.0).astype(jnp.float32)
+    return far, jnp.where(key <= query, 0.0, -1e30)
+
+
+def scores_of(keys_values, head, queries, masks):
+    span = slice(head * HEAD_DIM, (head + 1) * HEAD_DIM)
+    scale = HEAD_DIM ** (-0.5)
+    far = contract_first(keys_values[0, 0, span, :], queries) * scale + masks[0]
+    own = contract_first(keys_values[1, 0, span, :], queries) * scale + masks[1]
     return far, own
 
 
@@ -303,9 +305,10 @@
             queries_ref[span, :] = turn(joined[span], cosine, sine).astype(jnp.bfloat16)
 
         copy.wait()
+        masks = masks_of(count, side)
         for head in range(heads):
             span = slice(head * HEAD_DIM, (head + 1) * HEAD_DIM)
-            far, own = scores_of(both, head, queries_ref[span, :], side)
+            far, own = scores_of(both, head, queries_ref[span, :], masks)
             peak = jnp.maximum(
                 jnp.max(far, axis=0, keepdims=True), jnp.max(own, axis=0, keepdims=True)
             )
@@ -375,10 +378,11 @@
         scale = HEAD_DIM ** (-0.5)
         grads = contract_last(out_ref[...], grad_ref[...].reshape(count, D)).astype(jnp.bfloat16)
         own_grads = []
+        masks = masks_of(count, side)
         for head in range(heads):
             span = slice(head * HEAD_DIM, (head + 1) * HEAD_DIM)
             head_queries, head_grads = queries_ref[span, :], grads[span]
-            far, own = scores_of(both, head, head_queries, side)
+            far, own = scores_of(both, head, head_queries, masks)
             far, own = jnp.exp(far - logs_ref[head]), jnp.exp(own - logs_ref[head])
             far_grad = contract_first(both[0, 1, span, :], head_grads)
             own_grad = contract_first(both[1, 1, span, :], head_grads)
@@ -772,8 +776,8 @@
                 ]
             )
         for place in range(groups):
-            if line and 0 < place < 4:
-                line.steps(2)
+            if line and place < 4:
+                line.steps(3)
             copies = []
             for index, slot, rows, target in ((0, across, upper, across), (1, beside, lower, beside)):
                 first_copies[place][index].wait_recv()
@@ -784,8 +788,6 @@
             second_copies.append(copies)
         far_copies = []
         for place, target in enumerate(order):
-            if line and place < 4:
-                line.steps(2)
             copies = first_copies[place][2:] + second_copies[place]
             for copy in copies:
                 copy.wait_recv()
@@ -1133,12 +1135,19 @@
     )(stats)
 
 
-def spread_tokens(block, collective_id):
+def spread_tokens(block, slot_block, ends, blocks, half_rows, collective_id):
     tensors, groups = lax.axis_size("tensor"), lax.axis_size("dp")
     rows = 2 * tensors * groups
-
-    def kernel(block_ref, ids, targets, kept, count, held, own_sem, send_sems, recv_sems):
+    width = ends.shape[1]
+    vocab_rows = VOCAB // tensors
+    slots = slot_block.shape[0]
+
+    def kernel(
+        block_ref, slot_ref, ends_ref, ids, targets, kept, places, plan, count,
+        held, firsts, own_sem, send_sems, recv_sems,
+    ):
         group, side = lax.axis_index("dp"), lax.axis_index("seq")
+        first_id = lax.axis_index("tensor") * vocab_rows
         peers = [
             {"dp": lax.rem(group + step // 2, groups), "seq": lax.rem(side + step % 2, 2)}
             for step in range(1, 2 * groups)
@@ -1154,17 +1163,53 @@
         for copy in copies:
             copy.wait()
         lane = lax.broadcasted_iota(jnp.int32, (1, LANES), 1)
+        slot_ids = lax.broadcasted_iota(jnp.int32, (slots, LANES), 0)
+        slot_blocks = jnp.broadcast_to(slot_ref[...], (slots, LANES))
         total = jnp.zeros((1, LANES), jnp.int32)
+        hits = jnp.zeros((1, LANES), jnp.float32)
         for half in range(2):
             for source in range(groups):
                 limit = held[source, half, 2 * tensors : 2 * tensors + 1, :]
                 total = total + limit
                 for part in range(tensors):
                     row = (half * tensors + part) * groups + source
-                    ids[row] = held[source, half, part : part + 1, :]
+                    token = held[source, half, part : part + 1, :]
+                    ids[row] = token
                     targets[row] = held[source, half, tensors + part : tensors + part + 1, :]
                     kept[row] = jnp.where(lane + part * LANES < limit, 1.0, 0.0)
+                    firsts[row : row + 1, :] = jnp.where(part * LANES < limit, 1.0, 0.0)
+                    local = token - first_id
+                    inside = (local >= 0) & (local < vocab_rows)
+                    local = jnp.where(inside, local, 0).astype(jnp.float32)
+                    block_of = jnp.floor((local + 0.5) * (0.5 / half_rows))
+                    within = local - block_of * (2.0 * half_rows)
+                    lower = within >= half_rows
+                    inside = inside & (jnp.where(lower, 1, 0) == side)
+                    within = (within - jnp.where(lower, 1.0 * half_rows, 0.0)).astype(jnp.int32)
+                    same = slot_blocks == block_of.astype(jnp.int32) + blocks
+                    slot = jnp.sum(jnp.where(same, slot_ids + 1, 0), axis=0, keepdims=True) - 1
+                    inside = inside & (slot >= 0)
+                    places[row] = jnp.where(inside, slot * half_rows + within, -1)
+                    hits = hits + jnp.where(inside, 1.0, 0.0)
         count[...] = total.astype(jnp.float32)
+        shape = (rows, width)
+        active = jnp.concatenate([firsts[...]] * (width // LANES), axis=1)
+        square = (rows, rows)
+        above = jnp.where(
+            lax.broadcasted_iota(jnp.int32, square, 1) < lax.broadcasted_iota(jnp.int32, square, 0),
+            1.0,
+            0.0,
+        )
+        earlier = times(above.astype(jnp.bfloat16), active.astype(jnp.bfloat16))
+        number = jnp.sum(active, axis=0, keepdims=True)
+        index = lax.broadcasted_iota(jnp.int32, shape, 0).astype(jnp.float32)
+        turns = jnp.where(active > 0.0, earlier, number + index - earlier)
+        spot = lax.broadcasted_iota(jnp.int32, shape, 1).astype(jnp.float32) - PLAN_GROUPS
+        order = jnp.sum(jnp.where(turns == spot, index, 0.0), axis=0, keepdims=True)
+        spot = lax.broadcasted_iota(jnp.int32, (1, width), 1)
+        order = jnp.where(spot == 2, number, order)
+        order = jnp.where(spot == 3, jnp.sum(hits, axis=1, keepdims=True), order)
+        plan[...] = jnp.where(spot < 2, ends_ref[...], order.astype(jnp.int32))
 
     dma = pltpu.SemaphoreType.DMA
     vmem = pl.BlockSpec(memory_space=pltpu.VMEM)
@@ -1176,19 +1221,22 @@
             jax.ShapeDtypeStruct(shape, jnp.int32),
             jax.ShapeDtypeStruct(shape, jnp.int32),
             jax.ShapeDtypeStruct(shape, jnp.float32),
+            jax.ShapeDtypeStruct(shape, jnp.int32),
+            jax.ShapeDtypeStruct((1, width), jnp.int32),
             jax.ShapeDtypeStruct((1, LANES), jnp.float32),
         ],
-        in_specs=[vmem],
-        out_specs=[vmem] * 4,
+        in_specs=[vmem] * 3,
+        out_specs=[vmem] * 6,
         scratch_shapes=[
             pltpu.VMEM((groups, 2) + block.shape, jnp.int32),
+            pltpu.VMEM((rows, LANES), jnp.float32),
             dma,
             dma((2 * groups - 1,)),
             dma((2 * groups - 1,)),
         ],
         cost_estimate=SHORT,
         compiler_params=pltpu.CompilerParams(collective_id=collective_id, has_side_effects=True),
-    )(block)
+    )(block, slot_block, ends)
 
 
 def finish(gain_grads, states, grad_ys, home, keep, table_squares, count, smalls, collective_id):
@@ -1300,14 +1348,16 @@
 PREPARE_STEP = 20
 
 
-def prepare(slot_block, master, blocks):
+def prepare(slot_block, first_id, master, blocks):
     slots, half_rows, _ = master.shape
     total = slot_block.shape[0]
     steps = -(-total // PREPARE_STEP)
-    slot_block = jnp.pad(slot_block, (0, steps * PREPARE_STEP - total), constant_values=-1)
+    spare = steps * PREPARE_STEP - total
+    slot_block = jnp.pad(slot_block, (0, spare), constant_values=-1)
+    slot_block = jnp.concatenate([slot_block, first_id[None]])
     rows = PREPARE_STEP * half_rows
 
-    def kernel(plan_ref, master_ref, table_ref, halves_ref):
+    def kernel(plan_ref, master_ref, table_ref, halves_ref, ids_ref):
         @pl.when(pl.program_id(0) == 0)
         def _():
             halves_ref[...] = jnp.zeros_like(halves_ref)
@@ -1318,6 +1368,11 @@
             table_ref[place * half_rows : (place + 1) * half_rows, :] = value
 
             block = plan_ref[slot]
+            ids = plan_ref[steps * PREPARE_STEP] + (block - blocks) * (2 * half_rows)
+            ids = ids + lax.broadcasted_iota(jnp.int32, (half_rows, 1), 0)
+            ids_ref[place * half_rows : (place + 1) * half_rows, :] = jnp.where(
+                block >= blocks, ids, -1
+            )
 
             @pl.when((block >= 0) & (block < blocks))
             def _():
@@ -1338,11 +1393,13 @@
             out_specs=[
                 pl.BlockSpec((rows, D), lambda step, plan: (step, 0)),
                 pl.BlockSpec((blocks, half_rows, D), lambda step, plan: (0, 0, 0)),
+                pl.BlockSpec((rows, 1), lambda step, plan: (step, 0)),
             ],
         ),
         out_shape=[
             jax.ShapeDtypeStruct((total * half_rows, D), jnp.bfloat16),
             jax.ShapeDtypeStruct((blocks, half_rows, D), jnp.bfloat16),
+            jax.ShapeDtypeStruct((total * half_rows, 1), jnp.int32),
         ],
         cost_estimate=SHORT,
         compiler_params=pltpu.CompilerParams(vmem_limit_bytes=60 << 20),
@@ -1534,12 +1591,13 @@
         final_refs, (powers_ref, stats_ref, scores, hidden) = rest[:TILE_GROUPS], rest[TILE_GROUPS:]
         blank = jnp.zeros((1, TILE), jnp.float32)
         active = pl.program_id(0) <= last_tile(plan_ref)
+        own = groups_of(plan_ref)
 
         def put(top, total, target):
             pad = jnp.zeros((5, LANES), jnp.float32)
             for place in range(TILE_GROUPS):
                 lanes = slice(place * LANES, (place + 1) * LANES)
-                stats_ref[place] = jnp.concatenate(
+                stats_ref[own[place]] = jnp.concatenate(
                     [top[:, lanes], total[:, lanes], target[:, lanes], pad], axis=0
                 )
 
@@ -1549,7 +1607,7 @@
 
         @pl.when(active)
         def _():
-            wanted = row_of(labels_ref, groups_of(plan_ref))
+            wanted = row_of(labels_ref, own)
             for place, ref in enumerate(final_refs):
                 hidden[place * LANES : (place + 1) * LANES, :] = ref[...]
 
@@ -1587,10 +1645,7 @@
             jax.ShapeDtypeStruct((rows, groups * LANES), jnp.bfloat16),
             jax.ShapeDtypeStruct((groups, 8, LANES), jnp.float32),
         ],
-        [
-            powers_spec(rows),
-            pl.BlockSpec((TILE_GROUPS, 8, LANES), lambda step, plan: (step, 0, 0)),
-        ],
+        [powers_spec(rows), whole((groups, 8, LANES))],
         [pltpu.VMEM((rows, TILE), jnp.float32), pltpu.VMEM((TILE, D), jnp.bfloat16)],
     )
 
@@ -1632,7 +1687,7 @@
         def _():
             own = groups_of(plan_ref)
             wanted, kept = row_of(labels_ref, own), row_of(keep_ref, own)
-            tops = row_of(stats_ref, range(TILE_GROUPS))
+            tops = row_of(stats_ref, own)
             scale = jnp.exp(tops - row_of(logs_ref, own)) * kept
             for place, ref in enumerate(final_refs):
                 hidden[place * LANES : (place + 1) * LANES, :] = ref[...]
@@ -1669,7 +1724,7 @@
             whole((rows, 1)),
             whole(lanes),
             whole(lanes),
-            pl.BlockSpec((TILE_GROUPS, 8, LANES), lambda step, plan: (step, 0, 0)),
+            whole((groups, 8, LANES)),
             whole((groups, 8, LANES)),
             whole((rows, D)),
             powers_spec(rows),
@@ -1815,8 +1870,6 @@
 
 
 def grads_home(level):
-    if level == 0:
-        return [(0, 1), (1, 0), (0, 0)]
     return [(2 * level, 0), (2 * level + 1, 0), (2 * level + 1, 1)]
 
 
@@ -1858,16 +1911,8 @@
     mine = owners == group
     match = (jnp.arange(slots)[:, None] == slot_rank[None, :]) & mine[None, :]
     slot_block = jnp.sum(jnp.where(match, block_ids[None, :] + 1, 0), axis=1) - 1
-    row_ids = (
-        tensor_part * vocab_rows
-        + (slot_block[:, None] - blocks) * (2 * half_rows)
-        + seq_part * half_rows
-        + jnp.arange(half_rows, dtype=jnp.int32)[None, :]
-    )
-    row_ids = jnp.where(slot_block[:, None] >= blocks, row_ids, -1).reshape(-1, 1)
     spare = -(-ROW_STEP // half_rows)
     spare += -(slots + spare) % SLOT_STEP
-    row_ids = jnp.pad(row_ids, ((0, spare * half_rows), (0, 0)), constant_values=-1)
     held = jnp.sum(jnp.where(mine, 1, 0)) * half_rows
     first_held = jnp.sum(jnp.where(mine & (block_ids < blocks), 1, 0)) * half_rows
     slot_block_all = jnp.pad(slot_block, (0, spare), constant_values=-1).astype(jnp.int32)
@@ -1892,43 +1937,17 @@
         ],
         axis=0,
     )
-    ids_all, labels_all, keep_all, count = spread_tokens(packed, 15)
+    width = -(-(2 * tensors * groups + PLAN_GROUPS) // LANES) * LANES
+    lane = jnp.arange(width)[None, :]
+    ends = jnp.where(lane == 0, first_held, jnp.where(lane == 1, held, 0)).astype(jnp.int32)
+    ids_all, labels_all, keep_all, places, plan, count = spread_tokens(
+        packed, slot_block_all[:, None], ends, blocks, half_rows, 15
+    )
+    plan = plan.reshape(-1)
     order = (2, tensors, groups, share)
-    local_ids = ids_all - tensor_part * vocab_rows
-    inside = (local_ids >= 0) & (local_ids < vocab_rows)
-    block_of, within = local_ids // (2 * half_rows) + blocks, local_ids % (2 * half_rows)
-    inside = inside & (within // half_rows == seq_part)
-    same = block_of.reshape(1, -1) == jnp.where(slot_block < 0, -1, slot_block)[:, None]
-    slot_of = jnp.sum(jnp.where(same, jnp.arange(1, slots + 1)[:, None], 0), axis=0)
-    slot_of = slot_of.reshape(ids_all.shape) - 1
-    places = jnp.where(inside & (slot_of >= 0), slot_of * half_rows + within % half_rows, -1)
-    active = keep_all[:, 0, 0] > 0.0
-    group_ids = jnp.arange(active.shape[0])
-    earlier = group_ids[None, :] < group_ids[:, None]
-    turn_of = jnp.where(
-        active,
-        jnp.sum(jnp.where(earlier & active[None, :], 1, 0), axis=1),
-        jnp.sum(jnp.where(active, 1, 0))
-        + jnp.sum(jnp.where(earlier & ~active[None, :], 1, 0), axis=1),
-    )
-    group_order = jnp.sum(
-        jnp.where(turn_of[None, :] == group_ids[:, None], group_ids[None, :], 0), axis=1
-    )
-    plan = jnp.concatenate(
-        [
-            jnp.stack(
-                [
-                    first_held,
-                    held,
-                    jnp.sum(jnp.where(active, 1, 0)),
-                    jnp.sum(jnp.where(places >= 0, 1, 0)),
-                ]
-            ),
-            group_order,
-        ]
-    ).astype(jnp.int32)
-
-    table, halves = prepare(slot_block_all, master, blocks)
+
+    first_id = (tensor_part * vocab_rows + seq_part * half_rows).astype(jnp.int32)
+    table, halves, row_ids = prepare(slot_block_all, first_id, master, blocks)
 
     def weights_line(*starts):
         return Line([(halves, start * third, third) for start in starts], True)
@@ -1971,7 +1990,8 @@
     states, streams, inners, kept_all = [start], [start], [], []
     for level in range(LAYERS):
         here, last = 3 * level, level == LAYERS - 1
-        carried = [here + 1, here + 2] if level else [here + 2]
+        carried = [] if last else [here + 3]
+        carried += [here + 1, here + 2] if level else [here + 2]
         inner, normed_two, queries, both, logs, attended, joined = tensor_step(
             f"inner_{level}",
             inner_of,
@@ -1988,7 +2008,8 @@
         down = (joined, len(carried) - 1)
         up = (joined, len(carried) - 2) if level else up
         tables.append((attention_table, up, down))
-        outcome, stream, normed_next, hidden, activated, *joined = tensor_step(
+        attention_table = joined
+        outcome, stream, normed_next, hidden, activated = tensor_step(
             f"outcome_{level}",
             partial(outcome_of, (level + 1) * (level + 2) // 2 - 1),
             unit_work(normed_two, up, down),
@@ -1997,9 +2018,7 @@
             [piece, piece] + ([((share, D), jnp.bfloat16)] if last else []),
             not last,
             3 + level,
-            None if last else weights_line(here + 3),
         )
-        attention_table = None if last else as_table(joined[0])
         inners.append(inner)
         kept_all.append((normed, kept, normed_two, (hidden, activated)))
         states.append(outcome)
@@ -2009,7 +2028,7 @@
     final_all = gather_all(normed, 3 + LAYERS)[0].reshape(-1, D)
     powers, stats = head_forward(plan, row_ids, labels_all, table, final_all)
     home, log_totals = join_stats(
-        jnp.take(stats, turn_of, axis=0).reshape((2, tensors, groups, 8, LANES)), 4 + LAYERS
+        stats.reshape((2, tensors, groups, 8, LANES)), 4 + LAYERS
     )
     grad_final, grad_table = head_backward(
         plan,
@@ -2087,13 +2106,13 @@
                 [piece, piece, row] + ([] if level else [((share, D), jnp.bfloat16)]),
                 level > 0,
                 7 + LAYERS + level,
-                Line([(unit_grads, 0, 2 * third if level else third)], False),
+                Line([(unit_grads, 0, 2 * third)], False),
             )
         )
         layer_grads[2 * level + 1] = summed
 
     grad_start_all, layer_grads[0] = gather_all(
-        grad_branch, 13, Line([(unit_grads, third, third), (attention_grads, 0, third)], False)
+        grad_branch, 13, Line([(attention_grads, 0, third)], False)
     )
     grad_start_all = grad_start_all.reshape(-1, D)
     owned, table_squares = look_back(

time: 736 us -> 707 us (0.961)
  local copies, waits for them, and re-layouts: 30.1 us -> 7.19 us
    unnamed x110 -> x24, local copies, waits for them, and re-layouts: 21.3 us -> 3.4 us
    pallas_call x8, Pallas kernels: 273 us -> 290 us  [tensor_step(): pl.pallas_call(kernel, name=name, grid=(1,), out_shape=shapes, in_specs=i...]
    pallas_call x2, Pallas kernels: 94.7 us -> 80.9 us  [gather_all(): pl.pallas_call(kernel, name='gather_all', out_shape=[jax.ShapeDtypeStruct...]
    pallas_call x2, Pallas kernels: 142 us -> 134 us  [reduce_all(): pl.pallas_call(kernel, name='reduce_all', out_shape=results + ([line.out_...]
where the time goes in v9:
time: 707 us; the launch traced here: 696 us
  Pallas kernels  652 us (92%)
  other arithmetic  32.9 us (5%)
  local copies, waits for them, and re-layouts  7.19 us (1%)
    pallas_call x8, Pallas kernels, tensor_step(): pl.pallas_call(kernel, name=name, grid=(1,), out_shape=shapes, in_specs=i...  290 us
    pallas_call x2, Pallas kernels, reduce_all(): pl.pallas_call(kernel, name='reduce_all', out_shape=results + ([line.out_...  134 us
    pallas_call x2, Pallas kernels, gather_all(): pl.pallas_call(kernel, name='gather_all', out_shape=[jax.ShapeDtypeStruct...  80.9 us
    pallas_call x3, Pallas kernels, local_call(): pl.pallas_call(kernel, name=name, grid_spec=pltpu.PrefetchScalarGridSpec(...  65.5 us
    sub x1, other arithmetic, adam_update(): weight - rate * (first_hat / (jnp.sqrt(second_hat) + ADAM_EPS) + decay *...  26.5 us
    pallas_call x1, Pallas kernels, join_stats(): pl.pallas_call(kernel, name='join_stats', out_shape=[jax.ShapeDtypeStruct...  26.3 us
    pallas_call x1, Pallas kernels, look_back(): pl.pallas_call(kernel, name='look_back', grid_spec=pltpu.PrefetchScalarGr...  23.2 us

profile of v9, /device:TPU:0, one launch (start us, length us, event | category | flops | bytes accessed | tf_op | source)
XLA Modules:
  0.0 696.4 jit_solution(16750974846290237689)
XLA Ops:
  0.6 0.0 copy-start
  0.7 1.3 fusion.8
  2.0 0.9 select_reduce_fusion
  2.9 0.1 select_reduce_fusion.1
  3.1 0.7 copy.26.slot_ref
  5.1 0.5 compare_select_fusion.7.ends_ref
  6.3 0.1 pad.9.clone
  6.4 1.4 add_add_fusion.block_ref
  7.7 9.5 %spread_tokens.1 = (s32[32,1,128]{2,1,0:T(1,128)}, s32[32,1,128]{2,1,0:T(1,128)}, f32[32,1,128]{2,1,0:T(1,128)}, s32[32,1,128]{2,1,0:T(1,128)}, s32[1,128]{1,0:T(1,128)}, /*index=5*/f32[1,128]{1,0:T(1,128)}) custom-call(s32[16,128]{1,0:T(8,128)} %add_add_fusion.block_ref, s32[80,1]{1,0:T(8,128)} %copy.26.slot_ref, s32[1,128]{1,0:T(1,128)} %compare_select_fusion.7.ends_ref), custom_call_target="tpu_custom_call" | custom-call | flops 1000 | bytes 1000 | tf_op jit(solution)/shard_map/spread_tokens/pallas_call | solution.py:1217
  17.3 0.6 pad_add_fusion.plan_ref
  17.9 9.9 %prepare.1 = (bf16[3840,768]{1,0:T(8,128)(2,1)}, bf16[48,48,768]{2,1,0:T(8,128)(2,1)}, s32[3840,1]{1,0:T(8,128)}) custom-call(s32[81]{0:T(128)} %pad_add_fusion.plan_ref, f32[67,48,768]{2,1,0:T(8,128)} %master_ref.1), custom_call_target="tpu_custom_call" | custom-call | flops 1000 | bytes 1000 | tf_op jit(solution)/shard_map/prepare/pallas_call | solution.py:1382
  27.7 17.2 %look_up.1 = (bf16[4096,768]{1,0:T(8,128)(2,1)}, s32[32,1,128]{2,1,0:T(1,128)}, s32[8,768]{1,0:T(8,128)}) custom-call(s32[128]{0:T(128)} %bitcast.76, s32[3840,1]{1,0:T(8,128)} %get-tuple-element.93.ids_ref, s32[32,1,128]{2,1,0:T(1,128)} %get-tuple-element.94.tokens_ref, s32[32,1,128]{2,1,0:T(1,128)} %get-tuple-element.95.places_ref, ...), custom_call_target="tpu_custom_call" | custom-call | flops 1000 | bytes 1000 | tf_op jit(solution)/shard_map/look_up/pallas_call | solution.py:1468
  45.0 0.0 copy-done
  45.0 0.6 fusion.15
  45.6 73.3 %reduce_all.2 = (f32[128,768]{1,0:T(8,128)}, bf16[4,128,768]{2,1,0:T(8,128)(2,1)}, bf16[16,2,48,768]{3,2,1,0:T(8,128)(2,1)}) custom-call(bf16[2,4,4,128,768]{4,3,2,1,0:T(8,128)(2,1)} %bitcast.70, bf16[48,48,768]{2,1,0:T(8,128)(2,1)} %get-tuple-element.102.refs_1_.refs_2_.refs_7_.refs_8_, ...), custom_call_target="tpu_custom_call" | custom-call | flops 1000 | bytes 1000 | tf_op jit(solution)/shard_map/reduce_all/pallas_call | solution.py:849
  118.9 1.0 multiply_sine_fusion
  119.8 42.2 %inner_0.1 = (f32[128,768]{1,0:T(8,128)}, bf16[4,128,768]{2,1,0:T(8,128)(2,1)}, bf16[192,512]{1,0:T(8,128)(2,1)}, bf16[2,2,192,512]{3,2,1,0:T(8,128)(2,1)}, f32[...) custom-call(bf16[4,128,768]{2,1,0:T(8,128)(2,1)} %get-tuple-element.103.refs_0_.refs_1_, ...), custom_call_target="tpu_custom_call" | custom-call | flops 1000 | bytes 1000 | tf_op jit(solution)/shard_map/inner_0/pallas_call | solution.py:225
  162.1 28.3 %outcome_0.1 = (f32[128,768]{1,0:T(8,128)}, f32[128,768]{1,0:T(8,128)}, bf16[4,128,768]{2,1,0:T(8,128)(2,1)}, f32[768,512]{1,0:T(8,128)}, bf16[768,512]{1,0:T(8,128)(2,1)}) custom-call(bf16[4,128,768]{2,1,0:T(8,128)(2,1)} %get-tuple-element.106.refs_0_.refs_1_, bf16[1536,768]{1,0:T(8,128)(2,1)} %bitcast.56, bf16[1536,768]{1,0:T(8,128)(2,1)} %bitcast.60, ...), custom_call_target="tpu_custom_call" | custom-call | flops 1000 | bytes 1000 | tf_op jit(solution)/shard_map/outcome_0/pallas_call | solution.py:225
  190.4 42.2 %inner_1.1 = (f32[128,768]{1,0:T(8,128)}, bf16[4,128,768]{2,1,0:T(8,128)(2,1)}, bf16[192,512]{1,0:T(8,128)(2,1)}, bf16[2,2,192,512]{3,2,1,0:T(8,128)(2,1)}, f32[...) custom-call(bf16[4,128,768]{2,1,0:T(8,128)(2,1)} %get-tuple-element.109.refs_0_.refs_1_, ...), custom_call_target="tpu_custom_call" | custom-call | flops 1000 | bytes 1000 | tf_op jit(solution)/shard_map/inner_1/pallas_call | solution.py:225
  232.6 17.7 %outcome_1.1 = (f32[128,768]{1,0:T(8,128)}, f32[128,768]{1,0:T(8,128)}, bf16[128,768]{1,0:T(8,128)(2,1)}, f32[768,512]{1,0:T(8,128)}, bf16[768,512]{1,0:T(8,128)(2,1)}) custom-call(bf16[4,128,768]{2,1,0:T(8,128)(2,1)} %get-tuple-element.111.refs_0_.refs_1_, bf16[1536,768]{1,0:T(8,128)(2,1)} %bitcast.66, bf16[1536,768]{1,0:T(8,128)(2,1)} %bitcast.67, ...), custom_call_target="tpu_custom_call" | custom-call | flops 1000 | bytes 1000 | tf_op jit(solution)/shard_map/outcome_1/pallas_call | solution.py:225
  250.3 35.7 %gather_all.2 = bf16[2,4,4,128,768]{4,3,2,1,0:T(8,128)(2,1)} custom-call(bf16[128,768]{1,0:T(8,128)(2,1)} %get-tuple-element.115.refs_0_), custom_call_target="tpu_custom_call" | custom-call | flops 1000 | bytes 1000 | tf_op jit(solution)/shard_map/gather_all/pallas_call | solution.py:990
  286.1 18.0 %head_forward.1 = (bf16[3840,4096]{1,0:T(8,128)(2,1)}, f32[32,8,128]{2,1,0:T(8,128)}) custom-call(s32[128]{0:T(128)} %bitcast.77, s32[3840,1]{1,0:T(8,128)} %get-tuple-element.93.ids_ref, s32[32,1,128]{2,1,0:T(1,128)} %get-tuple-element.99.labels_ref, bf16[3840,768]{1,0:T(8,128)(2,1)} %get-tuple-element.96.table_ref, bf16[4096,768]{1,0:T(8,128)(2,1)} %bitcast.38, ...), custom_call_target="tpu_custom_call" | custom-call | flops 1000 | bytes 1000 | tf_op jit(solution)/shard_map/head_forward/pallas_call | solution.py:1468
  304.1 26.3 %join_stats.1 = (f32[8,128]{1,0:T(8,128)}, f32[2,4,4,8,128]{4,3,2,1,0:T(8,128)}) custom-call(f32[2,4,4,8,128]{4,3,2,1,0:T(8,128)} %bitcast.73), custom_call_target="tpu_custom_call" | custom-call | flops 1000 | bytes 1000 | tf_op jit(solution)/shard_map/join_stats/pallas_call | solution.py:1111
  330.4 30.2 %head_backward.1 = (bf16[32,128,768]{2,1,0:T(8,128)(2,1)}, f32[3840,768]{1,0:T(8,128)}) custom-call(s32[128]{0:T(128)} %bitcast.78, s32[3840,1]{1,0:T(8,128)} %get-tuple-element.93.ids_ref, s32[32,1,128]{2,1,0:T(1,128)} %get-tuple-element.99.labels_ref, f32[32,1,128]{2,1,0:T(1,128)} %get-tuple-element.100.keep_ref, ...), custom_call_target="tpu_custom_call" | custom-call | flops 1000 | bytes 1000 | tf_op jit(solution)/shard_map/head_backward/pallas_call | solution.py:1468
  360.7 60.5 %reduce_all.3 = (f32[128,768]{1,0:T(8,128)}, f32[128,768]{1,0:T(8,128)}, f32[1,768]{1,0:T(1,128)}, bf16[4,128,768]{2,1,0:T(8,128)(2,1)}) custom-call(bf16[2,4,4,128,768]{4,3,2,1,0:T(8,128)(2,1)} %bitcast.71, f32[128,768]{1,0:T(8,128)} %get-tuple-element.120.refs_1_, f32[1,768]{1,0:T(1,128)} %get-tuple-element.181.refs_4_.refs_2_, f32[5]{0:T(128)} %refs_15_.2), custom_call_target="tpu_custom_call" | custom-call | flops 1000 | bytes 1000 | tf_op jit(solution)/shard_map/reduce_all/pallas_call | solution.py:849
  421.1 28.2 %inner_back_1.1 = (f32[128,768]{1,0:T(8,128)}, f32[1,768]{1,0:T(1,128)}, bf16[4,128,768]{2,1,0:T(8,128)(2,1)}, bf16[16,48,768]{2,1,0:T(8,128)(2,1)}) custom-call(bf16[4,128,768]{2,1,0:T(8,128)(2,1)} %get-tuple-element.121.refs_0_, bf16[4,128,768]{2,1,0:T(8,128)(2,1)} %get-tuple-element.111.refs_0_.refs_1_, bf16[1536,768]{1,0:T(8,128)(2,1)} %bitcast.68, ...), custom_call_target="tpu_custom_call" | custom-call | flops 1000 | bytes 1000 | tf_op jit(solution)/shard_map/inner_back_1/pallas_call | solution.py:225
  449.4 49.9 %stream_back_1.1 = (f32[128,768]{1,0:T(8,128)}, f32[128,768]{1,0:T(8,128)}, f32[1,768]{1,0:T(1,128)}, bf16[4,128,768]{2,1,0:T(8,128)(2,1)}, bf16[8,48,768]{2,1,0:T(8,128)(2,1)}, /*index=5*/bf16[16,48,768]{2,1,0:T(8,128)(2,1)}) custom-call(bf16[4,128,768]{2,1,0:T(8,128)(2,1)} %get-tuple-element.125.refs_0_, ...), custom_call_target="tpu_custom_call" | custom-call | flops 1000 | bytes 1000 | tf_op jit(solution)/shard_map/stream_back_1/pallas_call | solution.py:225
  499.3 34.8 %inner_back_0.1 = (f32[128,768]{1,0:T(8,128)}, f32[1,768]{1,0:T(1,128)}, bf16[4,128,768]{2,1,0:T(8,128)(2,1)}, bf16[16,48,768]{2,1,0:T(8,128)(2,1)}, bf16[8,48,768]{2,1,0:T(8,128)(2,1)}) custom-call(bf16[4,128,768]{2,1,0:T(8,128)(2,1)} %get-tuple-element.133.refs_0_, bf16[4,128,768]{2,1,0:T(8,128)(2,1)} %get-tuple-element.106.refs_0_.refs_1_, ...), custom_call_target="tpu_custom_call" | custom-call | flops 1000 | bytes 1000 | tf_op jit(solution)/shard_map/inner_back_0/pallas_call | solution.py:225
  534.1 46.9 %stream_back_0.1 = (f32[128,768]{1,0:T(8,128)}, f32[128,768]{1,0:T(8,128)}, f32[1,768]{1,0:T(1,128)}, bf16[128,768]{1,0:T(8,128)(2,1)}, bf16[8,48,768]{2,1,0:T(8,128)(2,1)}, /*index=5*/bf16[16,48,768]{2,1,0:T(8,128)(2,1)}) custom-call(bf16[4,128,768]{2,1,0:T(8,128)(2,1)} %get-tuple-element.138.refs_0_, ...), custom_call_target="tpu_custom_call" | custom-call | flops 1000 | bytes 1000 | tf_op jit(solution)/shard_map/stream_back_0/pallas_call | solution.py:225
  581.0 45.1 %gather_all.3 = (bf16[2,4,4,128,768]{4,3,2,1,0:T(8,128)(2,1)}, bf16[8,48,768]{2,1,0:T(8,128)(2,1)}) custom-call(bf16[128,768]{1,0:T(8,128)(2,1)} %get-tuple-element.146.refs_0_, bf16[8,48,768]{2,1,0:T(8,128)(2,1)} %get-tuple-element.147.refs_1_), custom_call_target="tpu_custom_call" | custom-call | flops 1000 | bytes 1000 | tf_op jit(solution)/shard_map/gather_all/pallas_call | solution.py:990
  626.1 0.6 stack.23.slot_ref
  626.7 23.2 %look_back.1 = (f32[67,48,768]{2,1,0:T(8,128)}, f32[8,768]{1,0:T(8,128)}) custom-call(s32[128]{0:T(128)} %bitcast.79, s32[5,80]{1,0:T(8,128)} %stack.23.slot_ref, s32[3840,1]{1,0:T(8,128)} %get-tuple-element.93.ids_ref, s32[32,1,128]{2,1,0:T(1,128)} %get-tuple-element.94.tokens_ref, s32[32,1,128]{2,1,0:T(1,128)} %get-tuple-element.97.ranks_ref, ...), custom_call_target="tpu_custom_call" | custom-call | flops 1000 | bytes 1000 | tf_op jit(solution)/shard_map/look_back/pallas_call | solution.py:1825
  649.9 0.5 compare_select_fusion.refs_11_
  650.4 12.9 %finish.1 = (f32[5,768]{1,0:T(8,128)}, f32[5,768]{1,0:T(8,128)}, f32[5,768]{1,0:T(8,128)}, f32[1,5]{1,0:T(1,128)}, f32[1,5]{1,0:T(1,128)}, /*index=5*/f32[1,5]{1,0:T(1,128)}, f32[1,128]{1,0:T(1,128)}, f32[8,128]{1,0:T(8,128)}) custom-call(f32[1,768]{1,0:T(1,128)} %get-tuple-element.155.refs_0_, f32[1,768]{1,0:T(1,128)} %get-tuple-element.156.refs_1_, ...), custom_call_target="tpu_custom_call" | custom-call | flops 1000 | bytes 1000 | tf_op jit(solution)/shard_map/finish/pallas_call | solution.py:1321
  663.3 1.2 slice.32
  664.5 0.0 copy-start.8
  664.5 0.0 copy-start.7
  664.5 0.0 copy-start.6
  664.5 26.5 %multiply_subtract_fusion = (f32[67,48,768]{2,1,0:T(8,128)}, f32[67,48,768]{2,1,0:T(8,128)}, f32[67,48,768]{2,1,0:T(8,128)}) fusion(f32[67,48,768]{2,1,0:T(8,128)} %master_ref.1, f32[67,48,768]{2,1,0:T(8,128)} %get-tuple-element.154, f32[]{:T(128)} %bitcast.23, f32[67,48,768]{2,1,0:T(8,128)} %param.18, f32[67,48,768]{2,1,0:T(8,128)} %param.19), kind=kLoop, calls=%fused_computation.2 | loop fusion | flops 39518208 | bytes 69156864 | tf_op jit(solution)/shard_map/sub | solution.py:53
  691.0 0.6 fusion.16
  691.6 0.6 copy.35
  692.2 0.6 copy.36
  692.9 0.6 copy.37
  693.5 0.5 copy.38
  694.0 0.5 copy.39
  694.5 0.0 copy-done.6
  694.5 0.5 copy.40
  695.0 0.0 copy-done.5
  (17 shorter events, 0.1 us)
Async XLA Ops:
  0.6 44.3 %copy-start = (f32[5,768]{1,0:T(8,128)S(1)}, f32[5,768]{1,0:T(8,128)}, u32[]{:S(2)}) copy-start(f32[5,768]{1,0:T(8,128)} %refs_14_.3) | copy-start | bytes 46084
  664.5 26.6 %copy-start.4 = (f32[1,128]{1,0:T(1,128)S(1)}, f32[1,128]{1,0:T(1,128)}, u32[]{:S(2)}) copy-start(f32[1,128]{1,0:T(1,128)} %get-tuple-element.171) | copy-start | bytes 1540
  664.5 27.2 %copy-start.3 = (f32[5,768]{1,0:T(8,128)S(1)}, f32[5,768]{1,0:T(8,128)}, u32[]{:S(2)}) copy-start(f32[5,768]{1,0:T(8,128)} %get-tuple-element.214) | copy-start | bytes 46084
  664.5 27.8 %copy-start.2 = (f32[5,768]{1,0:T(8,128)S(1)}, f32[5,768]{1,0:T(8,128)}, u32[]{:S(2)}) copy-start(f32[5,768]{1,0:T(8,128)} %get-tuple-element.215) | copy-start | bytes 46084
  664.5 28.4 %copy-start.1 = (f32[5,768]{1,0:T(8,128)S(1)}, f32[5,768]{1,0:T(8,128)}, u32[]{:S(2)}) copy-start(f32[5,768]{1,0:T(8,128)} %get-tuple-element.216) | copy-start | bytes 46084
  664.5 29.0 %copy-start.8 = (f32[1,5]{1,0:T(1,128)S(1)}, f32[1,5]{1,0:T(1,128)}, u32[]{:S(2)}) copy-start(f32[1,5]{1,0:T(1,128)} %get-tuple-element.168) | copy-start | bytes 64
  664.5 29.5 %copy-start.7 = (f32[1,5]{1,0:T(1,128)S(1)}, f32[1,5]{1,0:T(1,128)}, u32[]{:S(2)}) copy-start(f32[1,5]{1,0:T(1,128)} %get-tuple-element.169) | copy-start | bytes 64
  664.5 30.0 %copy-start.6 = (f32[1,5]{1,0:T(1,128)S(1)}, f32[1,5]{1,0:T(1,128)}, u32[]{:S(2)}) copy-start(f32[1,5]{1,0:T(1,128)} %get-tuple-element.170) | copy-start | bytes 64
  664.5 30.5 %copy-start.5 = (f32[1,128]{1,0:T(1,128)S(1)}, f32[1,128]{1,0:T(1,128)}, u32[]{:S(2)}) copy-start(f32[1,128]{1,0:T(1,128)} %get-tuple-element.163.refs_13_) | copy-start | bytes 1540

commit v10 on v9

--- a/solution.py
+++ b/solution.py
@@ -535,6 +535,7 @@
 
 LINE_BLOCKS = 1
 LINE_LAG = 3
+LINE_SHARE = 4
 
 
 class Line:
@@ -556,18 +557,18 @@
             pltpu.VMEM((2,) + self.half, jnp.bfloat16),
             pltpu.VMEM((2,) + self.half, jnp.bfloat16),
             dma((len(sources),)),
-            dma((2, self.chunks)),
+            dma((2,)),
             dma((2, self.chunks)),
         ]
         if share:
-            self.scratch += [pltpu.VMEM(self.half, jnp.bfloat16)] + [dma((self.chunks,))] * 3
+            self.scratch += [pltpu.VMEM(self.half, jnp.bfloat16)] + [dma] * 3
 
     def bind(self, source_refs, out_ref, refs):
         self.source_refs, self.out = source_refs, out_ref
         self.own, self.came, self.going, self.own_sems, self.send_sems, self.recv_sems = refs[:6]
         self.total = out_ref
         if self.share:
-            self.total, self.keep_sems, self.twin_send, self.twin_recv = refs[6:]
+            self.total, self.keep_sem, self.twin_send, self.twin_recv = refs[6:]
         self.done = 0
         self.group = lax.axis_index("dp")
         self.first = jnp.where(self.group < self.groups // 2, 0, 1)
@@ -586,7 +587,7 @@
         return pltpu.make_async_remote_copy(
             src_ref=source,
             dst_ref=self.came.at[way, self.at(chunk)],
-            send_sem=self.send_sems.at[way, chunk],
+            send_sem=self.send_sems.at[way],
             recv_sem=self.recv_sems.at[way, chunk],
             device_id={"dp": target},
             device_id_type=MESH,
@@ -617,22 +618,20 @@
 
                 lax.fori_loop(0, self.chunks, start, 0)
 
-    def twin_copy(self, chunk):
+    def twin_copy(self, rows):
         side = lax.axis_index("seq")
         return pltpu.make_async_remote_copy(
-            src_ref=self.total.at[self.at(chunk)],
-            dst_ref=self.out.at[self.at(chunk), side],
-            send_sem=self.twin_send.at[chunk],
-            recv_sem=self.twin_recv.at[chunk],
+            src_ref=self.total.at[rows],
+            dst_ref=self.out.at[rows, side],
+            send_sem=self.twin_send,
+            recv_sem=self.twin_recv,
             device_id={"seq": 1 - side},
             device_id_type=MESH,
         )
 
-    def keep_copy(self, chunk):
+    def keep_copy(self, rows):
         return pltpu.make_async_copy(
-            self.total.at[self.at(chunk)],
-            self.out.at[self.at(chunk), lax.axis_index("seq")],
-            self.keep_sems.at[chunk],
+            self.total.at[rows], self.out.at[rows, lax.axis_index("seq")], self.keep_sem
         )
 
     def pass_on(self, way, chunk):
@@ -664,8 +663,12 @@
             value = value + self.came[1, rows].astype(jnp.float32)
             self.total[rows] = value.astype(jnp.bfloat16)
             if self.share:
-                self.keep_copy(chunk).start()
-                self.twin_copy(chunk).start()
+
+                @pl.when(lax.rem(chunk, LINE_SHARE) == LINE_SHARE - 1)
+                def _():
+                    done = pl.ds(chunk - (LINE_SHARE - 1), LINE_SHARE)
+                    self.keep_copy(done).start()
+                    self.twin_copy(done).start()
 
     def steps(self, count=None):
         last = self.chunks + LINE_LAG
@@ -679,19 +682,24 @@
         self.done = stop
 
     def end(self):
-        def one(chunk, carry):
-            for way in range(2):
-
-                @pl.when(self.goes(way))
-                def _():
-                    self.copy(self.going.at[way, self.at(chunk)], way, chunk).wait_send()
-
-            if self.share:
-                self.keep_copy(chunk).wait()
-                self.twin_copy(chunk).wait()
-            return carry
-
-        lax.fori_loop(0, self.chunks, one, 0)
+        for way in range(2):
+
+            @pl.when(self.goes(way))
+            def _():
+                whole_copy = pltpu.make_async_remote_copy(
+                    src_ref=self.going.at[way],
+                    dst_ref=self.came.at[way],
+                    send_sem=self.send_sems.at[way],
+                    recv_sem=self.recv_sems.at[way, 0],
+                    device_id={"dp": self.group},
+                    device_id_type=MESH,
+                )
+                whole_copy.wait_send()
+
+        if self.share:
+            everything = pl.ds(0, self.half[0])
+            self.keep_copy(everything).wait()
+            self.twin_copy(everything).wait()
 
 
 def reduce_all(terms, collective_id, line=None, tail=None):
@@ -1037,6 +1045,18 @@
     return list(results) + joined
 
 
+def plane_steps(tensors):
+    return [(step, turn_by) for step in range(tensors) for turn_by in range(2)][1:]
+
+
+def plane_peers(steps):
+    count, part = lax.axis_size("tensor"), lax.axis_index("tensor")
+    side = lax.axis_index("seq")
+    return [
+        (lax.rem(part + step, count), lax.rem(side + turn_by, 2)) for step, turn_by in steps
+    ]
+
+
 def join_stats(stats, collective_id):
     _, tensors, groups, _, _ = stats.shape
 
@@ -1049,32 +1069,32 @@
             [top, total, left[..., 2:3, :] + right[..., 2:3, :], left[..., 3:, :]], axis=-2
         )
 
+    plane = plane_steps(tensors)
+
     def kernel(
-        stats_ref, home, full, near, mid, mid_in, far, far_in,
-        near_send, near_recv, mid_send, mid_recv, far_send, far_recv,
+        stats_ref, home, full, mid_in, far, far_in, mid_send, mid_recv, far_send, far_recv
     ):
         group, part, side = lax.axis_index("dp"), lax.axis_index("tensor"), lax.axis_index("seq")
-        twin = 1 - side
-        parts, groups_else = others("tensor"), others("dp")
+        peers, groups_else = plane_peers(plane), others("dp")
         meet(
-            [{"seq": twin}]
-            + [{"tensor": peer} for peer in parts]
+            [{"tensor": peer, "seq": other} for peer, other in peers]
             + [{"dp": peer} for peer in groups_else]
         )
-        copy = send(stats_ref.at[twin], near, near_send.at[0], near_recv.at[0], {"seq": twin})
-        copy.wait()
-        for slot in range(tensors):
-            for spot in range(groups):
-                mid[slot, spot] = join(stats_ref[side, slot, spot], near[slot, spot])
         copies = [
-            send(mid.at[peer], mid_in.at[step], mid_send.at[0, step], mid_recv.at[0, step], {"tensor": peer})
-            for step, peer in enumerate(parts)
+            send(
+                stats_ref.at[other, peer],
+                mid_in.at[step],
+                mid_send.at[0, step],
+                mid_recv.at[0, step],
+                {"tensor": peer, "seq": other},
+            )
+            for step, (peer, other) in enumerate(peers)
         ]
         for copy in copies:
             copy.wait()
         for spot in range(groups):
-            total = mid[part, spot]
-            for step in range(tensors - 1):
+            total = stats_ref[side, part, spot]
+            for step in range(len(plane)):
                 total = join(total, mid_in[step, spot])
             far[spot] = total
         copies = [
@@ -1097,13 +1117,17 @@
             copy.wait()
         held = full.at[side, part]
         copies = [
-            send(held, held, mid_send.at[1, step], mid_recv.at[1, step], {"tensor": peer})
-            for step, peer in enumerate(parts)
+            send(
+                held,
+                held,
+                mid_send.at[1, step],
+                mid_recv.at[1, step],
+                {"tensor": peer, "seq": other},
+            )
+            for step, (peer, other) in enumerate(peers)
         ]
         for copy in copies:
             copy.wait()
-        held = full.at[side]
-        send(held, held, near_send.at[1], near_recv.at[1], {"seq": twin}).wait()
 
     tile = (8, LANES)
     dma = pltpu.SemaphoreType.DMA
@@ -1118,15 +1142,11 @@
         in_specs=[vmem],
         out_specs=[vmem, vmem],
         scratch_shapes=[
-            pltpu.VMEM((tensors, groups) + tile, jnp.float32),
-            pltpu.VMEM((tensors, groups) + tile, jnp.float32),
-            pltpu.VMEM((tensors - 1, groups) + tile, jnp.float32),
+            pltpu.VMEM((len(plane), groups) + tile, jnp.float32),
             pltpu.VMEM((groups,) + tile, jnp.float32),
             pltpu.VMEM((groups - 1,) + tile, jnp.float32),
-            dma((2,)),
-            dma((2,)),
-            dma((2, tensors - 1)),
-            dma((2, tensors - 1)),
+            dma((2, len(plane))),
+            dma((2, len(plane))),
             dma((2, groups - 1)),
             dma((2, groups - 1)),
         ],
@@ -1242,6 +1262,7 @@
 def finish(gain_grads, states, grad_ys, home, keep, table_squares, count, smalls, collective_id):
     tensors, groups = lax.axis_size("tensor"), lax.axis_size("dp")
     block = (8, D)
+    plane = plane_steps(tensors)
     gain_rows = 2 * LAYERS + 1
     operands = list(gain_grads) + list(states) + list(grad_ys) + [
         home, keep, table_squares, count
@@ -1255,12 +1276,11 @@
         home_ref, keep_ref, table_ref, count_ref = [refs.pop(0) for _ in range(4)]
         small_refs = [refs.pop(0) for _ in smalls]
         out_refs = [refs.pop(0) for _ in range(8)]
-        near, mid, far, near_send, near_recv, mid_send, mid_recv, far_send, far_recv = refs
+        mid, far, mid_send, mid_recv, far_send, far_recv = refs
         group, part, side = lax.axis_index("dp"), lax.axis_index("tensor"), lax.axis_index("seq")
-        parts, groups_else = others("tensor"), others("dp")
+        peers, groups_else = plane_peers(plane), others("dp")
         meet(
-            [{"seq": 1 - side}]
-            + [{"tensor": peer} for peer in parts]
+            [{"tensor": peer, "seq": other} for peer, other in peers]
             + [{"dp": peer} for peer in groups_else]
         )
         values = []
@@ -1278,15 +1298,20 @@
         blank = jnp.zeros((8 - gain_rows - 1, D), jnp.float32)
         total = jnp.concatenate([ref[...] for ref in gain_refs] + [row, blank], axis=0)
         stages = [
-            ("seq", near, side, [1 - side], near_send, near_recv),
-            ("tensor", mid, part, parts, mid_send, mid_recv),
-            ("dp", far, group, groups_else, far_send, far_recv),
+            (
+                mid,
+                2 * part + side,
+                [{"tensor": peer, "seq": other} for peer, other in peers],
+                mid_send,
+                mid_recv,
+            ),
+            (far, group, [{"dp": peer} for peer in groups_else], far_send, far_recv),
         ]
-        for axis, slots, me, peers, send_sems, recv_sems in stages:
+        for slots, me, targets, send_sems, recv_sems in stages:
             slots[me] = total
             copies = [
-                send(slots.at[me], slots.at[me], send_sems.at[step], recv_sems.at[step], {axis: peer})
-                for step, peer in enumerate(peers)
+                send(slots.at[me], slots.at[me], send_sems.at[step], recv_sems.at[step], target)
+                for step, target in enumerate(targets)
             ]
             for copy in copies:
                 copy.wait()
@@ -1329,13 +1354,10 @@
         in_specs=[vmem] * len(operands),
         out_specs=[vmem] * 8,
         scratch_shapes=[
-            pltpu.VMEM((2,) + block, jnp.float32),
-            pltpu.VMEM((tensors,) + block, jnp.float32),
+            pltpu.VMEM((2 * tensors,) + block, jnp.float32),
             pltpu.VMEM((groups,) + block, jnp.float32),
-            dma((1,)),
-            dma((1,)),
-            dma((tensors - 1,)),
-            dma((tensors - 1,)),
+            dma((len(plane),)),
+            dma((len(plane),)),
             dma((groups - 1,)),
             dma((groups - 1,)),
         ],

time: 707 us -> 705 us (level)
  no operation moved by 1% of the time
where the time goes in v10:
time: 705 us; the launch traced here: 698 us
  Pallas kernels  653 us (93%)
  other arithmetic  32.9 us (5%)
  local copies, waits for them, and re-layouts  7.19 us (1%)
    pallas_call x8, Pallas kernels, tensor_step(): pl.pallas_call(kernel, name=name, grid=(1,), out_shape=shapes, in_specs=i...  288 us
    pallas_call x2, Pallas kernels, reduce_all(): pl.pallas_call(kernel, name='reduce_all', out_shape=results + ([line.out_...  136 us
    pallas_call x2, Pallas kernels, gather_all(): pl.pallas_call(kernel, name='gather_all', out_shape=[jax.ShapeDtypeStruct...  81.2 us
    pallas_call x3, Pallas kernels, local_call(): pl.pallas_call(kernel, name=name, grid_spec=pltpu.PrefetchScalarGridSpec(...  65.5 us
    pallas_call x1, Pallas kernels, join_stats(): pl.pallas_call(kernel, name='join_stats', out_shape=[jax.ShapeDtypeStruct...  27.7 us
    sub x1, other arithmetic, adam_update(): weight - rate * (first_hat / (jnp.sqrt(second_hat) + ADAM_EPS) + decay *...  26.5 us
    pallas_call x1, Pallas kernels, look_back(): pl.pallas_call(kernel, name='look_back', grid_spec=pltpu.PrefetchScalarGr...  23.2 us

profile of v10, /device:TPU:0, one launch (start us, length us, event | category | flops | bytes accessed | tf_op | source)
XLA Modules:
  0.0 697.5 jit_solution(10277472456866538347)
XLA Ops:
  0.6 0.0 copy-start
  0.7 1.3 fusion.8
  2.0 0.9 select_reduce_fusion
  2.9 0.1 select_reduce_fusion.1
  3.1 0.7 copy.26.slot_ref
  5.1 0.5 compare_select_fusion.7.ends_ref
  6.3 0.1 pad.9.clone
  6.4 1.4 add_add_fusion.block_ref
  7.7 9.5 %spread_tokens.1 = (s32[32,1,128]{2,1,0:T(1,128)}, s32[32,1,128]{2,1,0:T(1,128)}, f32[32,1,128]{2,1,0:T(1,128)}, s32[32,1,128]{2,1,0:T(1,128)}, s32[1,128]{1,0:T(1,128)}, /*index=5*/f32[1,128]{1,0:T(1,128)}) custom-call(s32[16,128]{1,0:T(8,128)} %add_add_fusion.block_ref, s32[80,1]{1,0:T(8,128)} %copy.26.slot_ref, s32[1,128]{1,0:T(1,128)} %compare_select_fusion.7.ends_ref), custom_call_target="tpu_custom_call" | custom-call | flops 1000 | bytes 1000 | tf_op jit(solution)/shard_map/spread_tokens/pallas_call | solution.py:1237
  17.3 0.6 pad_add_fusion.plan_ref
  17.9 9.9 %prepare.1 = (bf16[3840,768]{1,0:T(8,128)(2,1)}, bf16[48,48,768]{2,1,0:T(8,128)(2,1)}, s32[3840,1]{1,0:T(8,128)}) custom-call(s32[81]{0:T(128)} %pad_add_fusion.plan_ref, f32[67,48,768]{2,1,0:T(8,128)} %master_ref.1), custom_call_target="tpu_custom_call" | custom-call | flops 1000 | bytes 1000 | tf_op jit(solution)/shard_map/prepare/pallas_call | solution.py:1404
  27.7 17.2 %look_up.1 = (bf16[4096,768]{1,0:T(8,128)(2,1)}, s32[32,1,128]{2,1,0:T(1,128)}, s32[8,768]{1,0:T(8,128)}) custom-call(s32[128]{0:T(128)} %bitcast.76, s32[3840,1]{1,0:T(8,128)} %get-tuple-element.93.ids_ref, s32[32,1,128]{2,1,0:T(1,128)} %get-tuple-element.94.tokens_ref, s32[32,1,128]{2,1,0:T(1,128)} %get-tuple-element.95.places_ref, ...), custom_call_target="tpu_custom_call" | custom-call | flops 1000 | bytes 1000 | tf_op jit(solution)/shard_map/look_up/pallas_call | solution.py:1490
  45.0 0.0 copy-done
  45.0 0.6 fusion.15
  45.6 72.3 %reduce_all.2 = (f32[128,768]{1,0:T(8,128)}, bf16[4,128,768]{2,1,0:T(8,128)(2,1)}, bf16[16,2,48,768]{3,2,1,0:T(8,128)(2,1)}) custom-call(bf16[2,4,4,128,768]{4,3,2,1,0:T(8,128)(2,1)} %bitcast.70, bf16[48,48,768]{2,1,0:T(8,128)(2,1)} %get-tuple-element.102.refs_1_.refs_2_.refs_7_.refs_8_, ...), custom_call_target="tpu_custom_call" | custom-call | flops 1000 | bytes 1000 | tf_op jit(solution)/shard_map/reduce_all/pallas_call | solution.py:857
  118.0 1.0 multiply_sine_fusion
  118.9 41.4 %inner_0.1 = (f32[128,768]{1,0:T(8,128)}, bf16[4,128,768]{2,1,0:T(8,128)(2,1)}, bf16[192,512]{1,0:T(8,128)(2,1)}, bf16[2,2,192,512]{3,2,1,0:T(8,128)(2,1)}, f32[...) custom-call(bf16[4,128,768]{2,1,0:T(8,128)(2,1)} %get-tuple-element.103.refs_0_.refs_1_, ...), custom_call_target="tpu_custom_call" | custom-call | flops 1000 | bytes 1000 | tf_op jit(solution)/shard_map/inner_0/pallas_call | solution.py:225
  160.4 28.5 %outcome_0.1 = (f32[128,768]{1,0:T(8,128)}, f32[128,768]{1,0:T(8,128)}, bf16[4,128,768]{2,1,0:T(8,128)(2,1)}, f32[768,512]{1,0:T(8,128)}, bf16[768,512]{1,0:T(8,128)(2,1)}) custom-call(bf16[4,128,768]{2,1,0:T(8,128)(2,1)} %get-tuple-element.106.refs_0_.refs_1_, bf16[1536,768]{1,0:T(8,128)(2,1)} %bitcast.56, bf16[1536,768]{1,0:T(8,128)(2,1)} %bitcast.60, ...), custom_call_target="tpu_custom_call" | custom-call | flops 1000 | bytes 1000 | tf_op jit(solution)/shard_map/outcome_0/pallas_call | solution.py:225
  188.9 41.6 %inner_1.1 = (f32[128,768]{1,0:T(8,128)}, bf16[4,128,768]{2,1,0:T(8,128)(2,1)}, bf16[192,512]{1,0:T(8,128)(2,1)}, bf16[2,2,192,512]{3,2,1,0:T(8,128)(2,1)}, f32[...) custom-call(bf16[4,128,768]{2,1,0:T(8,128)(2,1)} %get-tuple-element.109.refs_0_.refs_1_, ...), custom_call_target="tpu_custom_call" | custom-call | flops 1000 | bytes 1000 | tf_op jit(solution)/shard_map/inner_1/pallas_call | solution.py:225
  230.5 18.1 %outcome_1.1 = (f32[128,768]{1,0:T(8,128)}, f32[128,768]{1,0:T(8,128)}, bf16[128,768]{1,0:T(8,128)(2,1)}, f32[768,512]{1,0:T(8,128)}, bf16[768,512]{1,0:T(8,128)(2,1)}) custom-call(bf16[4,128,768]{2,1,0:T(8,128)(2,1)} %get-tuple-element.111.refs_0_.refs_1_, bf16[1536,768]{1,0:T(8,128)(2,1)} %bitcast.66, bf16[1536,768]{1,0:T(8,128)(2,1)} %bitcast.67, ...), custom_call_target="tpu_custom_call" | custom-call | flops 1000 | bytes 1000 | tf_op jit(solution)/shard_map/outcome_1/pallas_call | solution.py:225
  248.6 35.0 %gather_all.2 = bf16[2,4,4,128,768]{4,3,2,1,0:T(8,128)(2,1)} custom-call(bf16[128,768]{1,0:T(8,128)(2,1)} %get-tuple-element.115.refs_0_), custom_call_target="tpu_custom_call" | custom-call | flops 1000 | bytes 1000 | tf_op jit(solution)/shard_map/gather_all/pallas_call | solution.py:998
  283.6 18.0 %head_forward.1 = (bf16[3840,4096]{1,0:T(8,128)(2,1)}, f32[32,8,128]{2,1,0:T(8,128)}) custom-call(s32[128]{0:T(128)} %bitcast.77, s32[3840,1]{1,0:T(8,128)} %get-tuple-element.93.ids_ref, s32[32,1,128]{2,1,0:T(1,128)} %get-tuple-element.99.labels_ref, bf16[3840,768]{1,0:T(8,128)(2,1)} %get-tuple-element.96.table_ref, bf16[4096,768]{1,0:T(8,128)(2,1)} %bitcast.38, ...), custom_call_target="tpu_custom_call" | custom-call | flops 1000 | bytes 1000 | tf_op jit(solution)/shard_map/head_forward/pallas_call | solution.py:1490
  301.6 27.7 %join_stats.1 = (f32[8,128]{1,0:T(8,128)}, f32[2,4,4,8,128]{4,3,2,1,0:T(8,128)}) custom-call(f32[2,4,4,8,128]{4,3,2,1,0:T(8,128)} %bitcast.73), custom_call_target="tpu_custom_call" | custom-call | flops 1000 | bytes 1000 | tf_op jit(solution)/shard_map/join_stats/pallas_call | solution.py:1135
  329.3 30.2 %head_backward.1 = (bf16[32,128,768]{2,1,0:T(8,128)(2,1)}, f32[3840,768]{1,0:T(8,128)}) custom-call(s32[128]{0:T(128)} %bitcast.78, s32[3840,1]{1,0:T(8,128)} %get-tuple-element.93.ids_ref, s32[32,1,128]{2,1,0:T(1,128)} %get-tuple-element.99.labels_ref, f32[32,1,128]{2,1,0:T(1,128)} %get-tuple-element.100.keep_ref, ...), custom_call_target="tpu_custom_call" | custom-call | flops 1000 | bytes 1000 | tf_op jit(solution)/shard_map/head_backward/pallas_call | solution.py:1490
  359.5 63.4 %reduce_all.3 = (f32[128,768]{1,0:T(8,128)}, f32[128,768]{1,0:T(8,128)}, f32[1,768]{1,0:T(1,128)}, bf16[4,128,768]{2,1,0:T(8,128)(2,1)}) custom-call(bf16[2,4,4,128,768]{4,3,2,1,0:T(8,128)(2,1)} %bitcast.71, f32[128,768]{1,0:T(8,128)} %get-tuple-element.120.refs_1_, f32[1,768]{1,0:T(1,128)} %get-tuple-element.181.refs_4_.refs_2_, f32[5]{0:T(128)} %refs_15_.2), custom_call_target="tpu_custom_call" | custom-call | flops 1000 | bytes 1000 | tf_op jit(solution)/shard_map/reduce_all/pallas_call | solution.py:857
  422.9 28.1 %inner_back_1.1 = (f32[128,768]{1,0:T(8,128)}, f32[1,768]{1,0:T(1,128)}, bf16[4,128,768]{2,1,0:T(8,128)(2,1)}, bf16[16,48,768]{2,1,0:T(8,128)(2,1)}) custom-call(bf16[4,128,768]{2,1,0:T(8,128)(2,1)} %get-tuple-element.121.refs_0_, bf16[4,128,768]{2,1,0:T(8,128)(2,1)} %get-tuple-element.111.refs_0_.refs_1_, bf16[1536,768]{1,0:T(8,128)(2,1)} %bitcast.68, ...), custom_call_target="tpu_custom_call" | custom-call | flops 1000 | bytes 1000 | tf_op jit(solution)/shard_map/inner_back_1/pallas_call | solution.py:225
  451.0 50.2 %stream_back_1.1 = (f32[128,768]{1,0:T(8,128)}, f32[128,768]{1,0:T(8,128)}, f32[1,768]{1,0:T(1,128)}, bf16[4,128,768]{2,1,0:T(8,128)(2,1)}, bf16[8,48,768]{2,1,0:T(8,128)(2,1)}, /*index=5*/bf16[16,48,768]{2,1,0:T(8,128)(2,1)}) custom-call(bf16[4,128,768]{2,1,0:T(8,128)(2,1)} %get-tuple-element.125.refs_0_, ...), custom_call_target="tpu_custom_call" | custom-call | flops 1000 | bytes 1000 | tf_op jit(solution)/shard_map/stream_back_1/pallas_call | solution.py:225
  501.2 34.3 %inner_back_0.1 = (f32[128,768]{1,0:T(8,128)}, f32[1,768]{1,0:T(1,128)}, bf16[4,128,768]{2,1,0:T(8,128)(2,1)}, bf16[16,48,768]{2,1,0:T(8,128)(2,1)}, bf16[8,48,768]{2,1,0:T(8,128)(2,1)}) custom-call(bf16[4,128,768]{2,1,0:T(8,128)(2,1)} %get-tuple-element.133.refs_0_, bf16[4,128,768]{2,1,0:T(8,128)(2,1)} %get-tuple-element.106.refs_0_.refs_1_, ...), custom_call_target="tpu_custom_call" | custom-call | flops 1000 | bytes 1000 | tf_op jit(solution)/shard_map/inner_back_0/pallas_call | solution.py:225
  535.5 46.1 %stream_back_0.1 = (f32[128,768]{1,0:T(8,128)}, f32[128,768]{1,0:T(8,128)}, f32[1,768]{1,0:T(1,128)}, bf16[128,768]{1,0:T(8,128)(2,1)}, bf16[8,48,768]{2,1,0:T(8,128)(2,1)}, /*index=5*/bf16[16,48,768]{2,1,0:T(8,128)(2,1)}) custom-call(bf16[4,128,768]{2,1,0:T(8,128)(2,1)} %get-tuple-element.138.refs_0_, ...), custom_call_target="tpu_custom_call" | custom-call | flops 1000 | bytes 1000 | tf_op jit(solution)/shard_map/stream_back_0/pallas_call | solution.py:225
  581.6 46.2 %gather_all.3 = (bf16[2,4,4,128,768]{4,3,2,1,0:T(8,128)(2,1)}, bf16[8,48,768]{2,1,0:T(8,128)(2,1)}) custom-call(bf16[128,768]{1,0:T(8,128)(2,1)} %get-tuple-element.146.refs_0_, bf16[8,48,768]{2,1,0:T(8,128)(2,1)} %get-tuple-element.147.refs_1_), custom_call_target="tpu_custom_call" | custom-call | flops 1000 | bytes 1000 | tf_op jit(solution)/shard_map/gather_all/pallas_call | solution.py:998
  627.8 0.6 stack.23.slot_ref
  628.4 23.2 %look_back.1 = (f32[67,48,768]{2,1,0:T(8,128)}, f32[8,768]{1,0:T(8,128)}) custom-call(s32[128]{0:T(128)} %bitcast.79, s32[5,80]{1,0:T(8,128)} %stack.23.slot_ref, s32[3840,1]{1,0:T(8,128)} %get-tuple-element.93.ids_ref, s32[32,1,128]{2,1,0:T(1,128)} %get-tuple-element.94.tokens_ref, s32[32,1,128]{2,1,0:T(1,128)} %get-tuple-element.97.ranks_ref, ...), custom_call_target="tpu_custom_call" | custom-call | flops 1000 | bytes 1000 | tf_op jit(solution)/shard_map/look_back/pallas_call | solution.py:1847
  651.6 0.5 compare_select_fusion.refs_11_
  652.1 12.2 %finish.1 = (f32[5,768]{1,0:T(8,128)}, f32[5,768]{1,0:T(8,128)}, f32[5,768]{1,0:T(8,128)}, f32[1,5]{1,0:T(1,128)}, f32[1,5]{1,0:T(1,128)}, /*index=5*/f32[1,5]{1,0:T(1,128)}, f32[1,128]{1,0:T(1,128)}, f32[8,128]{1,0:T(8,128)}) custom-call(f32[1,768]{1,0:T(1,128)} %get-tuple-element.155.refs_0_, f32[1,768]{1,0:T(1,128)} %get-tuple-element.156.refs_1_, ...), custom_call_target="tpu_custom_call" | custom-call | flops 1000 | bytes 1000 | tf_op jit(solution)/shard_map/finish/pallas_call | solution.py:1346
  664.4 1.2 slice.32
  665.6 0.0 copy-start.8
  665.6 0.0 copy-start.7
  665.6 0.0 copy-start.6
  665.6 26.5 %multiply_subtract_fusion = (f32[67,48,768]{2,1,0:T(8,128)}, f32[67,48,768]{2,1,0:T(8,128)}, f32[67,48,768]{2,1,0:T(8,128)}) fusion(f32[67,48,768]{2,1,0:T(8,128)} %master_ref.1, f32[67,48,768]{2,1,0:T(8,128)} %get-tuple-element.154, f32[]{:T(128)} %bitcast.23, f32[67,48,768]{2,1,0:T(8,128)} %param.18, f32[67,48,768]{2,1,0:T(8,128)} %param.19), kind=kLoop, calls=%fused_computation.2 | loop fusion | flops 39518208 | bytes 69156864 | tf_op jit(solution)/shard_map/sub | solution.py:53
  692.1 0.6 fusion.16
  692.7 0.6 copy.35
  693.3 0.6 copy.36
  694.0 0.6 copy.37
  694.6 0.5 copy.38
  695.1 0.5 copy.39
  695.6 0.0 copy-done.6
  695.6 0.5 copy.40
  696.1 0.0 copy-done.5
  (17 shorter events, 0.1 us)
Async XLA Ops:
  0.6 44.3 %copy-start = (f32[5,768]{1,0:T(8,128)S(1)}, f32[5,768]{1,0:T(8,128)}, u32[]{:S(2)}) copy-start(f32[5,768]{1,0:T(8,128)} %refs_14_.3) | copy-start | bytes 46084
  665.6 26.6 %copy-start.4 = (f32[1,128]{1,0:T(1,128)S(1)}, f32[1,128]{1,0:T(1,128)}, u32[]{:S(2)}) copy-start(f32[1,128]{1,0:T(1,128)} %get-tuple-element.171) | copy-start | bytes 1540
  665.6 27.2 %copy-start.3 = (f32[5,768]{1,0:T(8,128)S(1)}, f32[5,768]{1,0:T(8,128)}, u32[]{:S(2)}) copy-start(f32[5,768]{1,0:T(8,128)} %get-tuple-element.214) | copy-start | bytes 46084
  665.6 27.8 %copy-start.2 = (f32[5,768]{1,0:T(8,128)S(1)}, f32[5,768]{1,0:T(8,128)}, u32[]{:S(2)}) copy-start(f32[5,768]{1,0:T(8,128)} %get-tuple-element.215) | copy-start | bytes 46084
  665.6 28.4 %copy-start.1 = (f32[5,768]{1,0:T(8,128)S(1)}, f32[5,768]{1,0:T(8,128)}, u32[]{:S(2)}) copy-start(f32[5,768]{1,0:T(8,128)} %get-tuple-element.216) | copy-start | bytes 46084
  665.6 29.0 %copy-start.8 = (f32[1,5]{1,0:T(1,128)S(1)}, f32[1,5]{1,0:T(1,128)}, u32[]{:S(2)}) copy-start(f32[1,5]{1,0:T(1,128)} %get-tuple-element.168) | copy-start | bytes 64
  665.6 29.5 %copy-start.7 = (f32[1,5]{1,0:T(1,128)S(1)}, f32[1,5]{1,0:T(1,128)}, u32[]{:S(2)}) copy-start(f32[1,5]{1,0:T(1,128)} %get-tuple-element.169) | copy-start | bytes 64
  665.6 30.0 %copy-start.6 = (f32[1,5]{1,0:T(1,128)S(1)}, f32[1,5]{1,0:T(1,128)}, u32[]{:S(2)}) copy-start(f32[1,5]{1,0:T(1,128)} %get-tuple-element.170) | copy-start | bytes 64
  665.6 30.5 %copy-start.5 = (f32[1,128]{1,0:T(1,128)S(1)}, f32[1,128]{1,0:T(1,128)}, u32[]{:S(2)}) copy-start(f32[1,128]{1,0:T(1,128)} %get-tuple-element.163.refs_13_) | copy-start | bytes 1540

commit v11 on v10

--- a/solution.py
+++ b/solution.py
@@ -285,6 +285,7 @@
         cosine, sine = cosine_ref[...], sine_ref[...]
         rows = normed_ref[...].reshape(count, D)
         joined = contract_last(qkv_ref[...], rows)
+        tick()
         for head in range(heads):
             span = slice(head * HEAD_DIM, (head + 1) * HEAD_DIM)
             keys = joined[width + head * HEAD_DIM : width + (head + 1) * HEAD_DIM]
@@ -377,6 +378,7 @@
         cosine, sine = cosine_ref[...], -sine_ref[...]
         scale = HEAD_DIM ** (-0.5)
         grads = contract_last(out_ref[...], grad_ref[...].reshape(count, D)).astype(jnp.bfloat16)
+        tick()
         own_grads = []
         masks = masks_of(count, side)
         for head in range(heads):
@@ -771,6 +773,8 @@
         for place in range(groups):
             near_copies[place].wait_recv()
             own_copies[place].wait()
+            if line and place == 2:
+                line.steps(1)
             for slot in range(tensors):
                 mid[place, slot] = (
                     own[place, slot].astype(jnp.float32) + near[place, slot].astype(jnp.float32)
@@ -1832,7 +1836,7 @@
                 def _():
                     out_ref[part, :] = jnp.zeros((half_rows, D), jnp.float32)
 
-                slots_ref[place] = out_ref[part, :]
+                slots_ref[place] = out_ref[part, :].astype(jnp.bfloat16)
 
             values = out_ref[...]
             squares_ref[...] += (values * values).reshape(block // 8, 8, D).sum(axis=0)
@@ -1873,7 +1877,7 @@
             ],
         ),
         out_shape=[
-            jax.ShapeDtypeStruct((slots, half_rows, D), jnp.float32),
+            jax.ShapeDtypeStruct((slots, half_rows, D), jnp.bfloat16),
             jax.ShapeDtypeStruct((8, D), jnp.float32),
         ],
         cost_estimate=SHORT,
@@ -2167,7 +2171,7 @@
     new_mix, new_mix_first, new_mix_second = [value[0] for value in news[3:6]]
     loss_sum, clip_norm = news[6][0, 0], news[6][0, 1]
     token_count = count[0, 0]
-    owned = owned * news[7][0, 0]
+    owned = owned.astype(jnp.float32) * news[7][0, 0]
     new_master, new_first, new_second = adam_update(
         master, first_moment, second_moment, owned, RATE_MATRIX, DECAY_MATRIX
     )

time: 705 us -> 705 us (level)
  no operation moved by 1% of the time
where the time goes in v11:
time: 705 us; the launch traced here: 701 us
  Pallas kernels  658 us (93%)
  other arithmetic  31.9 us (5%)
  local copies, waits for them, and re-layouts  7.19 us (1%)
    pallas_call x8, Pallas kernels, tensor_step(): pl.pallas_call(kernel, name=name, grid=(1,), out_shape=shapes, in_specs=i...  295 us
    pallas_call x2, Pallas kernels, reduce_all(): pl.pallas_call(kernel, name='reduce_all', out_shape=results + ([line.out_...  138 us
    pallas_call x2, Pallas kernels, gather_all(): pl.pallas_call(kernel, name='gather_all', out_shape=[jax.ShapeDtypeStruct...  81.9 us
    pallas_call x3, Pallas kernels, local_call(): pl.pallas_call(kernel, name=name, grid_spec=pltpu.PrefetchScalarGridSpec(...  58.8 us
    pallas_call x1, Pallas kernels, join_stats(): pl.pallas_call(kernel, name='join_stats', out_shape=[jax.ShapeDtypeStruct...  30 us
    sub x1, other arithmetic, adam_update(): weight - rate * (first_hat / (jnp.sqrt(second_hat) + ADAM_EPS) + decay *...  25.6 us
    pallas_call x1, Pallas kernels, look_back(): pl.pallas_call(kernel, name='look_back', grid_spec=pltpu.PrefetchScalarGr...  22.2 us

profile of v11, /device:TPU:0, one launch (start us, length us, event | category | flops | bytes accessed | tf_op | source)
XLA Modules:
  0.0 701.3 jit_solution(16858087877219743590)
XLA Ops:
  0.6 0.0 copy-start
  0.7 1.3 fusion.8
  2.0 0.9 select_reduce_fusion
  2.9 0.1 select_reduce_fusion.1
  3.1 0.7 copy.26.slot_ref
  5.1 0.5 compare_select_fusion.7.ends_ref
  6.3 0.1 pad.9.clone
  6.4 1.4 add_add_fusion.block_ref
  7.7 9.5 %spread_tokens.1 = (s32[32,1,128]{2,1,0:T(1,128)}, s32[32,1,128]{2,1,0:T(1,128)}, f32[32,1,128]{2,1,0:T(1,128)}, s32[32,1,128]{2,1,0:T(1,128)}, s32[1,128]{1,0:T(1,128)}, /*index=5*/f32[1,128]{1,0:T(1,128)}) custom-call(s32[16,128]{1,0:T(8,128)} %add_add_fusion.block_ref, s32[80,1]{1,0:T(8,128)} %copy.26.slot_ref, s32[1,128]{1,0:T(1,128)} %compare_select_fusion.7.ends_ref), custom_call_target="tpu_custom_call" | custom-call | flops 1000 | bytes 1000 | tf_op jit(solution)/shard_map/spread_tokens/pallas_call | solution.py:1241
  17.3 0.6 pad_add_fusion.plan_ref
  17.9 9.9 %prepare.1 = (bf16[3840,768]{1,0:T(8,128)(2,1)}, bf16[48,48,768]{2,1,0:T(8,128)(2,1)}, s32[3840,1]{1,0:T(8,128)}) custom-call(s32[81]{0:T(128)} %pad_add_fusion.plan_ref, f32[67,48,768]{2,1,0:T(8,128)} %master_ref.1), custom_call_target="tpu_custom_call" | custom-call | flops 1000 | bytes 1000 | tf_op jit(solution)/shard_map/prepare/pallas_call | solution.py:1408
  27.8 16.4 %look_up.1 = (bf16[4096,768]{1,0:T(8,128)(2,1)}, s32[32,1,128]{2,1,0:T(1,128)}, s32[8,768]{1,0:T(8,128)}) custom-call(s32[128]{0:T(128)} %bitcast.76, s32[3840,1]{1,0:T(8,128)} %get-tuple-element.93.ids_ref, s32[32,1,128]{2,1,0:T(1,128)} %get-tuple-element.94.tokens_ref, s32[32,1,128]{2,1,0:T(1,128)} %get-tuple-element.95.places_ref, ...), custom_call_target="tpu_custom_call" | custom-call | flops 1000 | bytes 1000 | tf_op jit(solution)/shard_map/look_up/pallas_call | solution.py:1494
  44.1 0.0 copy-done
  44.1 0.6 fusion.15
  44.7 71.5 %reduce_all.2 = (f32[128,768]{1,0:T(8,128)}, bf16[4,128,768]{2,1,0:T(8,128)(2,1)}, bf16[16,2,48,768]{3,2,1,0:T(8,128)(2,1)}) custom-call(bf16[2,4,4,128,768]{4,3,2,1,0:T(8,128)(2,1)} %bitcast.70, bf16[48,48,768]{2,1,0:T(8,128)(2,1)} %get-tuple-element.102.refs_1_.refs_2_.refs_7_.refs_8_, ...), custom_call_target="tpu_custom_call" | custom-call | flops 1000 | bytes 1000 | tf_op jit(solution)/shard_map/reduce_all/pallas_call | solution.py:861
  116.2 1.0 multiply_sine_fusion
  117.2 43.6 %inner_0.1 = (f32[128,768]{1,0:T(8,128)}, bf16[4,128,768]{2,1,0:T(8,128)(2,1)}, bf16[192,512]{1,0:T(8,128)(2,1)}, bf16[2,2,192,512]{3,2,1,0:T(8,128)(2,1)}, f32[...) custom-call(bf16[4,128,768]{2,1,0:T(8,128)(2,1)} %get-tuple-element.103.refs_0_.refs_1_, ...), custom_call_target="tpu_custom_call" | custom-call | flops 1000 | bytes 1000 | tf_op jit(solution)/shard_map/inner_0/pallas_call | solution.py:225
  160.8 29.2 %outcome_0.1 = (f32[128,768]{1,0:T(8,128)}, f32[128,768]{1,0:T(8,128)}, bf16[4,128,768]{2,1,0:T(8,128)(2,1)}, f32[768,512]{1,0:T(8,128)}, bf16[768,512]{1,0:T(8,128)(2,1)}) custom-call(bf16[4,128,768]{2,1,0:T(8,128)(2,1)} %get-tuple-element.106.refs_0_.refs_1_, bf16[1536,768]{1,0:T(8,128)(2,1)} %bitcast.56, bf16[1536,768]{1,0:T(8,128)(2,1)} %bitcast.60, ...), custom_call_target="tpu_custom_call" | custom-call | flops 1000 | bytes 1000 | tf_op jit(solution)/shard_map/outcome_0/pallas_call | solution.py:225
  190.0 43.5 %inner_1.1 = (f32[128,768]{1,0:T(8,128)}, bf16[4,128,768]{2,1,0:T(8,128)(2,1)}, bf16[192,512]{1,0:T(8,128)(2,1)}, bf16[2,2,192,512]{3,2,1,0:T(8,128)(2,1)}, f32[...) custom-call(bf16[4,128,768]{2,1,0:T(8,128)(2,1)} %get-tuple-element.109.refs_0_.refs_1_, ...), custom_call_target="tpu_custom_call" | custom-call | flops 1000 | bytes 1000 | tf_op jit(solution)/shard_map/inner_1/pallas_call | solution.py:225
  233.5 18.3 %outcome_1.1 = (f32[128,768]{1,0:T(8,128)}, f32[128,768]{1,0:T(8,128)}, bf16[128,768]{1,0:T(8,128)(2,1)}, f32[768,512]{1,0:T(8,128)}, bf16[768,512]{1,0:T(8,128)(2,1)}) custom-call(bf16[4,128,768]{2,1,0:T(8,128)(2,1)} %get-tuple-element.111.refs_0_.refs_1_, bf16[1536,768]{1,0:T(8,128)(2,1)} %bitcast.66, bf16[1536,768]{1,0:T(8,128)(2,1)} %bitcast.67, ...), custom_call_target="tpu_custom_call" | custom-call | flops 1000 | bytes 1000 | tf_op jit(solution)/shard_map/outcome_1/pallas_call | solution.py:225
  251.9 35.7 %gather_all.2 = bf16[2,4,4,128,768]{4,3,2,1,0:T(8,128)(2,1)} custom-call(bf16[128,768]{1,0:T(8,128)(2,1)} %get-tuple-element.115.refs_0_), custom_call_target="tpu_custom_call" | custom-call | flops 1000 | bytes 1000 | tf_op jit(solution)/shard_map/gather_all/pallas_call | solution.py:1002
  287.5 15.7 %head_forward.1 = (bf16[3840,4096]{1,0:T(8,128)(2,1)}, f32[32,8,128]{2,1,0:T(8,128)}) custom-call(s32[128]{0:T(128)} %bitcast.77, s32[3840,1]{1,0:T(8,128)} %get-tuple-element.93.ids_ref, s32[32,1,128]{2,1,0:T(1,128)} %get-tuple-element.99.labels_ref, bf16[3840,768]{1,0:T(8,128)(2,1)} %get-tuple-element.96.table_ref, bf16[4096,768]{1,0:T(8,128)(2,1)} %bitcast.38, ...), custom_call_target="tpu_custom_call" | custom-call | flops 1000 | bytes 1000 | tf_op jit(solution)/shard_map/head_forward/pallas_call | solution.py:1494
  303.3 30.0 %join_stats.1 = (f32[8,128]{1,0:T(8,128)}, f32[2,4,4,8,128]{4,3,2,1,0:T(8,128)}) custom-call(f32[2,4,4,8,128]{4,3,2,1,0:T(8,128)} %bitcast.73), custom_call_target="tpu_custom_call" | custom-call | flops 1000 | bytes 1000 | tf_op jit(solution)/shard_map/join_stats/pallas_call | solution.py:1139
  333.3 26.8 %head_backward.1 = (bf16[32,128,768]{2,1,0:T(8,128)(2,1)}, f32[3840,768]{1,0:T(8,128)}) custom-call(s32[128]{0:T(128)} %bitcast.78, s32[3840,1]{1,0:T(8,128)} %get-tuple-element.93.ids_ref, s32[32,1,128]{2,1,0:T(1,128)} %get-tuple-element.99.labels_ref, f32[32,1,128]{2,1,0:T(1,128)} %get-tuple-element.100.keep_ref, ...), custom_call_target="tpu_custom_call" | custom-call | flops 1000 | bytes 1000 | tf_op jit(solution)/shard_map/head_backward/pallas_call | solution.py:1494
  360.1 66.8 %reduce_all.3 = (f32[128,768]{1,0:T(8,128)}, f32[128,768]{1,0:T(8,128)}, f32[1,768]{1,0:T(1,128)}, bf16[4,128,768]{2,1,0:T(8,128)(2,1)}) custom-call(bf16[2,4,4,128,768]{4,3,2,1,0:T(8,128)(2,1)} %bitcast.71, f32[128,768]{1,0:T(8,128)} %get-tuple-element.120.refs_1_, f32[1,768]{1,0:T(1,128)} %get-tuple-element.181.refs_4_.refs_2_, f32[5]{0:T(128)} %refs_15_.2), custom_call_target="tpu_custom_call" | custom-call | flops 1000 | bytes 1000 | tf_op jit(solution)/shard_map/reduce_all/pallas_call | solution.py:861
  426.9 28.0 %inner_back_1.1 = (f32[128,768]{1,0:T(8,128)}, f32[1,768]{1,0:T(1,128)}, bf16[4,128,768]{2,1,0:T(8,128)(2,1)}, bf16[16,48,768]{2,1,0:T(8,128)(2,1)}) custom-call(bf16[4,128,768]{2,1,0:T(8,128)(2,1)} %get-tuple-element.121.refs_0_, bf16[4,128,768]{2,1,0:T(8,128)(2,1)} %get-tuple-element.111.refs_0_.refs_1_, bf16[1536,768]{1,0:T(8,128)(2,1)} %bitcast.68, ...), custom_call_target="tpu_custom_call" | custom-call | flops 1000 | bytes 1000 | tf_op jit(solution)/shard_map/inner_back_1/pallas_call | solution.py:225
  455.0 51.9 %stream_back_1.1 = (f32[128,768]{1,0:T(8,128)}, f32[128,768]{1,0:T(8,128)}, f32[1,768]{1,0:T(1,128)}, bf16[4,128,768]{2,1,0:T(8,128)(2,1)}, bf16[8,48,768]{2,1,0:T(8,128)(2,1)}, /*index=5*/bf16[16,48,768]{2,1,0:T(8,128)(2,1)}) custom-call(bf16[4,128,768]{2,1,0:T(8,128)(2,1)} %get-tuple-element.125.refs_0_, ...), custom_call_target="tpu_custom_call" | custom-call | flops 1000 | bytes 1000 | tf_op jit(solution)/shard_map/stream_back_1/pallas_call | solution.py:225
  506.8 34.3 %inner_back_0.1 = (f32[128,768]{1,0:T(8,128)}, f32[1,768]{1,0:T(1,128)}, bf16[4,128,768]{2,1,0:T(8,128)(2,1)}, bf16[16,48,768]{2,1,0:T(8,128)(2,1)}, bf16[8,48,768]{2,1,0:T(8,128)(2,1)}) custom-call(bf16[4,128,768]{2,1,0:T(8,128)(2,1)} %get-tuple-element.133.refs_0_, bf16[4,128,768]{2,1,0:T(8,128)(2,1)} %get-tuple-element.106.refs_0_.refs_1_, ...), custom_call_target="tpu_custom_call" | custom-call | flops 1000 | bytes 1000 | tf_op jit(solution)/shard_map/inner_back_0/pallas_call | solution.py:225
  541.1 46.1 %stream_back_0.1 = (f32[128,768]{1,0:T(8,128)}, f32[128,768]{1,0:T(8,128)}, f32[1,768]{1,0:T(1,128)}, bf16[128,768]{1,0:T(8,128)(2,1)}, bf16[8,48,768]{2,1,0:T(8,128)(2,1)}, /*index=5*/bf16[16,48,768]{2,1,0:T(8,128)(2,1)}) custom-call(bf16[4,128,768]{2,1,0:T(8,128)(2,1)} %get-tuple-element.138.refs_0_, ...), custom_call_target="tpu_custom_call" | custom-call | flops 1000 | bytes 1000 | tf_op jit(solution)/shard_map/stream_back_0/pallas_call | solution.py:225
  587.2 46.3 %gather_all.3 = (bf16[2,4,4,128,768]{4,3,2,1,0:T(8,128)(2,1)}, bf16[8,48,768]{2,1,0:T(8,128)(2,1)}) custom-call(bf16[128,768]{1,0:T(8,128)(2,1)} %get-tuple-element.146.refs_0_, bf16[8,48,768]{2,1,0:T(8,128)(2,1)} %get-tuple-element.147.refs_1_), custom_call_target="tpu_custom_call" | custom-call | flops 1000 | bytes 1000 | tf_op jit(solution)/shard_map/gather_all/pallas_call | solution.py:1002
  633.5 0.6 stack.23.slot_ref
  634.1 22.2 %look_back.1 = (bf16[67,48,768]{2,1,0:T(8,128)(2,1)}, f32[8,768]{1,0:T(8,128)}) custom-call(s32[128]{0:T(128)} %bitcast.79, s32[5,80]{1,0:T(8,128)} %stack.23.slot_ref, s32[3840,1]{1,0:T(8,128)} %get-tuple-element.93.ids_ref, s32[32,1,128]{2,1,0:T(1,128)} %get-tuple-element.94.tokens_ref, s32[32,1,128]{2,1,0:T(1,128)} %get-tuple-element.97.ranks_ref, ...), custom_call_target="tpu_custom_call" | custom-call | flops 1000 | bytes 1000 | tf_op jit(solution)/shard_map/look_back/pallas_call | solution.py:1851
  656.3 0.5 compare_select_fusion.refs_11_
  656.8 12.2 %finish.1 = (f32[5,768]{1,0:T(8,128)}, f32[5,768]{1,0:T(8,128)}, f32[5,768]{1,0:T(8,128)}, f32[1,5]{1,0:T(1,128)}, f32[1,5]{1,0:T(1,128)}, /*index=5*/f32[1,5]{1,0:T(1,128)}, f32[1,128]{1,0:T(1,128)}, f32[8,128]{1,0:T(8,128)}) custom-call(f32[1,768]{1,0:T(1,128)} %get-tuple-element.155.refs_0_, f32[1,768]{1,0:T(1,128)} %get-tuple-element.156.refs_1_, ...), custom_call_target="tpu_custom_call" | custom-call | flops 1000 | bytes 1000 | tf_op jit(solution)/shard_map/finish/pallas_call | solution.py:1350
  669.1 1.2 slice.32
  670.3 0.0 copy-start.8
  670.3 0.0 copy-start.7
  670.3 0.0 copy-start.6
  670.3 25.6 %multiply_subtract_fusion = (f32[67,48,768]{2,1,0:T(8,128)}, f32[67,48,768]{2,1,0:T(8,128)}, f32[67,48,768]{2,1,0:T(8,128)}) fusion(f32[67,48,768]{2,1,0:T(8,128)} %master_ref.1, f32[]{:T(128)} %bitcast.23, bf16[67,48,768]{2,1,0:T(8,128)(2,1)} %get-tuple-element.154, f32[67,48,768]{2,1,0:T(8,128)} %param.18, f32[67,48,768]{2,1,0:T(8,128)} %param.19), kind=kLoop, calls=%fused_computation.2 | loop fusion | flops 41988096 | bytes 64217092 | tf_op jit(solution)/shard_map/sub | solution.py:53
  695.9 0.0 copy-done.4
  695.9 0.6 fusion.16
  696.5 0.6 copy.35
  697.1 0.6 copy.36
  697.7 0.0 copy-done.1
  697.7 0.6 copy.37
  698.3 0.5 copy.38
  698.8 0.5 copy.39
  699.3 0.5 copy.40
  (17 shorter events, 0.1 us)
Async XLA Ops:
  0.6 43.5 %copy-start = (f32[5,768]{1,0:T(8,128)S(1)}, f32[5,768]{1,0:T(8,128)}, u32[]{:S(2)}) copy-start(f32[5,768]{1,0:T(8,128)} %refs_14_.3) | copy-start | bytes 46084
  670.3 25.6 %copy-start.4 = (f32[1,128]{1,0:T(1,128)S(1)}, f32[1,128]{1,0:T(1,128)}, u32[]{:S(2)}) copy-start(f32[1,128]{1,0:T(1,128)} %get-tuple-element.171) | copy-start | bytes 1540
  670.3 26.2 %copy-start.3 = (f32[5,768]{1,0:T(8,128)S(1)}, f32[5,768]{1,0:T(8,128)}, u32[]{:S(2)}) copy-start(f32[5,768]{1,0:T(8,128)} %get-tuple-element.211) | copy-start | bytes 46084
  670.3 26.8 %copy-start.2 = (f32[5,768]{1,0:T(8,128)S(1)}, f32[5,768]{1,0:T(8,128)}, u32[]{:S(2)}) copy-start(f32[5,768]{1,0:T(8,128)} %get-tuple-element.212) | copy-start | bytes 46084
  670.3 27.4 %copy-start.1 = (f32[5,768]{1,0:T(8,128)S(1)}, f32[5,768]{1,0:T(8,128)}, u32[]{:S(2)}) copy-start(f32[5,768]{1,0:T(8,128)} %get-tuple-element.213) | copy-start | bytes 46084
  670.3 28.0 %copy-start.8 = (f32[1,5]{1,0:T(1,128)S(1)}, f32[1,5]{1,0:T(1,128)}, u32[]{:S(2)}) copy-start(f32[1,5]{1,0:T(1,128)} %get-tuple-element.168) | copy-start | bytes 64
  670.3 28.5 %copy-start.7 = (f32[1,5]{1,0:T(1,128)S(1)}, f32[1,5]{1,0:T(1,128)}, u32[]{:S(2)}) copy-start(f32[1,5]{1,0:T(1,128)} %get-tuple-element.169) | copy-start | bytes 64
  670.3 29.0 %copy-start.6 = (f32[1,5]{1,0:T(1,128)S(1)}, f32[1,5]{1,0:T(1,128)}, u32[]{:S(2)}) copy-start(f32[1,5]{1,0:T(1,128)} %get-tuple-element.170) | copy-start | bytes 64
  670.3 29.5 %copy-start.5 = (f32[1,128]{1,0:T(1,128)S(1)}, f32[1,128]{1,0:T(1,128)}, u32[]{:S(2)}) copy-start(f32[1,128]{1,0:T(1,128)} %get-tuple-element.163.refs_13_) | copy-start | bytes 1540

commit v12 on v11

--- a/solution.py
+++ b/solution.py
@@ -119,6 +119,8 @@
     share = extras[0].shape[0]
     reduce = work is not None
     work = work or Work(None, None, [], [], [], [])
+    arrays = list(work.operands) + list(extras)
+    parts_of = list(work.specs) + [None] * len(extras)
 
     def kernel(*refs):
         refs = list(refs)
@@ -126,14 +128,22 @@
         def take(count):
             return [refs.pop(0) for _ in range(count)]
 
-        work_refs = take(len(work.operands))
-        extra_refs = take(len(extras))
+        array_refs = take(len(arrays))
         scalar_refs = take(len(scalars))
         source_refs = take(len(line.operands)) if line else []
         out_refs = take(len(outs))
         (full,) = take(1) if gather else [None]
         work_outs = take(len(work.outs))
         (joined,) = take(1) if line else [None]
+        held = take(len(arrays))
+        (load_sems,) = take(1)
+        loads = []
+        for index, (ref, part, target) in enumerate(zip(array_refs, parts_of, held)):
+            if part:
+                ref = ref.at[pl.ds(part[0] * part[1], part[0])]
+            loads.append(pltpu.make_async_copy(ref, target, load_sems.at[index]))
+            loads[-1].start()
+        work_refs, extra_refs = held[: len(work.operands)], held[len(work.operands) :]
         send_sems, recv_sems = take(2)
         partial_ref, outgoing, arrived = take(3) if reduce else [None] * 3
         if line:
@@ -155,6 +165,8 @@
         )
         if line:
             line.begin()
+        for load in loads:
+            load.wait()
         total = None
         if reduce:
             work.before(work_refs, work_outs, refs, partial_ref, tick)
@@ -209,10 +221,14 @@
         shapes.append(jax.ShapeDtypeStruct((parts, share, D), jnp.bfloat16))
     shapes += [jax.ShapeDtypeStruct(shape, dtype) for shape, dtype in work.outs]
     out_specs = [vmem] * len(shapes)
-    operands = list(work.operands) + list(extras) + list(scalars)
-    in_specs = list(work.specs) + [vmem] * len(extras) + [smem] * len(scalars)
+    operands = arrays + list(scalars)
+    in_specs = [pl.BlockSpec(memory_space=pl.ANY)] * len(arrays) + [smem] * len(scalars)
     dma = pltpu.SemaphoreType.DMA
-    buffers = [dma((2, parts - 1))] * 2
+    buffers = [
+        pltpu.VMEM((part[0], D) if part else array.shape, array.dtype)
+        for array, part in zip(arrays, parts_of)
+    ]
+    buffers += [dma((len(arrays),))] + [dma((2, parts - 1))] * 2
     if reduce:
         buffers += [pltpu.VMEM((parts * share, D), jnp.float32)]
         buffers += [pltpu.VMEM((parts - 1, share, D), jnp.bfloat16)] * 2
@@ -241,7 +257,7 @@
 
 
 def part_spec(rows, index):
-    return pl.BlockSpec((rows, D), lambda step: (index, 0), pipeline_mode=pl.Buffered(1))
+    return rows, index
 
 
 def turn(block, cosine, sine):
@@ -285,7 +301,6 @@
         cosine, sine = cosine_ref[...], sine_ref[...]
         rows = normed_ref[...].reshape(count, D)
         joined = contract_last(qkv_ref[...], rows)
-        tick()
         for head in range(heads):
             span = slice(head * HEAD_DIM, (head + 1) * HEAD_DIM)
             keys = joined[width + head * HEAD_DIM : width + (head + 1) * HEAD_DIM]
@@ -328,7 +343,7 @@
         before,
         None,
         [normed, table, table, cosine, sine],
-        [VMEM_SPEC, part_spec(3 * width, 0), part_spec(width, 3), VMEM_SPEC, VMEM_SPEC],
+        [None, part_spec(3 * width, 0), part_spec(width, 3), None, None],
         [
             ((width, count), low),
             ((2, 2, width, count), low),
@@ -378,7 +393,6 @@
         cosine, sine = cosine_ref[...], -sine_ref[...]
         scale = HEAD_DIM ** (-0.5)
         grads = contract_last(out_ref[...], grad_ref[...].reshape(count, D)).astype(jnp.bfloat16)
-        tick()
         own_grads = []
         masks = masks_of(count, side)
         for head in range(heads):
@@ -437,7 +451,7 @@
         before,
         during,
         [grad, normed, table, table, queries, both, logs, attended, cosine, sine],
-        [VMEM_SPEC, VMEM_SPEC, part_spec(3 * width, 0), part_spec(width, 3)] + [VMEM_SPEC] * 6,
+        [None, None, part_spec(3 * width, 0), part_spec(width, 3)] + [None] * 6,
         [((blocks, half_rows, D), low)],
         [
             pltpu.VMEM((2, width, count), low),
@@ -477,7 +491,7 @@
         before,
         None,
         [normed, up[0], down[0]],
-        [VMEM_SPEC, part_spec(units, up[1]), part_spec(units, down[1])],
+        [None, part_spec(units, up[1]), part_spec(units, down[1])],
         [((units, count), jnp.float32), ((units, count), jnp.bfloat16)],
         [],
     )
@@ -520,8 +534,8 @@
         before,
         during,
         [grad, normed, up[0], down[0], hidden, activated],
-        [VMEM_SPEC, VMEM_SPEC, part_spec(units, up[1]), part_spec(units, down[1])]
-        + [VMEM_SPEC] * 2,
+        [None, None, part_spec(units, up[1]), part_spec(units, down[1])]
+        + [None] * 2,
         [((2 * blocks, half_rows, D), low)],
         [
             pltpu.VMEM((units, count), low),

time: 705 us -> 691 us (0.980)
  Pallas kernels: 658 us -> 640 us
    pallas_call x8, Pallas kernels: 295 us -> 282 us  [tensor_step(): pl.pallas_call(kernel, name=name, grid=(1,), out_shape=shapes, in_specs=i...]
where the time goes in v12:
time: 691 us; the launch traced here: 684 us
  Pallas kernels  640 us (93%)
  other arithmetic  31.9 us (5%)
  local copies, waits for them, and re-layouts  7.19 us (1%)
    pallas_call x8, Pallas kernels, tensor_step(): pl.pallas_call(kernel, name=name, grid=(1,), out_shape=shapes, in_specs=i...  282 us
    pallas_call x2, Pallas kernels, reduce_all(): pl.pallas_call(kernel, name='reduce_all', out_shape=results + ([line.out_...  132 us
    pallas_call x2, Pallas kernels, gather_all(): pl.pallas_call(kernel, name='gather_all', out_shape=[jax.ShapeDtypeStruct...  82 us
    pallas_call x3, Pallas kernels, local_call(): pl.pallas_call(kernel, name=name, grid_spec=pltpu.PrefetchScalarGridSpec(...  65.5 us
    sub x1, other arithmetic, adam_update(): weight - rate * (first_hat / (jnp.sqrt(second_hat) + ADAM_EPS) + decay *...  25.6 us
    pallas_call x1, Pallas kernels, join_stats(): pl.pallas_call(kernel, name='join_stats', out_shape=[jax.ShapeDtypeStruct...  25.5 us
    pallas_call x1, Pallas kernels, look_back(): pl.pallas_call(kernel, name='look_back', grid_spec=pltpu.PrefetchScalarGr...  22.2 us

profile of v12, /device:TPU:0, one launch (start us, length us, event | category | flops | bytes accessed | tf_op | source)
XLA Modules:
  0.0 683.9 jit_solution(16766263869900302926)
XLA Ops:
  0.6 0.0 copy-start
  0.7 1.3 fusion.8
  2.0 0.9 select_reduce_fusion
  2.9 0.1 select_reduce_fusion.1
  3.1 0.7 copy.26.slot_ref
  5.1 0.5 compare_select_fusion.7.ends_ref
  6.3 0.1 pad.9.clone
  6.4 1.4 add_add_fusion.block_ref
  7.7 9.5 %spread_tokens.1 = (s32[32,1,128]{2,1,0:T(1,128)}, s32[32,1,128]{2,1,0:T(1,128)}, f32[32,1,128]{2,1,0:T(1,128)}, s32[32,1,128]{2,1,0:T(1,128)}, s32[1,128]{1,0:T(1,128)}, /*index=5*/f32[1,128]{1,0:T(1,128)}) custom-call(s32[16,128]{1,0:T(8,128)} %add_add_fusion.block_ref, s32[80,1]{1,0:T(8,128)} %copy.26.slot_ref, s32[1,128]{1,0:T(1,128)} %compare_select_fusion.7.ends_ref), custom_call_target="tpu_custom_call" | custom-call | flops 1000 | bytes 1000 | tf_op jit(solution)/shard_map/spread_tokens/pallas_call | solution.py:1255
  17.3 0.6 pad_add_fusion.plan_ref
  17.9 9.9 %prepare.1 = (bf16[3840,768]{1,0:T(8,128)(2,1)}, bf16[48,48,768]{2,1,0:T(8,128)(2,1)}, s32[3840,1]{1,0:T(8,128)}) custom-call(s32[81]{0:T(128)} %pad_add_fusion.plan_ref, f32[67,48,768]{2,1,0:T(8,128)} %master_ref.1), custom_call_target="tpu_custom_call" | custom-call | flops 1000 | bytes 1000 | tf_op jit(solution)/shard_map/prepare/pallas_call | solution.py:1422
  27.7 17.2 %look_up.1 = (bf16[4096,768]{1,0:T(8,128)(2,1)}, s32[32,1,128]{2,1,0:T(1,128)}, s32[8,768]{1,0:T(8,128)}) custom-call(s32[128]{0:T(128)} %bitcast.76, s32[3840,1]{1,0:T(8,128)} %get-tuple-element.93.ids_ref, s32[32,1,128]{2,1,0:T(1,128)} %get-tuple-element.94.tokens_ref, s32[32,1,128]{2,1,0:T(1,128)} %get-tuple-element.95.places_ref, ...), custom_call_target="tpu_custom_call" | custom-call | flops 1000 | bytes 1000 | tf_op jit(solution)/shard_map/look_up/pallas_call | solution.py:1508
  45.0 0.0 copy-done
  45.0 0.6 fusion.15
  45.6 70.9 %reduce_all.2 = (f32[128,768]{1,0:T(8,128)}, bf16[4,128,768]{2,1,0:T(8,128)(2,1)}, bf16[16,2,48,768]{3,2,1,0:T(8,128)(2,1)}) custom-call(bf16[2,4,4,128,768]{4,3,2,1,0:T(8,128)(2,1)} %bitcast.70, bf16[48,48,768]{2,1,0:T(8,128)(2,1)} %get-tuple-element.102.refs_1_.refs_2_.refs_7_.refs_8_, ...), custom_call_target="tpu_custom_call" | custom-call | flops 1000 | bytes 1000 | tf_op jit(solution)/shard_map/reduce_all/pallas_call | solution.py:875
  116.6 1.0 multiply_sine_fusion
  117.5 40.9 %inner_0.1 = (f32[128,768]{1,0:T(8,128)}, bf16[4,128,768]{2,1,0:T(8,128)(2,1)}, bf16[192,512]{1,0:T(8,128)(2,1)}, bf16[2,2,192,512]{3,2,1,0:T(8,128)(2,1)}, f32[...) custom-call(bf16[4,128,768]{2,1,0:T(8,128)(2,1)} %get-tuple-element.103.refs_0_.refs_1_, ...), custom_call_target="tpu_custom_call" | custom-call | flops 1000 | bytes 1000 | tf_op jit(solution)/shard_map/inner_0/pallas_call | solution.py:241
  158.5 27.8 %outcome_0.1 = (f32[128,768]{1,0:T(8,128)}, f32[128,768]{1,0:T(8,128)}, bf16[4,128,768]{2,1,0:T(8,128)(2,1)}, f32[768,512]{1,0:T(8,128)}, bf16[768,512]{1,0:T(8,128)(2,1)}) custom-call(bf16[4,128,768]{2,1,0:T(8,128)(2,1)} %get-tuple-element.106.refs_0_.refs_1_, bf16[1536,768]{1,0:T(8,128)(2,1)} %bitcast.56, bf16[1536,768]{1,0:T(8,128)(2,1)} %bitcast.60, ...), custom_call_target="tpu_custom_call" | custom-call | flops 1000 | bytes 1000 | tf_op jit(solution)/shard_map/outcome_0/pallas_call | solution.py:241
  186.3 40.6 %inner_1.1 = (f32[128,768]{1,0:T(8,128)}, bf16[4,128,768]{2,1,0:T(8,128)(2,1)}, bf16[192,512]{1,0:T(8,128)(2,1)}, bf16[2,2,192,512]{3,2,1,0:T(8,128)(2,1)}, f32[...) custom-call(bf16[4,128,768]{2,1,0:T(8,128)(2,1)} %get-tuple-element.109.refs_0_.refs_1_, ...), custom_call_target="tpu_custom_call" | custom-call | flops 1000 | bytes 1000 | tf_op jit(solution)/shard_map/inner_1/pallas_call | solution.py:241
  226.9 17.8 %outcome_1.1 = (f32[128,768]{1,0:T(8,128)}, f32[128,768]{1,0:T(8,128)}, bf16[128,768]{1,0:T(8,128)(2,1)}, f32[768,512]{1,0:T(8,128)}, bf16[768,512]{1,0:T(8,128)(2,1)}) custom-call(bf16[4,128,768]{2,1,0:T(8,128)(2,1)} %get-tuple-element.111.refs_0_.refs_1_, bf16[1536,768]{1,0:T(8,128)(2,1)} %bitcast.66, bf16[1536,768]{1,0:T(8,128)(2,1)} %bitcast.67, ...), custom_call_target="tpu_custom_call" | custom-call | flops 1000 | bytes 1000 | tf_op jit(solution)/shard_map/outcome_1/pallas_call | solution.py:241
  244.7 35.3 %gather_all.2 = bf16[2,4,4,128,768]{4,3,2,1,0:T(8,128)(2,1)} custom-call(bf16[128,768]{1,0:T(8,128)(2,1)} %get-tuple-element.115.refs_0_), custom_call_target="tpu_custom_call" | custom-call | flops 1000 | bytes 1000 | tf_op jit(solution)/shard_map/gather_all/pallas_call | solution.py:1016
  280.0 18.0 %head_forward.1 = (bf16[3840,4096]{1,0:T(8,128)(2,1)}, f32[32,8,128]{2,1,0:T(8,128)}) custom-call(s32[128]{0:T(128)} %bitcast.77, s32[3840,1]{1,0:T(8,128)} %get-tuple-element.93.ids_ref, s32[32,1,128]{2,1,0:T(1,128)} %get-tuple-element.99.labels_ref, bf16[3840,768]{1,0:T(8,128)(2,1)} %get-tuple-element.96.table_ref, bf16[4096,768]{1,0:T(8,128)(2,1)} %bitcast.38, ...), custom_call_target="tpu_custom_call" | custom-call | flops 1000 | bytes 1000 | tf_op jit(solution)/shard_map/head_forward/pallas_call | solution.py:1508
  298.1 25.5 %join_stats.1 = (f32[8,128]{1,0:T(8,128)}, f32[2,4,4,8,128]{4,3,2,1,0:T(8,128)}) custom-call(f32[2,4,4,8,128]{4,3,2,1,0:T(8,128)} %bitcast.73), custom_call_target="tpu_custom_call" | custom-call | flops 1000 | bytes 1000 | tf_op jit(solution)/shard_map/join_stats/pallas_call | solution.py:1153
  323.6 30.2 %head_backward.1 = (bf16[32,128,768]{2,1,0:T(8,128)(2,1)}, f32[3840,768]{1,0:T(8,128)}) custom-call(s32[128]{0:T(128)} %bitcast.78, s32[3840,1]{1,0:T(8,128)} %get-tuple-element.93.ids_ref, s32[32,1,128]{2,1,0:T(1,128)} %get-tuple-element.99.labels_ref, f32[32,1,128]{2,1,0:T(1,128)} %get-tuple-element.100.keep_ref, ...), custom_call_target="tpu_custom_call" | custom-call | flops 1000 | bytes 1000 | tf_op jit(solution)/shard_map/head_backward/pallas_call | solution.py:1508
  353.8 60.8 %reduce_all.3 = (f32[128,768]{1,0:T(8,128)}, f32[128,768]{1,0:T(8,128)}, f32[1,768]{1,0:T(1,128)}, bf16[4,128,768]{2,1,0:T(8,128)(2,1)}) custom-call(bf16[2,4,4,128,768]{4,3,2,1,0:T(8,128)(2,1)} %bitcast.71, f32[128,768]{1,0:T(8,128)} %get-tuple-element.120.refs_1_, f32[1,768]{1,0:T(1,128)} %get-tuple-element.181.refs_4_.refs_2_, f32[5]{0:T(128)} %refs_15_.2), custom_call_target="tpu_custom_call" | custom-call | flops 1000 | bytes 1000 | tf_op jit(solution)/shard_map/reduce_all/pallas_call | solution.py:875
  414.6 26.8 %inner_back_1.1 = (f32[128,768]{1,0:T(8,128)}, f32[1,768]{1,0:T(1,128)}, bf16[4,128,768]{2,1,0:T(8,128)(2,1)}, bf16[16,48,768]{2,1,0:T(8,128)(2,1)}) custom-call(bf16[4,128,768]{2,1,0:T(8,128)(2,1)} %get-tuple-element.121.refs_0_, bf16[4,128,768]{2,1,0:T(8,128)(2,1)} %get-tuple-element.111.refs_0_.refs_1_, bf16[1536,768]{1,0:T(8,128)(2,1)} %bitcast.68, ...), custom_call_target="tpu_custom_call" | custom-call | flops 1000 | bytes 1000 | tf_op jit(solution)/shard_map/inner_back_1/pallas_call | solution.py:241
  441.5 48.7 %stream_back_1.1 = (f32[128,768]{1,0:T(8,128)}, f32[128,768]{1,0:T(8,128)}, f32[1,768]{1,0:T(1,128)}, bf16[4,128,768]{2,1,0:T(8,128)(2,1)}, bf16[8,48,768]{2,1,0:T(8,128)(2,1)}, /*index=5*/bf16[16,48,768]{2,1,0:T(8,128)(2,1)}) custom-call(bf16[4,128,768]{2,1,0:T(8,128)(2,1)} %get-tuple-element.125.refs_0_, ...), custom_call_target="tpu_custom_call" | custom-call | flops 1000 | bytes 1000 | tf_op jit(solution)/shard_map/stream_back_1/pallas_call | solution.py:241
  490.2 33.5 %inner_back_0.1 = (f32[128,768]{1,0:T(8,128)}, f32[1,768]{1,0:T(1,128)}, bf16[4,128,768]{2,1,0:T(8,128)(2,1)}, bf16[16,48,768]{2,1,0:T(8,128)(2,1)}, bf16[8,48,768]{2,1,0:T(8,128)(2,1)}) custom-call(bf16[4,128,768]{2,1,0:T(8,128)(2,1)} %get-tuple-element.133.refs_0_, bf16[4,128,768]{2,1,0:T(8,128)(2,1)} %get-tuple-element.106.refs_0_.refs_1_, ...), custom_call_target="tpu_custom_call" | custom-call | flops 1000 | bytes 1000 | tf_op jit(solution)/shard_map/inner_back_0/pallas_call | solution.py:241
  523.6 45.7 %stream_back_0.1 = (f32[128,768]{1,0:T(8,128)}, f32[128,768]{1,0:T(8,128)}, f32[1,768]{1,0:T(1,128)}, bf16[128,768]{1,0:T(8,128)(2,1)}, bf16[8,48,768]{2,1,0:T(8,128)(2,1)}, /*index=5*/bf16[16,48,768]{2,1,0:T(8,128)(2,1)}) custom-call(bf16[4,128,768]{2,1,0:T(8,128)(2,1)} %get-tuple-element.138.refs_0_, ...), custom_call_target="tpu_custom_call" | custom-call | flops 1000 | bytes 1000 | tf_op jit(solution)/shard_map/stream_back_0/pallas_call | solution.py:241
  569.4 46.6 %gather_all.3 = (bf16[2,4,4,128,768]{4,3,2,1,0:T(8,128)(2,1)}, bf16[8,48,768]{2,1,0:T(8,128)(2,1)}) custom-call(bf16[128,768]{1,0:T(8,128)(2,1)} %get-tuple-element.146.refs_0_, bf16[8,48,768]{2,1,0:T(8,128)(2,1)} %get-tuple-element.147.refs_1_), custom_call_target="tpu_custom_call" | custom-call | flops 1000 | bytes 1000 | tf_op jit(solution)/shard_map/gather_all/pallas_call | solution.py:1016
  616.0 0.6 stack.23.slot_ref
  616.6 22.2 %look_back.1 = (bf16[67,48,768]{2,1,0:T(8,128)(2,1)}, f32[8,768]{1,0:T(8,128)}) custom-call(s32[128]{0:T(128)} %bitcast.79, s32[5,80]{1,0:T(8,128)} %stack.23.slot_ref, s32[3840,1]{1,0:T(8,128)} %get-tuple-element.93.ids_ref, s32[32,1,128]{2,1,0:T(1,128)} %get-tuple-element.94.tokens_ref, s32[32,1,128]{2,1,0:T(1,128)} %get-tuple-element.97.ranks_ref, ...), custom_call_target="tpu_custom_call" | custom-call | flops 1000 | bytes 1000 | tf_op jit(solution)/shard_map/look_back/pallas_call | solution.py:1865
  638.8 0.5 compare_select_fusion.refs_11_
  639.4 12.3 %finish.1 = (f32[5,768]{1,0:T(8,128)}, f32[5,768]{1,0:T(8,128)}, f32[5,768]{1,0:T(8,128)}, f32[1,5]{1,0:T(1,128)}, f32[1,5]{1,0:T(1,128)}, /*index=5*/f32[1,5]{1,0:T(1,128)}, f32[1,128]{1,0:T(1,128)}, f32[8,128]{1,0:T(8,128)}) custom-call(f32[1,768]{1,0:T(1,128)} %get-tuple-element.155.refs_0_, f32[1,768]{1,0:T(1,128)} %get-tuple-element.156.refs_1_, ...), custom_call_target="tpu_custom_call" | custom-call | flops 1000 | bytes 1000 | tf_op jit(solution)/shard_map/finish/pallas_call | solution.py:1364
  651.7 1.2 slice.32
  652.9 0.0 copy-start.8
  652.9 0.0 copy-start.7
  652.9 25.6 %multiply_subtract_fusion = (f32[67,48,768]{2,1,0:T(8,128)}, f32[67,48,768]{2,1,0:T(8,128)}, f32[67,48,768]{2,1,0:T(8,128)}) fusion(f32[67,48,768]{2,1,0:T(8,128)} %master_ref.1, f32[]{:T(128)} %bitcast.23, bf16[67,48,768]{2,1,0:T(8,128)(2,1)} %get-tuple-element.154, f32[67,48,768]{2,1,0:T(8,128)} %param.18, f32[67,48,768]{2,1,0:T(8,128)} %param.19), kind=kLoop, calls=%fused_computation.2 | loop fusion | flops 41988096 | bytes 64217092 | tf_op jit(solution)/shard_map/sub | solution.py:53
  678.5 0.6 fusion.16
  679.1 0.6 copy.35
  679.7 0.0 copy-done.2
  679.7 0.6 copy.36
  680.3 0.6 copy.37
  680.9 0.5 copy.38
  681.4 0.5 copy.39
  681.9 0.0 copy-done.6
  681.9 0.5 copy.40
  682.4 0.0 copy-done.5
  (17 shorter events, 0.1 us)
Async XLA Ops:
  0.6 44.3 %copy-start = (f32[5,768]{1,0:T(8,128)S(1)}, f32[5,768]{1,0:T(8,128)}, u32[]{:S(2)}) copy-start(f32[5,768]{1,0:T(8,128)} %refs_14_.3) | copy-start | bytes 46084
  652.9 25.6 %copy-start.4 = (f32[1,128]{1,0:T(1,128)S(1)}, f32[1,128]{1,0:T(1,128)}, u32[]{:S(2)}) copy-start(f32[1,128]{1,0:T(1,128)} %get-tuple-element.171) | copy-start | bytes 1540
  652.9 26.2 %copy-start.3 = (f32[5,768]{1,0:T(8,128)S(1)}, f32[5,768]{1,0:T(8,128)}, u32[]{:S(2)}) copy-start(f32[5,768]{1,0:T(8,128)} %get-tuple-element.211) | copy-start | bytes 46084
  652.9 26.8 %copy-start.2 = (f32[5,768]{1,0:T(8,128)S(1)}, f32[5,768]{1,0:T(8,128)}, u32[]{:S(2)}) copy-start(f32[5,768]{1,0:T(8,128)} %get-tuple-element.212) | copy-start | bytes 46084
  652.9 27.4 %copy-start.1 = (f32[5,768]{1,0:T(8,128)S(1)}, f32[5,768]{1,0:T(8,128)}, u32[]{:S(2)}) copy-start(f32[5,768]{1,0:T(8,128)} %get-tuple-element.213) | copy-start | bytes 46084
  652.9 28.0 %copy-start.8 = (f32[1,5]{1,0:T(1,128)S(1)}, f32[1,5]{1,0:T(1,128)}, u32[]{:S(2)}) copy-start(f32[1,5]{1,0:T(1,128)} %get-tuple-element.168) | copy-start | bytes 64
  652.9 28.5 %copy-start.7 = (f32[1,5]{1,0:T(1,128)S(1)}, f32[1,5]{1,0:T(1,128)}, u32[]{:S(2)}) copy-start(f32[1,5]{1,0:T(1,128)} %get-tuple-element.169) | copy-start | bytes 64
  652.9 29.0 %copy-start.6 = (f32[1,5]{1,0:T(1,128)S(1)}, f32[1,5]{1,0:T(1,128)}, u32[]{:S(2)}) copy-start(f32[1,5]{1,0:T(1,128)} %get-tuple-element.170) | copy-start | bytes 64
  652.9 29.5 %copy-start.5 = (f32[1,128]{1,0:T(1,128)S(1)}, f32[1,128]{1,0:T(1,128)}, u32[]{:S(2)}) copy-start(f32[1,128]{1,0:T(1,128)} %get-tuple-element.163.refs_13_) | copy-start | bytes 1540

commit v13 on v12

--- a/solution.py
+++ b/solution.py
@@ -59,6 +59,7 @@
 TILE_GROUPS = 8
 LANES = 128
 SHORT = pl.CostEstimate(flops=1000, bytes_accessed=1000, transcendentals=0)
+LONG = pl.CostEstimate(flops=10**12, bytes_accessed=1 << 30, transcendentals=0)
 
 
 def meet(peers):
@@ -1379,8 +1380,10 @@
             dma((groups - 1,)),
             dma((groups - 1,)),
         ],
-        cost_estimate=SHORT,
-        compiler_params=pltpu.CompilerParams(collective_id=collective_id, has_side_effects=True),
+        cost_estimate=LONG,
+        compiler_params=pltpu.CompilerParams(
+            collective_id=collective_id, has_side_effects=True, vmem_limit_bytes=8 << 20
+        ),
     )(*operands)
 
 

time: 691 us -> 686 us (level)
    pallas_call x2, Pallas kernels: 132 us -> 140 us  [reduce_all(): pl.pallas_call(kernel, name='reduce_all', out_shape=results + ([line.out_...]
where the time goes in v13:
time: 686 us; the launch traced here: 679 us
  Pallas kernels  638 us (93%)
  other arithmetic  28.5 us (4%)
  local copies, waits for them, and re-layouts  7.29 us (1%)
    pallas_call x8, Pallas kernels, tensor_step(): pl.pallas_call(kernel, name=name, grid=(1,), out_shape=shapes, in_specs=i...  281 us
    pallas_call x2, Pallas kernels, reduce_all(): pl.pallas_call(kernel, name='reduce_all', out_shape=results + ([line.out_...  140 us
    pallas_call x2, Pallas kernels, gather_all(): pl.pallas_call(kernel, name='gather_all', out_shape=[jax.ShapeDtypeStruct...  81.7 us
    pallas_call x3, Pallas kernels, local_call(): pl.pallas_call(kernel, name=name, grid_spec=pltpu.PrefetchScalarGridSpec(...  59.1 us
    pallas_call x1, Pallas kernels, join_stats(): pl.pallas_call(kernel, name='join_stats', out_shape=[jax.ShapeDtypeStruct...  24.8 us
    sub x1, other arithmetic, adam_update(): weight - rate * (first_hat / (jnp.sqrt(second_hat) + ADAM_EPS) + decay *...  22.6 us
    pallas_call x1, Pallas kernels, look_back(): pl.pallas_call(kernel, name='look_back', grid_spec=pltpu.PrefetchScalarGr...  22.4 us

profile of v13, /device:TPU:0, one launch (start us, length us, event | category | flops | bytes accessed | tf_op | source)
XLA Modules:
  0.0 678.7 jit_solution(10088974789217195659)
XLA Ops:
  0.7 1.3 fusion.8
  2.0 0.9 select_reduce_fusion
  2.9 0.1 select_reduce_fusion.1
  3.1 0.7 copy.26.slot_ref
  5.1 0.5 compare_select_fusion.7.ends_ref
  6.3 0.1 pad.9.clone
  6.4 1.4 add_add_fusion.block_ref
  7.7 9.5 %spread_tokens.1 = (s32[32,1,128]{2,1,0:T(1,128)}, s32[32,1,128]{2,1,0:T(1,128)}, f32[32,1,128]{2,1,0:T(1,128)}, s32[32,1,128]{2,1,0:T(1,128)}, s32[1,128]{1,0:T(1,128)}, /*index=5*/f32[1,128]{1,0:T(1,128)}) custom-call(s32[16,128]{1,0:T(8,128)} %add_add_fusion.block_ref, s32[80,1]{1,0:T(8,128)} %copy.26.slot_ref, s32[1,128]{1,0:T(1,128)} %compare_select_fusion.7.ends_ref), custom_call_target="tpu_custom_call" | custom-call | flops 1000 | bytes 1000 | tf_op jit(solution)/shard_map/spread_tokens/pallas_call | solution.py:1256
  17.2 0.6 pad_add_fusion.plan_ref
  17.8 9.9 %prepare.1 = (bf16[3840,768]{1,0:T(8,128)(2,1)}, bf16[48,48,768]{2,1,0:T(8,128)(2,1)}, s32[3840,1]{1,0:T(8,128)}) custom-call(s32[81]{0:T(128)} %pad_add_fusion.plan_ref, f32[67,48,768]{2,1,0:T(8,128)} %master_ref.1), custom_call_target="tpu_custom_call" | custom-call | flops 1000 | bytes 1000 | tf_op jit(solution)/shard_map/prepare/pallas_call | solution.py:1425
  27.7 16.4 %look_up.1 = (bf16[4096,768]{1,0:T(8,128)(2,1)}, s32[32,1,128]{2,1,0:T(1,128)}, s32[8,768]{1,0:T(8,128)}) custom-call(s32[128]{0:T(128)} %bitcast.82, s32[3840,1]{1,0:T(8,128)} %get-tuple-element.93.ids_ref, s32[32,1,128]{2,1,0:T(1,128)} %get-tuple-element.94.tokens_ref, s32[32,1,128]{2,1,0:T(1,128)} %get-tuple-element.95.places_ref, ...), custom_call_target="tpu_custom_call" | custom-call | flops 1000 | bytes 1000 | tf_op jit(solution)/shard_map/look_up/pallas_call | solution.py:1511
  44.1 0.6 fusion.15
  44.7 71.5 %reduce_all.2 = (f32[128,768]{1,0:T(8,128)}, bf16[4,128,768]{2,1,0:T(8,128)(2,1)}, bf16[16,2,48,768]{3,2,1,0:T(8,128)(2,1)}) custom-call(bf16[2,4,4,128,768]{4,3,2,1,0:T(8,128)(2,1)} %bitcast.77, bf16[48,48,768]{2,1,0:T(8,128)(2,1)} %get-tuple-element.102.refs_1_.refs_2_.refs_7_.refs_8_, ...), custom_call_target="tpu_custom_call" | custom-call | flops 1000 | bytes 1000 | tf_op jit(solution)/shard_map/reduce_all/pallas_call | solution.py:876
  116.3 1.0 multiply_sine_fusion
  117.2 40.7 %inner_0.1 = (f32[128,768]{1,0:T(8,128)}, bf16[4,128,768]{2,1,0:T(8,128)(2,1)}, bf16[192,512]{1,0:T(8,128)(2,1)}, bf16[2,2,192,512]{3,2,1,0:T(8,128)(2,1)}, f32[...) custom-call(bf16[4,128,768]{2,1,0:T(8,128)(2,1)} %get-tuple-element.103.refs_0_.refs_1_, ...), custom_call_target="tpu_custom_call" | custom-call | flops 1000 | bytes 1000 | tf_op jit(solution)/shard_map/inner_0/pallas_call | solution.py:242
  157.9 28.0 %outcome_0.1 = (f32[128,768]{1,0:T(8,128)}, f32[128,768]{1,0:T(8,128)}, bf16[4,128,768]{2,1,0:T(8,128)(2,1)}, f32[768,512]{1,0:T(8,128)}, bf16[768,512]{1,0:T(8,128)(2,1)}) custom-call(bf16[4,128,768]{2,1,0:T(8,128)(2,1)} %get-tuple-element.106.refs_0_.refs_1_, bf16[1536,768]{1,0:T(8,128)(2,1)} %bitcast.63, bf16[1536,768]{1,0:T(8,128)(2,1)} %bitcast.67, ...), custom_call_target="tpu_custom_call" | custom-call | flops 1000 | bytes 1000 | tf_op jit(solution)/shard_map/outcome_0/pallas_call | solution.py:242
  185.9 40.4 %inner_1.1 = (f32[128,768]{1,0:T(8,128)}, bf16[4,128,768]{2,1,0:T(8,128)(2,1)}, bf16[192,512]{1,0:T(8,128)(2,1)}, bf16[2,2,192,512]{3,2,1,0:T(8,128)(2,1)}, f32[...) custom-call(bf16[4,128,768]{2,1,0:T(8,128)(2,1)} %get-tuple-element.109.refs_0_.refs_1_, ...), custom_call_target="tpu_custom_call" | custom-call | flops 1000 | bytes 1000 | tf_op jit(solution)/shard_map/inner_1/pallas_call | solution.py:242
  226.3 18.0 %outcome_1.1 = (f32[128,768]{1,0:T(8,128)}, f32[128,768]{1,0:T(8,128)}, bf16[128,768]{1,0:T(8,128)(2,1)}, f32[768,512]{1,0:T(8,128)}, bf16[768,512]{1,0:T(8,128)(2,1)}) custom-call(bf16[4,128,768]{2,1,0:T(8,128)(2,1)} %get-tuple-element.111.refs_0_.refs_1_, bf16[1536,768]{1,0:T(8,128)(2,1)} %bitcast.73, bf16[1536,768]{1,0:T(8,128)(2,1)} %bitcast.74, ...), custom_call_target="tpu_custom_call" | custom-call | flops 1000 | bytes 1000 | tf_op jit(solution)/shard_map/outcome_1/pallas_call | solution.py:242
  244.3 35.3 %gather_all.2 = bf16[2,4,4,128,768]{4,3,2,1,0:T(8,128)(2,1)} custom-call(bf16[128,768]{1,0:T(8,128)(2,1)} %get-tuple-element.115.refs_0_), custom_call_target="tpu_custom_call" | custom-call | flops 1000 | bytes 1000 | tf_op jit(solution)/shard_map/gather_all/pallas_call | solution.py:1017
  279.6 15.7 %head_forward.1 = (bf16[3840,4096]{1,0:T(8,128)(2,1)}, f32[32,8,128]{2,1,0:T(8,128)}) custom-call(s32[128]{0:T(128)} %bitcast.83, s32[3840,1]{1,0:T(8,128)} %get-tuple-element.93.ids_ref, s32[32,1,128]{2,1,0:T(1,128)} %get-tuple-element.99.labels_ref, bf16[3840,768]{1,0:T(8,128)(2,1)} %get-tuple-element.96.table_ref, bf16[4096,768]{1,0:T(8,128)(2,1)} %bitcast.45, ...), custom_call_target="tpu_custom_call" | custom-call | flops 1000 | bytes 1000 | tf_op jit(solution)/shard_map/head_forward/pallas_call | solution.py:1511
  295.3 24.8 %join_stats.1 = (f32[8,128]{1,0:T(8,128)}, f32[2,4,4,8,128]{4,3,2,1,0:T(8,128)}) custom-call(f32[2,4,4,8,128]{4,3,2,1,0:T(8,128)} %bitcast.80), custom_call_target="tpu_custom_call" | custom-call | flops 1000 | bytes 1000 | tf_op jit(solution)/shard_map/join_stats/pallas_call | solution.py:1154
  320.2 27.0 %head_backward.1 = (bf16[32,128,768]{2,1,0:T(8,128)(2,1)}, f32[3840,768]{1,0:T(8,128)}) custom-call(s32[128]{0:T(128)} %bitcast.84, s32[3840,1]{1,0:T(8,128)} %get-tuple-element.93.ids_ref, s32[32,1,128]{2,1,0:T(1,128)} %get-tuple-element.99.labels_ref, f32[32,1,128]{2,1,0:T(1,128)} %get-tuple-element.100.keep_ref, ...), custom_call_target="tpu_custom_call" | custom-call | flops 1000 | bytes 1000 | tf_op jit(solution)/shard_map/head_backward/pallas_call | solution.py:1511
  347.2 68.1 %reduce_all.3 = (f32[128,768]{1,0:T(8,128)}, f32[128,768]{1,0:T(8,128)}, f32[1,768]{1,0:T(1,128)}, bf16[4,128,768]{2,1,0:T(8,128)(2,1)}) custom-call(bf16[2,4,4,128,768]{4,3,2,1,0:T(8,128)(2,1)} %bitcast.78, f32[128,768]{1,0:T(8,128)} %get-tuple-element.120.refs_1_, f32[1,768]{1,0:T(1,128)} %get-tuple-element.181.refs_4_.refs_2_, f32[5]{0:T(128)} %refs_15_.2), custom_call_target="tpu_custom_call" | custom-call | flops 1000 | bytes 1000 | tf_op jit(solution)/shard_map/reduce_all/pallas_call | solution.py:876
  415.3 27.1 %inner_back_1.1 = (f32[128,768]{1,0:T(8,128)}, f32[1,768]{1,0:T(1,128)}, bf16[4,128,768]{2,1,0:T(8,128)(2,1)}, bf16[16,48,768]{2,1,0:T(8,128)(2,1)}) custom-call(bf16[4,128,768]{2,1,0:T(8,128)(2,1)} %get-tuple-element.121.refs_0_, bf16[4,128,768]{2,1,0:T(8,128)(2,1)} %get-tuple-element.111.refs_0_.refs_1_, bf16[1536,768]{1,0:T(8,128)(2,1)} %bitcast.75, ...), custom_call_target="tpu_custom_call" | custom-call | flops 1000 | bytes 1000 | tf_op jit(solution)/shard_map/inner_back_1/pallas_call | solution.py:242
  442.5 49.3 %stream_back_1.1 = (f32[128,768]{1,0:T(8,128)}, f32[128,768]{1,0:T(8,128)}, f32[1,768]{1,0:T(1,128)}, bf16[4,128,768]{2,1,0:T(8,128)(2,1)}, bf16[8,48,768]{2,1,0:T(8,128)(2,1)}, /*index=5*/bf16[16,48,768]{2,1,0:T(8,128)(2,1)}) custom-call(bf16[4,128,768]{2,1,0:T(8,128)(2,1)} %get-tuple-element.125.refs_0_, ...), custom_call_target="tpu_custom_call" | custom-call | flops 1000 | bytes 1000 | tf_op jit(solution)/shard_map/stream_back_1/pallas_call | solution.py:242
  491.8 32.9 %inner_back_0.1 = (f32[128,768]{1,0:T(8,128)}, f32[1,768]{1,0:T(1,128)}, bf16[4,128,768]{2,1,0:T(8,128)(2,1)}, bf16[16,48,768]{2,1,0:T(8,128)(2,1)}, bf16[8,48,768]{2,1,0:T(8,128)(2,1)}) custom-call(bf16[4,128,768]{2,1,0:T(8,128)(2,1)} %get-tuple-element.133.refs_0_, bf16[4,128,768]{2,1,0:T(8,128)(2,1)} %get-tuple-element.106.refs_0_.refs_1_, ...), custom_call_target="tpu_custom_call" | custom-call | flops 1000 | bytes 1000 | tf_op jit(solution)/shard_map/inner_back_0/pallas_call | solution.py:242
  524.7 45.0 %stream_back_0.1 = (f32[128,768]{1,0:T(8,128)}, f32[128,768]{1,0:T(8,128)}, f32[1,768]{1,0:T(1,128)}, bf16[128,768]{1,0:T(8,128)(2,1)}, bf16[8,48,768]{2,1,0:T(8,128)(2,1)}, /*index=5*/bf16[16,48,768]{2,1,0:T(8,128)(2,1)}) custom-call(bf16[4,128,768]{2,1,0:T(8,128)(2,1)} %get-tuple-element.138.refs_0_, ...), custom_call_target="tpu_custom_call" | custom-call | flops 1000 | bytes 1000 | tf_op jit(solution)/shard_map/stream_back_0/pallas_call | solution.py:242
  569.7 46.4 %gather_all.3 = (bf16[2,4,4,128,768]{4,3,2,1,0:T(8,128)(2,1)}, bf16[8,48,768]{2,1,0:T(8,128)(2,1)}) custom-call(bf16[128,768]{1,0:T(8,128)(2,1)} %get-tuple-element.146.refs_0_, bf16[8,48,768]{2,1,0:T(8,128)(2,1)} %get-tuple-element.147.refs_1_), custom_call_target="tpu_custom_call" | custom-call | flops 1000 | bytes 1000 | tf_op jit(solution)/shard_map/gather_all/pallas_call | solution.py:1017
  616.0 0.6 stack.23.slot_ref
  616.7 0.0 copy-start.4
  616.7 0.0 copy-start.7
  616.7 0.0 copy-start.8
  616.8 0.0 copy-start.16
  616.8 0.0 copy-start.17
  616.8 0.0 copy-start.18
  616.8 22.4 %look_back.1 = (bf16[67,48,768]{2,1,0:T(8,128)(2,1)}, f32[8,768]{1,0:T(8,128)}) custom-call(s32[128]{0:T(128)} %bitcast.85, s32[5,80]{1,0:T(8,128)} %stack.23.slot_ref, s32[3840,1]{1,0:T(8,128)} %get-tuple-element.93.ids_ref, s32[32,1,128]{2,1,0:T(1,128)} %get-tuple-element.94.tokens_ref, s32[32,1,128]{2,1,0:T(1,128)} %get-tuple-element.97.ranks_ref, ...), custom_call_target="tpu_custom_call" | custom-call | flops 1000 | bytes 1000 | tf_op jit(solution)/shard_map/look_back/pallas_call | solution.py:1868
  639.3 0.0 copy-start.9
  639.4 0.7 copy-done.9
  640.1 10.1 %finish.1 = (f32[5,768]{1,0:T(8,128)S(1)}, f32[5,768]{1,0:T(8,128)S(1)}, f32[5,768]{1,0:T(8,128)S(1)}, f32[1,5]{1,0:T(1,128)S(1)}, f32[1,5]{1,0:T(1,128)S(1)}, /...) custom-call(f32[1,768]{1,0:T(1,128)S(1)} %copy-done.15, f32[1,768]{1,0:T(1,128)S(1)} %copy-done.14, ...), custom_call_target="tpu_custom_call" | custom-call | flops 999999995904 | bytes 1073741824 | tf_op jit(solution)/shard_map/finish/pallas_call | solution.py:1365
  650.2 0.5 slice.32
  650.7 22.6 %multiply_subtract_fusion = (f32[67,48,768]{2,1,0:T(8,128)}, f32[67,48,768]{2,1,0:T(8,128)}, f32[67,48,768]{2,1,0:T(8,128)}) fusion(f32[67,48,768]{2,1,0:T(8,128)S(1)} %copy-done.19, f32[]{:T(128)} %bitcast.23, bf16[67,48,768]{2,1,0:T(8,128)(2,1)} %get-tuple-element.154, f32[67,48,768]{2,1,0:T(8,128)} %param.18, f32[67,48,768]{2,1,0:T(8,128)} %param.19), kind=kLoop, calls=%fused_computation.2 | loop fusion | flops 41988096 | bytes 64217092 | tf_op jit(solution)/shard_map/sub | solution.py:53
  673.3 0.6 fusion.16
  673.9 0.6 copy.35
  674.5 0.6 copy.36
  675.1 0.6 copy.37
  675.7 0.5 copy.38
  676.2 0.5 copy.39
  676.8 0.5 copy.40
  (39 shorter events, 0.1 us)
Async XLA Ops:
  0.6 43.4 %copy-start.5 = (f32[5,768]{1,0:T(8,128)S(1)}, f32[5,768]{1,0:T(8,128)}, u32[]{:S(2)}) copy-start(f32[5,768]{1,0:T(8,128)} %refs_14_.3) | copy-start | bytes 46084
  616.7 22.5 %copy-start = (f32[128,768]{1,0:T(8,128)S(1)}, f32[128,768]{1,0:T(8,128)}, u32[]{:S(2)}) copy-start(f32[128,768]{1,0:T(8,128)} %get-tuple-element.105.refs_5_.refs_11_) | copy-start | bytes 1179652
  616.7 22.5 %copy-start.1 = (f32[128,768]{1,0:T(8,128)S(1)}, f32[128,768]{1,0:T(8,128)}, u32[]{:S(2)}) copy-start(f32[128,768]{1,0:T(8,128)} %get-tuple-element.131.refs_13_.refs_14_.refs_9_) | copy-start | bytes 1179652
  616.7 22.5 %copy-start.2 = (f32[128,768]{1,0:T(8,128)S(1)}, f32[128,768]{1,0:T(8,128)}, u32[]{:S(2)}) copy-start(f32[128,768]{1,0:T(8,128)} %get-tuple-element.144.refs_13_.refs_8_) | copy-start | bytes 1179652
  616.7 22.5 %copy-start.3 = (f32[128,768]{1,0:T(8,128)S(1)}, f32[128,768]{1,0:T(8,128)}, u32[]{:S(2)}) copy-start(f32[128,768]{1,0:T(8,128)} %get-tuple-element.114.refs_6_) | copy-start | bytes 1179652
  616.7 22.5 %copy-start.4 = (f32[5]{0:T(128)S(1)}, f32[5]{0:T(128)}, u32[]{:S(2)}) copy-start(f32[5]{0:T(128)} %refs_15_.2) | copy-start | bytes 64
  616.7 22.5 %copy-start.6 = (f32[128,768]{1,0:T(8,128)S(1)}, f32[128,768]{1,0:T(8,128)}, u32[]{:S(2)}) copy-start(f32[128,768]{1,0:T(8,128)} %get-tuple-element.160.refs_7_) | copy-start | bytes 1179652
  616.7 22.5 %copy-start.7 = (f32[5,768]{1,0:T(8,128)S(1)}, f32[5,768]{1,0:T(8,128)}, u32[]{:S(2)}) copy-start(f32[5,768]{1,0:T(8,128)} %refs_15_.3) | copy-start | bytes 46084
  616.7 22.5 %copy-start.8 = (f32[5,768]{1,0:T(8,128)S(1)}, f32[5,768]{1,0:T(8,128)}, u32[]{:S(2)}) copy-start(f32[5,768]{1,0:T(8,128)} %refs_16_.1) | copy-start | bytes 46084
  616.7 22.5 %copy-start.10 = (f32[8,128]{1,0:T(8,128)S(1)}, f32[8,128]{1,0:T(8,128)}, u32[]{:S(2)}) copy-start(f32[8,128]{1,0:T(8,128)} %get-tuple-element.161.refs_10_) | copy-start | bytes 12292
  616.7 22.5 %copy-start.11 = (f32[1,768]{1,0:T(1,128)S(1)}, f32[1,768]{1,0:T(1,128)}, u32[]{:S(2)}) copy-start(f32[1,768]{1,0:T(1,128)} %get-tuple-element.159.refs_4_) | copy-start | bytes 9220
  616.7 22.5 %copy-start.12 = (f32[1,768]{1,0:T(1,128)S(1)}, f32[1,768]{1,0:T(1,128)}, u32[]{:S(2)}) copy-start(f32[1,768]{1,0:T(1,128)} %get-tuple-element.158.refs_3_) | copy-start | bytes 9220
  616.7 22.5 %copy-start.13 = (f32[1,768]{1,0:T(1,128)S(1)}, f32[1,768]{1,0:T(1,128)}, u32[]{:S(2)}) copy-start(f32[1,768]{1,0:T(1,128)} %get-tuple-element.157.refs_2_) | copy-start | bytes 9220
  616.8 22.5 %copy-start.14 = (f32[1,768]{1,0:T(1,128)S(1)}, f32[1,768]{1,0:T(1,128)}, u32[]{:S(2)}) copy-start(f32[1,768]{1,0:T(1,128)} %get-tuple-element.156.refs_1_) | copy-start | bytes 9220
  616.8 22.5 %copy-start.15 = (f32[1,768]{1,0:T(1,128)S(1)}, f32[1,768]{1,0:T(1,128)}, u32[]{:S(2)}) copy-start(f32[1,768]{1,0:T(1,128)} %get-tuple-element.155.refs_0_) | copy-start | bytes 9220
  616.8 22.5 %copy-start.16 = (f32[5]{0:T(128)S(1)}, f32[5]{0:T(128)}, u32[]{:S(2)}) copy-start(f32[5]{0:T(128)} %param.24) | copy-start | bytes 64
  616.8 22.5 %copy-start.17 = (f32[5]{0:T(128)S(1)}, f32[5]{0:T(128)}, u32[]{:S(2)}) copy-start(f32[5]{0:T(128)} %param.25) | copy-start | bytes 64
  616.8 22.5 %copy-start.18 = (f32[1,128]{1,0:T(1,128)S(1)}, f32[1,128]{1,0:T(1,128)}, u32[]{:S(2)}) copy-start(f32[1,128]{1,0:T(1,128)} %get-tuple-element.163.refs_13_) | copy-start | bytes 1540
  639.3 0.7 copy-start.9
  640.1 10.6 %copy-start.19 = (f32[67,48,768]{2,1,0:T(8,128)S(1)}, f32[67,48,768]{2,1,0:T(8,128)}, u32[]{:S(2)}) copy-start(f32[67,48,768]{2,1,0:T(8,128)} %master_ref.1) | copy-start | bytes 29638660

commit v14 on v13

--- a/solution.py
+++ b/solution.py
@@ -186,7 +186,7 @@
                 )
             if work.during:
                 work.during(work_refs, work_outs, refs)
-            tick(6)
+            tick(4)
             total = partial_ref[pl.ds(pl.multiple_of(me * share, share), share), :]
             for step, copy in enumerate(copies):
                 copy.wait()

time: 686 us -> 687 us (level)
    pallas_call x3, Pallas kernels: 59.1 us -> 79.3 us  [local_call(): pl.pallas_call(kernel, name=name, grid_spec=pltpu.PrefetchScalarGridSpec(...]
    pallas_call x2, Pallas kernels: 140 us -> 123 us  [reduce_all(): pl.pallas_call(kernel, name='reduce_all', out_shape=results + ([line.out_...]
    pallas_call x1, Pallas kernels: 24.8 us -> 17.6 us  [join_stats(): pl.pallas_call(kernel, name='join_stats', out_shape=[jax.ShapeDtypeStruct...]
where the time goes in v14:
time: 687 us; the launch traced here: 680 us
  Pallas kernels  640 us (93%)
  other arithmetic  28.5 us (4%)
  local copies, waits for them, and re-layouts  7.29 us (1%)
    pallas_call x8, Pallas kernels, tensor_step(): pl.pallas_call(kernel, name=name, grid=(1,), out_shape=shapes, in_specs=i...  285 us
    pallas_call x2, Pallas kernels, reduce_all(): pl.pallas_call(kernel, name='reduce_all', out_shape=results + ([line.out_...  123 us
    pallas_call x2, Pallas kernels, gather_all(): pl.pallas_call(kernel, name='gather_all', out_shape=[jax.ShapeDtypeStruct...  82.3 us
    pallas_call x3, Pallas kernels, local_call(): pl.pallas_call(kernel, name=name, grid_spec=pltpu.PrefetchScalarGridSpec(...  79.3 us
    sub x1, other arithmetic, adam_update(): weight - rate * (first_hat / (jnp.sqrt(second_hat) + ADAM_EPS) + decay *...  22.6 us
    pallas_call x1, Pallas kernels, look_back(): pl.pallas_call(kernel, name='look_back', grid_spec=pltpu.PrefetchScalarGr...  22.3 us
    pallas_call x1, Pallas kernels, join_stats(): pl.pallas_call(kernel, name='join_stats', out_shape=[jax.ShapeDtypeStruct...  17.6 us

profile of v14, /device:TPU:0, one launch (start us, length us, event | category | flops | bytes accessed | tf_op | source)
XLA Modules:
  0.0 679.8 jit_solution(13355859231558304291)
XLA Ops:
  0.7 1.3 fusion.8
  2.0 0.9 select_reduce_fusion
  2.9 0.1 select_reduce_fusion.1
  3.1 0.7 copy.26.slot_ref
  5.1 0.5 compare_select_fusion.7.ends_ref
  6.3 0.1 pad.9.clone
  6.4 1.4 add_add_fusion.block_ref
  7.7 9.5 %spread_tokens.1 = (s32[32,1,128]{2,1,0:T(1,128)}, s32[32,1,128]{2,1,0:T(1,128)}, f32[32,1,128]{2,1,0:T(1,128)}, s32[32,1,128]{2,1,0:T(1,128)}, s32[1,128]{1,0:T(1,128)}, /*index=5*/f32[1,128]{1,0:T(1,128)}) custom-call(s32[16,128]{1,0:T(8,128)} %add_add_fusion.block_ref, s32[80,1]{1,0:T(8,128)} %copy.26.slot_ref, s32[1,128]{1,0:T(1,128)} %compare_select_fusion.7.ends_ref), custom_call_target="tpu_custom_call" | custom-call | flops 1000 | bytes 1000 | tf_op jit(solution)/shard_map/spread_tokens/pallas_call | solution.py:1256
  17.2 0.6 pad_add_fusion.plan_ref
  17.8 9.9 %prepare.1 = (bf16[3840,768]{1,0:T(8,128)(2,1)}, bf16[48,48,768]{2,1,0:T(8,128)(2,1)}, s32[3840,1]{1,0:T(8,128)}) custom-call(s32[81]{0:T(128)} %pad_add_fusion.plan_ref, f32[67,48,768]{2,1,0:T(8,128)} %master_ref.1), custom_call_target="tpu_custom_call" | custom-call | flops 1000 | bytes 1000 | tf_op jit(solution)/shard_map/prepare/pallas_call | solution.py:1425
  27.7 18.9 %look_up.1 = (bf16[4096,768]{1,0:T(8,128)(2,1)}, s32[32,1,128]{2,1,0:T(1,128)}, s32[8,768]{1,0:T(8,128)}) custom-call(s32[128]{0:T(128)} %bitcast.82, s32[3840,1]{1,0:T(8,128)} %get-tuple-element.93.ids_ref, s32[32,1,128]{2,1,0:T(1,128)} %get-tuple-element.94.tokens_ref, s32[32,1,128]{2,1,0:T(1,128)} %get-tuple-element.95.places_ref, ...), custom_call_target="tpu_custom_call" | custom-call | flops 1000 | bytes 1000 | tf_op jit(solution)/shard_map/look_up/pallas_call | solution.py:1511
  46.7 0.6 fusion.15
  47.3 68.0 %reduce_all.2 = (f32[128,768]{1,0:T(8,128)}, bf16[4,128,768]{2,1,0:T(8,128)(2,1)}, bf16[16,2,48,768]{3,2,1,0:T(8,128)(2,1)}) custom-call(bf16[2,4,4,128,768]{4,3,2,1,0:T(8,128)(2,1)} %bitcast.77, bf16[48,48,768]{2,1,0:T(8,128)(2,1)} %get-tuple-element.102.refs_1_.refs_2_.refs_7_.refs_8_, ...), custom_call_target="tpu_custom_call" | custom-call | flops 1000 | bytes 1000 | tf_op jit(solution)/shard_map/reduce_all/pallas_call | solution.py:876
  115.4 1.0 multiply_sine_fusion
  116.3 41.8 %inner_0.1 = (f32[128,768]{1,0:T(8,128)}, bf16[4,128,768]{2,1,0:T(8,128)(2,1)}, bf16[192,512]{1,0:T(8,128)(2,1)}, bf16[2,2,192,512]{3,2,1,0:T(8,128)(2,1)}, f32[...) custom-call(bf16[4,128,768]{2,1,0:T(8,128)(2,1)} %get-tuple-element.103.refs_0_.refs_1_, ...), custom_call_target="tpu_custom_call" | custom-call | flops 1000 | bytes 1000 | tf_op jit(solution)/shard_map/inner_0/pallas_call | solution.py:242
  158.2 28.5 %outcome_0.1 = (f32[128,768]{1,0:T(8,128)}, f32[128,768]{1,0:T(8,128)}, bf16[4,128,768]{2,1,0:T(8,128)(2,1)}, f32[768,512]{1,0:T(8,128)}, bf16[768,512]{1,0:T(8,128)(2,1)}) custom-call(bf16[4,128,768]{2,1,0:T(8,128)(2,1)} %get-tuple-element.106.refs_0_.refs_1_, bf16[1536,768]{1,0:T(8,128)(2,1)} %bitcast.63, bf16[1536,768]{1,0:T(8,128)(2,1)} %bitcast.67, ...), custom_call_target="tpu_custom_call" | custom-call | flops 1000 | bytes 1000 | tf_op jit(solution)/shard_map/outcome_0/pallas_call | solution.py:242
  186.7 41.6 %inner_1.1 = (f32[128,768]{1,0:T(8,128)}, bf16[4,128,768]{2,1,0:T(8,128)(2,1)}, bf16[192,512]{1,0:T(8,128)(2,1)}, bf16[2,2,192,512]{3,2,1,0:T(8,128)(2,1)}, f32[...) custom-call(bf16[4,128,768]{2,1,0:T(8,128)(2,1)} %get-tuple-element.109.refs_0_.refs_1_, ...), custom_call_target="tpu_custom_call" | custom-call | flops 1000 | bytes 1000 | tf_op jit(solution)/shard_map/inner_1/pallas_call | solution.py:242
  228.3 17.2 %outcome_1.1 = (f32[128,768]{1,0:T(8,128)}, f32[128,768]{1,0:T(8,128)}, bf16[128,768]{1,0:T(8,128)(2,1)}, f32[768,512]{1,0:T(8,128)}, bf16[768,512]{1,0:T(8,128)(2,1)}) custom-call(bf16[4,128,768]{2,1,0:T(8,128)(2,1)} %get-tuple-element.111.refs_0_.refs_1_, bf16[1536,768]{1,0:T(8,128)(2,1)} %bitcast.73, bf16[1536,768]{1,0:T(8,128)(2,1)} %bitcast.74, ...), custom_call_target="tpu_custom_call" | custom-call | flops 1000 | bytes 1000 | tf_op jit(solution)/shard_map/outcome_1/pallas_call | solution.py:242
  245.5 35.6 %gather_all.2 = bf16[2,4,4,128,768]{4,3,2,1,0:T(8,128)(2,1)} custom-call(bf16[128,768]{1,0:T(8,128)(2,1)} %get-tuple-element.115.refs_0_), custom_call_target="tpu_custom_call" | custom-call | flops 1000 | bytes 1000 | tf_op jit(solution)/shard_map/gather_all/pallas_call | solution.py:1017
  281.1 22.7 %head_forward.1 = (bf16[3840,4096]{1,0:T(8,128)(2,1)}, f32[32,8,128]{2,1,0:T(8,128)}) custom-call(s32[128]{0:T(128)} %bitcast.83, s32[3840,1]{1,0:T(8,128)} %get-tuple-element.93.ids_ref, s32[32,1,128]{2,1,0:T(1,128)} %get-tuple-element.99.labels_ref, bf16[3840,768]{1,0:T(8,128)(2,1)} %get-tuple-element.96.table_ref, bf16[4096,768]{1,0:T(8,128)(2,1)} %bitcast.45, ...), custom_call_target="tpu_custom_call" | custom-call | flops 1000 | bytes 1000 | tf_op jit(solution)/shard_map/head_forward/pallas_call | solution.py:1511
  303.8 17.6 %join_stats.1 = (f32[8,128]{1,0:T(8,128)}, f32[2,4,4,8,128]{4,3,2,1,0:T(8,128)}) custom-call(f32[2,4,4,8,128]{4,3,2,1,0:T(8,128)} %bitcast.80), custom_call_target="tpu_custom_call" | custom-call | flops 1000 | bytes 1000 | tf_op jit(solution)/shard_map/join_stats/pallas_call | solution.py:1154
  321.4 37.7 %head_backward.1 = (bf16[32,128,768]{2,1,0:T(8,128)(2,1)}, f32[3840,768]{1,0:T(8,128)}) custom-call(s32[128]{0:T(128)} %bitcast.84, s32[3840,1]{1,0:T(8,128)} %get-tuple-element.93.ids_ref, s32[32,1,128]{2,1,0:T(1,128)} %get-tuple-element.99.labels_ref, f32[32,1,128]{2,1,0:T(1,128)} %get-tuple-element.100.keep_ref, ...), custom_call_target="tpu_custom_call" | custom-call | flops 1000 | bytes 1000 | tf_op jit(solution)/shard_map/head_backward/pallas_call | solution.py:1511
  359.2 54.7 %reduce_all.3 = (f32[128,768]{1,0:T(8,128)}, f32[128,768]{1,0:T(8,128)}, f32[1,768]{1,0:T(1,128)}, bf16[4,128,768]{2,1,0:T(8,128)(2,1)}) custom-call(bf16[2,4,4,128,768]{4,3,2,1,0:T(8,128)(2,1)} %bitcast.78, f32[128,768]{1,0:T(8,128)} %get-tuple-element.120.refs_1_, f32[1,768]{1,0:T(1,128)} %get-tuple-element.181.refs_4_.refs_2_, f32[5]{0:T(128)} %refs_15_.2), custom_call_target="tpu_custom_call" | custom-call | flops 1000 | bytes 1000 | tf_op jit(solution)/shard_map/reduce_all/pallas_call | solution.py:876
  413.9 27.0 %inner_back_1.1 = (f32[128,768]{1,0:T(8,128)}, f32[1,768]{1,0:T(1,128)}, bf16[4,128,768]{2,1,0:T(8,128)(2,1)}, bf16[16,48,768]{2,1,0:T(8,128)(2,1)}) custom-call(bf16[4,128,768]{2,1,0:T(8,128)(2,1)} %get-tuple-element.121.refs_0_, bf16[4,128,768]{2,1,0:T(8,128)(2,1)} %get-tuple-element.111.refs_0_.refs_1_, bf16[1536,768]{1,0:T(8,128)(2,1)} %bitcast.75, ...), custom_call_target="tpu_custom_call" | custom-call | flops 1000 | bytes 1000 | tf_op jit(solution)/shard_map/inner_back_1/pallas_call | solution.py:242
  440.9 50.3 %stream_back_1.1 = (f32[128,768]{1,0:T(8,128)}, f32[128,768]{1,0:T(8,128)}, f32[1,768]{1,0:T(1,128)}, bf16[4,128,768]{2,1,0:T(8,128)(2,1)}, bf16[8,48,768]{2,1,0:T(8,128)(2,1)}, /*index=5*/bf16[16,48,768]{2,1,0:T(8,128)(2,1)}) custom-call(bf16[4,128,768]{2,1,0:T(8,128)(2,1)} %get-tuple-element.125.refs_0_, ...), custom_call_target="tpu_custom_call" | custom-call | flops 1000 | bytes 1000 | tf_op jit(solution)/shard_map/stream_back_1/pallas_call | solution.py:242
  491.3 31.3 %inner_back_0.1 = (f32[128,768]{1,0:T(8,128)}, f32[1,768]{1,0:T(1,128)}, bf16[4,128,768]{2,1,0:T(8,128)(2,1)}, bf16[16,48,768]{2,1,0:T(8,128)(2,1)}, bf16[8,48,768]{2,1,0:T(8,128)(2,1)}) custom-call(bf16[4,128,768]{2,1,0:T(8,128)(2,1)} %get-tuple-element.133.refs_0_, bf16[4,128,768]{2,1,0:T(8,128)(2,1)} %get-tuple-element.106.refs_0_.refs_1_, ...), custom_call_target="tpu_custom_call" | custom-call | flops 1000 | bytes 1000 | tf_op jit(solution)/shard_map/inner_back_0/pallas_call | solution.py:242
  522.5 47.6 %stream_back_0.1 = (f32[128,768]{1,0:T(8,128)}, f32[128,768]{1,0:T(8,128)}, f32[1,768]{1,0:T(1,128)}, bf16[128,768]{1,0:T(8,128)(2,1)}, bf16[8,48,768]{2,1,0:T(8,128)(2,1)}, /*index=5*/bf16[16,48,768]{2,1,0:T(8,128)(2,1)}) custom-call(bf16[4,128,768]{2,1,0:T(8,128)(2,1)} %get-tuple-element.138.refs_0_, ...), custom_call_target="tpu_custom_call" | custom-call | flops 1000 | bytes 1000 | tf_op jit(solution)/shard_map/stream_back_0/pallas_call | solution.py:242
  570.2 46.7 %gather_all.3 = (bf16[2,4,4,128,768]{4,3,2,1,0:T(8,128)(2,1)}, bf16[8,48,768]{2,1,0:T(8,128)(2,1)}) custom-call(bf16[128,768]{1,0:T(8,128)(2,1)} %get-tuple-element.146.refs_0_, bf16[8,48,768]{2,1,0:T(8,128)(2,1)} %get-tuple-element.147.refs_1_), custom_call_target="tpu_custom_call" | custom-call | flops 1000 | bytes 1000 | tf_op jit(solution)/shard_map/gather_all/pallas_call | solution.py:1017
  616.9 0.6 stack.23.slot_ref
  617.5 0.0 copy-start.4
  617.5 0.0 copy-start.6
  617.5 0.0 copy-start.7
  617.5 0.0 copy-start.8
  617.6 0.0 copy-start.16
  617.6 0.0 copy-start.17
  617.6 22.3 %look_back.1 = (bf16[67,48,768]{2,1,0:T(8,128)(2,1)}, f32[8,768]{1,0:T(8,128)}) custom-call(s32[128]{0:T(128)} %bitcast.85, s32[5,80]{1,0:T(8,128)} %stack.23.slot_ref, s32[3840,1]{1,0:T(8,128)} %get-tuple-element.93.ids_ref, s32[32,1,128]{2,1,0:T(1,128)} %get-tuple-element.94.tokens_ref, s32[32,1,128]{2,1,0:T(1,128)} %get-tuple-element.97.ranks_ref, ...), custom_call_target="tpu_custom_call" | custom-call | flops 1000 | bytes 1000 | tf_op jit(solution)/shard_map/look_back/pallas_call | solution.py:1868
  640.1 0.0 copy-start.9
  640.1 0.7 copy-done.9
  640.9 10.5 %finish.1 = (f32[5,768]{1,0:T(8,128)S(1)}, f32[5,768]{1,0:T(8,128)S(1)}, f32[5,768]{1,0:T(8,128)S(1)}, f32[1,5]{1,0:T(1,128)S(1)}, f32[1,5]{1,0:T(1,128)S(1)}, /...) custom-call(f32[1,768]{1,0:T(1,128)S(1)} %copy-done.15, f32[1,768]{1,0:T(1,128)S(1)} %copy-done.14, ...), custom_call_target="tpu_custom_call" | custom-call | flops 999999995904 | bytes 1073741824 | tf_op jit(solution)/shard_map/finish/pallas_call | solution.py:1365
  651.4 0.5 slice.32
  651.9 22.6 %multiply_subtract_fusion = (f32[67,48,768]{2,1,0:T(8,128)}, f32[67,48,768]{2,1,0:T(8,128)}, f32[67,48,768]{2,1,0:T(8,128)}) fusion(f32[67,48,768]{2,1,0:T(8,128)S(1)} %copy-done.19, f32[]{:T(128)} %bitcast.23, bf16[67,48,768]{2,1,0:T(8,128)(2,1)} %get-tuple-element.154, f32[67,48,768]{2,1,0:T(8,128)} %param.18, f32[67,48,768]{2,1,0:T(8,128)} %param.19), kind=kLoop, calls=%fused_computation.2 | loop fusion | flops 41988096 | bytes 64217092 | tf_op jit(solution)/shard_map/sub | solution.py:53
  674.5 0.6 fusion.16
  675.0 0.6 copy.35
  675.7 0.6 copy.36
  676.3 0.6 copy.37
  676.9 0.5 copy.38
  677.4 0.5 copy.39
  677.9 0.5 copy.40
  (39 shorter events, 0.1 us)
Async XLA Ops:
  0.6 46.0 %copy-start.5 = (f32[5,768]{1,0:T(8,128)S(1)}, f32[5,768]{1,0:T(8,128)}, u32[]{:S(2)}) copy-start(f32[5,768]{1,0:T(8,128)} %refs_14_.3) | copy-start | bytes 46084
  617.5 22.5 %copy-start = (f32[128,768]{1,0:T(8,128)S(1)}, f32[128,768]{1,0:T(8,128)}, u32[]{:S(2)}) copy-start(f32[128,768]{1,0:T(8,128)} %get-tuple-element.105.refs_5_.refs_11_) | copy-start | bytes 1179652
  617.5 22.5 %copy-start.1 = (f32[128,768]{1,0:T(8,128)S(1)}, f32[128,768]{1,0:T(8,128)}, u32[]{:S(2)}) copy-start(f32[128,768]{1,0:T(8,128)} %get-tuple-element.131.refs_13_.refs_14_.refs_9_) | copy-start | bytes 1179652
  617.5 22.5 %copy-start.2 = (f32[128,768]{1,0:T(8,128)S(1)}, f32[128,768]{1,0:T(8,128)}, u32[]{:S(2)}) copy-start(f32[128,768]{1,0:T(8,128)} %get-tuple-element.144.refs_13_.refs_8_) | copy-start | bytes 1179652
  617.5 22.5 %copy-start.3 = (f32[128,768]{1,0:T(8,128)S(1)}, f32[128,768]{1,0:T(8,128)}, u32[]{:S(2)}) copy-start(f32[128,768]{1,0:T(8,128)} %get-tuple-element.114.refs_6_) | copy-start | bytes 1179652
  617.5 22.5 %copy-start.4 = (f32[5]{0:T(128)S(1)}, f32[5]{0:T(128)}, u32[]{:S(2)}) copy-start(f32[5]{0:T(128)} %refs_15_.2) | copy-start | bytes 64
  617.5 22.5 %copy-start.6 = (f32[128,768]{1,0:T(8,128)S(1)}, f32[128,768]{1,0:T(8,128)}, u32[]{:S(2)}) copy-start(f32[128,768]{1,0:T(8,128)} %get-tuple-element.160.refs_7_) | copy-start | bytes 1179652
  617.5 22.5 %copy-start.7 = (f32[5,768]{1,0:T(8,128)S(1)}, f32[5,768]{1,0:T(8,128)}, u32[]{:S(2)}) copy-start(f32[5,768]{1,0:T(8,128)} %refs_15_.3) | copy-start | bytes 46084
  617.5 22.5 %copy-start.8 = (f32[5,768]{1,0:T(8,128)S(1)}, f32[5,768]{1,0:T(8,128)}, u32[]{:S(2)}) copy-start(f32[5,768]{1,0:T(8,128)} %refs_16_.1) | copy-start | bytes 46084
  617.6 22.5 %copy-start.10 = (f32[8,128]{1,0:T(8,128)S(1)}, f32[8,128]{1,0:T(8,128)}, u32[]{:S(2)}) copy-start(f32[8,128]{1,0:T(8,128)} %get-tuple-element.161.refs_10_) | copy-start | bytes 12292
  617.6 22.5 %copy-start.11 = (f32[1,768]{1,0:T(1,128)S(1)}, f32[1,768]{1,0:T(1,128)}, u32[]{:S(2)}) copy-start(f32[1,768]{1,0:T(1,128)} %get-tuple-element.159.refs_4_) | copy-start | bytes 9220
  617.6 22.5 %copy-start.12 = (f32[1,768]{1,0:T(1,128)S(1)}, f32[1,768]{1,0:T(1,128)}, u32[]{:S(2)}) copy-start(f32[1,768]{1,0:T(1,128)} %get-tuple-element.158.refs_3_) | copy-start | bytes 9220
  617.6 22.5 %copy-start.13 = (f32[1,768]{1,0:T(1,128)S(1)}, f32[1,768]{1,0:T(1,128)}, u32[]{:S(2)}) copy-start(f32[1,768]{1,0:T(1,128)} %get-tuple-element.157.refs_2_) | copy-start | bytes 9220
  617.6 22.5 %copy-start.14 = (f32[1,768]{1,0:T(1,128)S(1)}, f32[1,768]{1,0:T(1,128)}, u32[]{:S(2)}) copy-start(f32[1,768]{1,0:T(1,128)} %get-tuple-element.156.refs_1_) | copy-start | bytes 9220
  617.6 22.5 %copy-start.15 = (f32[1,768]{1,0:T(1,128)S(1)}, f32[1,768]{1,0:T(1,128)}, u32[]{:S(2)}) copy-start(f32[1,768]{1,0:T(1,128)} %get-tuple-element.155.refs_0_) | copy-start | bytes 9220
  617.6 22.5 %copy-start.16 = (f32[5]{0:T(128)S(1)}, f32[5]{0:T(128)}, u32[]{:S(2)}) copy-start(f32[5]{0:T(128)} %param.24) | copy-start | bytes 64
  617.6 22.5 %copy-start.17 = (f32[5]{0:T(128)S(1)}, f32[5]{0:T(128)}, u32[]{:S(2)}) copy-start(f32[5]{0:T(128)} %param.25) | copy-start | bytes 64
  617.6 22.5 %copy-start.18 = (f32[1,128]{1,0:T(1,128)S(1)}, f32[1,128]{1,0:T(1,128)}, u32[]{:S(2)}) copy-start(f32[1,128]{1,0:T(1,128)} %get-tuple-element.163.refs_13_) | copy-start | bytes 1540
  640.1 0.7 copy-start.9
  640.9 11.0 %copy-start.19 = (f32[67,48,768]{2,1,0:T(8,128)S(1)}, f32[67,48,768]{2,1,0:T(8,128)}, u32[]{:S(2)}) copy-start(f32[67,48,768]{2,1,0:T(8,128)} %master_ref.1) | copy-start | bytes 29638660
